TPU v7x, 128 devices: a whole 4x4x4 slice. The times are simulated.
128 devices in a mesh: tm: 32 (over x, y, core), expert: 4 (over z).
Axes of the slice: x: 4, y: 4, z: 4, core: 2. Of those that a mesh axis runs over, the one named last changes fastest.
Arguments:
- queries: bfloat16 [32768, 1536], P(('tm', 'expert')), may hold values from -300 to 300
- key_value: bfloat16 [2, 32768, 1536], P(None, ('tm', 'expert')), may hold values from -64 to 64
- conv_kernel: float32 [31, 1536], replicated, may hold values from -1 to 1
- conv_gain: float32 [1536], replicated, may hold values from 0.1 to 1.9
- ffn_gain: float32 [1536], replicated, may hold values from 0.1 to 1.9
- expert_gate: float32 [32768], P(('tm', 'expert')), may hold values from 0.5 to 2
- primary: int32 [32768], P(('tm', 'expert')), may hold values from 0 to 63, as said below
- secondary: int32 [32768], P(('tm', 'expert')), may hold values from 0 to 63, as said below
- overflow: int32 [32768], P(('tm', 'expert')), may hold values from 0 to 1
- slot: int32 [32768], P(('tm', 'expert')), may hold values from 0 to 5, as said below
- w_in: bfloat16 [64, 1536, 6144], P('tm', None, 'expert'), may hold values from -0.15625 to 0.15625
- w_out: bfloat16 [64, 6144, 1536], P('tm', 'expert'), may hold values from -0.078125 to 0.078125
Outputs:
- block_out: bfloat16 [32768, 1536], P(('tm', 'expert'))
Inputs may be any that keep to these rules, and one draw needn't show every extreme that they name: `primary`: differs from secondary in every frame. `secondary`: differs from primary in every frame. Among the 256 frames of one device (aligned blocks), no two with the same serving expert share a slot; so at most 6 frames of one device go to one expert, and in every draw one expert receives exactly 6 frames from every device.
All inputs are finite; a program needn't handle non-finite values.
Results may differ from a plain program's by a relative error of at most 0.012.
Values may be sent and summed in bfloat16 or wider, within the bound.
No kernel may reach another device: no remote copies, remote signals or barrier semaphores. Data moves between devices by JAX's collectives and lax.ppermute only.
A program may use at most 128 MiB of HBM per device.

v0:
```python
import math

import jax
import jax.numpy as jnp
from jax import lax
from jax.sharding import PartitionSpec as P

HEADS = 24
HALF = 256


def with_halo(block, sides, width):
    for axis, dim in sides:
        count = lax.axis_size(axis)
        forward = [(i, i + 1) for i in range(count - 1)]
        backward = [(target, source) for source, target in forward]
        low = lax.ppermute(
            lax.slice_in_dim(block, block.shape[dim] - width, None, axis=dim), axis, forward
        )
        high = lax.ppermute(lax.slice_in_dim(block, 0, width, axis=dim), axis, backward)
        block = jnp.concatenate([low, block, high], axis=dim)
    return block


def rms_scale(values, gain):
    return values * lax.rsqrt(jnp.mean(values * values, axis=-1, keepdims=True) + 1e-06) * gain


def attend(query_block, key_block, first_row, total_rows):
    block_rows, model_width = query_block.shape
    head_width = model_width // HEADS
    key_span = key_block.shape[1]
    query_heads = query_block.reshape(block_rows, HEADS, head_width)
    key_heads = key_block[0].reshape(key_span, HEADS, head_width)
    value_heads = key_block[1].reshape(key_span, HEADS, head_width)
    scores = jnp.einsum(
        "qhd,khd->hqk", query_heads, key_heads, preferred_element_type=jnp.float32
    ) / math.sqrt(head_width)
    query_pos = first_row + jnp.arange(block_rows, dtype=jnp.int32)
    key_pos = first_row - HALF + jnp.arange(key_span, dtype=jnp.int32)
    allowed = (
        (jnp.abs(query_pos[:, None] - key_pos[None, :]) < HALF)
        & (key_pos[None, :] >= 0)
        & (key_pos[None, :] < total_rows)
    )
    scores = jnp.where(allowed[None], scores, -1e30)
    highest = jnp.max(scores, axis=-1, keepdims=True)
    expos = jnp.exp(scores - highest)
    probs = (expos / jnp.sum(expos, axis=-1, keepdims=True)).astype(jnp.bfloat16)
    result = jnp.einsum("hqk,khd->qhd", probs, value_heads, preferred_element_type=jnp.float32)
    return result.reshape(block_rows, model_width)


def on_device(
    queries,
    key_value,
    conv_kernel,
    conv_gain,
    ffn_gain,
    expert_gate,
    primary,
    secondary,
    overflow,
    slot,
    w_in,
    w_out,
):
    frame_rows, model_width = queries.shape
    time_count = lax.axis_size("tm")
    group_count = lax.axis_size("expert")
    time_devices = time_count * group_count
    first_row = (lax.axis_index("tm") * group_count + lax.axis_index("expert")) * frame_rows
    extended = with_halo(key_value, ((("tm", "expert"), 1),), HALF)
    attended = attend(queries, extended, first_row, time_devices * frame_rows)
    normed = rms_scale(attended, conv_gain).astype(jnp.bfloat16)
    reach = (conv_kernel.shape[0] - 1) // 2
    padded = with_halo(normed, ((("tm", "expert"), 0),), reach)
    conv_sum = jnp.zeros((frame_rows, model_width), jnp.float32)
    for offset in range(conv_kernel.shape[0]):
        conv_sum = conv_sum + conv_kernel[offset] * padded[offset : offset + frame_rows].astype(
            jnp.float32
        )
    mixed = (normed.astype(jnp.float32) + jax.nn.silu(conv_sum)).astype(jnp.bfloat16)
    expert_in = rms_scale(mixed.astype(jnp.float32), ffn_gain).astype(jnp.bfloat16)
    served = jnp.where(overflow == 1, secondary, primary)
    group_size = w_in.shape[0]
    experts_all = group_size * time_count
    capacity = max(2, 3 * frame_rows // (2 * experts_all))
    place = slot * experts_all + served
    filled = jnp.zeros((capacity * experts_all, model_width), jnp.bfloat16).at[place].set(expert_in)
    outgoing = filled.reshape(capacity, experts_all, model_width)
    arrived = lax.all_to_all(outgoing, "tm", split_axis=1, concat_axis=0, tiled=True)
    hidden = jax.nn.silu(
        jnp.einsum(
            "red,edf->ref",
            lax.all_gather(arrived, "expert", axis=0, tiled=True),
            w_in,
            preferred_element_type=jnp.float32,
        )
    ).astype(jnp.bfloat16)
    summed = lax.psum_scatter(
        jnp.einsum("ref,efd->red", hidden, w_out, preferred_element_type=jnp.float32).astype(
            jnp.bfloat16
        ),
        "expert",
        scatter_dimension=0,
        tiled=True,
    )
    returned = lax.all_to_all(summed, "tm", split_axis=0, concat_axis=1, tiled=True)
    picked = returned.reshape(capacity * experts_all, model_width)[place]
    return (mixed.astype(jnp.float32) + expert_gate[:, None] * picked.astype(jnp.float32)).astype(
        jnp.bfloat16
    )


def solution(mesh):
    in_specs = (
        P(("tm", "expert"), None),
        P(None, ("tm", "expert"), None),
        P(),
        P(),
        P(),
        P(("tm", "expert")),
        P(("tm", "expert")),
        P(("tm", "expert")),
        P(("tm", "expert")),
        P(("tm", "expert")),
        P("tm", None, "expert"),
        P("tm", "expert", None),
    )
    out_specs = P(("tm", "expert"), None)
    return jax.shard_map(
        on_device, mesh=mesh, in_specs=in_specs, out_specs=out_specs, check_vma=False
    )
```

profile of v0, /device:TPU:1, one launch (start us, length us, event | category | flops | bytes accessed | tf_op | source)
XLA Modules:
  0.0 304.3 jit_solution(7445048938861143759)
XLA Ops:
  6.5 0.0 all-gather.2.cloned.1.call-start
  6.6 4.5 %collective-permute-start = (bf16[2,256,1536]{2,1,0:T(8,128)(2,1)}, bf16[2,256,1536]{2,1,0:T(8,128)(2,1)S(1)}, u32[]{:S(2)}, u32[]{:S(2)}) collective-permute-start(bf16[2,256,1536]{2,1,0:T(8,128)(2,1)} %param.13), channel_id=1, source_target_pairs={{0,1},{1,2},{2,3},{3,4},{4,5},{5,6},{6,7},{7,8},{8,9},{9,10},{10,1... | collective-permute-start | bytes 4718600 | tf_op jit(solution)/shard_map/ppermute | solution.py:17
  11.1 4.6 %collective-permute-start.1 = (bf16[2,256,1536]{2,1,0:T(8,128)(2,1)}, bf16[2,256,1536]{2,1,0:T(8,128)(2,1)S(1)}, u32[]{:S(2)}, u32[]{:S(2)}) collective-permute-start(bf16[2,256,1536]{2,1,0:T(8,128)(2,1)} %param.13), channel_id=1, source_target_pairs={{1,0},{2,1},{3,2},{4,3},{5,4},{6,5},{7,6},{8,7},{9,8},{10,9},{11,1... | collective-permute-start | bytes 4718600 | tf_op jit(solution)/shard_map/ppermute | solution.py:20
  15.7 2.3 copy.40
  18.0 0.0 copy-done.3
  18.0 0.9 slice_reduce_fusion.30
  19.0 0.0 copy-done.25
  19.0 0.0 copy-done.26
  19.0 0.0 copy-done.27
  19.0 0.0 copy-done.28
  19.0 0.6 compare_select_fusion
  19.5 0.7 fusion.67
  20.3 0.0 copy-start.1
  20.3 24.2 %collective-permute-done = bf16[2,256,1536]{2,1,0:T(8,128)(2,1)S(1)} collective-permute-done((bf16[2,256,1536]{2,1,0:T(8,128)(2,1)}, bf16[2,256,1536]{2,1,0:T(8,128)(2,1)S(1)}, u32[]{:S(2)}, u32[]{:S(2)}) %collective-permute-start) | collective-permute-done | bytes 1572896 | tf_op jit(solution)/shard_map/ppermute | solution.py:17
  44.5 0.1 constant_dynamic-update-slice_fusion.2
  44.6 0.0 copy-done.1
  44.6 0.1 constant_dynamic-update-slice_fusion.1
  44.7 5.5 %collective-permute-done.1 = bf16[2,256,1536]{2,1,0:T(8,128)(2,1)S(1)} collective-permute-done((bf16[2,256,1536]{2,1,0:T(8,128)(2,1)}, bf16[2,256,1536]{2,1,0:T(8,128)(2,1)S(1)}, u32[]{:S(2)}, u32[]{:S(2)}) %collective-permute-start.1) | collective-permute-done | bytes 1572896 | tf_op jit(solution)/shard_map/ppermute | solution.py:20
  50.2 0.1 constant_dynamic-update-slice_fusion
  50.3 1.7 fusion.75
  52.1 4.3 %copy.38 = bf16[1,768,1536]{1,2,0:T(8,128)(2,1)} copy(bf16[1,768,1536]{2,1,0:T(8,128)(2,1)} %get-tuple-element.39) | data formatting | bytes 4718592 | tf_op jit(solution)/shard_map/slice | solution.py:35
  56.3 2.5 copy.39
  58.8 0.0 copy-done.2
  58.8 11.8 %fusion.77 = (f32[24,256]{1,0:T(8,128)}, f32[24,256,768]{1,2,0:T(8,128)}) fusion(pred[256,768]{0,1:T(8,128)(4,1)S(1)} %fusion.67, bf16[768,24,64]{0,2,1:T(8,128)(2,1)} %bitcast.58, bf16[256,24,64]{0,2,1:T(8,128)(2,1)S(1)} %bitcast.60), kind=kOutput, calls=%fused_computation.178 | convolution fusion | flops 622854912 | bytes 22241280 | tf_op jit(solution)/shard_map/sub | solution.py:48
  70.6 0.0 copy-done
  70.6 9.3 %fusion.33 = (f32[256]{0:T(256)S(1)}, f32[24,64,256]{2,1,0:T(8,128)}) fusion(bf16[768,24,64]{0,2,1:T(8,128)(2,1)S(1)} %bitcast.57, f32[24,256,768]{1,2,0:T(8,128)} %get-tuple-element.43, f32[24,256]{1,0:T(8,128)} %get-tuple-element.42), kind=kOutput, calls=%fused_computation.74 | convolution fusion | flops 614203136 | bytes 22832128 | tf_op jit(solution)/shard_map/hqk,khd->qhd/dot_general | solution.py:50
  80.0 1.9 copy.42
  81.8 0.0 copy-start.4
  81.9 0.0 copy-start.5
  81.9 0.0 copy-start.6
  81.9 0.0 copy-start.7
  82.0 0.0 copy-done.21
  82.0 0.2 multiply_convert_fusion
  82.2 0.0 copy-start.22
  82.3 5.5 %collective-permute-start.3 = (bf16[15,1536]{1,0:T(8,128)(2,1)S(1)}, bf16[15,1536]{1,0:T(8,128)(2,1)S(1)}, u32[]{:S(2)}, u32[]{:S(2)}) collective-permute-start(bf16[15,1536]{1,0:T(8,128)(2,1)S(1)} %get-tuple-element.41), channel_id=1, source_target_pairs={{1,0},{2,1},{3,2},{4,3},{5,4},{6,5},{7,6},{8,7},{9,8},{10,9},{11,1... | collective-permute-start | bytes 138248 | tf_op jit(solution)/shard_map/ppermute | solution.py:20
  87.8 1.9 collective-permute-start.2
  89.7 0.2 slice_reduce_fusion.29
  89.9 0.0 collective-permute-done.3
  89.9 4.5 %collective-permute-done.2 = bf16[15,1536]{1,0:T(8,128)(2,1)S(1)} collective-permute-done((bf16[15,1536]{1,0:T(8,128)(2,1)S(1)}, bf16[15,1536]{1,0:T(8,128)(2,1)S(1)}, u32[]{:S(2)}, u32[]{:S(2)}) %collective-permute-start.2) | collective-permute-done | bytes 46112 | tf_op jit(solution)/shard_map/ppermute | solution.py:17
  94.4 0.0 copy-done.5
  94.6 9.4 %fusion.29 = (f32[256]{0:T(256)S(1)}, bf16[256,1536]{1,0:T(8,128)(2,1)S(1)}) fusion(bf16[15,1536]{1,0:T(8,128)(2,1)S(1)} %collective-permute-done.3, bf16[256,1536]{1,0:T(8,128)(2,1)S(1)} %multiply_convert_fusion, f32[1536]{0:T(1024)S(1)} %get-tuple-element.34, f32[1536]{0:T(1024)S(1)} %get-tuple-element.35, f32[1536]{0:T(1024)S(1)} %get-tuple-element.6, ...), kind=kLoop, calls=%fused_computation.69 | loop fusion | flops 75104000 | bytes 1856512 | tf_op jit(solution)/shard_map/reduce_sum | solution.py:26
  103.9 0.0 copy-done.22
  103.9 0.0 copy-done.23
  104.0 2.5 scatter_custom_fusion
  106.4 0.7 copy.43
  107.1 29.9 %all_to_all.33 = bf16[6,64,1536]{2,0,1:T(8,128)(2,1)S(1)} all-to-all(bf16[6,64,1536]{2,0,1:T(8,128)(2,1)S(1)} %copy.43), channel_id=1, replica_groups=mesh['tm'=32,'expert'=4] {'tm'}, dimensions={1} | all-to-all | bytes 2359296 | tf_op jit(solution)/shard_map/all_to_all | solution.py:92
  136.9 0.9 copy.51
  137.9 1.2 copy.46
  139.0 0.0 all-gather.2.cloned.1.call-update
  139.1 0.0 reduce-scatter.2.cloned.1.call-start
  139.1 47.7 %all-gather.2.cloned.1.call-done = bf16[768,2,1536]{2,0,1:T(8,128)(2,1)} async-done(((bf16[192,2,1536]{2,0,1:T(8,128)(2,1)}), bf16[768,2,1536]{2,0,1:T(8,128)(2,1)}) %all-gather.2.cloned.1.call-update) | async-done | bytes 4718608 | tf_op jit(solution)/shard_map/all_gather | solution.py:96
  186.8 12.9 %fusion.7 = bf16[768,2,1536]{2,0,1:T(8,128)(2,1)S(1)} fusion(bf16[768,2,1536]{2,0,1:T(8,128)(2,1)} %all-gather.2.cloned.1.call-done, bf16[2,1536,1536]{2,1,0:T(8,128)(2,1)} %param.22), kind=kOutput, calls=%fused_computation.14 | convolution fusion | flops 7259553792 | bytes 18874368 | tf_op jit(solution)/shard_map/red,edf->ref/dot_general | solution.py:94
  199.7 12.8 %convert_bitcast_fusion = bf16[768,2,1536]{2,0,1:T(8,128)(2,1)} fusion(bf16[768,2,1536]{2,0,1:T(8,128)(2,1)S(1)} %fusion.7, bf16[2,1536,1536]{2,1,0:T(8,128)(2,1)} %param.23), kind=kOutput, calls=%fused_computation.17 | convolution fusion | flops 7250116608 | bytes 18874368 | tf_op jit(solution)/shard_map/ref,efd->red/dot_general | solution.py:102
  212.5 0.0 reduce-scatter.2.cloned.1.call-update
  212.5 51.8 %reduce-scatter.2.cloned.1.call-done = bf16[192,2,1536]{2,0,1:T(8,128)(2,1)} async-done(((bf16[768,2,1536]{2,0,1:T(8,128)(2,1)}), bf16[192,2,1536]{2,0,1:T(8,128)(2,1)}) %reduce-scatter.2.cloned.1.call-update) | async-done | bytes 1179664 | tf_op jit(solution)/shard_map/reduce_scatter | solution.py:101
  264.3 3.5 %copy.47 = bf16[192,2,1536]{2,1,0:T(2,128)(2,1)} copy(bf16[192,2,1536]{2,0,1:T(8,128)(2,1)} %reduce-scatter.2.cloned.1.call-done) | data formatting | bytes 2359296 | tf_op jit(solution)/shard_map/reduce_scatter | solution.py:101
  267.8 7.5 %all-to-all-start.1 = ((bf16[192,2,1536]{2,1,0:T(2,128)(2,1)}), bf16[192,2,1536]{2,1,0:T(2,128)(2,1)S(1)}, u32[]{:S(2)}, u32[]{:S(2)}) async-start(bf16[192,2,1536]{2,1,0:T(2,128)(2,1)} %copy.47), calls=%async_computation.2 | async-start | bytes 2359296 | tf_op jit(solution)/shard_map/all_to_all | solution.py:109
  275.3 18.3 %all-to-all-done.1 = bf16[192,2,1536]{2,1,0:T(2,128)(2,1)S(1)} async-done(((bf16[192,2,1536]{2,1,0:T(2,128)(2,1)}), bf16[192,2,1536]{2,1,0:T(2,128)(2,1)S(1)}, u32[]{:S(2)}, u32[]{:S(2)}) %all-to-all-start.1) | async-done | bytes 1179680 | tf_op jit(solution)/shard_map/all_to_all | solution.py:109
  293.7 0.8 copy.48
  294.5 0.5 reshape.112
  295.0 0.0 copy-start.24
  295.0 1.3 gather_fusion
  296.3 0.0 copy-done.24
  296.3 1.2 fusion.32
  (45 shorter events, 0.1 us)
Async XLA Ops:
  6.5 11.5 %copy-start.3 = (f32[31,1536]{1,0:T(8,128)S(1)}, f32[31,1536]{1,0:T(8,128)}, u32[]{:S(2)}) copy-start(f32[31,1536]{1,0:T(8,128)} %param.14) | copy-start | bytes 571396
  6.5 12.4 %copy-start.25 = (s32[256]{0:T(256)S(1)}, s32[256]{0:T(256)}, u32[]{:S(2)}) copy-start(s32[256]{0:T(256)} %param.19) | copy-start | bytes 3076
  6.5 12.4 %copy-start.26 = (s32[256]{0:T(256)S(1)}, s32[256]{0:T(256)}, u32[]{:S(2)}) copy-start(s32[256]{0:T(256)} %param.18) | copy-start | bytes 3076
  6.5 12.4 %copy-start.27 = (s32[256]{0:T(256)S(1)}, s32[256]{0:T(256)}, u32[]{:S(2)}) copy-start(s32[256]{0:T(256)} %param.20) | copy-start | bytes 3076
  6.5 12.4 %copy-start.28 = (s32[256]{0:T(256)S(1)}, s32[256]{0:T(256)}, u32[]{:S(2)}) copy-start(s32[256]{0:T(256)} %param.21) | copy-start | bytes 3076
  6.5 180.3 %all-gather.2.cloned.1.call-start = ((), (), s32[]{:S(2)}) async-start(), calls=%async_computation.3 | async-start | bytes 5898240 | tf_op jit(solution)/shard_map/all_gather | solution.py:96
  6.6 37.9 %collective-permute-start = (bf16[2,256,1536]{2,1,0:T(8,128)(2,1)}, bf16[2,256,1536]{2,1,0:T(8,128)(2,1)S(1)}, u32[]{:S(2)}, u32[]{:S(2)}) collective-permute-start(bf16[2,256,1536]{2,1,0:T(8,128)(2,1)} %param.13), channel_id=1, source_target_pairs={{0,1},{1,2},{2,3},{3,4},{4,5},{5,6},{6,7},{7,8},{8,9},{9,10},{10,1... | collective-permute-start | bytes 4718600 | tf_op jit(solution)/shard_map/ppermute | solution.py:17
  11.1 39.1 %collective-permute-start.1 = (bf16[2,256,1536]{2,1,0:T(8,128)(2,1)}, bf16[2,256,1536]{2,1,0:T(8,128)(2,1)S(1)}, u32[]{:S(2)}, u32[]{:S(2)}) collective-permute-start(bf16[2,256,1536]{2,1,0:T(8,128)(2,1)} %param.13), channel_id=1, source_target_pairs={{1,0},{2,1},{3,2},{4,3},{5,4},{6,5},{7,6},{8,7},{9,8},{10,9},{11,1... | collective-permute-start | bytes 4718600 | tf_op jit(solution)/shard_map/ppermute | solution.py:20
  20.3 24.3 %copy-start.1 = (bf16[2,256,1536]{2,1,0:T(8,128)(2,1)S(1)}, bf16[2,256,1536]{2,1,0:T(8,128)(2,1)}, u32[]{:S(2)}) copy-start(bf16[2,256,1536]{2,1,0:T(8,128)(2,1)} %param.13) | copy-start | bytes 4718596
  56.3 2.5 copy-start.2
  58.8 11.8 %copy-start = (bf16[1,768,1536]{1,2,0:T(8,128)(2,1)S(1)}, bf16[1,768,1536]{1,2,0:T(8,128)(2,1)}, u32[]{:S(2)}) copy-start(bf16[1,768,1536]{1,2,0:T(8,128)(2,1)} %copy.38) | copy-start | bytes 7077892
  79.9 2.1 copy-start.21
  81.8 12.6 %copy-start.4 = (f32[1536]{0:T(1024)S(1)}, f32[1536]{0:T(1024)}, u32[]{:S(2)}) copy-start(f32[1536]{0:T(1024)} %get-tuple-element.7) | copy-start | bytes 18436
  81.9 12.6 %copy-start.5 = (f32[1536]{0:T(1024)S(1)}, f32[1536]{0:T(1024)}, u32[]{:S(2)}) copy-start(f32[1536]{0:T(1024)} %get-tuple-element.8) | copy-start | bytes 18436
  81.9 12.6 %copy-start.6 = (f32[1536]{0:T(1024)S(1)}, f32[1536]{0:T(1024)}, u32[]{:S(2)}) copy-start(f32[1536]{0:T(1024)} %get-tuple-element.9) | copy-start | bytes 18436
  81.9 12.6 %copy-start.7 = (f32[1536]{0:T(1024)S(1)}, f32[1536]{0:T(1024)}, u32[]{:S(2)}) copy-start(f32[1536]{0:T(1024)} %get-tuple-element.10) | copy-start | bytes 18436
  81.9 12.6 %copy-start.8 = (f32[1536]{0:T(1024)S(1)}, f32[1536]{0:T(1024)}, u32[]{:S(2)}) copy-start(f32[1536]{0:T(1024)} %get-tuple-element.11) | copy-start | bytes 18436
  81.9 12.6 %copy-start.9 = (f32[1536]{0:T(1024)S(1)}, f32[1536]{0:T(1024)}, u32[]{:S(2)}) copy-start(f32[1536]{0:T(1024)} %get-tuple-element.12) | copy-start | bytes 18436
  81.9 12.6 %copy-start.10 = (f32[1536]{0:T(1024)S(1)}, f32[1536]{0:T(1024)}, u32[]{:S(2)}) copy-start(f32[1536]{0:T(1024)} %get-tuple-element.13) | copy-start | bytes 18436
  81.9 12.6 %copy-start.11 = (f32[1536]{0:T(1024)S(1)}, f32[1536]{0:T(1024)}, u32[]{:S(2)}) copy-start(f32[1536]{0:T(1024)} %get-tuple-element.14) | copy-start | bytes 18436
  81.9 12.6 %copy-start.12 = (f32[1536]{0:T(1024)S(1)}, f32[1536]{0:T(1024)}, u32[]{:S(2)}) copy-start(f32[1536]{0:T(1024)} %get-tuple-element.15) | copy-start | bytes 18436
  81.9 12.6 %copy-start.13 = (f32[1536]{0:T(1024)S(1)}, f32[1536]{0:T(1024)}, u32[]{:S(2)}) copy-start(f32[1536]{0:T(1024)} %get-tuple-element.16) | copy-start | bytes 18436
  81.9 12.6 %copy-start.14 = (f32[1536]{0:T(1024)S(1)}, f32[1536]{0:T(1024)}, u32[]{:S(2)}) copy-start(f32[1536]{0:T(1024)} %get-tuple-element.17) | copy-start | bytes 18436
  82.0 12.6 %copy-start.15 = (f32[1536]{0:T(1024)S(1)}, f32[1536]{0:T(1024)}, u32[]{:S(2)}) copy-start(f32[1536]{0:T(1024)} %get-tuple-element.18) | copy-start | bytes 18436
  82.0 12.6 %copy-start.16 = (f32[1536]{0:T(1024)S(1)}, f32[1536]{0:T(1024)}, u32[]{:S(2)}) copy-start(f32[1536]{0:T(1024)} %get-tuple-element.19) | copy-start | bytes 18436
  82.0 12.6 %copy-start.17 = (f32[1536]{0:T(1024)S(1)}, f32[1536]{0:T(1024)}, u32[]{:S(2)}) copy-start(f32[1536]{0:T(1024)} %get-tuple-element.20) | copy-start | bytes 18436
  82.0 12.6 %copy-start.18 = (f32[1536]{0:T(1024)S(1)}, f32[1536]{0:T(1024)}, u32[]{:S(2)}) copy-start(f32[1536]{0:T(1024)} %get-tuple-element.21) | copy-start | bytes 18436
  82.0 12.6 %copy-start.19 = (f32[1536]{0:T(1024)S(1)}, f32[1536]{0:T(1024)}, u32[]{:S(2)}) copy-start(f32[1536]{0:T(1024)} %get-tuple-element.22) | copy-start | bytes 18436
  82.0 12.6 %copy-start.20 = (f32[1536]{0:T(1024)S(1)}, f32[1536]{0:T(1024)}, u32[]{:S(2)}) copy-start(f32[1536]{0:T(1024)} %get-tuple-element.23) | copy-start | bytes 18436
  82.2 21.7 %copy-start.22 = (f32[1536]{0:T(1024)S(1)}, f32[1536]{0:T(1024)}, u32[]{:S(2)}) copy-start(f32[1536]{0:T(1024)} %param.16) | copy-start | bytes 18436
  82.3 21.7 %copy-start.23 = (s32[256]{0:T(256)S(1)}, s32[256]{0:T(256)}, u32[]{:S(2)}) copy-start(s32[256]{0:T(256)} %compare_select_fusion) | copy-start | bytes 3076
  82.3 7.6 %collective-permute-start.3 = (bf16[15,1536]{1,0:T(8,128)(2,1)S(1)}, bf16[15,1536]{1,0:T(8,128)(2,1)S(1)}, u32[]{:S(2)}, u32[]{:S(2)}) collective-permute-start(bf16[15,1536]{1,0:T(8,128)(2,1)S(1)} %get-tuple-element.41), channel_id=1, source_target_pairs={{1,0},{2,1},{3,2},{4,3},{5,4},{6,5},{7,6},{8,7},{9,8},{10,9},{11,1... | collective-permute-start | bytes 138248 | tf_op jit(solution)/shard_map/ppermute | solution.py:20
  87.8 6.6 %collective-permute-start.2 = (bf16[15,1536]{1,0:T(8,128)(2,1)S(1)}, bf16[15,1536]{1,0:T(8,128)(2,1)S(1)}, u32[]{:S(2)}, u32[]{:S(2)}) collective-permute-start(bf16[15,1536]{1,0:T(8,128)(2,1)S(1)} %get-tuple-element.40), channel_id=1, source_target_pairs={{0,1},{1,2},{2,3},{3,4},{4,5},{5,6},{6,7},{7,8},{8,9},{9,10},{10,1... | collective-permute-start | bytes 138248 | tf_op jit(solution)/shard_map/ppermute | solution.py:17
  139.1 125.3 %reduce-scatter.2.cloned.1.call-start = ((), (), s32[]{:S(2)}) async-start(), calls=%async_computation.4 | async-start | bytes 5898240 | tf_op jit(solution)/shard_map/reduce_scatter | solution.py:101
  267.8 25.8 %all-to-all-start.1 = ((bf16[192,2,1536]{2,1,0:T(2,128)(2,1)}), bf16[192,2,1536]{2,1,0:T(2,128)(2,1)S(1)}, u32[]{:S(2)}, u32[]{:S(2)}) async-start(bf16[192,2,1536]{2,1,0:T(2,128)(2,1)} %copy.47), calls=%async_computation.2 | async-start | bytes 2359296 | tf_op jit(solution)/shard_map/all_to_all | solution.py:109
  295.0 1.3 copy-start.24
Sparse Core Ops, SparseCore 0:
  139.2 47.5 all-gather.1
  212.6 51.6 reduce-scatter.1
where the time goes:
time: 305 us; the launch traced here: 304 us
  waiting for transfers between devices  152 us (50%)
  matrix products  46.8 us (15%)
  blocking collectives  29.9 us (10%)
  starting transfers between devices  24.1 us (8%)
  local copies, waits for them, and re-layouts  23 us (8%)
  other arithmetic  14.5 us (5%)
  between operations  13.9 us (5%)
    reduce_scatter x1, waiting for transfers between devices, on_device(): lax.psum_scatter(jnp.einsum('ref,efd->red', hidden, w_out, preferred_elem...  51.8 us
    all_gather x1, waiting for transfers between devices, on_device(): lax.all_gather(arrived, 'expert', axis=0, tiled=True)  47.7 us
    all_to_all x1, blocking collectives, on_device(): lax.all_to_all(outgoing, 'tm', split_axis=1, concat_axis=0, tiled=True)  29.9 us
    ppermute x2, waiting for transfers between devices, with_halo(): lax.ppermute(lax.slice_in_dim(block, block.shape[dim] - width, None, axis...  28.7 us
    all_to_all x1, waiting for transfers between devices, on_device(): lax.all_to_all(summed, 'tm', split_axis=0, concat_axis=1, tiled=True)  18.3 us
    dot_general x1, matrix products, on_device(): jnp.einsum('red,edf->ref', lax.all_gather(arrived, 'expert', axis=0, tile...  12.9 us
    dot_general x1, matrix products, on_device(): jnp.einsum('ref,efd->red', hidden, w_out, preferred_element_type=jnp.floa...  12.8 us
    sub x1, matrix products, attend(): expos = jnp.exp(scores - highest)  11.8 us
  transfers between devices with their start and end apart: 7, of which 6 were waited for; matrix products, arithmetic and copies ran while one was open for 2% of the time, Pallas kernels for 0%

commit v1 on v0

v1 whole, which is shorter than its diff:
```python
import functools

import jax
import jax.numpy as jnp
from jax import lax
from jax.experimental import pallas as pl
from jax.experimental.pallas import tpu as pltpu
from jax.sharding import PartitionSpec as P

HEAD = 64
PAIR = 2 * HEAD
HALF = 256
TILE = 128
SPAN = 2 * HALF + TILE
EDGE = 16
GROUPS = (3, 3, 3, 3)
CHUNKS = 3
F32 = jnp.float32
BF16 = jnp.bfloat16


def call(body, out_shape, cost, **kw):
    flops, moved = cost
    return pl.pallas_call(
        body,
        out_shape=out_shape,
        cost_estimate=pl.CostEstimate(flops=flops, bytes_accessed=moved, transcendentals=0),
        compiler_params=pltpu.CompilerParams(vmem_limit_bytes=40 * 1024 * 1024),
        **kw,
    )


def attend_pair(edge_ref, q_ref, kv_ref, lo_ref, hi_ref, bias):
    @pl.when(pl.program_id(0) == 0)
    def _():
        row = lax.broadcasted_iota(jnp.int32, (TILE, SPAN), 0)
        col = lax.broadcasted_iota(jnp.int32, (TILE, SPAN), 1)
        for r in range(2):
            low = jnp.where(edge_ref[0] == 1, HALF - TILE * r, 0)
            high = jnp.where(edge_ref[1] == 1, 2 * HALF - TILE * r, SPAN)
            kept = (col > row) & (col - row < 2 * HALF) & (col >= low) & (col < high)
            bias[r] = jnp.where(kept, 0.0, -1e30)

    keys = jnp.concatenate([lo_ref[0], kv_ref[0], hi_ref[0]], axis=0)
    values = jnp.concatenate([lo_ref[1], kv_ref[1], hi_ref[1]], axis=0)
    q = q_ref[...]
    lane = lax.broadcasted_iota(jnp.int32, (1, PAIR), 1)
    first = lane < HEAD
    parts = [[], []]
    for h in range(2):
        mine = first if h == 0 else jnp.logical_not(first)
        qh = q * jnp.where(mine, 0.125, 0.0).astype(BF16)
        vh = values * jnp.where(mine, 1.0, 0.0).astype(BF16) + jnp.where(mine, 0.0, 1.0).astype(BF16)
        for r in range(2):
            rows = slice(r * TILE, r * TILE + TILE)
            span = slice(r * TILE, r * TILE + SPAN)
            s = lax.dot_general(
                qh[rows], keys[span], (((1,), (1,)), ((), ())), preferred_element_type=F32
            )
            s = s + bias[r]
            p = jnp.exp(s - jnp.max(s, axis=1, keepdims=True)).astype(BF16)
            parts[r].append(jnp.dot(p, vh[span], preferred_element_type=F32))
    halves = []
    for o0, o1 in parts:
        below = pltpu.roll(jnp.where(first, o1, o0), HEAD, 1)
        halves.append(jnp.where(first, o0, o1) / below)
    return halves


def attend_body(edge_ref, q_ref, kv_ref, lo_ref, hi_ref, out_ref, bias):
    for r, half in enumerate(attend_pair(edge_ref, q_ref, kv_ref, lo_ref, hi_ref, bias)):
        out_ref[r * TILE : (r + 1) * TILE] = half


def attend_norm_body(groups, edge_ref, q_ref, kv_ref, lo_ref, hi_ref, gain_ref, *rest):
    n = len(groups)
    earlier, (out_ref, low_ref, high_ref, bias, mine) = rest[:n], rest[n:]
    step = pl.program_id(0)
    for r, half in enumerate(attend_pair(edge_ref, q_ref, kv_ref, lo_ref, hi_ref, bias)):
        mine[step, r * TILE : (r + 1) * TILE] = half

    @pl.when(step == pl.num_programs(0) - 1)
    def _():
        blocks = [(ref, c) for ref, g in zip(earlier, groups) for c in range(g)]
        pieces = [(lambda ref=ref, c=c: ref[:, c * PAIR : (c + 1) * PAIR]) for ref, c in blocks]
        pieces += [(lambda c=c: mine[c]) for c in range(mine.shape[0])]
        total = jnp.zeros((2 * TILE, PAIR), F32)
        for piece in pieces:
            v = piece()
            total = total + v * v
        width = len(pieces) * PAIR
        scale = lax.rsqrt(jnp.sum(total, axis=1, keepdims=True) * (1.0 / width) + 1e-6)
        for c, piece in enumerate(pieces):
            cols = slice(c * PAIR, (c + 1) * PAIR)
            out_ref[:, cols] = (piece() * scale * gain_ref[:, cols]).astype(BF16)
        low_ref[...] = out_ref[:EDGE]
        high_ref[...] = out_ref[2 * TILE - EDGE :]


def attention(queries, key_value, low, high, edge, conv_gain):
    rows, width = queries.shape
    outs = []
    start = 0
    for g, pairs in enumerate(GROUPS):
        last = g == len(GROUPS) - 1
        base = [
            pl.BlockSpec(memory_space=pltpu.SMEM),
            pl.BlockSpec((rows, PAIR), lambda j, s=start: (0, s + j)),
            pl.BlockSpec((2, rows, PAIR), lambda j, s=start: (0, 0, s + j)),
            pl.BlockSpec((2, rows, PAIR), lambda j: (0, 0, j)),
            pl.BlockSpec((2, rows, PAIR), lambda j: (0, 0, j)),
        ]
        scratch = [pltpu.VMEM((2, TILE, SPAN), F32)]
        cost = (pairs * 16 * rows * SPAN * PAIR, pairs * 7 * rows * PAIR * 2)
        args = (edge, queries, key_value, low[g], high[g])
        if not last:
            outs.append(
                call(
                    attend_body,
                    jax.ShapeDtypeStruct((rows, pairs * PAIR), F32),
                    cost,
                    grid=(pairs,),
                    in_specs=base,
                    out_specs=pl.BlockSpec((rows, PAIR), lambda j: (0, j)),
                    scratch_shapes=scratch,
                )(*args)
            )
        else:
            whole = lambda *shape: pl.BlockSpec(shape, lambda j: (0,) * len(shape))
            return call(
                functools.partial(attend_norm_body, GROUPS[:-1]),
                [
                    jax.ShapeDtypeStruct((rows, width), BF16),
                    jax.ShapeDtypeStruct((EDGE, width), BF16),
                    jax.ShapeDtypeStruct((EDGE, width), BF16),
                ],
                cost,
                grid=(pairs,),
                in_specs=base + [whole(1, width)] + [whole(*o.shape) for o in outs],
                out_specs=[whole(rows, width), whole(EDGE, width), whole(EDGE, width)],
                scratch_shapes=scratch + [pltpu.VMEM((pairs, rows, PAIR), F32)],
            )(*args, conv_gain[None], *outs)
        start += pairs


def silu(v):
    return v / (1.0 + jnp.exp(-v))


def conv_rows(source, taps, first, count):
    total = jnp.zeros((count, PAIR), F32)
    for k in range(taps.shape[0]):
        total = total + taps[k : k + 1] * source[first + k : first + k + count]
    return source[first + 15 : first + 15 + count] + silu(total)


def inner_conv_body(normed_ref, taps_ref, out_ref, wide):
    wide[...] = normed_ref[...].astype(F32)
    count = 32
    for t in range(0, out_ref.shape[0], count):
        out_ref[t : t + count] = conv_rows(wide, taps_ref, EDGE + t - 15, count).astype(BF16)


def inner_conv(normed, taps):
    rows, width = normed.shape
    inner = rows - 2 * EDGE
    return call(
        inner_conv_body,
        jax.ShapeDtypeStruct((inner, width), BF16),
        (62 * inner * width * 64, 4 * rows * width),
        grid=(width // PAIR,),
        in_specs=[
            pl.BlockSpec((rows, PAIR), lambda j: (0, j)),
            pl.BlockSpec((taps.shape[0], PAIR), lambda j: (0, j)),
        ],
        out_specs=pl.BlockSpec((inner, PAIR), lambda j: (0, j)),
        scratch_shapes=[pltpu.VMEM((rows, PAIR), F32)],
    )(normed, taps)


def dispatch_body(normed_ref, inner_ref, low_ref, high_ref, taps_ref, gain_ref, place_ref, *rest):
    mixed_ref, outs, (wide,) = rest[0], rest[1:-1], rest[-1:]
    rows, width = normed_ref.shape
    for c in range(width // PAIR):
        cols = slice(c * PAIR, (c + 1) * PAIR)
        wide[0, :EDGE] = low_ref[:, cols].astype(F32)
        wide[0, EDGE:] = normed_ref[: 2 * EDGE, cols].astype(F32)
        wide[1, : 2 * EDGE] = normed_ref[rows - 2 * EDGE :, cols].astype(F32)
        wide[1, 2 * EDGE :] = high_ref[:, cols].astype(F32)
        taps = taps_ref.at[:, cols]
        mixed_ref[:EDGE, cols] = conv_rows(wide.at[0], taps, 1, EDGE).astype(BF16)
        mixed_ref[rows - EDGE :, cols] = conv_rows(wide.at[1], taps, 1, EDGE).astype(BF16)
    mixed_ref[EDGE : rows - EDGE] = inner_ref[...]
    mixed = mixed_ref[...].astype(F32)
    scale = lax.rsqrt(jnp.mean(mixed * mixed, axis=1, keepdims=True) + 1e-6)
    expert_in = (mixed * scale * gain_ref[...]).astype(BF16)
    first = 0
    for out_ref in outs:
        count = out_ref.shape[0]
        place = first + lax.broadcasted_iota(jnp.int32, (count, rows), 0)
        pick = jnp.where(place == place_ref[...], 1.0, 0.0).astype(BF16)
        out_ref[...] = jnp.dot(pick, expert_in, preferred_element_type=F32).astype(BF16)
        first += count


def dispatch(normed, inner, low, high, taps, gain, place, count):
    rows, width = normed.shape
    return call(
        dispatch_body,
        [jax.ShapeDtypeStruct((rows, width), BF16)]
        + [jax.ShapeDtypeStruct((count, width), BF16)] * CHUNKS,
        (2 * CHUNKS * count * rows * width, 8 * rows * width),
        scratch_shapes=[pltpu.VMEM((2, 3 * EDGE, PAIR), F32)],
    )(normed, inner, low, high, taps, gain[None], place[None])


def combine_body(mixed_ref, gate_ref, place_ref, *rest):
    parts, out_ref = rest[:-1], rest[-1]
    rows = mixed_ref.shape[0]
    total = None
    first = 0
    for part in parts:
        count = part.shape[0]
        place = first + lax.broadcasted_iota(jnp.int32, (rows, count), 1)
        pick = jnp.where(place == place_ref[...], 1.0, 0.0).astype(BF16)
        got = jnp.dot(pick, part[...], preferred_element_type=F32)
        total = got if total is None else total + got
        first += count
    out_ref[...] = (mixed_ref[...].astype(F32) + gate_ref[...] * total).astype(BF16)


def combine(mixed, gate, place, parts):
    rows, width = mixed.shape
    block = 256
    column = lambda n: pl.BlockSpec((n, block), lambda j: (0, j))
    fixed = pl.BlockSpec((rows, 1), lambda j: (0, 0))
    return call(
        combine_body,
        jax.ShapeDtypeStruct((rows, width), BF16),
        (2 * sum(p.shape[0] for p in parts) * rows * width, 8 * rows * width),
        grid=(width // block,),
        in_specs=[column(rows), fixed, fixed] + [column(p.shape[0]) for p in parts],
        out_specs=column(rows),
    )(mixed, gate[:, None], place[:, None], *parts)


def ffn_body(own, left, right, far0, far1, w_in, w_out, keep, up, down, up2, down2, rows_in, total):
    e, f = pl.program_id(0), pl.program_id(1)
    n = own.shape[1]

    @pl.when(f == 0)
    def _():
        rows_in[:n] = own[0]
        rows_in[n : 2 * n] = left[0]
        rows_in[2 * n : 3 * n] = right[0]

    @pl.when((f == 0) & (e == 0))
    def _():
        rows_in[3 * n :] = far0[...]

    @pl.when((f == 0) & (e == 1))
    def _():
        rows_in[3 * n :] = far1[...]

    hidden = silu(jnp.dot(rows_in[...], w_in[0], preferred_element_type=F32)).astype(BF16)
    part = jnp.dot(hidden, w_out[0], preferred_element_type=F32)

    @pl.when(f == 0)
    def _():
        total[...] = part

    @pl.when(f > 0)
    def _():
        total[...] += part

    done = f == pl.num_programs(1) - 1

    @pl.when(done)
    def _():
        keep[0] = total[:n].astype(BF16)

    @pl.when(done & (e == 0))
    def _():
        down[1] = total[n : 2 * n].astype(BF16)
        up2[...] = total[2 * n : 3 * n].astype(BF16)
        up[0] = total[3 * n :].astype(BF16)

    @pl.when(done & (e == 1))
    def _():
        down2[...] = total[n : 2 * n].astype(BF16)
        up[1] = total[2 * n : 3 * n].astype(BF16)
        down[0] = total[3 * n :].astype(BF16)


def ffn(own, left, right, far0, far1, w_in, w_out):
    experts, n, width = own.shape
    units = w_in.shape[2]
    step = 512
    each = pl.BlockSpec((1, n, width), lambda e, f: (e, 0, 0))
    both = pl.BlockSpec((2, n, width), lambda e, f: (0, 0, 0))
    one = pl.BlockSpec((n, width), lambda e, f: (0, 0))
    pair = jax.ShapeDtypeStruct((2, n, width), BF16)
    single = jax.ShapeDtypeStruct((n, width), BF16)
    return call(
        ffn_body,
        [pair, pair, pair, single, single],
        (experts * 4 * n * width * units * 4, 2 * experts * width * units * 2),
        grid=(experts, units // step),
        in_specs=[
            each,
            each,
            each,
            one,
            one,
            pl.BlockSpec((1, width, step), lambda e, f: (e, 0, f)),
            pl.BlockSpec((1, step, width), lambda e, f: (e, f, 0)),
        ],
        out_specs=[each, both, both, one, one],
        scratch_shapes=[pltpu.VMEM((4 * n, width), BF16), pltpu.VMEM((4 * n, width), F32)],
    )(own, left, right, far0, far1, w_in, w_out)


def on_device(
    queries,
    key_value,
    conv_kernel,
    conv_gain,
    ffn_gain,
    expert_gate,
    primary,
    secondary,
    overflow,
    slot,
    w_in,
    w_out,
):
    frame_rows, width = queries.shape
    time_count = lax.axis_size("tm")
    group_count = lax.axis_size("expert")
    devices = time_count * group_count
    index = lax.axis_index("tm") * group_count + lax.axis_index("expert")
    edge = jnp.stack([index == 0, index == devices - 1]).astype(jnp.int32)
    order = ("tm", "expert")
    onward = [(i, i + 1) for i in range(devices - 1)]
    back = [(i + 1, i) for i in range(devices - 1)]

    low, high = [], []
    start = 0
    for pairs in GROUPS:
        part = lax.slice_in_dim(key_value, start * PAIR, (start + pairs) * PAIR, axis=2)
        low.append(lax.ppermute(part, order, onward))
        high.append(lax.ppermute(part, order, back))
        start += pairs
    normed, first_rows, last_rows = attention(queries, key_value, low, high, edge, conv_gain)

    before = lax.ppermute(last_rows, order, onward)
    after = lax.ppermute(first_rows, order, back)
    inner = inner_conv(normed, conv_kernel)

    local = w_in.shape[0]
    experts = local * time_count
    slots = max(2, 3 * frame_rows // (2 * experts)) // CHUNKS
    count = experts * slots
    served = jnp.where(overflow == 1, secondary, primary)
    place = (slot // slots) * count + served * slots + slot % slots
    mixed, *chunks = dispatch(
        normed, inner, before, after, conv_kernel, ffn_gain, place, count
    )

    up = [(i, (i + 1) % group_count) for i in range(group_count)]
    down = [((i + 1) % group_count, i) for i in range(group_count)]
    returned = []
    for chunk in chunks:
        sent = chunk.reshape(time_count, local * slots, width)
        own = lax.all_to_all(sent, "tm", split_axis=0, concat_axis=0, tiled=True)
        own = own.reshape(time_count, local, slots, width).transpose(1, 0, 2, 3)
        own = own.reshape(local, time_count * slots, width)
        left = lax.ppermute(own, "expert", up)
        right = lax.ppermute(own, "expert", down)
        far0 = lax.ppermute(left[0], "expert", up)
        far1 = lax.ppermute(right[1], "expert", down)
        keep, go_up, go_down, up2, down2 = ffn(own, left, right, far0, far1, w_in, w_out)
        from_below = lax.ppermute(go_up, "expert", up)
        from_above = lax.ppermute(go_down, "expert", down)
        add = lambda *vs: sum(v.astype(F32) for v in vs).astype(BF16)
        up3 = lax.ppermute(add(up2, from_below[0]), "expert", up)
        down3 = lax.ppermute(add(down2, from_above[0]), "expert", down)
        summed = jnp.stack(
            [add(keep[0], from_above[1], up3), add(keep[1], from_below[1], down3)]
        )
        summed = summed.reshape(local, time_count, slots, width).transpose(1, 0, 2, 3)
        summed = summed.reshape(time_count, local * slots, width)
        got = lax.all_to_all(summed, "tm", split_axis=0, concat_axis=0, tiled=True)
        returned.append(got.reshape(count, width))
    return combine(mixed, expert_gate, place, returned)


def solution(mesh):
    in_specs = (
        P(("tm", "expert"), None),
        P(None, ("tm", "expert"), None),
        P(),
        P(),
        P(),
        P(("tm", "expert")),
        P(("tm", "expert")),
        P(("tm", "expert")),
        P(("tm", "expert")),
        P(("tm", "expert")),
        P("tm", None, "expert"),
        P("tm", "expert", None),
    )
    out_specs = P(("tm", "expert"), None)
    return jax.shard_map(
        on_device, mesh=mesh, in_specs=in_specs, out_specs=out_specs, check_vma=False
    )
```

time: 305 us -> 270 us (0.89)
  waiting for transfers between devices: 152 us -> 56.4 us
  starting transfers between devices: 24.1 us -> 116 us
  Pallas kernels: 0 us -> 62.2 us
  matrix products: 46.8 us -> 0 us
  blocking collectives: 29.9 us -> 0 us
  between operations: 13.9 us -> 0.74 us
  other arithmetic: 14.5 us -> 11.1 us
    pallas_call x0 -> x10, Pallas kernels: none -> 62.2 us  [the longest x3 32.7 us: ffn(): call(ffn_body, [pair, pair, pair, single, single], (experts * 4 * n * wid...]
    ppermute x4 -> x34, starting transfers between devices: 16.5 us -> 68.7 us  [the longest x4 19.2 us: on_device(): high.append(lax.ppermute(part, order, back))]
    reduce_scatter x1 -> x0, waiting for transfers between devices: 51.8 us -> none  [on_device(): lax.psum_scatter(jnp.einsum('ref,efd->red', hidden, w_out, preferred_elem...]
    all_gather x1 -> x0, waiting for transfers between devices: 47.7 us -> none  [on_device(): lax.all_gather(arrived, 'expert', axis=0, tiled=True)]
    all_to_all x1 -> x6, starting transfers between devices: 7.48 us -> 47.1 us  [the longest x3 26.1 us: on_device(): own = lax.all_to_all(sent, 'tm', split_axis=0, concat_axis=0, tiled=True)]
    dot_general x3 -> x0, matrix products: 35 us -> none  [the longest x1 12.9 us: on_device(): jnp.einsum('red,edf->ref', lax.all_gather(arrived, 'expert', axis=0, tile...]
    all_to_all x1 -> x0, blocking collectives: 29.9 us -> none  [on_device(): lax.all_to_all(outgoing, 'tm', split_axis=1, concat_axis=0, tiled=True)]
    all_to_all x1 -> x6, waiting for transfers between devices: 18.3 us -> 44.8 us  [the longest x3 23.8 us: on_device(): got = lax.all_to_all(summed, 'tm', split_axis=0, concat_axis=0, tiled=True)]
  transfers between devices with their start and end apart: 7 -> 40, of which waited for: 6 -> 12; matrix products, arithmetic and copies ran while one was open for 2% -> 8% of each run, Pallas kernels for 0% -> 19%
where the time goes in v1:
time: 270 us; the launch traced here: 268 us
  starting transfers between devices  116 us (43%)
  Pallas kernels  62.2 us (23%)
  waiting for transfers between devices  56.4 us (21%)
  local copies, waits for them, and re-layouts  22 us (8%)
  other arithmetic  11.1 us (4%)
    pallas_call x3, Pallas kernels, ffn(): call(ffn_body, [pair, pair, pair, single, single], (experts * 4 * n * wid...  32.7 us
    all_to_all x3, starting transfers between devices, on_device(): own = lax.all_to_all(sent, 'tm', split_axis=0, concat_axis=0, tiled=True)  26.1 us
    all_to_all x3, waiting for transfers between devices, on_device(): got = lax.all_to_all(summed, 'tm', split_axis=0, concat_axis=0, tiled=True)  23.8 us
    all_to_all x3, waiting for transfers between devices, on_device(): own = lax.all_to_all(sent, 'tm', split_axis=0, concat_axis=0, tiled=True)  21.1 us
    all_to_all x3, starting transfers between devices, on_device(): got = lax.all_to_all(summed, 'tm', split_axis=0, concat_axis=0, tiled=True)  21 us
    ppermute x4, starting transfers between devices, on_device(): high.append(lax.ppermute(part, order, back))  19.2 us
    pallas_call x3, Pallas kernels, attention(): call(attend_body, jax.ShapeDtypeStruct((rows, pairs * PAIR), F32), cost,...  15.6 us
    ppermute x3, starting transfers between devices, on_device(): right = lax.ppermute(own, 'expert', down)  10.2 us
  transfers between devices with their start and end apart: 40, of which 12 were waited for; matrix products, arithmetic and copies ran while one was open for 8% of the time, Pallas kernels for 19%

profile of v1, /device:TPU:1, one launch (start us, length us, event | category | flops | bytes accessed | tf_op | source)
XLA Modules:
  0.0 268.3 jit_solution(1139066113313962883)
XLA Ops:
  0.0 2.5 fusion.15
  2.5 4.4 %collective-permute-start.4 = (bf16[2,256,384]{2,1,0:T(8,128)(2,1)}, bf16[2,256,384]{2,1,0:T(8,128)(2,1)S(1)}, u32[]{:S(2)}, u32[]{:S(2)}) collective-permute-start(bf16[2,256,384]{2,1,0:T(8,128)(2,1)} %get-tuple-element.50), channel_id=1, source_target_pairs={{0,1},{1,2},{2,3},{3,4},{4,5},{5,6},{6,7},{7,8},{8,9},{9,10},{10,1... | collective-permute-start | bytes 1179656 | tf_op jit(solution)/shard_map/ppermute | solution.py:351
  6.8 4.6 %collective-permute-start.5 = (bf16[2,256,384]{2,1,0:T(8,128)(2,1)}, bf16[2,256,384]{2,1,0:T(8,128)(2,1)S(1)}, u32[]{:S(2)}, u32[]{:S(2)}) collective-permute-start(bf16[2,256,384]{2,1,0:T(8,128)(2,1)} %get-tuple-element.50), channel_id=1, source_target_pairs={{1,0},{2,1},{3,2},{4,3},{5,4},{6,5},{7,6},{8,7},{9,8},{10,9},{11,1... | collective-permute-start | bytes 1179656 | tf_op jit(solution)/shard_map/ppermute | solution.py:352
  11.4 1.9 collective-permute-start.6
  13.4 4.9 %collective-permute-start.7 = (bf16[2,256,384]{2,1,0:T(8,128)(2,1)}, bf16[2,256,384]{2,1,0:T(8,128)(2,1)S(1)}, u32[]{:S(2)}, u32[]{:S(2)}) collective-permute-start(bf16[2,256,384]{2,1,0:T(8,128)(2,1)} %get-tuple-element.49), channel_id=1, source_target_pairs={{1,0},{2,1},{3,2},{4,3},{5,4},{6,5},{7,6},{8,7},{9,8},{10,9},{11,1... | collective-permute-start | bytes 1179656 | tf_op jit(solution)/shard_map/ppermute | solution.py:352
  18.2 1.9 collective-permute-start.2
  20.2 4.9 %collective-permute-start.3 = (bf16[2,256,384]{2,1,0:T(8,128)(2,1)S(1)}, bf16[2,256,384]{2,1,0:T(8,128)(2,1)S(1)}, u32[]{:S(2)}, u32[]{:S(2)}) collective-permute-start(bf16[2,256,384]{2,1,0:T(8,128)(2,1)S(1)} %get-tuple-element.51), channel_id=1, source_target_pairs={{1,0},{2,1},{3,2},{4,3},{5,4},{6,5},{7,6},{8,7},{9,8},{10,9},{11,1... | collective-permute-start | bytes 1179656 | tf_op jit(solution)/shard_map/ppermute | solution.py:352
  27.2 1.9 collective-permute-start
  29.1 4.9 %collective-permute-start.1 = (bf16[2,256,384]{2,1,0:T(8,128)(2,1)S(1)}, bf16[2,256,384]{2,1,0:T(8,128)(2,1)S(1)}, u32[]{:S(2)}, u32[]{:S(2)}) collective-permute-start(bf16[2,256,384]{2,1,0:T(8,128)(2,1)S(1)} %get-tuple-element.52), channel_id=1, source_target_pairs={{1,0},{2,1},{3,2},{4,3},{5,4},{6,5},{7,6},{8,7},{9,8},{10,9},{11,1... | collective-permute-start | bytes 1179656 | tf_op jit(solution)/shard_map/ppermute | solution.py:352
  34.1 1.4 copy-done.1
  35.5 1.1 copy-done.2
  36.6 5.2 %shard_map.119.rest_1_ = f32[256,384]{1,0:T(8,128)S(1)} custom-call(s32[2]{0:T(128)S(1)} %add_convert_fusion.edge_ref, bf16[256,1536]{1,0:T(8,128)(2,1)S(1)} %copy-done.2, bf16[2,256,1536]{2,1,0:T(8,128)(2,1)S(1)} %copy-done.1, bf16[2,256,384]{2,1,0:T(8,128)(2,1)S(1)} %collective-permute-done.4.lo_ref, bf16[2,256,384]{2,1,0:T(8,128)(2,1)S(1)} %collective-permute-done.5.hi_ref), custom_call_target="tpu_custom_call" | custom-call | flops 1006632960 | bytes 1376256 | tf_op jit(solution)/shard_map/pallas_call | solution.py:118
  41.8 5.2 %shard_map.120.rest_2_ = f32[256,384]{1,0:T(8,128)S(1)} custom-call(s32[2]{0:T(128)S(1)} %add_convert_fusion.edge_ref, bf16[256,1536]{1,0:T(8,128)(2,1)S(1)} %copy-done.2, bf16[2,256,1536]{2,1,0:T(8,128)(2,1)S(1)} %copy-done.1, bf16[2,256,384]{2,1,0:T(8,128)(2,1)S(1)} %collective-permute-done.6.lo_ref, bf16[2,256,384]{2,1,0:T(8,128)(2,1)S(1)} %collective-permute-done.7.hi_ref), custom_call_target="tpu_custom_call" | custom-call | flops 1006632960 | bytes 1376256 | tf_op jit(solution)/shard_map/pallas_call | solution.py:118
  47.1 5.2 %shard_map.118.rest_0_ = f32[256,384]{1,0:T(8,128)S(1)} custom-call(s32[2]{0:T(128)S(1)} %add_convert_fusion.edge_ref, bf16[256,1536]{1,0:T(8,128)(2,1)S(1)} %copy-done.2, bf16[2,256,1536]{2,1,0:T(8,128)(2,1)S(1)} %copy-done.1, bf16[2,256,384]{2,1,0:T(8,128)(2,1)S(1)} %collective-permute-done.2.lo_ref, bf16[2,256,384]{2,1,0:T(8,128)(2,1)S(1)} %collective-permute-done.3.hi_ref), custom_call_target="tpu_custom_call" | custom-call | flops 1006632960 | bytes 1376256 | tf_op jit(solution)/shard_map/pallas_call | solution.py:118
  52.3 5.5 %shard_map.121 = (bf16[256,1536]{1,0:T(8,128)(2,1)S(1)}, bf16[16,1536]{1,0:T(8,128)(2,1)S(1)}, bf16[16,1536]{1,0:T(8,128)(2,1)S(1)}) custom-call(s32[2]{0:T(128)S(1)} %add_convert_fusion.edge_ref, bf16[256,1536]{1,0:T(8,128)(2,1)S(1)} %copy-done.2, bf16[2,256,1536]{2,1,0:T(8,128)(2,1)S(1)} %copy-done.1, ...), custom_call_target="tpu_custom_call" | custom-call | flops 1006632960 | bytes 1376256 | tf_op jit(solution)/shard_map/pallas_call | solution.py:130
  57.9 1.9 collective-permute-start.8
  59.8 4.9 %collective-permute-start.9 = (bf16[16,1536]{1,0:T(8,128)(2,1)S(1)}, bf16[16,1536]{1,0:T(8,128)(2,1)S(1)}, u32[]{:S(2)}, u32[]{:S(2)}) collective-permute-start(bf16[16,1536]{1,0:T(8,128)(2,1)S(1)} %get-tuple-element.29), channel_id=1, source_target_pairs={{1,0},{2,1},{3,2},{4,3},{5,4},{6,5},{7,6},{8,7},{9,8},{10,9},{11,1... | collective-permute-start | bytes 147464 | tf_op jit(solution)/shard_map/ppermute | solution.py:357
  64.7 3.7 %shard_map.122.inner_ref = bf16[224,1536]{1,0:T(8,128)(2,1)S(1)} custom-call(bf16[256,1536]{1,0:T(8,128)(2,1)S(1)} %get-tuple-element.27.normed_ref, f32[31,1536]{1,0:T(8,128)S(1)} %copy-done.7), custom_call_target="tpu_custom_call" | custom-call | flops 1365245952 | bytes 1572864 | tf_op jit(solution)/shard_map/pallas_call | solution.py:167
  68.4 1.4 shard_map.123
  69.8 0.9 copy-done.3
  70.6 0.8 reshape.100
  71.5 18.8 %all-to-all-start.4 = ((bf16[32,4,1536]{2,1,0:T(4,128)(2,1)}), bf16[32,4,1536]{2,1,0:T(4,128)(2,1)S(1)}, u32[]{:S(2)}, u32[]{:S(2)}) async-start(bf16[32,4,1536]{2,1,0:T(4,128)(2,1)} %reshape.100), calls=%async_computation.4 | async-start | bytes 786432 | tf_op jit(solution)/shard_map/all_to_all | solution.py:375
  90.3 0.9 reshape.95
  91.1 9.4 %all-to-all-done.4 = bf16[32,4,1536]{2,1,0:T(4,128)(2,1)S(1)} async-done(((bf16[32,4,1536]{2,1,0:T(4,128)(2,1)}), bf16[32,4,1536]{2,1,0:T(4,128)(2,1)S(1)}, u32[]{:S(2)}, u32[]{:S(2)}) %all-to-all-start.4) | async-done | bytes 393248 | tf_op jit(solution)/shard_map/all_to_all | solution.py:375
  100.6 3.7 %all-to-all-start.2 = ((bf16[32,4,1536]{2,1,0:T(4,128)(2,1)}), bf16[32,4,1536]{2,1,0:T(4,128)(2,1)S(1)}, u32[]{:S(2)}, u32[]{:S(2)}) async-start(bf16[32,4,1536]{2,1,0:T(4,128)(2,1)} %reshape.95), calls=%async_computation.2 | async-start | bytes 786432 | tf_op jit(solution)/shard_map/all_to_all | solution.py:375
  105.0 0.8 reshape.90
  105.8 8.6 %all-to-all-done.2 = bf16[32,4,1536]{2,1,0:T(4,128)(2,1)S(1)} async-done(((bf16[32,4,1536]{2,1,0:T(4,128)(2,1)}), bf16[32,4,1536]{2,1,0:T(4,128)(2,1)S(1)}, u32[]{:S(2)}, u32[]{:S(2)}) %all-to-all-start.2) | async-done | bytes 393248 | tf_op jit(solution)/shard_map/all_to_all | solution.py:375
  114.4 3.7 %all-to-all-start = ((bf16[32,4,1536]{2,1,0:T(4,128)(2,1)}), bf16[32,4,1536]{2,1,0:T(4,128)(2,1)S(1)}, u32[]{:S(2)}, u32[]{:S(2)}) async-start(bf16[32,4,1536]{2,1,0:T(4,128)(2,1)} %reshape.90), calls=%async_computation | async-start | bytes 786432 | tf_op jit(solution)/shard_map/all_to_all | solution.py:375
  118.1 3.8 %collective-permute-start.27 = (bf16[2,64,1536]{2,1,0:T(8,128)(2,1)S(1)}, bf16[2,64,1536]{2,1,0:T(8,128)(2,1)S(1)}, u32[]{:S(2)}, u32[]{:S(2)}) collective-permute-start(bf16[2,64,1536]{2,1,0:T(8,128)(2,1)S(1)} %reshape.102.own), channel_id=1, source_target_pairs={{1,0},{2,1},{3,2},{0,3},{5,4},{6,5},{7,6},{4,7},{9,8},{10,9},{11,1... | collective-permute-start | bytes 1179656 | tf_op jit(solution)/shard_map/ppermute | solution.py:379
  122.6 2.7 collective-permute-start.19
  125.3 3.0 %all-to-all-done = bf16[32,4,1536]{2,1,0:T(4,128)(2,1)S(1)} async-done(((bf16[32,4,1536]{2,1,0:T(4,128)(2,1)}), bf16[32,4,1536]{2,1,0:T(4,128)(2,1)S(1)}, u32[]{:S(2)}, u32[]{:S(2)}) %all-to-all-start) | async-done | bytes 393248 | tf_op jit(solution)/shard_map/all_to_all | solution.py:375
  129.0 3.7 %collective-permute-start.11 = (bf16[2,64,1536]{2,1,0:T(8,128)(2,1)S(1)}, bf16[2,64,1536]{2,1,0:T(8,128)(2,1)S(1)}, u32[]{:S(2)}, u32[]{:S(2)}) collective-permute-start(bf16[2,64,1536]{2,1,0:T(8,128)(2,1)S(1)} %reshape.92.own), channel_id=1, source_target_pairs={{1,0},{2,1},{3,2},{0,3},{5,4},{6,5},{7,6},{4,7},{9,8},{10,9},{11,1... | collective-permute-start | bytes 1179656 | tf_op jit(solution)/shard_map/ppermute | solution.py:379
  132.9 1.2 collective-permute-done.18.left
  134.1 1.5 collective-permute-start.29
  135.6 3.1 %collective-permute-done.19.right = bf16[2,64,1536]{2,1,0:T(8,128)(2,1)S(1)} collective-permute-done((bf16[2,64,1536]{2,1,0:T(8,128)(2,1)S(1)}, bf16[2,64,1536]{2,1,0:T(8,128)(2,1)S(1)}, u32[]{:S(2)}, u32[]{:S(2)}) %collective-permute-start.19) | collective-permute-done | bytes 393248 | tf_op jit(solution)/shard_map/ppermute | solution.py:379
  139.4 3.1 %collective-permute-done.10.left = bf16[2,64,1536]{2,1,0:T(8,128)(2,1)S(1)} collective-permute-done((bf16[2,64,1536]{2,1,0:T(8,128)(2,1)S(1)}, bf16[2,64,1536]{2,1,0:T(8,128)(2,1)S(1)}, u32[]{:S(2)}, u32[]{:S(2)}) %collective-permute-start.10) | collective-permute-done | bytes 393248 | tf_op jit(solution)/shard_map/ppermute | solution.py:378
  142.6 0.9 collective-permute-start.21
  143.5 3.7 %collective-permute-done.11.right = bf16[2,64,1536]{2,1,0:T(8,128)(2,1)S(1)} collective-permute-done((bf16[2,64,1536]{2,1,0:T(8,128)(2,1)S(1)}, bf16[2,64,1536]{2,1,0:T(8,128)(2,1)S(1)}, u32[]{:S(2)}, u32[]{:S(2)}) %collective-permute-start.11) | collective-permute-done | bytes 393248 | tf_op jit(solution)/shard_map/ppermute | solution.py:379
  147.9 3.4 %collective-permute-start.13 = (bf16[64,1536]{1,0:T(8,128)(2,1)}, bf16[64,1536]{1,0:T(8,128)(2,1)S(1)}, u32[]{:S(2)}, u32[]{:S(2)}) collective-permute-start(bf16[64,1536]{1,0:T(8,128)(2,1)} %slice_bitcast_fusion.10), channel_id=1, source_target_pairs={{1,0},{2,1},{3,2},{0,3},{5,4},{6,5},{7,6},{4,7},{9,8},{10,9},{11,1... | collective-permute-start | bytes 589832 | tf_op jit(solution)/shard_map/ppermute | solution.py:381
  151.4 3.7 %copy-done = bf16[2,1536,1536]{2,1,0:T(8,128)(2,1)S(1)} copy-done((bf16[2,1536,1536]{2,1,0:T(8,128)(2,1)S(1)}, bf16[2,1536,1536]{2,1,0:T(8,128)(2,1)}, u32[]{:S(2)}) %copy-start) | copy-done | bytes 9437208
  155.1 11.0 %shard_map.126 = (bf16[2,64,1536]{2,1,0:T(8,128)(2,1)S(1)}, bf16[2,64,1536]{2,1,0:T(8,128)(2,1)}, bf16[2,64,1536]{2,1,0:T(8,128)(2,1)}, bf16[64,1536]{1,0:T(8,128)(2,1)S(1)}, bf16[64,1536]{1,0:T(8,128)(2,1)S(1)}) custom-call(bf16[2,64,1536]{2,1,0:T(8,128)(2,1)S(1)} %reshape.102.own, bf16[2,64,1536]{2,1,0:T(8,128)(2,1)S(1)} %collective-permute-done.26.left, ...), custom_call_target="tpu_custom_call" | custom-call | flops 4831838208 | bytes 18874368 | tf_op jit(solution)/shard_map/pallas_call | solution.py:304
  166.1 3.4 %collective-permute-start.30 = (bf16[2,64,1536]{2,1,0:T(8,128)(2,1)}, bf16[2,64,1536]{2,1,0:T(8,128)(2,1)}, u32[]{:S(2)}, u32[]{:S(2)}) collective-permute-start(bf16[2,64,1536]{2,1,0:T(8,128)(2,1)} %get-tuple-element.45), channel_id=1, source_target_pairs={{1,0},{2,1},{3,2},{0,3},{5,4},{6,5},{7,6},{4,7},{9,8},{10,9},{11,1... | collective-permute-start | bytes 1179656 | tf_op jit(solution)/shard_map/ppermute | solution.py:384
  169.6 11.6 %shard_map.125 = (bf16[2,64,1536]{2,1,0:T(8,128)(2,1)S(1)}, bf16[2,64,1536]{2,1,0:T(8,128)(2,1)}, bf16[2,64,1536]{2,1,0:T(8,128)(2,1)}, bf16[64,1536]{1,0:T(8,128)(2,1)S(1)}, bf16[64,1536]{1,0:T(8,128)(2,1)S(1)}) custom-call(bf16[2,64,1536]{2,1,0:T(8,128)(2,1)S(1)} %reshape.97.own, bf16[2,64,1536]{2,1,0:T(8,128)(2,1)S(1)} %collective-permute-done.18.left, ...), custom_call_target="tpu_custom_call" | custom-call | flops 4831838208 | bytes 18874368 | tf_op jit(solution)/shard_map/pallas_call | solution.py:304
  181.8 2.0 collective-permute-start.22
  183.9 10.1 %shard_map.124 = (bf16[2,64,1536]{2,1,0:T(8,128)(2,1)S(1)}, bf16[2,64,1536]{2,1,0:T(8,128)(2,1)S(1)}, bf16[2,64,1536]{2,1,0:T(8,128)(2,1)S(1)}, bf16[64,1536]{1,0:T(8,128)(2,1)S(1)}, bf16[64,1536]{1,0:T(8,128)(2,1)S(1)}) custom-call(bf16[2,64,1536]{2,1,0:T(8,128)(2,1)S(1)} %reshape.92.own, bf16[2,64,1536]{2,1,0:T(8,128)(2,1)S(1)} %collective-permute-done.10.left, ...), custom_call_target="tpu_custom_call" | custom-call | flops 4831838208 | bytes 18874368 | tf_op jit(solution)/shard_map/pallas_call | solution.py:304
  194.0 2.7 %collective-permute-start.14 = (bf16[2,64,1536]{2,1,0:T(8,128)(2,1)S(1)}, bf16[2,64,1536]{2,1,0:T(8,128)(2,1)S(1)}, u32[]{:S(2)}, u32[]{:S(2)}) collective-permute-start(bf16[2,64,1536]{2,1,0:T(8,128)(2,1)S(1)} %get-tuple-element.33), channel_id=1, source_target_pairs={{1,0},{2,1},{3,2},{0,3},{5,4},{6,5},{7,6},{4,7},{9,8},{10,9},{11,1... | collective-permute-start | bytes 1179656 | tf_op jit(solution)/shard_map/ppermute | solution.py:384
  196.7 1.0 fusion
  197.7 2.7 %collective-permute-start.33 = (bf16[64,1536]{1,0:T(8,128)(2,1)S(1)}, bf16[64,1536]{1,0:T(8,128)(2,1)S(1)}, u32[]{:S(2)}, u32[]{:S(2)}) collective-permute-start(bf16[64,1536]{1,0:T(8,128)(2,1)S(1)} %fusion), channel_id=1, source_target_pairs={{1,0},{2,1},{3,2},{0,3},{5,4},{6,5},{7,6},{4,7},{9,8},{10,9},{11,1... | collective-permute-start | bytes 589832 | tf_op jit(solution)/shard_map/ppermute | solution.py:387
  200.5 1.0 fusion.1
  202.3 2.6 collective-permute-start.25
  206.4 2.7 collective-permute-start.17
  210.0 1.2 fusion.7
  212.3 0.9 reshape.103
  213.2 13.7 %all-to-all-start.5 = ((bf16[32,4,1536]{2,1,0:T(4,128)(2,1)}), bf16[32,4,1536]{2,1,0:T(4,128)(2,1)S(1)}, u32[]{:S(2)}, u32[]{:S(2)}) async-start(bf16[32,4,1536]{2,1,0:T(4,128)(2,1)} %reshape.103), calls=%async_computation.5 | async-start | bytes 786432 | tf_op jit(solution)/shard_map/all_to_all | solution.py:393
  226.9 1.3 fusion.9
  229.1 0.9 reshape.98
  230.1 7.1 %all-to-all-done.5 = bf16[32,4,1536]{2,1,0:T(4,128)(2,1)S(1)} async-done(((bf16[32,4,1536]{2,1,0:T(4,128)(2,1)}), bf16[32,4,1536]{2,1,0:T(4,128)(2,1)S(1)}, u32[]{:S(2)}, u32[]{:S(2)}) %all-to-all-start.5) | async-done | bytes 393248 | tf_op jit(solution)/shard_map/all_to_all | solution.py:393
  237.2 3.7 %all-to-all-start.3 = ((bf16[32,4,1536]{2,1,0:T(4,128)(2,1)}), bf16[32,4,1536]{2,1,0:T(4,128)(2,1)S(1)}, u32[]{:S(2)}, u32[]{:S(2)}) async-start(bf16[32,4,1536]{2,1,0:T(4,128)(2,1)} %reshape.98), calls=%async_computation.3 | async-start | bytes 786432 | tf_op jit(solution)/shard_map/all_to_all | solution.py:393
  240.8 1.3 fusion.11
  243.1 0.9 reshape.93
  244.0 7.0 %all-to-all-done.3 = bf16[32,4,1536]{2,1,0:T(4,128)(2,1)S(1)} async-done(((bf16[32,4,1536]{2,1,0:T(4,128)(2,1)}), bf16[32,4,1536]{2,1,0:T(4,128)(2,1)S(1)}, u32[]{:S(2)}, u32[]{:S(2)}) %all-to-all-start.3) | async-done | bytes 393248 | tf_op jit(solution)/shard_map/all_to_all | solution.py:393
  251.0 3.7 %all-to-all-start.1 = ((bf16[32,4,1536]{2,1,0:T(4,128)(2,1)}), bf16[32,4,1536]{2,1,0:T(4,128)(2,1)S(1)}, u32[]{:S(2)}, u32[]{:S(2)}) async-start(bf16[32,4,1536]{2,1,0:T(4,128)(2,1)} %reshape.93), calls=%async_computation.1 | async-start | bytes 786432 | tf_op jit(solution)/shard_map/all_to_all | solution.py:393
  255.2 9.7 %all-to-all-done.1 = bf16[32,4,1536]{2,1,0:T(4,128)(2,1)S(1)} async-done(((bf16[32,4,1536]{2,1,0:T(4,128)(2,1)}), bf16[32,4,1536]{2,1,0:T(4,128)(2,1)S(1)}, u32[]{:S(2)}, u32[]{:S(2)}) %all-to-all-start.1) | async-done | bytes 393248 | tf_op jit(solution)/shard_map/all_to_all | solution.py:393
  265.0 3.3 %shard_map.127 = bf16[256,1536]{1,0:T(8,128)(2,1)} custom-call(bf16[256,1536]{1,0:T(8,128)(2,1)S(1)} %copy-done.4, f32[256,1]{1,0:T(8,128)S(1)} %copy.36.gate_ref, s32[256,1]{1,0:T(8,128)S(1)} %copy.37.place_ref, bf16[128,1536]{1,0:T(8,128)(2,1)S(1)} %reshape.94.rest_0_, bf16[128,1536]{1,0:T(8,128)(2,1)S(1)} %reshape.99.rest_1_, ...), custom_call_target="tpu_custom_call" | custom-call | flops 301989888 | bytes 3145728 | tf_op jit(solution)/shard_map/pallas_call | solution.py:237
  (109 shorter events, 13.5 us)
Async XLA Ops:
  0.0 64.6 %copy-start.7 = (f32[31,1536]{1,0:T(8,128)S(1)}, f32[31,1536]{1,0:T(8,128)}, u32[]{:S(2)}) copy-start(f32[31,1536]{1,0:T(8,128)} %taps_ref.3) | copy-start | bytes 571396
  2.5 17.7 %collective-permute-start.4 = (bf16[2,256,384]{2,1,0:T(8,128)(2,1)}, bf16[2,256,384]{2,1,0:T(8,128)(2,1)S(1)}, u32[]{:S(2)}, u32[]{:S(2)}) collective-permute-start(bf16[2,256,384]{2,1,0:T(8,128)(2,1)} %get-tuple-element.50), channel_id=1, source_target_pairs={{0,1},{1,2},{2,3},{3,4},{4,5},{5,6},{6,7},{7,8},{8,9},{9,10},{10,1... | collective-permute-start | bytes 1179656 | tf_op jit(solution)/shard_map/ppermute | solution.py:351
  6.8 20.4 %collective-permute-start.5 = (bf16[2,256,384]{2,1,0:T(8,128)(2,1)}, bf16[2,256,384]{2,1,0:T(8,128)(2,1)S(1)}, u32[]{:S(2)}, u32[]{:S(2)}) collective-permute-start(bf16[2,256,384]{2,1,0:T(8,128)(2,1)} %get-tuple-element.50), channel_id=1, source_target_pairs={{1,0},{2,1},{3,2},{4,3},{5,4},{6,5},{7,6},{8,7},{9,8},{10,9},{11,1... | collective-permute-start | bytes 1179656 | tf_op jit(solution)/shard_map/ppermute | solution.py:352
  11.4 17.7 %collective-permute-start.6 = (bf16[2,256,384]{2,1,0:T(8,128)(2,1)}, bf16[2,256,384]{2,1,0:T(8,128)(2,1)S(1)}, u32[]{:S(2)}, u32[]{:S(2)}) collective-permute-start(bf16[2,256,384]{2,1,0:T(8,128)(2,1)} %get-tuple-element.49), channel_id=1, source_target_pairs={{0,1},{1,2},{2,3},{3,4},{4,5},{5,6},{6,7},{7,8},{8,9},{9,10},{10,1... | collective-permute-start | bytes 1179656 | tf_op jit(solution)/shard_map/ppermute | solution.py:351
  13.4 28.4 %collective-permute-start.7 = (bf16[2,256,384]{2,1,0:T(8,128)(2,1)}, bf16[2,256,384]{2,1,0:T(8,128)(2,1)S(1)}, u32[]{:S(2)}, u32[]{:S(2)}) collective-permute-start(bf16[2,256,384]{2,1,0:T(8,128)(2,1)} %get-tuple-element.49), channel_id=1, source_target_pairs={{1,0},{2,1},{3,2},{4,3},{5,4},{6,5},{7,6},{8,7},{9,8},{10,9},{11,1... | collective-permute-start | bytes 1179656 | tf_op jit(solution)/shard_map/ppermute | solution.py:352
  18.2 28.8 %collective-permute-start.2 = (bf16[2,256,384]{2,1,0:T(8,128)(2,1)S(1)}, bf16[2,256,384]{2,1,0:T(8,128)(2,1)S(1)}, u32[]{:S(2)}, u32[]{:S(2)}) collective-permute-start(bf16[2,256,384]{2,1,0:T(8,128)(2,1)S(1)} %get-tuple-element.51), channel_id=1, source_target_pairs={{0,1},{1,2},{2,3},{3,4},{4,5},{5,6},{6,7},{7,8},{8,9},{9,10},{10,1... | collective-permute-start | bytes 1179656 | tf_op jit(solution)/shard_map/ppermute | solution.py:351
  20.2 26.9 %collective-permute-start.3 = (bf16[2,256,384]{2,1,0:T(8,128)(2,1)S(1)}, bf16[2,256,384]{2,1,0:T(8,128)(2,1)S(1)}, u32[]{:S(2)}, u32[]{:S(2)}) collective-permute-start(bf16[2,256,384]{2,1,0:T(8,128)(2,1)S(1)} %get-tuple-element.51), channel_id=1, source_target_pairs={{1,0},{2,1},{3,2},{4,3},{5,4},{6,5},{7,6},{8,7},{9,8},{10,9},{11,1... | collective-permute-start | bytes 1179656 | tf_op jit(solution)/shard_map/ppermute | solution.py:352
  27.2 25.1 %collective-permute-start = (bf16[2,256,384]{2,1,0:T(8,128)(2,1)S(1)}, bf16[2,256,384]{2,1,0:T(8,128)(2,1)S(1)}, u32[]{:S(2)}, u32[]{:S(2)}) collective-permute-start(bf16[2,256,384]{2,1,0:T(8,128)(2,1)S(1)} %get-tuple-element.52), channel_id=1, source_target_pairs={{0,1},{1,2},{2,3},{3,4},{4,5},{5,6},{6,7},{7,8},{8,9},{9,10},{10,1... | collective-permute-start | bytes 1179656 | tf_op jit(solution)/shard_map/ppermute | solution.py:351
  29.1 23.2 %collective-permute-start.1 = (bf16[2,256,384]{2,1,0:T(8,128)(2,1)S(1)}, bf16[2,256,384]{2,1,0:T(8,128)(2,1)S(1)}, u32[]{:S(2)}, u32[]{:S(2)}) collective-permute-start(bf16[2,256,384]{2,1,0:T(8,128)(2,1)S(1)} %get-tuple-element.52), channel_id=1, source_target_pairs={{1,0},{2,1},{3,2},{4,3},{5,4},{6,5},{7,6},{8,7},{9,8},{10,9},{11,1... | collective-permute-start | bytes 1179656 | tf_op jit(solution)/shard_map/ppermute | solution.py:352
  34.1 1.4 copy-start.1
  35.5 1.1 copy-start.2
  57.9 10.5 %collective-permute-start.8 = (bf16[16,1536]{1,0:T(8,128)(2,1)S(1)}, bf16[16,1536]{1,0:T(8,128)(2,1)S(1)}, u32[]{:S(2)}, u32[]{:S(2)}) collective-permute-start(bf16[16,1536]{1,0:T(8,128)(2,1)S(1)} %get-tuple-element.28), channel_id=1, source_target_pairs={{0,1},{1,2},{2,3},{3,4},{4,5},{5,6},{6,7},{7,8},{8,9},{9,10},{10,1... | collective-permute-start | bytes 147464 | tf_op jit(solution)/shard_map/ppermute | solution.py:356
  59.8 8.6 %collective-permute-start.9 = (bf16[16,1536]{1,0:T(8,128)(2,1)S(1)}, bf16[16,1536]{1,0:T(8,128)(2,1)S(1)}, u32[]{:S(2)}, u32[]{:S(2)}) collective-permute-start(bf16[16,1536]{1,0:T(8,128)(2,1)S(1)} %get-tuple-element.29), channel_id=1, source_target_pairs={{1,0},{2,1},{3,2},{4,3},{5,4},{6,5},{7,6},{8,7},{9,8},{10,9},{11,1... | collective-permute-start | bytes 147464 | tf_op jit(solution)/shard_map/ppermute | solution.py:357
  69.7 0.9 copy-start.3
  71.5 29.1 %all-to-all-start.4 = ((bf16[32,4,1536]{2,1,0:T(4,128)(2,1)}), bf16[32,4,1536]{2,1,0:T(4,128)(2,1)S(1)}, u32[]{:S(2)}, u32[]{:S(2)}) async-start(bf16[32,4,1536]{2,1,0:T(4,128)(2,1)} %reshape.100), calls=%async_computation.4 | async-start | bytes 786432 | tf_op jit(solution)/shard_map/all_to_all | solution.py:375
  100.6 13.9 %all-to-all-start.2 = ((bf16[32,4,1536]{2,1,0:T(4,128)(2,1)}), bf16[32,4,1536]{2,1,0:T(4,128)(2,1)S(1)}, u32[]{:S(2)}, u32[]{:S(2)}) async-start(bf16[32,4,1536]{2,1,0:T(4,128)(2,1)} %reshape.95), calls=%async_computation.2 | async-start | bytes 786432 | tf_op jit(solution)/shard_map/all_to_all | solution.py:375
  104.9 24.1 %collective-permute-start.26 = (bf16[2,64,1536]{2,1,0:T(8,128)(2,1)S(1)}, bf16[2,64,1536]{2,1,0:T(8,128)(2,1)S(1)}, u32[]{:S(2)}, u32[]{:S(2)}) collective-permute-start(bf16[2,64,1536]{2,1,0:T(8,128)(2,1)S(1)} %reshape.102.own), channel_id=1, source_target_pairs={{0,1},{1,2},{2,3},{3,0},{4,5},{5,6},{6,7},{7,4},{8,9},{9,10},{10,1... | collective-permute-start | bytes 1179656 | tf_op jit(solution)/shard_map/ppermute | solution.py:378
  114.4 13.9 %all-to-all-start = ((bf16[32,4,1536]{2,1,0:T(4,128)(2,1)}), bf16[32,4,1536]{2,1,0:T(4,128)(2,1)S(1)}, u32[]{:S(2)}, u32[]{:S(2)}) async-start(bf16[32,4,1536]{2,1,0:T(4,128)(2,1)} %reshape.90), calls=%async_computation | async-start | bytes 786432 | tf_op jit(solution)/shard_map/all_to_all | solution.py:375
  118.1 14.7 %collective-permute-start.27 = (bf16[2,64,1536]{2,1,0:T(8,128)(2,1)S(1)}, bf16[2,64,1536]{2,1,0:T(8,128)(2,1)S(1)}, u32[]{:S(2)}, u32[]{:S(2)}) collective-permute-start(bf16[2,64,1536]{2,1,0:T(8,128)(2,1)S(1)} %reshape.102.own), channel_id=1, source_target_pairs={{1,0},{2,1},{3,2},{0,3},{5,4},{6,5},{7,6},{4,7},{9,8},{10,9},{11,1... | collective-permute-start | bytes 1179656 | tf_op jit(solution)/shard_map/ppermute | solution.py:379
  122.5 11.6 %collective-permute-start.18 = (bf16[2,64,1536]{2,1,0:T(8,128)(2,1)S(1)}, bf16[2,64,1536]{2,1,0:T(8,128)(2,1)S(1)}, u32[]{:S(2)}, u32[]{:S(2)}) collective-permute-start(bf16[2,64,1536]{2,1,0:T(8,128)(2,1)S(1)} %reshape.97.own), channel_id=1, source_target_pairs={{0,1},{1,2},{2,3},{3,0},{4,5},{5,6},{6,7},{7,4},{8,9},{9,10},{10,1... | collective-permute-start | bytes 1179656 | tf_op jit(solution)/shard_map/ppermute | solution.py:378
  122.6 16.2 %collective-permute-start.19 = (bf16[2,64,1536]{2,1,0:T(8,128)(2,1)S(1)}, bf16[2,64,1536]{2,1,0:T(8,128)(2,1)S(1)}, u32[]{:S(2)}, u32[]{:S(2)}) collective-permute-start(bf16[2,64,1536]{2,1,0:T(8,128)(2,1)S(1)} %reshape.97.own), channel_id=1, source_target_pairs={{1,0},{2,1},{3,2},{0,3},{5,4},{6,5},{7,6},{4,7},{9,8},{10,9},{11,1... | collective-permute-start | bytes 1179656 | tf_op jit(solution)/shard_map/ppermute | solution.py:379
  128.9 13.6 %collective-permute-start.10 = (bf16[2,64,1536]{2,1,0:T(8,128)(2,1)S(1)}, bf16[2,64,1536]{2,1,0:T(8,128)(2,1)S(1)}, u32[]{:S(2)}, u32[]{:S(2)}) collective-permute-start(bf16[2,64,1536]{2,1,0:T(8,128)(2,1)S(1)} %reshape.92.own), channel_id=1, source_target_pairs={{0,1},{1,2},{2,3},{3,0},{4,5},{5,6},{6,7},{7,4},{8,9},{9,10},{10,1... | collective-permute-start | bytes 1179656 | tf_op jit(solution)/shard_map/ppermute | solution.py:378
  129.0 18.2 %collective-permute-start.11 = (bf16[2,64,1536]{2,1,0:T(8,128)(2,1)S(1)}, bf16[2,64,1536]{2,1,0:T(8,128)(2,1)S(1)}, u32[]{:S(2)}, u32[]{:S(2)}) collective-permute-start(bf16[2,64,1536]{2,1,0:T(8,128)(2,1)S(1)} %reshape.92.own), channel_id=1, source_target_pairs={{1,0},{2,1},{3,2},{0,3},{5,4},{6,5},{7,6},{4,7},{9,8},{10,9},{11,1... | collective-permute-start | bytes 1179656 | tf_op jit(solution)/shard_map/ppermute | solution.py:379
  132.8 15.1 %collective-permute-start.28 = (bf16[64,1536]{1,0:T(8,128)(2,1)S(1)}, bf16[64,1536]{1,0:T(8,128)(2,1)S(1)}, u32[]{:S(2)}, u32[]{:S(2)}) collective-permute-start(bf16[64,1536]{1,0:T(8,128)(2,1)S(1)} %slice_bitcast_fusion.3), channel_id=1, source_target_pairs={{0,1},{1,2},{2,3},{3,0},{4,5},{5,6},{6,7},{7,4},{8,9},{9,10},{10,1... | collective-permute-start | bytes 589832 | tf_op jit(solution)/shard_map/ppermute | solution.py:380
  134.1 17.3 %collective-permute-start.29 = (bf16[64,1536]{1,0:T(8,128)(2,1)S(1)}, bf16[64,1536]{1,0:T(8,128)(2,1)S(1)}, u32[]{:S(2)}, u32[]{:S(2)}) collective-permute-start(bf16[64,1536]{1,0:T(8,128)(2,1)S(1)} %slice_bitcast_fusion.2), channel_id=1, source_target_pairs={{1,0},{2,1},{3,2},{0,3},{5,4},{6,5},{7,6},{4,7},{9,8},{10,9},{11,1... | collective-permute-start | bytes 589832 | tf_op jit(solution)/shard_map/ppermute | solution.py:381
  138.8 30.7 %collective-permute-start.20 = (bf16[64,1536]{1,0:T(8,128)(2,1)S(1)}, bf16[64,1536]{1,0:T(8,128)(2,1)S(1)}, u32[]{:S(2)}, u32[]{:S(2)}) collective-permute-start(bf16[64,1536]{1,0:T(8,128)(2,1)S(1)} %slice_bitcast_fusion.7), channel_id=1, source_target_pairs={{0,1},{1,2},{2,3},{3,0},{4,5},{5,6},{6,7},{7,4},{8,9},{9,10},{10,1... | collective-permute-start | bytes 589832 | tf_op jit(solution)/shard_map/ppermute | solution.py:380
  142.6 27.0 %collective-permute-start.21 = (bf16[64,1536]{1,0:T(8,128)(2,1)}, bf16[64,1536]{1,0:T(8,128)(2,1)S(1)}, u32[]{:S(2)}, u32[]{:S(2)}) collective-permute-start(bf16[64,1536]{1,0:T(8,128)(2,1)} %slice_bitcast_fusion.6), channel_id=1, source_target_pairs={{1,0},{2,1},{3,2},{0,3},{5,4},{6,5},{7,6},{4,7},{9,8},{10,9},{11,1... | collective-permute-start | bytes 589832 | tf_op jit(solution)/shard_map/ppermute | solution.py:381
  147.2 36.7 %collective-permute-start.12 = (bf16[64,1536]{1,0:T(8,128)(2,1)S(1)}, bf16[64,1536]{1,0:T(8,128)(2,1)S(1)}, u32[]{:S(2)}, u32[]{:S(2)}) collective-permute-start(bf16[64,1536]{1,0:T(8,128)(2,1)S(1)} %slice_bitcast_fusion.11), channel_id=1, source_target_pairs={{0,1},{1,2},{2,3},{3,0},{4,5},{5,6},{6,7},{7,4},{8,9},{9,10},{10,1... | collective-permute-start | bytes 589832 | tf_op jit(solution)/shard_map/ppermute | solution.py:380
  147.9 36.0 %collective-permute-start.13 = (bf16[64,1536]{1,0:T(8,128)(2,1)}, bf16[64,1536]{1,0:T(8,128)(2,1)S(1)}, u32[]{:S(2)}, u32[]{:S(2)}) collective-permute-start(bf16[64,1536]{1,0:T(8,128)(2,1)} %slice_bitcast_fusion.10), channel_id=1, source_target_pairs={{1,0},{2,1},{3,2},{0,3},{5,4},{6,5},{7,6},{4,7},{9,8},{10,9},{11,1... | collective-permute-start | bytes 589832 | tf_op jit(solution)/shard_map/ppermute | solution.py:381
  151.4 3.7 %copy-start = (bf16[2,1536,1536]{2,1,0:T(8,128)(2,1)S(1)}, bf16[2,1536,1536]{2,1,0:T(8,128)(2,1)}, u32[]{:S(2)}) copy-start(bf16[2,1536,1536]{2,1,0:T(8,128)(2,1)} %w_in.5) | copy-start | bytes 28311556
  166.1 30.7 %collective-permute-start.30 = (bf16[2,64,1536]{2,1,0:T(8,128)(2,1)}, bf16[2,64,1536]{2,1,0:T(8,128)(2,1)}, u32[]{:S(2)}, u32[]{:S(2)}) collective-permute-start(bf16[2,64,1536]{2,1,0:T(8,128)(2,1)} %get-tuple-element.45), channel_id=1, source_target_pairs={{1,0},{2,1},{3,2},{0,3},{5,4},{6,5},{7,6},{4,7},{9,8},{10,9},{11,1... | collective-permute-start | bytes 1179656 | tf_op jit(solution)/shard_map/ppermute | solution.py:384
  169.5 14.4 %slice-start = ((s8[9437184]{0:T(1024)(128)(4,1)}), s8[4194304]{0:T(1024)(128)(4,1)S(1)}, s32[]{:S(2)}) async-start(s8[9437184]{0:T(1024)(128)(4,1)} %bitcast.86), calls=%async_computation.6 | async-start | bytes 8388608
  169.5 14.4 %slice-start.1 = ((s8[9437184]{0:T(1024)(128)(4,1)}), s8[4194304]{0:T(1024)(128)(4,1)S(1)}, s32[]{:S(2)}) async-start(s8[9437184]{0:T(1024)(128)(4,1)} %bitcast.86), calls=%async_computation.7 | async-start | bytes 8388608
  169.5 14.4 %slice-start.2 = ((s8[9437184]{0:T(1024)(128)(4,1)}), s8[1048576]{0:T(1024)(128)(4,1)S(1)}, s32[]{:S(2)}) async-start(s8[9437184]{0:T(1024)(128)(4,1)} %bitcast.86), calls=%async_computation.8 | async-start | bytes 2097152
  169.5 28.2 %collective-permute-start.31 = (bf16[2,64,1536]{2,1,0:T(8,128)(2,1)}, bf16[2,64,1536]{2,1,0:T(8,128)(2,1)}, u32[]{:S(2)}, u32[]{:S(2)}) collective-permute-start(bf16[2,64,1536]{2,1,0:T(8,128)(2,1)} %get-tuple-element.47), channel_id=1, source_target_pairs={{0,1},{1,2},{2,3},{3,0},{4,5},{5,6},{6,7},{7,4},{8,9},{9,10},{10,1... | collective-permute-start | bytes 1179656 | tf_op jit(solution)/shard_map/ppermute | solution.py:383
  181.1 0.7 copy-start.5
  181.8 19.6 %collective-permute-start.22 = (bf16[2,64,1536]{2,1,0:T(8,128)(2,1)}, bf16[2,64,1536]{2,1,0:T(8,128)(2,1)S(1)}, u32[]{:S(2)}, u32[]{:S(2)}) collective-permute-start(bf16[2,64,1536]{2,1,0:T(8,128)(2,1)} %get-tuple-element.39), channel_id=1, source_target_pairs={{1,0},{2,1},{3,2},{0,3},{5,4},{6,5},{7,6},{4,7},{9,8},{10,9},{11,1... | collective-permute-start | bytes 1179656 | tf_op jit(solution)/shard_map/ppermute | solution.py:384
  183.9 17.7 %copy-start.6 = (bf16[64,1536]{1,0:T(8,128)(2,1)S(1)}, bf16[64,1536]{1,0:T(8,128)(2,1)}, u32[]{:S(2)}) copy-start(bf16[64,1536]{1,0:T(8,128)(2,1)} %copy-done.5) | copy-start | bytes 589828
  183.9 18.4 %collective-permute-start.23 = (bf16[2,64,1536]{2,1,0:T(8,128)(2,1)}, bf16[2,64,1536]{2,1,0:T(8,128)(2,1)S(1)}, u32[]{:S(2)}, u32[]{:S(2)}) collective-permute-start(bf16[2,64,1536]{2,1,0:T(8,128)(2,1)} %get-tuple-element.41), channel_id=1, source_target_pairs={{0,1},{1,2},{2,3},{3,0},{4,5},{5,6},{6,7},{7,4},{8,9},{9,10},{10,1... | collective-permute-start | bytes 1179656 | tf_op jit(solution)/shard_map/ppermute | solution.py:383
  194.0 11.7 %collective-permute-start.14 = (bf16[2,64,1536]{2,1,0:T(8,128)(2,1)S(1)}, bf16[2,64,1536]{2,1,0:T(8,128)(2,1)S(1)}, u32[]{:S(2)}, u32[]{:S(2)}) collective-permute-start(bf16[2,64,1536]{2,1,0:T(8,128)(2,1)S(1)} %get-tuple-element.33), channel_id=1, source_target_pairs={{1,0},{2,1},{3,2},{0,3},{5,4},{6,5},{7,6},{4,7},{9,8},{10,9},{11,1... | collective-permute-start | bytes 1179656 | tf_op jit(solution)/shard_map/ppermute | solution.py:384
  196.7 9.7 %collective-permute-start.15 = (bf16[2,64,1536]{2,1,0:T(8,128)(2,1)S(1)}, bf16[2,64,1536]{2,1,0:T(8,128)(2,1)S(1)}, u32[]{:S(2)}, u32[]{:S(2)}) collective-permute-start(bf16[2,64,1536]{2,1,0:T(8,128)(2,1)S(1)} %get-tuple-element.35), channel_id=1, source_target_pairs={{0,1},{1,2},{2,3},{3,0},{4,5},{5,6},{6,7},{7,4},{8,9},{9,10},{10,1... | collective-permute-start | bytes 1179656 | tf_op jit(solution)/shard_map/ppermute | solution.py:383
  197.7 12.1 %collective-permute-start.33 = (bf16[64,1536]{1,0:T(8,128)(2,1)S(1)}, bf16[64,1536]{1,0:T(8,128)(2,1)S(1)}, u32[]{:S(2)}, u32[]{:S(2)}) collective-permute-start(bf16[64,1536]{1,0:T(8,128)(2,1)S(1)} %fusion), channel_id=1, source_target_pairs={{1,0},{2,1},{3,2},{0,3},{5,4},{6,5},{7,6},{4,7},{9,8},{10,9},{11,1... | collective-permute-start | bytes 589832 | tf_op jit(solution)/shard_map/ppermute | solution.py:387
  201.5 8.6 %copy-start.9 = (bf16[2,64,1536]{2,1,0:T(8,128)(2,1)}, bf16[2,64,1536]{2,1,0:T(8,128)(2,1)S(1)}, u32[]{:S(2)}) copy-start(bf16[2,64,1536]{2,1,0:T(8,128)(2,1)S(1)} %collective-permute-done.22) | copy-start | bytes 1179652
  201.5 8.5 %collective-permute-start.32 = (bf16[64,1536]{1,0:T(8,128)(2,1)S(1)}, bf16[64,1536]{1,0:T(8,128)(2,1)S(1)}, u32[]{:S(2)}, u32[]{:S(2)}) collective-permute-start(bf16[64,1536]{1,0:T(8,128)(2,1)S(1)} %fusion.1), channel_id=1, source_target_pairs={{0,1},{1,2},{2,3},{3,0},{4,5},{5,6},{6,7},{7,4},{8,9},{9,10},{10,1... | collective-permute-start | bytes 589832 | tf_op jit(solution)/shard_map/ppermute | solution.py:386
  201.6 53.3 %copy-start.11 = (f32[256]{0:T(256)S(1)}, f32[256]{0:T(256)}, u32[]{:S(2)}) copy-start(f32[256]{0:T(256)} %param.17) | copy-start | bytes 3076
  202.3 9.0 %copy-start.10 = (bf16[2,64,1536]{2,1,0:T(8,128)(2,1)}, bf16[2,64,1536]{2,1,0:T(8,128)(2,1)S(1)}, u32[]{:S(2)}) copy-start(bf16[2,64,1536]{2,1,0:T(8,128)(2,1)S(1)} %collective-permute-done.23) | copy-start | bytes 1179652
  202.3 24.5 %collective-permute-start.25 = (bf16[64,1536]{1,0:T(8,128)(2,1)}, bf16[64,1536]{1,0:T(8,128)(2,1)}, u32[]{:S(2)}, u32[]{:S(2)}) collective-permute-start(bf16[64,1536]{1,0:T(8,128)(2,1)} %fusion.2), channel_id=1, source_target_pairs={{1,0},{2,1},{3,2},{0,3},{5,4},{6,5},{7,6},{4,7},{9,8},{10,9},{11,1... | collective-permute-start | bytes 589832 | tf_op jit(solution)/shard_map/ppermute | solution.py:387
  205.7 21.2 %collective-permute-start.24 = (bf16[64,1536]{1,0:T(8,128)(2,1)}, bf16[64,1536]{1,0:T(8,128)(2,1)S(1)}, u32[]{:S(2)}, u32[]{:S(2)}) collective-permute-start(bf16[64,1536]{1,0:T(8,128)(2,1)} %fusion.3), channel_id=1, source_target_pairs={{0,1},{1,2},{2,3},{3,0},{4,5},{5,6},{6,7},{7,4},{8,9},{9,10},{10,1... | collective-permute-start | bytes 589832 | tf_op jit(solution)/shard_map/ppermute | solution.py:386
  206.4 3.6 %copy-start.8 = (bf16[2,64,1536]{2,1,0:T(8,128)(2,1)}, bf16[2,64,1536]{2,1,0:T(8,128)(2,1)S(1)}, u32[]{:S(2)}) copy-start(bf16[2,64,1536]{2,1,0:T(8,128)(2,1)S(1)} %collective-permute-done.15) | copy-start | bytes 1179652
  206.4 34.4 %collective-permute-start.17 = (bf16[64,1536]{1,0:T(8,128)(2,1)}, bf16[64,1536]{1,0:T(8,128)(2,1)}, u32[]{:S(2)}, u32[]{:S(2)}) collective-permute-start(bf16[64,1536]{1,0:T(8,128)(2,1)} %fusion.4), channel_id=1, source_target_pairs={{1,0},{2,1},{3,2},{0,3},{5,4},{6,5},{7,6},{4,7},{9,8},{10,9},{11,1... | collective-permute-start | bytes 589832 | tf_op jit(solution)/shard_map/ppermute | solution.py:387
  209.8 31.0 %collective-permute-start.16 = (bf16[64,1536]{1,0:T(8,128)(2,1)}, bf16[64,1536]{1,0:T(8,128)(2,1)}, u32[]{:S(2)}, u32[]{:S(2)}) collective-permute-start(bf16[64,1536]{1,0:T(8,128)(2,1)} %fusion.5), channel_id=1, source_target_pairs={{0,1},{1,2},{2,3},{3,0},{4,5},{5,6},{6,7},{7,4},{8,9},{9,10},{10,1... | collective-permute-start | bytes 589832 | tf_op jit(solution)/shard_map/ppermute | solution.py:386
  210.0 54.9 %copy-start.4 = (bf16[256,1536]{1,0:T(8,128)(2,1)S(1)}, bf16[256,1536]{1,0:T(8,128)(2,1)}, u32[]{:S(2)}) copy-start(bf16[256,1536]{1,0:T(8,128)(2,1)} %copy-done.3) | copy-start | bytes 2359300
  213.2 24.0 %all-to-all-start.5 = ((bf16[32,4,1536]{2,1,0:T(4,128)(2,1)}), bf16[32,4,1536]{2,1,0:T(4,128)(2,1)S(1)}, u32[]{:S(2)}, u32[]{:S(2)}) async-start(bf16[32,4,1536]{2,1,0:T(4,128)(2,1)} %reshape.103), calls=%async_computation.5 | async-start | bytes 786432 | tf_op jit(solution)/shard_map/all_to_all | solution.py:393
  237.2 13.9 %all-to-all-start.3 = ((bf16[32,4,1536]{2,1,0:T(4,128)(2,1)}), bf16[32,4,1536]{2,1,0:T(4,128)(2,1)S(1)}, u32[]{:S(2)}, u32[]{:S(2)}) async-start(bf16[32,4,1536]{2,1,0:T(4,128)(2,1)} %reshape.98), calls=%async_computation.3 | async-start | bytes 786432 | tf_op jit(solution)/shard_map/all_to_all | solution.py:393
  251.0 13.9 %all-to-all-start.1 = ((bf16[32,4,1536]{2,1,0:T(4,128)(2,1)}), bf16[32,4,1536]{2,1,0:T(4,128)(2,1)S(1)}, u32[]{:S(2)}, u32[]{:S(2)}) async-start(bf16[32,4,1536]{2,1,0:T(4,128)(2,1)} %reshape.93), calls=%async_computation.1 | async-start | bytes 786432 | tf_op jit(solution)/shard_map/all_to_all | solution.py:393

commit v2 on v1

--- a/solution.py
+++ b/solution.py
@@ -13,19 +13,20 @@
 TILE = 128
 SPAN = 2 * HALF + TILE
 EDGE = 16
-GROUPS = (3, 3, 3, 3)
-CHUNKS = 3
+GROUPS = (6, 4, 2)
+MIB = 1024 * 1024
+STEP = 512
 F32 = jnp.float32
 BF16 = jnp.bfloat16
 
 
-def call(body, out_shape, cost, **kw):
+def call(body, out_shape, cost, vmem, **kw):
     flops, moved = cost
     return pl.pallas_call(
         body,
         out_shape=out_shape,
         cost_estimate=pl.CostEstimate(flops=flops, bytes_accessed=moved, transcendentals=0),
-        compiler_params=pltpu.CompilerParams(vmem_limit_bytes=40 * 1024 * 1024),
+        compiler_params=pltpu.CompilerParams(vmem_limit_bytes=vmem * MIB),
         **kw,
     )
 
@@ -41,29 +42,28 @@
             kept = (col > row) & (col - row < 2 * HALF) & (col >= low) & (col < high)
             bias[r] = jnp.where(kept, 0.0, -1e30)
 
-    keys = jnp.concatenate([lo_ref[0], kv_ref[0], hi_ref[0]], axis=0)
-    values = jnp.concatenate([lo_ref[1], kv_ref[1], hi_ref[1]], axis=0)
-    q = q_ref[...]
     lane = lax.broadcasted_iota(jnp.int32, (1, PAIR), 1)
     first = lane < HEAD
-    parts = [[], []]
-    for h in range(2):
-        mine = first if h == 0 else jnp.logical_not(first)
-        qh = q * jnp.where(mine, 0.125, 0.0).astype(BF16)
-        vh = values * jnp.where(mine, 1.0, 0.0).astype(BF16) + jnp.where(mine, 0.0, 1.0).astype(BF16)
-        for r in range(2):
-            rows = slice(r * TILE, r * TILE + TILE)
-            span = slice(r * TILE, r * TILE + SPAN)
-            s = lax.dot_general(
-                qh[rows], keys[span], (((1,), (1,)), ((), ())), preferred_element_type=F32
-            )
-            s = s + bias[r]
-            p = jnp.exp(s - jnp.max(s, axis=1, keepdims=True)).astype(BF16)
-            parts[r].append(jnp.dot(p, vh[span], preferred_element_type=F32))
+    only0 = jnp.where(first, 0.125, 0.0).astype(BF16)
+    only1 = jnp.where(first, 0.0, 0.125).astype(BF16)
+    ones = jnp.ones((SPAN, PAIR), BF16)
     halves = []
-    for o0, o1 in parts:
-        below = pltpu.roll(jnp.where(first, o1, o0), HEAD, 1)
-        halves.append(jnp.where(first, o0, o1) / below)
+    for r in range(2):
+        if r == 0:
+            join = lambda i: [lo_ref[i], kv_ref[i], hi_ref[i, :TILE]]
+        else:
+            join = lambda i: [lo_ref[i, TILE:], kv_ref[i], hi_ref[i]]
+        q = q_ref[r * TILE : (r + 1) * TILE]
+        both = jnp.concatenate([q * only0, q * only1], axis=0)
+        s = lax.dot_general(
+            both, jnp.concatenate(join(0), axis=0), (((1,), (1,)), ((), ())), preferred_element_type=F32
+        )
+        s = s + jnp.concatenate([bias[r], bias[r]], axis=0)
+        p = jnp.exp(s - jnp.max(s, axis=1, keepdims=True)).astype(BF16)
+        values = jnp.concatenate([jnp.concatenate(join(1), axis=0), ones], axis=1)
+        o = jnp.dot(p, values, preferred_element_type=F32)
+        o = o[:, :PAIR] / o[:, PAIR:]
+        halves.append(jnp.where(first, o[:TILE], o[TILE:]))
     return halves
 
 
@@ -112,13 +112,17 @@
         ]
         scratch = [pltpu.VMEM((2, TILE, SPAN), F32)]
         cost = (pairs * 16 * rows * SPAN * PAIR, pairs * 7 * rows * PAIR * 2)
-        args = (edge, queries, key_value, low[g], high[g])
+        before, after = low[g], high[g]
+        if outs:
+            before, after, _ = lax.optimization_barrier((before, after, outs[-1]))
+        args = (edge, queries, key_value, before, after)
         if not last:
             outs.append(
                 call(
                     attend_body,
                     jax.ShapeDtypeStruct((rows, pairs * PAIR), F32),
                     cost,
+                    16,
                     grid=(pairs,),
                     in_specs=base,
                     out_specs=pl.BlockSpec((rows, PAIR), lambda j: (0, j)),
@@ -135,6 +139,7 @@
                     jax.ShapeDtypeStruct((EDGE, width), BF16),
                 ],
                 cost,
+                20,
                 grid=(pairs,),
                 in_specs=base + [whole(1, width)] + [whole(*o.shape) for o in outs],
                 out_specs=[whole(rows, width), whole(EDGE, width), whole(EDGE, width)],
@@ -144,7 +149,8 @@
 
 
 def silu(v):
-    return v / (1.0 + jnp.exp(-v))
+    half = 0.5 * v
+    return half + half * jnp.tanh(half)
 
 
 def conv_rows(source, taps, first, count):
@@ -168,6 +174,7 @@
         inner_conv_body,
         jax.ShapeDtypeStruct((inner, width), BF16),
         (62 * inner * width * 64, 4 * rows * width),
+        16,
         grid=(width // PAIR,),
         in_specs=[
             pl.BlockSpec((rows, PAIR), lambda j: (0, j)),
@@ -203,13 +210,14 @@
         first += count
 
 
-def dispatch(normed, inner, low, high, taps, gain, place, count):
+def dispatch(normed, inner, low, high, taps, gain, place, counts):
     rows, width = normed.shape
     return call(
         dispatch_body,
         [jax.ShapeDtypeStruct((rows, width), BF16)]
-        + [jax.ShapeDtypeStruct((count, width), BF16)] * CHUNKS,
-        (2 * CHUNKS * count * rows * width, 8 * rows * width),
+        + [jax.ShapeDtypeStruct((count, width), BF16) for count in counts],
+        (2 * sum(counts) * rows * width, 8 * rows * width),
+        24,
         scratch_shapes=[pltpu.VMEM((2, 3 * EDGE, PAIR), F32)],
     )(normed, inner, low, high, taps, gain[None], place[None])
 
@@ -238,85 +246,69 @@
         combine_body,
         jax.ShapeDtypeStruct((rows, width), BF16),
         (2 * sum(p.shape[0] for p in parts) * rows * width, 8 * rows * width),
+        16,
         grid=(width // block,),
         in_specs=[column(rows), fixed, fixed] + [column(p.shape[0]) for p in parts],
         out_specs=column(rows),
     )(mixed, gate[:, None], place[:, None], *parts)
 
 
-def ffn_body(own, left, right, far0, far1, w_in, w_out, keep, up, down, up2, down2, rows_in, total):
-    e, f = pl.program_id(0), pl.program_id(1)
-    n = own.shape[1]
-
-    @pl.when(f == 0)
-    def _():
-        rows_in[:n] = own[0]
-        rows_in[n : 2 * n] = left[0]
-        rows_in[2 * n : 3 * n] = right[0]
-
-    @pl.when((f == 0) & (e == 0))
-    def _():
-        rows_in[3 * n :] = far0[...]
-
-    @pl.when((f == 0) & (e == 1))
-    def _():
-        rows_in[3 * n :] = far1[...]
-
-    hidden = silu(jnp.dot(rows_in[...], w_in[0], preferred_element_type=F32)).astype(BF16)
-    part = jnp.dot(hidden, w_out[0], preferred_element_type=F32)
-
-    @pl.when(f == 0)
-    def _():
-        total[...] = part
-
-    @pl.when(f > 0)
-    def _():
-        total[...] += part
-
-    done = f == pl.num_programs(1) - 1
-
-    @pl.when(done)
-    def _():
-        keep[0] = total[:n].astype(BF16)
-
-    @pl.when(done & (e == 0))
-    def _():
-        down[1] = total[n : 2 * n].astype(BF16)
-        up2[...] = total[2 * n : 3 * n].astype(BF16)
-        up[0] = total[3 * n :].astype(BF16)
-
-    @pl.when(done & (e == 1))
-    def _():
-        down2[...] = total[n : 2 * n].astype(BF16)
-        up[1] = total[2 * n : 3 * n].astype(BF16)
-        down[0] = total[3 * n :].astype(BF16)
+def ffn_body(own, left, right, far0, far1, w_in, w_out, keep, up, down, up2, down2, *scratch):
+    rows_in, hidden, first, second, sems = scratch
+    n, width = own.shape[1:]
+    units = hidden.shape[1]
+    step = STEP
+    copies = {}
+    for e in range(2):
+        for which, (weight, held) in enumerate(((w_in, first), (w_out, second))):
+            for t in range(weight.shape[2] // step):
+                cols = slice(t * step, (t + 1) * step)
+                copies[e, which, t] = pltpu.make_async_copy(
+                    weight.at[e, :, cols], held.at[e, t], sems.at[e, which, t]
+                )
+                copies[e, which, t].start()
+    for e in range(2):
+        rows_in[:n] = own[e]
+        rows_in[n : 2 * n] = left[e]
+        rows_in[2 * n : 3 * n] = right[e]
+        rows_in[3 * n :] = (far0 if e == 0 else far1)[...]
+        for t in range(units // step):
+            copies[e, 0, t].wait()
+            part = jnp.dot(rows_in[...], first[e, t], preferred_element_type=F32)
+            hidden[:, t * step : (t + 1) * step] = silu(part).astype(BF16)
+        for t in range(width // step):
+            copies[e, 1, t].wait()
+            cols = slice(t * step, (t + 1) * step)
+            part = jnp.dot(hidden[...], second[e, t], preferred_element_type=F32).astype(BF16)
+            keep[e, :, cols] = part[:n]
+            if e == 0:
+                down[1, :, cols] = part[n : 2 * n]
+                up2[:, cols] = part[2 * n : 3 * n]
+                up[0, :, cols] = part[3 * n :]
+            else:
+                down2[:, cols] = part[n : 2 * n]
+                up[1, :, cols] = part[2 * n : 3 * n]
+                down[0, :, cols] = part[3 * n :]
 
 
 def ffn(own, left, right, far0, far1, w_in, w_out):
     experts, n, width = own.shape
     units = w_in.shape[2]
-    step = 512
-    each = pl.BlockSpec((1, n, width), lambda e, f: (e, 0, 0))
-    both = pl.BlockSpec((2, n, width), lambda e, f: (0, 0, 0))
-    one = pl.BlockSpec((n, width), lambda e, f: (0, 0))
     pair = jax.ShapeDtypeStruct((2, n, width), BF16)
     single = jax.ShapeDtypeStruct((n, width), BF16)
     return call(
         ffn_body,
         [pair, pair, pair, single, single],
         (experts * 4 * n * width * units * 4, 2 * experts * width * units * 2),
-        grid=(experts, units // step),
-        in_specs=[
-            each,
-            each,
-            each,
-            one,
-            one,
-            pl.BlockSpec((1, width, step), lambda e, f: (e, 0, f)),
-            pl.BlockSpec((1, step, width), lambda e, f: (e, f, 0)),
+        50,
+        in_specs=[pl.BlockSpec(memory_space=pltpu.VMEM)] * 5 + [pl.BlockSpec(memory_space=pl.ANY)] * 2,
+        scratch_shapes=[
+            pltpu.VMEM((4 * n, width), BF16),
+            pltpu.VMEM((4 * n, units), BF16),
+            pltpu.VMEM((2, units // STEP, width, STEP), BF16),
+            pltpu.VMEM((2, width // STEP, units, STEP), BF16),
+            pltpu.SemaphoreType.DMA((2, 2, max(units, width) // STEP)),
         ],
-        out_specs=[each, both, both, one, one],
-        scratch_shapes=[pltpu.VMEM((4 * n, width), BF16), pltpu.VMEM((4 * n, width), F32)],
     )(own, left, right, far0, far1, w_in, w_out)
 
 
@@ -346,11 +338,13 @@
 
     low, high = [], []
     start = 0
+    source = key_value
     for pairs in GROUPS:
-        part = lax.slice_in_dim(key_value, start * PAIR, (start + pairs) * PAIR, axis=2)
+        part = lax.slice_in_dim(source, start * PAIR, (start + pairs) * PAIR, axis=2)
         low.append(lax.ppermute(part, order, onward))
         high.append(lax.ppermute(part, order, back))
         start += pairs
+        source, _ = lax.optimization_barrier((key_value, part))
     normed, first_rows, last_rows = attention(queries, key_value, low, high, edge, conv_gain)
 
     before = lax.ppermute(last_rows, order, onward)
@@ -359,40 +353,67 @@
 
     local = w_in.shape[0]
     experts = local * time_count
-    slots = max(2, 3 * frame_rows // (2 * experts)) // CHUNKS
-    count = experts * slots
+    slots = max(2, 3 * frame_rows // (2 * experts))
+    early = 2 * slots // 3
+    sizes = (early, slots - early)
     served = jnp.where(overflow == 1, secondary, primary)
-    place = (slot // slots) * count + served * slots + slot % slots
+    place = jnp.where(
+        slot < early,
+        served * early + slot,
+        experts * early + served * (slots - early) + slot - early,
+    )
     mixed, *chunks = dispatch(
-        normed, inner, before, after, conv_kernel, ffn_gain, place, count
+        normed, inner, before, after, conv_kernel, ffn_gain, place, [experts * c for c in sizes]
     )
 
     up = [(i, (i + 1) % group_count) for i in range(group_count)]
     down = [((i + 1) % group_count, i) for i in range(group_count)]
-    returned = []
-    for chunk in chunks:
-        sent = chunk.reshape(time_count, local * slots, width)
+    add = lambda *vs: sum(v.astype(F32) for v in vs).astype(BF16)
+
+    def arrive(chunk, size):
+        sent = chunk.reshape(time_count, local * size, width)
         own = lax.all_to_all(sent, "tm", split_axis=0, concat_axis=0, tiled=True)
-        own = own.reshape(time_count, local, slots, width).transpose(1, 0, 2, 3)
-        own = own.reshape(local, time_count * slots, width)
-        left = lax.ppermute(own, "expert", up)
-        right = lax.ppermute(own, "expert", down)
-        far0 = lax.ppermute(left[0], "expert", up)
-        far1 = lax.ppermute(right[1], "expert", down)
-        keep, go_up, go_down, up2, down2 = ffn(own, left, right, far0, far1, w_in, w_out)
-        from_below = lax.ppermute(go_up, "expert", up)
-        from_above = lax.ppermute(go_down, "expert", down)
-        add = lambda *vs: sum(v.astype(F32) for v in vs).astype(BF16)
-        up3 = lax.ppermute(add(up2, from_below[0]), "expert", up)
-        down3 = lax.ppermute(add(down2, from_above[0]), "expert", down)
-        summed = jnp.stack(
-            [add(keep[0], from_above[1], up3), add(keep[1], from_below[1], down3)]
-        )
-        summed = summed.reshape(local, time_count, slots, width).transpose(1, 0, 2, 3)
-        summed = summed.reshape(time_count, local * slots, width)
+        own = own.reshape(time_count, local, size, width).transpose(1, 0, 2, 3)
+        return own.reshape(local, time_count * size, width)
+
+    def near(own):
+        return lax.ppermute(own, "expert", up), lax.ppermute(own, "expert", down)
+
+    def far(left, right):
+        return lax.ppermute(left[0], "expert", up), lax.ppermute(right[1], "expert", down)
+
+    def leave(summed, size):
+        summed = summed.reshape(local, time_count, size, width).transpose(1, 0, 2, 3)
+        summed = summed.reshape(time_count, local * size, width)
         got = lax.all_to_all(summed, "tm", split_axis=0, concat_axis=0, tiled=True)
-        returned.append(got.reshape(count, width))
-    return combine(mixed, expert_gate, place, returned)
+        return got.reshape(experts * size, width)
+
+    after = lambda values, *others: lax.optimization_barrier((tuple(values), others))[0]
+    own_a = arrive(chunks[0], sizes[0])
+    left_a, right_a = near(own_a)
+    own_b = arrive(chunks[1], sizes[1])
+    left_a, right_a = after((left_a, right_a), own_b)
+    far_a = far(left_a, right_a)
+    left_b, right_b = near(own_b)
+    keep_a, go_up_a, go_down_a, up2_a, down2_a = ffn(own_a, left_a, right_a, *far_a, w_in, w_out)
+    below_a, above_a = lax.ppermute(go_up_a, "expert", up), lax.ppermute(go_down_a, "expert", down)
+    left_b, right_b = after((left_b, right_b), keep_a)
+    far_b = far(left_b, right_b)
+    up2_a, down2_a = add(up2_a, below_a[0]), add(down2_a, above_a[0])
+    up3_a, down3_a = lax.ppermute(up2_a, "expert", up), lax.ppermute(down2_a, "expert", down)
+    (own_b,) = after((own_b,), up2_a, down2_a)
+    keep_b, go_up_b, go_down_b, up2_b, down2_b = ffn(own_b, left_b, right_b, *far_b, w_in, w_out)
+    go_up_b, go_down_b = after((go_up_b, go_down_b), up3_a, down3_a)
+    below_b, above_b = lax.ppermute(go_up_b, "expert", up), lax.ppermute(go_down_b, "expert", down)
+    total_a = jnp.stack([add(keep_a[0], above_a[1], up3_a), add(keep_a[1], below_a[1], down3_a)])
+    back_a = leave(total_a, sizes[0])
+    below_b, above_b = after((below_b, above_b), total_a)
+    up3_b = lax.ppermute(add(up2_b, below_b[0]), "expert", up)
+    down3_b = lax.ppermute(add(down2_b, above_b[0]), "expert", down)
+    total_b = jnp.stack([add(keep_b[0], above_b[1], up3_b), add(keep_b[1], below_b[1], down3_b)])
+    (total_b,) = after((total_b,), back_a)
+    back_b = leave(total_b, sizes[1])
+    return combine(mixed, expert_gate, place, [back_a, back_b])
 
 
 def solution(mesh):

time: 270 us -> 235 us (0.87)
  starting transfers between devices: 116 us -> 72.1 us
  blocking collectives: 0 us -> 39.4 us
  Pallas kernels: 62.2 us -> 47.2 us
  local copies, waits for them, and re-layouts: 22 us -> 15.8 us
  other arithmetic: 11.1 us -> 5.37 us
  waiting for transfers between devices: 56.4 us -> 53.6 us
    all_to_all x0 -> x2, blocking collectives: none -> 39.4 us  [arrive(): own = lax.all_to_all(sent, 'tm', split_axis=0, concat_axis=0, tiled=True)]
    all_to_all x6 -> x2, starting transfers between devices: 47.1 us -> 15.6 us  [leave(): got = lax.all_to_all(summed, 'tm', split_axis=0, concat_axis=0, tiled=True)]
    all_to_all x6 -> x2, waiting for transfers between devices: 44.8 us -> 23.1 us  [leave(): got = lax.all_to_all(summed, 'tm', split_axis=0, concat_axis=0, tiled=True)]
    ppermute x24 -> x16, waiting for transfers between devices: 11.5 us -> 27.9 us  [the longest x1 11.1 us: on_device(): lax.ppermute(go_down_a, 'expert', down)]
    pallas_call x3 -> x2, Pallas kernels: 32.7 us -> 24.8 us  [ffn(): call(ffn_body, [pair, pair, pair, single, single], (experts * 4 * n * wid...]
    ppermute x24 -> x16, starting transfers between devices: 32.6 us -> 25 us  [the longest x4 6.61 us: near(): return (lax.ppermute(own, 'expert', up), lax.ppermute(own, 'expert', down))]
    convert_element_type x9 -> x5, other arithmetic: 8.63 us -> 2.87 us  [on_device(): add = lambda *vs: sum((v.astype(F32) for v in vs)).astype(BF16)]
    unnamed x30 -> x16, local copies, waits for them, and re-layouts: 7.81 us -> 2.57 us
  transfers between devices with their start and end apart: 40 -> 26, of which waited for: 12 -> 8; matrix products, arithmetic and copies ran while one was open for 8% -> 5% of each run, Pallas kernels for 19% -> 17%
where the time goes in v2:
time: 235 us; the launch traced here: 234 us
  starting transfers between devices  72.1 us (31%)
  waiting for transfers between devices  53.6 us (23%)
  Pallas kernels  47.2 us (20%)
  blocking collectives  39.4 us (17%)
  local copies, waits for them, and re-layouts  15.8 us (7%)
  other arithmetic  5.37 us (2%)
    all_to_all x2, blocking collectives, arrive(): own = lax.all_to_all(sent, 'tm', split_axis=0, concat_axis=0, tiled=True)  39.4 us
    pallas_call x2, Pallas kernels, ffn(): call(ffn_body, [pair, pair, pair, single, single], (experts * 4 * n * wid...  24.8 us
    all_to_all x2, waiting for transfers between devices, leave(): got = lax.all_to_all(summed, 'tm', split_axis=0, concat_axis=0, tiled=True)  23.1 us
    ppermute x3, starting transfers between devices, on_device(): high.append(lax.ppermute(part, order, back))  15.7 us
    all_to_all x2, starting transfers between devices, leave(): got = lax.all_to_all(summed, 'tm', split_axis=0, concat_axis=0, tiled=True)  15.6 us
    pallas_call x2, Pallas kernels, attention(): call(attend_body, jax.ShapeDtypeStruct((rows, pairs * PAIR), F32), cost,...  11.4 us
    ppermute x1, waiting for transfers between devices, on_device(): lax.ppermute(go_down_a, 'expert', down)  11.1 us
    ppermute x3, starting transfers between devices, on_device(): low.append(lax.ppermute(part, order, onward))  8.31 us
  transfers between devices with their start and end apart: 26, of which 8 were waited for; matrix products, arithmetic and copies ran while one was open for 5% of the time, Pallas kernels for 17%

profile of v2, /device:TPU:1, one launch (start us, length us, event | category | flops | bytes accessed | tf_op | source)
XLA Modules:
  0.0 233.9 jit_solution(5264220566530154522)
XLA Ops:
  0.0 2.2 slice.57
  2.2 4.5 %collective-permute-start.4 = (bf16[2,256,768]{2,1,0:T(8,128)(2,1)}, bf16[2,256,768]{2,1,0:T(8,128)(2,1)}, u32[]{:S(2)}, u32[]{:S(2)}) collective-permute-start(bf16[2,256,768]{2,1,0:T(8,128)(2,1)} %slice.57), channel_id=1, source_target_pairs={{0,1},{1,2},{2,3},{3,4},{4,5},{5,6},{6,7},{7,8},{8,9},{9,10},{10,1... | collective-permute-start | bytes 2359304 | tf_op jit(solution)/shard_map/ppermute | solution.py:344
  6.7 4.6 %collective-permute-start.5 = (bf16[2,256,768]{2,1,0:T(8,128)(2,1)}, bf16[2,256,768]{2,1,0:T(8,128)(2,1)}, u32[]{:S(2)}, u32[]{:S(2)}) collective-permute-start(bf16[2,256,768]{2,1,0:T(8,128)(2,1)} %slice.57), channel_id=1, source_target_pairs={{1,0},{2,1},{3,2},{4,3},{5,4},{6,5},{7,6},{8,7},{9,8},{10,9},{11,1... | collective-permute-start | bytes 2359304 | tf_op jit(solution)/shard_map/ppermute | solution.py:345
  11.3 1.9 slice.58
  13.2 1.9 collective-permute-start.2
  15.1 4.9 %collective-permute-start.3 = (bf16[2,256,512]{2,1,0:T(8,128)(2,1)}, bf16[2,256,512]{2,1,0:T(8,128)(2,1)}, u32[]{:S(2)}, u32[]{:S(2)}) collective-permute-start(bf16[2,256,512]{2,1,0:T(8,128)(2,1)} %slice.58), channel_id=1, source_target_pairs={{1,0},{2,1},{3,2},{4,3},{5,4},{6,5},{7,6},{8,7},{9,8},{10,9},{11,1... | collective-permute-start | bytes 1572872 | tf_op jit(solution)/shard_map/ppermute | solution.py:345
  20.0 1.7 slice.59
  21.7 1.9 collective-permute-start
  23.6 0.7 broadcast_in_dim.15.gain_ref
  24.3 0.7 broadcast_in_dim.16.gain_ref
  25.1 0.7 compare_select_fusion.1
  25.8 6.2 %collective-permute-start.1 = (bf16[2,256,256]{2,1,0:T(8,128)(2,1)}, bf16[2,256,256]{2,1,0:T(8,128)(2,1)S(1)}, u32[]{:S(2)}, u32[]{:S(2)}) collective-permute-start(bf16[2,256,256]{2,1,0:T(8,128)(2,1)} %slice.59), channel_id=1, source_target_pairs={{1,0},{2,1},{3,2},{4,3},{5,4},{6,5},{7,6},{8,7},{9,8},{10,9},{11,1... | collective-permute-start | bytes 786440 | tf_op jit(solution)/shard_map/ppermute | solution.py:345
  32.0 2.6 %collective-permute-done.5.hi_ref = bf16[2,256,768]{2,1,0:T(8,128)(2,1)} collective-permute-done((bf16[2,256,768]{2,1,0:T(8,128)(2,1)}, bf16[2,256,768]{2,1,0:T(8,128)(2,1)}, u32[]{:S(2)}, u32[]{:S(2)}) %collective-permute-start.5) | collective-permute-done | bytes 786464 | tf_op jit(solution)/shard_map/ppermute | solution.py:345
  34.6 1.4 copy-done
  36.0 1.1 copy-done.2
  37.1 6.7 %shard_map.118.rest_0_ = f32[256,768]{1,0:T(8,128)S(1)} custom-call(s32[2]{0:T(128)S(1)} %add_convert_fusion.edge_ref, bf16[256,1536]{1,0:T(8,128)(2,1)S(1)} %copy-done.2, bf16[2,256,1536]{2,1,0:T(8,128)(2,1)S(1)} %copy-done, bf16[2,256,768]{2,1,0:T(8,128)(2,1)} %collective-permute-done.4.lo_ref, bf16[2,256,768]{2,1,0:T(8,128)(2,1)} %collective-permute-done.5.hi_ref), custom_call_target="tpu_custom_call" | custom-call | flops 2013265920 | bytes 2752512 | tf_op jit(solution)/shard_map/pallas_call | solution.py:121
  43.9 4.7 %shard_map.119.rest_1_ = f32[256,512]{1,0:T(8,128)S(1)} custom-call(s32[2]{0:T(128)S(1)} %add_convert_fusion.edge_ref, bf16[256,1536]{1,0:T(8,128)(2,1)S(1)} %copy-done.2, bf16[2,256,1536]{2,1,0:T(8,128)(2,1)S(1)} %copy-done, bf16[2,256,512]{2,1,0:T(8,128)(2,1)S(1)} %collective-permute-done.2.lo_ref, bf16[2,256,512]{2,1,0:T(8,128)(2,1)} %collective-permute-done.3.hi_ref), custom_call_target="tpu_custom_call" | custom-call | flops 1342177280 | bytes 1835008 | tf_op jit(solution)/shard_map/pallas_call | solution.py:121
  48.6 2.8 %shard_map.120 = (bf16[256,1536]{1,0:T(8,128)(2,1)S(1)}, bf16[16,1536]{1,0:T(8,128)(2,1)S(1)}, bf16[16,1536]{1,0:T(8,128)(2,1)S(1)}) custom-call(s32[2]{0:T(128)S(1)} %add_convert_fusion.edge_ref, bf16[256,1536]{1,0:T(8,128)(2,1)S(1)} %copy-done.3, bf16[2,256,1536]{2,1,0:T(8,128)(2,1)S(1)} %copy-done.1, ...), custom_call_target="tpu_custom_call" | custom-call | flops 671088640 | bytes 917504 | tf_op jit(solution)/shard_map/pallas_call | solution.py:134
  51.4 1.9 collective-permute-start.6
  53.3 5.6 %collective-permute-start.7 = (bf16[16,1536]{1,0:T(8,128)(2,1)S(1)}, bf16[16,1536]{1,0:T(8,128)(2,1)S(1)}, u32[]{:S(2)}, u32[]{:S(2)}) collective-permute-start(bf16[16,1536]{1,0:T(8,128)(2,1)S(1)} %get-tuple-element.45), channel_id=1, source_target_pairs={{1,0},{2,1},{3,2},{4,3},{5,4},{6,5},{7,6},{8,7},{9,8},{10,9},{11,1... | collective-permute-start | bytes 147464 | tf_op jit(solution)/shard_map/ppermute | solution.py:351
  59.0 3.6 %shard_map.121.inner_ref = bf16[224,1536]{1,0:T(8,128)(2,1)S(1)} custom-call(bf16[256,1536]{1,0:T(8,128)(2,1)S(1)} %get-tuple-element.43.normed_ref, f32[31,1536]{1,0:T(8,128)S(1)} %copy-done.4), custom_call_target="tpu_custom_call" | custom-call | flops 1365245952 | bytes 1572864 | tf_op jit(solution)/shard_map/pallas_call | solution.py:173
  62.6 1.4 shard_map.122
  64.0 25.1 %all_to_all.20 = bf16[32,8,1536]{2,1,0:T(8,128)(2,1)S(1)} all-to-all(bf16[32,8,1536]{2,1,0:T(8,128)(2,1)S(1)} %bitcast.65), channel_id=1, replica_groups=mesh['tm'=32,'expert'=4] {'tm'}, dimensions={0} | all-to-all | bytes 1572864 | tf_op jit(solution)/shard_map/all_to_all | solution.py:375
  89.1 0.2 copy.23
  89.4 0.6 copy.24
  90.0 0.2 reshape.60.own
  90.3 3.9 %collective-permute-start.9 = (bf16[2,128,1536]{2,1,0:T(8,128)(2,1)S(1)}, bf16[2,128,1536]{2,1,0:T(8,128)(2,1)}, u32[]{:S(2)}, u32[]{:S(2)}) collective-permute-start(bf16[2,128,1536]{2,1,0:T(8,128)(2,1)S(1)} %reshape.60.own), channel_id=1, source_target_pairs={{1,0},{2,1},{3,2},{0,3},{5,4},{6,5},{7,6},{4,7},{9,8},{10,9},{11,1... | collective-permute-start | bytes 2359304 | tf_op jit(solution)/shard_map/ppermute | solution.py:380
  94.2 14.2 %all_to_all.21 = bf16[32,4,1536]{2,1,0:T(4,128)(2,1)S(1)} all-to-all(bf16[32,4,1536]{2,1,0:T(4,128)(2,1)S(1)} %reshape.61), channel_id=1, replica_groups=mesh['tm'=32,'expert'=4] {'tm'}, dimensions={0} | all-to-all | bytes 786432 | tf_op jit(solution)/shard_map/all_to_all | solution.py:375
  108.5 0.4 copy.26
  108.9 0.1 reshape.63.own
  109.1 3.0 %collective-permute-done.8.left = bf16[2,128,1536]{2,1,0:T(8,128)(2,1)S(1)} collective-permute-done((bf16[2,128,1536]{2,1,0:T(8,128)(2,1)S(1)}, bf16[2,128,1536]{2,1,0:T(8,128)(2,1)S(1)}, u32[]{:S(2)}, u32[]{:S(2)}) %collective-permute-start.8) | collective-permute-done | bytes 786464 | tf_op jit(solution)/shard_map/ppermute | solution.py:380
  112.1 0.7 collective-permute-start.10
  112.9 1.0 slice_bitcast_fusion.2
  113.9 2.1 collective-permute-start.11
  116.0 2.7 %collective-permute-start.17 = (bf16[2,64,1536]{2,1,0:T(8,128)(2,1)S(1)}, bf16[2,64,1536]{2,1,0:T(8,128)(2,1)S(1)}, u32[]{:S(2)}, u32[]{:S(2)}) collective-permute-start(bf16[2,64,1536]{2,1,0:T(8,128)(2,1)S(1)} %reshape.63.own), channel_id=1, source_target_pairs={{1,0},{2,1},{3,2},{0,3},{5,4},{6,5},{7,6},{4,7},{9,8},{10,9},{11,1... | collective-permute-start | bytes 1179656 | tf_op jit(solution)/shard_map/ppermute | solution.py:380
  118.7 5.0 %collective-permute-done.10.far0 = bf16[128,1536]{1,0:T(8,128)(2,1)S(1)} collective-permute-done((bf16[128,1536]{1,0:T(8,128)(2,1)S(1)}, bf16[128,1536]{1,0:T(8,128)(2,1)S(1)}, u32[]{:S(2)}, u32[]{:S(2)}) %collective-permute-start.10) | collective-permute-done | bytes 393248 | tf_op jit(solution)/shard_map/ppermute | solution.py:383
  123.7 15.4 %shard_map.123 = (bf16[2,128,1536]{2,1,0:T(8,128)(2,1)S(1)}, bf16[2,128,1536]{2,1,0:T(8,128)(2,1)S(1)}, bf16[2,128,1536]{2,1,0:T(8,128)(2,1)S(1)}, bf16[128,1536]{1,0:T(8,128)(2,1)S(1)}, bf16[128,1536]{1,0:T(8,128)(2,1)S(1)}) custom-call(bf16[2,128,1536]{2,1,0:T(8,128)(2,1)} %copy-done.5, bf16[2,128,1536]{2,1,0:T(8,128)(2,1)} %copy-done.6, ...), custom_call_target="tpu_custom_call" | custom-call | flops 9663676416 | bytes 18874368 | tf_op jit(solution)/shard_map/pallas_call | solution.py:299
  139.1 3.5 %collective-permute-start.12 = (bf16[2,128,1536]{2,1,0:T(8,128)(2,1)S(1)}, bf16[2,128,1536]{2,1,0:T(8,128)(2,1)S(1)}, u32[]{:S(2)}, u32[]{:S(2)}) collective-permute-start(bf16[2,128,1536]{2,1,0:T(8,128)(2,1)S(1)} %get-tuple-element.52), channel_id=1, source_target_pairs={{1,0},{2,1},{3,2},{0,3},{5,4},{6,5},{7,6},{4,7},{9,8},{10,9},{11,1... | collective-permute-start | bytes 2359304 | tf_op jit(solution)/shard_map/ppermute | solution.py:399
  142.8 2.7 %collective-permute-start.19 = (bf16[64,1536]{1,0:T(8,128)(2,1)S(1)}, bf16[64,1536]{1,0:T(8,128)(2,1)S(1)}, u32[]{:S(2)}, u32[]{:S(2)}) collective-permute-start(bf16[64,1536]{1,0:T(8,128)(2,1)S(1)} %slice_bitcast_fusion.4), channel_id=1, source_target_pairs={{1,0},{2,1},{3,2},{0,3},{5,4},{6,5},{7,6},{4,7},{9,8},{10,9},{11,1... | collective-permute-start | bytes 589832 | tf_op jit(solution)/shard_map/ppermute | solution.py:383
  145.6 11.1 %collective-permute-done.12 = bf16[2,128,1536]{2,1,0:T(8,128)(2,1)S(1)} collective-permute-done((bf16[2,128,1536]{2,1,0:T(8,128)(2,1)S(1)}, bf16[2,128,1536]{2,1,0:T(8,128)(2,1)S(1)}, u32[]{:S(2)}, u32[]{:S(2)}) %collective-permute-start.12) | collective-permute-done | bytes 786464 | tf_op jit(solution)/shard_map/ppermute | solution.py:399
  156.8 3.5 %collective-permute-start.15 = (bf16[128,1536]{1,0:T(8,128)(2,1)S(1)}, bf16[128,1536]{1,0:T(8,128)(2,1)S(1)}, u32[]{:S(2)}, u32[]{:S(2)}) collective-permute-start(bf16[128,1536]{1,0:T(8,128)(2,1)S(1)} %fusion), channel_id=1, source_target_pairs={{1,0},{2,1},{3,2},{0,3},{5,4},{6,5},{7,6},{4,7},{9,8},{10,9},{11,1... | collective-permute-start | bytes 1179656 | tf_op jit(solution)/shard_map/ppermute | solution.py:403
  160.3 3.9 %collective-permute-done.13 = bf16[2,128,1536]{2,1,0:T(8,128)(2,1)S(1)} collective-permute-done((bf16[2,128,1536]{2,1,0:T(8,128)(2,1)S(1)}, bf16[2,128,1536]{2,1,0:T(8,128)(2,1)S(1)}, u32[]{:S(2)}, u32[]{:S(2)}) %collective-permute-start.13) | collective-permute-done | bytes 786464 | tf_op jit(solution)/shard_map/ppermute | solution.py:399
  164.2 0.3 collective-permute-start.14
  164.5 9.4 %shard_map.124 = (bf16[2,64,1536]{2,1,0:T(8,128)(2,1)S(1)}, bf16[2,64,1536]{2,1,0:T(8,128)(2,1)}, bf16[2,64,1536]{2,1,0:T(8,128)(2,1)S(1)}, bf16[64,1536]{1,0:T(8,128)(2,1)S(1)}, bf16[64,1536]{1,0:T(8,128)(2,1)S(1)}) custom-call(bf16[2,64,1536]{2,1,0:T(8,128)(2,1)S(1)} %reshape.63.own, bf16[2,64,1536]{2,1,0:T(8,128)(2,1)S(1)} %collective-permute-done.16.left, ...), custom_call_target="tpu_custom_call" | custom-call | flops 4831838208 | bytes 18874368 | tf_op jit(solution)/shard_map/pallas_call | solution.py:299
  174.1 2.7 %collective-permute-start.21 = (bf16[2,64,1536]{2,1,0:T(8,128)(2,1)S(1)}, bf16[2,64,1536]{2,1,0:T(8,128)(2,1)}, u32[]{:S(2)}, u32[]{:S(2)}) collective-permute-start(bf16[2,64,1536]{2,1,0:T(8,128)(2,1)S(1)} %get-tuple-element.63), channel_id=1, source_target_pairs={{1,0},{2,1},{3,2},{0,3},{5,4},{6,5},{7,6},{4,7},{9,8},{10,9},{11,1... | collective-permute-start | bytes 1179656 | tf_op jit(solution)/shard_map/ppermute | solution.py:407
  176.8 0.3 fusion.3
  177.3 4.8 %collective-permute-done.20 = bf16[2,64,1536]{2,1,0:T(8,128)(2,1)S(1)} collective-permute-done((bf16[2,64,1536]{2,1,0:T(8,128)(2,1)}, bf16[2,64,1536]{2,1,0:T(8,128)(2,1)S(1)}, u32[]{:S(2)}, u32[]{:S(2)}) %collective-permute-start.20) | collective-permute-done | bytes 393248 | tf_op jit(solution)/shard_map/ppermute | solution.py:407
  182.1 1.7 fusion.4
  183.8 2.6 %collective-permute-start.23 = (bf16[64,1536]{1,0:T(8,128)(2,1)}, bf16[64,1536]{1,0:T(8,128)(2,1)S(1)}, u32[]{:S(2)}, u32[]{:S(2)}) collective-permute-start(bf16[64,1536]{1,0:T(8,128)(2,1)} %fusion.4), channel_id=1, source_target_pairs={{1,0},{2,1},{3,2},{0,3},{5,4},{6,5},{7,6},{4,7},{9,8},{10,9},{11,1... | collective-permute-start | bytes 589832 | tf_op jit(solution)/shard_map/ppermute | solution.py:412
  186.4 0.7 fusion.5
  187.1 0.6 maximum_bitcast_fusion
  187.7 0.3 copy.27
  188.0 1.1 reshape.64
  189.0 11.8 %all-to-all-start.2 = ((bf16[32,8,1536]{2,1,0:T(8,128)(2,1)}), bf16[32,8,1536]{2,1,0:T(8,128)(2,1)S(1)}, u32[]{:S(2)}, u32[]{:S(2)}) async-start(bf16[32,8,1536]{2,1,0:T(8,128)(2,1)} %reshape.64), calls=%async_computation.2 | async-start | bytes 1572864 | tf_op jit(solution)/shard_map/all_to_all | solution.py:388
  200.8 1.1 fusion.8
  202.0 13.1 %all-to-all-done.2 = bf16[32,8,1536]{2,1,0:T(8,128)(2,1)S(1)} async-done(((bf16[32,8,1536]{2,1,0:T(8,128)(2,1)}), bf16[32,8,1536]{2,1,0:T(8,128)(2,1)S(1)}, u32[]{:S(2)}, u32[]{:S(2)}) %all-to-all-start.2) | async-done | bytes 786464 | tf_op jit(solution)/shard_map/all_to_all | solution.py:388
  215.1 0.1 reshape.66
  215.2 0.3 copy.28
  215.5 0.9 reshape.67
  216.4 3.8 %all-to-all-start.3 = ((bf16[32,4,1536]{2,1,0:T(4,128)(2,1)}), bf16[32,4,1536]{2,1,0:T(4,128)(2,1)S(1)}, u32[]{:S(2)}, u32[]{:S(2)}) async-start(bf16[32,4,1536]{2,1,0:T(4,128)(2,1)} %reshape.67), calls=%async_computation.3 | async-start | bytes 786432 | tf_op jit(solution)/shard_map/all_to_all | solution.py:388
  220.2 0.1 copy.30.place_ref
  220.4 0.1 copy.29.gate_ref
  220.5 10.0 %all-to-all-done.3 = bf16[32,4,1536]{2,1,0:T(4,128)(2,1)S(1)} async-done(((bf16[32,4,1536]{2,1,0:T(4,128)(2,1)}), bf16[32,4,1536]{2,1,0:T(4,128)(2,1)S(1)}, u32[]{:S(2)}, u32[]{:S(2)}) %all-to-all-start.3) | async-done | bytes 393248 | tf_op jit(solution)/shard_map/all_to_all | solution.py:388
  230.6 3.3 %shard_map.125 = bf16[256,1536]{1,0:T(8,128)(2,1)} custom-call(bf16[256,1536]{1,0:T(8,128)(2,1)S(1)} %get-tuple-element.46.mixed_ref, f32[256,1]{1,0:T(8,128)S(1)} %copy.29.gate_ref, s32[256,1]{1,0:T(8,128)S(1)} %copy.30.place_ref, bf16[256,1536]{1,0:T(8,128)(2,1)S(1)} %bitcast.64, bf16[128,1536]{1,0:T(8,128)(2,1)S(1)} %reshape.68.rest_1_), custom_call_target="tpu_custom_call" | custom-call | flops 301989888 | bytes 3145728 | tf_op jit(solution)/shard_map/pallas_call | solution.py:245
  (50 shorter events, 1.2 us)
Async XLA Ops:
  0.0 48.6 %copy-start.1 = (bf16[2,256,1536]{2,1,0:T(8,128)(2,1)S(1)}, bf16[2,256,1536]{2,1,0:T(8,128)(2,1)}, u32[]{:S(2)}) copy-start(bf16[2,256,1536]{2,1,0:T(8,128)(2,1)} %kv_ref.5) | copy-start | bytes 4718596
  0.0 48.6 %copy-start.3 = (bf16[256,1536]{1,0:T(8,128)(2,1)S(1)}, bf16[256,1536]{1,0:T(8,128)(2,1)}, u32[]{:S(2)}) copy-start(bf16[256,1536]{1,0:T(8,128)(2,1)} %q_ref.5) | copy-start | bytes 2359300
  2.2 56.7 %copy-start.4 = (f32[31,1536]{1,0:T(8,128)S(1)}, f32[31,1536]{1,0:T(8,128)}, u32[]{:S(2)}) copy-start(f32[31,1536]{1,0:T(8,128)} %taps_ref.3) | copy-start | bytes 571396
  2.2 23.6 %collective-permute-start.4 = (bf16[2,256,768]{2,1,0:T(8,128)(2,1)}, bf16[2,256,768]{2,1,0:T(8,128)(2,1)}, u32[]{:S(2)}, u32[]{:S(2)}) collective-permute-start(bf16[2,256,768]{2,1,0:T(8,128)(2,1)} %slice.57), channel_id=1, source_target_pairs={{0,1},{1,2},{2,3},{3,4},{4,5},{5,6},{6,7},{7,8},{8,9},{9,10},{10,1... | collective-permute-start | bytes 2359304 | tf_op jit(solution)/shard_map/ppermute | solution.py:344
  6.7 27.9 %collective-permute-start.5 = (bf16[2,256,768]{2,1,0:T(8,128)(2,1)}, bf16[2,256,768]{2,1,0:T(8,128)(2,1)}, u32[]{:S(2)}, u32[]{:S(2)}) collective-permute-start(bf16[2,256,768]{2,1,0:T(8,128)(2,1)} %slice.57), channel_id=1, source_target_pairs={{1,0},{2,1},{3,2},{4,3},{5,4},{6,5},{7,6},{8,7},{9,8},{10,9},{11,1... | collective-permute-start | bytes 2359304 | tf_op jit(solution)/shard_map/ppermute | solution.py:345
  13.2 30.6 %collective-permute-start.2 = (bf16[2,256,512]{2,1,0:T(8,128)(2,1)}, bf16[2,256,512]{2,1,0:T(8,128)(2,1)S(1)}, u32[]{:S(2)}, u32[]{:S(2)}) collective-permute-start(bf16[2,256,512]{2,1,0:T(8,128)(2,1)} %slice.58), channel_id=1, source_target_pairs={{0,1},{1,2},{2,3},{3,4},{4,5},{5,6},{6,7},{7,8},{8,9},{9,10},{10,1... | collective-permute-start | bytes 1572872 | tf_op jit(solution)/shard_map/ppermute | solution.py:344
  15.1 28.7 %collective-permute-start.3 = (bf16[2,256,512]{2,1,0:T(8,128)(2,1)}, bf16[2,256,512]{2,1,0:T(8,128)(2,1)}, u32[]{:S(2)}, u32[]{:S(2)}) collective-permute-start(bf16[2,256,512]{2,1,0:T(8,128)(2,1)} %slice.58), channel_id=1, source_target_pairs={{1,0},{2,1},{3,2},{4,3},{5,4},{6,5},{7,6},{8,7},{9,8},{10,9},{11,1... | collective-permute-start | bytes 1572872 | tf_op jit(solution)/shard_map/ppermute | solution.py:345
  21.7 26.9 %collective-permute-start = (bf16[2,256,256]{2,1,0:T(8,128)(2,1)}, bf16[2,256,256]{2,1,0:T(8,128)(2,1)S(1)}, u32[]{:S(2)}, u32[]{:S(2)}) collective-permute-start(bf16[2,256,256]{2,1,0:T(8,128)(2,1)} %slice.59), channel_id=1, source_target_pairs={{0,1},{1,2},{2,3},{3,4},{4,5},{5,6},{6,7},{7,8},{8,9},{9,10},{10,1... | collective-permute-start | bytes 786440 | tf_op jit(solution)/shard_map/ppermute | solution.py:344
  25.8 22.8 %collective-permute-start.1 = (bf16[2,256,256]{2,1,0:T(8,128)(2,1)}, bf16[2,256,256]{2,1,0:T(8,128)(2,1)S(1)}, u32[]{:S(2)}, u32[]{:S(2)}) collective-permute-start(bf16[2,256,256]{2,1,0:T(8,128)(2,1)} %slice.59), channel_id=1, source_target_pairs={{1,0},{2,1},{3,2},{4,3},{5,4},{6,5},{7,6},{8,7},{9,8},{10,9},{11,1... | collective-permute-start | bytes 786440 | tf_op jit(solution)/shard_map/ppermute | solution.py:345
  34.6 1.4 copy-start
  36.0 1.1 copy-start.2
  51.4 11.1 %collective-permute-start.6 = (bf16[16,1536]{1,0:T(8,128)(2,1)S(1)}, bf16[16,1536]{1,0:T(8,128)(2,1)S(1)}, u32[]{:S(2)}, u32[]{:S(2)}) collective-permute-start(bf16[16,1536]{1,0:T(8,128)(2,1)S(1)} %get-tuple-element.44), channel_id=1, source_target_pairs={{0,1},{1,2},{2,3},{3,4},{4,5},{5,6},{6,7},{7,8},{8,9},{9,10},{10,1... | collective-permute-start | bytes 147464 | tf_op jit(solution)/shard_map/ppermute | solution.py:350
  53.3 9.2 %collective-permute-start.7 = (bf16[16,1536]{1,0:T(8,128)(2,1)S(1)}, bf16[16,1536]{1,0:T(8,128)(2,1)S(1)}, u32[]{:S(2)}, u32[]{:S(2)}) collective-permute-start(bf16[16,1536]{1,0:T(8,128)(2,1)S(1)} %get-tuple-element.45), channel_id=1, source_target_pairs={{1,0},{2,1},{3,2},{4,3},{5,4},{6,5},{7,6},{8,7},{9,8},{10,9},{11,1... | collective-permute-start | bytes 147464 | tf_op jit(solution)/shard_map/ppermute | solution.py:351
  90.2 33.6 %copy-start.5 = (bf16[2,128,1536]{2,1,0:T(8,128)(2,1)}, bf16[2,128,1536]{2,1,0:T(8,128)(2,1)S(1)}, u32[]{:S(2)}) copy-start(bf16[2,128,1536]{2,1,0:T(8,128)(2,1)S(1)} %reshape.60.own) | copy-start | bytes 2359300
  90.2 21.9 %collective-permute-start.8 = (bf16[2,128,1536]{2,1,0:T(8,128)(2,1)S(1)}, bf16[2,128,1536]{2,1,0:T(8,128)(2,1)S(1)}, u32[]{:S(2)}, u32[]{:S(2)}) collective-permute-start(bf16[2,128,1536]{2,1,0:T(8,128)(2,1)S(1)} %reshape.60.own), channel_id=1, source_target_pairs={{0,1},{1,2},{2,3},{3,0},{4,5},{5,6},{6,7},{7,4},{8,9},{9,10},{10,1... | collective-permute-start | bytes 2359304 | tf_op jit(solution)/shard_map/ppermute | solution.py:380
  90.3 21.8 %collective-permute-start.9 = (bf16[2,128,1536]{2,1,0:T(8,128)(2,1)S(1)}, bf16[2,128,1536]{2,1,0:T(8,128)(2,1)}, u32[]{:S(2)}, u32[]{:S(2)}) collective-permute-start(bf16[2,128,1536]{2,1,0:T(8,128)(2,1)S(1)} %reshape.60.own), channel_id=1, source_target_pairs={{1,0},{2,1},{3,2},{0,3},{5,4},{6,5},{7,6},{4,7},{9,8},{10,9},{11,1... | collective-permute-start | bytes 2359304 | tf_op jit(solution)/shard_map/ppermute | solution.py:380
  112.1 11.6 %copy-start.6 = (bf16[2,128,1536]{2,1,0:T(8,128)(2,1)}, bf16[2,128,1536]{2,1,0:T(8,128)(2,1)S(1)}, u32[]{:S(2)}) copy-start(bf16[2,128,1536]{2,1,0:T(8,128)(2,1)S(1)} %collective-permute-done.8.left) | copy-start | bytes 2359300
  112.1 11.5 %collective-permute-start.10 = (bf16[128,1536]{1,0:T(8,128)(2,1)S(1)}, bf16[128,1536]{1,0:T(8,128)(2,1)S(1)}, u32[]{:S(2)}, u32[]{:S(2)}) collective-permute-start(bf16[128,1536]{1,0:T(8,128)(2,1)S(1)} %slice_bitcast_fusion.3), channel_id=1, source_target_pairs={{0,1},{1,2},{2,3},{3,0},{4,5},{5,6},{6,7},{7,4},{8,9},{9,10},{10,1... | collective-permute-start | bytes 1179656 | tf_op jit(solution)/shard_map/ppermute | solution.py:383
  113.9 9.8 %collective-permute-start.11 = (bf16[128,1536]{1,0:T(8,128)(2,1)S(1)}, bf16[128,1536]{1,0:T(8,128)(2,1)S(1)}, u32[]{:S(2)}, u32[]{:S(2)}) collective-permute-start(bf16[128,1536]{1,0:T(8,128)(2,1)S(1)} %slice_bitcast_fusion.2), channel_id=1, source_target_pairs={{1,0},{2,1},{3,2},{0,3},{5,4},{6,5},{7,6},{4,7},{9,8},{10,9},{11,1... | collective-permute-start | bytes 1179656 | tf_op jit(solution)/shard_map/ppermute | solution.py:383
  116.0 23.1 %collective-permute-start.16 = (bf16[2,64,1536]{2,1,0:T(8,128)(2,1)S(1)}, bf16[2,64,1536]{2,1,0:T(8,128)(2,1)S(1)}, u32[]{:S(2)}, u32[]{:S(2)}) collective-permute-start(bf16[2,64,1536]{2,1,0:T(8,128)(2,1)S(1)} %reshape.63.own), channel_id=1, source_target_pairs={{0,1},{1,2},{2,3},{3,0},{4,5},{5,6},{6,7},{7,4},{8,9},{9,10},{10,1... | collective-permute-start | bytes 1179656 | tf_op jit(solution)/shard_map/ppermute | solution.py:380
  116.0 23.1 %collective-permute-start.17 = (bf16[2,64,1536]{2,1,0:T(8,128)(2,1)S(1)}, bf16[2,64,1536]{2,1,0:T(8,128)(2,1)S(1)}, u32[]{:S(2)}, u32[]{:S(2)}) collective-permute-start(bf16[2,64,1536]{2,1,0:T(8,128)(2,1)S(1)} %reshape.63.own), channel_id=1, source_target_pairs={{1,0},{2,1},{3,2},{0,3},{5,4},{6,5},{7,6},{4,7},{9,8},{10,9},{11,1... | collective-permute-start | bytes 1179656 | tf_op jit(solution)/shard_map/ppermute | solution.py:380
  139.1 17.5 %collective-permute-start.12 = (bf16[2,128,1536]{2,1,0:T(8,128)(2,1)S(1)}, bf16[2,128,1536]{2,1,0:T(8,128)(2,1)S(1)}, u32[]{:S(2)}, u32[]{:S(2)}) collective-permute-start(bf16[2,128,1536]{2,1,0:T(8,128)(2,1)S(1)} %get-tuple-element.52), channel_id=1, source_target_pairs={{1,0},{2,1},{3,2},{0,3},{5,4},{6,5},{7,6},{4,7},{9,8},{10,9},{11,1... | collective-permute-start | bytes 2359304 | tf_op jit(solution)/shard_map/ppermute | solution.py:399
  142.6 21.9 %collective-permute-start.18 = (bf16[64,1536]{1,0:T(8,128)(2,1)S(1)}, bf16[64,1536]{1,0:T(8,128)(2,1)S(1)}, u32[]{:S(2)}, u32[]{:S(2)}) collective-permute-start(bf16[64,1536]{1,0:T(8,128)(2,1)S(1)} %slice_bitcast_fusion.5), channel_id=1, source_target_pairs={{0,1},{1,2},{2,3},{3,0},{4,5},{5,6},{6,7},{7,4},{8,9},{9,10},{10,1... | collective-permute-start | bytes 589832 | tf_op jit(solution)/shard_map/ppermute | solution.py:383
  142.7 21.4 %collective-permute-start.13 = (bf16[2,128,1536]{2,1,0:T(8,128)(2,1)S(1)}, bf16[2,128,1536]{2,1,0:T(8,128)(2,1)S(1)}, u32[]{:S(2)}, u32[]{:S(2)}) collective-permute-start(bf16[2,128,1536]{2,1,0:T(8,128)(2,1)S(1)} %get-tuple-element.54), channel_id=1, source_target_pairs={{0,1},{1,2},{2,3},{3,0},{4,5},{5,6},{6,7},{7,4},{8,9},{9,10},{10,1... | collective-permute-start | bytes 2359304 | tf_op jit(solution)/shard_map/ppermute | solution.py:399
  142.8 21.7 %collective-permute-start.19 = (bf16[64,1536]{1,0:T(8,128)(2,1)S(1)}, bf16[64,1536]{1,0:T(8,128)(2,1)S(1)}, u32[]{:S(2)}, u32[]{:S(2)}) collective-permute-start(bf16[64,1536]{1,0:T(8,128)(2,1)S(1)} %slice_bitcast_fusion.4), channel_id=1, source_target_pairs={{1,0},{2,1},{3,2},{0,3},{5,4},{6,5},{7,6},{4,7},{9,8},{10,9},{11,1... | collective-permute-start | bytes 589832 | tf_op jit(solution)/shard_map/ppermute | solution.py:383
  156.8 17.2 %collective-permute-start.15 = (bf16[128,1536]{1,0:T(8,128)(2,1)S(1)}, bf16[128,1536]{1,0:T(8,128)(2,1)S(1)}, u32[]{:S(2)}, u32[]{:S(2)}) collective-permute-start(bf16[128,1536]{1,0:T(8,128)(2,1)S(1)} %fusion), channel_id=1, source_target_pairs={{1,0},{2,1},{3,2},{0,3},{5,4},{6,5},{7,6},{4,7},{9,8},{10,9},{11,1... | collective-permute-start | bytes 1179656 | tf_op jit(solution)/shard_map/ppermute | solution.py:403
  164.2 9.8 %collective-permute-start.14 = (bf16[128,1536]{1,0:T(8,128)(2,1)S(1)}, bf16[128,1536]{1,0:T(8,128)(2,1)S(1)}, u32[]{:S(2)}, u32[]{:S(2)}) collective-permute-start(bf16[128,1536]{1,0:T(8,128)(2,1)S(1)} %fusion.1), channel_id=1, source_target_pairs={{0,1},{1,2},{2,3},{3,0},{4,5},{5,6},{6,7},{7,4},{8,9},{9,10},{10,1... | collective-permute-start | bytes 1179656 | tf_op jit(solution)/shard_map/ppermute | solution.py:403
  174.0 46.4 %copy-start.7 = (f32[256]{0:T(256)S(1)}, f32[256]{0:T(256)}, u32[]{:S(2)}) copy-start(f32[256]{0:T(256)} %param.17) | copy-start | bytes 3076
  174.0 8.1 %collective-permute-start.20 = (bf16[2,64,1536]{2,1,0:T(8,128)(2,1)}, bf16[2,64,1536]{2,1,0:T(8,128)(2,1)S(1)}, u32[]{:S(2)}, u32[]{:S(2)}) collective-permute-start(bf16[2,64,1536]{2,1,0:T(8,128)(2,1)} %get-tuple-element.62), channel_id=1, source_target_pairs={{0,1},{1,2},{2,3},{3,0},{4,5},{5,6},{6,7},{7,4},{8,9},{9,10},{10,1... | collective-permute-start | bytes 1179656 | tf_op jit(solution)/shard_map/ppermute | solution.py:407
  174.1 8.0 %collective-permute-start.21 = (bf16[2,64,1536]{2,1,0:T(8,128)(2,1)S(1)}, bf16[2,64,1536]{2,1,0:T(8,128)(2,1)}, u32[]{:S(2)}, u32[]{:S(2)}) collective-permute-start(bf16[2,64,1536]{2,1,0:T(8,128)(2,1)S(1)} %get-tuple-element.63), channel_id=1, source_target_pairs={{1,0},{2,1},{3,2},{0,3},{5,4},{6,5},{7,6},{4,7},{9,8},{10,9},{11,1... | collective-permute-start | bytes 1179656 | tf_op jit(solution)/shard_map/ppermute | solution.py:407
  183.8 17.1 %collective-permute-start.23 = (bf16[64,1536]{1,0:T(8,128)(2,1)}, bf16[64,1536]{1,0:T(8,128)(2,1)S(1)}, u32[]{:S(2)}, u32[]{:S(2)}) collective-permute-start(bf16[64,1536]{1,0:T(8,128)(2,1)} %fusion.4), channel_id=1, source_target_pairs={{1,0},{2,1},{3,2},{0,3},{5,4},{6,5},{7,6},{4,7},{9,8},{10,9},{11,1... | collective-permute-start | bytes 589832 | tf_op jit(solution)/shard_map/ppermute | solution.py:412
  187.1 13.7 %collective-permute-start.22 = (bf16[64,1536]{1,0:T(8,128)(2,1)}, bf16[64,1536]{1,0:T(8,128)(2,1)S(1)}, u32[]{:S(2)}, u32[]{:S(2)}) collective-permute-start(bf16[64,1536]{1,0:T(8,128)(2,1)} %fusion.5), channel_id=1, source_target_pairs={{0,1},{1,2},{2,3},{3,0},{4,5},{5,6},{6,7},{7,4},{8,9},{9,10},{10,1... | collective-permute-start | bytes 589832 | tf_op jit(solution)/shard_map/ppermute | solution.py:411
  189.0 26.0 %all-to-all-start.2 = ((bf16[32,8,1536]{2,1,0:T(8,128)(2,1)}), bf16[32,8,1536]{2,1,0:T(8,128)(2,1)S(1)}, u32[]{:S(2)}, u32[]{:S(2)}) async-start(bf16[32,8,1536]{2,1,0:T(8,128)(2,1)} %reshape.64), calls=%async_computation.2 | async-start | bytes 1572864 | tf_op jit(solution)/shard_map/all_to_all | solution.py:388
  216.4 14.1 %all-to-all-start.3 = ((bf16[32,4,1536]{2,1,0:T(4,128)(2,1)}), bf16[32,4,1536]{2,1,0:T(4,128)(2,1)S(1)}, u32[]{:S(2)}, u32[]{:S(2)}) async-start(bf16[32,4,1536]{2,1,0:T(4,128)(2,1)} %reshape.67), calls=%async_computation.3 | async-start | bytes 786432 | tf_op jit(solution)/shard_map/all_to_all | solution.py:388

commit v3 on v2

--- a/solution.py
+++ b/solution.py
@@ -13,7 +13,9 @@
 TILE = 128
 SPAN = 2 * HALF + TILE
 EDGE = 16
-GROUPS = (6, 4, 2)
+GROUPS = (8, 4)
+SIDE = 2
+BLOCK = SIDE * PAIR
 MIB = 1024 * 1024
 STEP = 512
 F32 = jnp.float32
@@ -31,7 +33,7 @@
     )
 
 
-def attend_pair(edge_ref, q_ref, kv_ref, lo_ref, hi_ref, bias):
+def fill_bias(edge_ref, bias):
     @pl.when(pl.program_id(0) == 0)
     def _():
         row = lax.broadcasted_iota(jnp.int32, (TILE, SPAN), 0)
@@ -42,42 +44,56 @@
             kept = (col > row) & (col - row < 2 * HALF) & (col >= low) & (col < high)
             bias[r] = jnp.where(kept, 0.0, -1e30)
 
+
+def attend_pairs(q_ref, kv_ref, lo_ref, hi_ref, bias, put):
     lane = lax.broadcasted_iota(jnp.int32, (1, PAIR), 1)
     first = lane < HEAD
     only0 = jnp.where(first, 0.125, 0.0).astype(BF16)
     only1 = jnp.where(first, 0.0, 0.125).astype(BF16)
     ones = jnp.ones((SPAN, PAIR), BF16)
-    halves = []
-    for r in range(2):
-        if r == 0:
-            join = lambda i: [lo_ref[i], kv_ref[i], hi_ref[i, :TILE]]
-        else:
-            join = lambda i: [lo_ref[i, TILE:], kv_ref[i], hi_ref[i]]
-        q = q_ref[r * TILE : (r + 1) * TILE]
-        both = jnp.concatenate([q * only0, q * only1], axis=0)
-        s = lax.dot_general(
-            both, jnp.concatenate(join(0), axis=0), (((1,), (1,)), ((), ())), preferred_element_type=F32
-        )
-        s = s + jnp.concatenate([bias[r], bias[r]], axis=0)
-        p = jnp.exp(s - jnp.max(s, axis=1, keepdims=True)).astype(BF16)
-        values = jnp.concatenate([jnp.concatenate(join(1), axis=0), ones], axis=1)
-        o = jnp.dot(p, values, preferred_element_type=F32)
-        o = o[:, :PAIR] / o[:, PAIR:]
-        halves.append(jnp.where(first, o[:TILE], o[TILE:]))
-    return halves
+    for c in range(SIDE):
+        cols = slice(c * PAIR, (c + 1) * PAIR)
+        for r in range(2):
+            if r == 0:
+                join = lambda i: [lo_ref[i, :, cols], kv_ref[i, :, cols], hi_ref[i, :TILE, cols]]
+            else:
+                join = lambda i: [lo_ref[i, TILE:, cols], kv_ref[i, :, cols], hi_ref[i, :, cols]]
+            rows = slice(r * TILE, (r + 1) * TILE)
+            q = q_ref[rows, cols]
+            both = jnp.concatenate([q * only0, q * only1], axis=0)
+            s = lax.dot_general(
+                both,
+                jnp.concatenate(join(0), axis=0),
+                (((1,), (1,)), ((), ())),
+                preferred_element_type=F32,
+            )
+            s = s + jnp.concatenate([bias[r], bias[r]], axis=0)
+            p = jnp.exp(s - jnp.max(s, axis=1, keepdims=True)).astype(BF16)
+            values = jnp.concatenate([jnp.concatenate(join(1), axis=0), ones], axis=1)
+            o = jnp.dot(p, values, preferred_element_type=F32)
+            o = o[:, :PAIR] / o[:, PAIR:]
+            put(c, rows, jnp.where(first, o[:TILE], o[TILE:]))
 
 
 def attend_body(edge_ref, q_ref, kv_ref, lo_ref, hi_ref, out_ref, bias):
-    for r, half in enumerate(attend_pair(edge_ref, q_ref, kv_ref, lo_ref, hi_ref, bias)):
-        out_ref[r * TILE : (r + 1) * TILE] = half
+    fill_bias(edge_ref, bias)
+
+    def put(c, rows, value):
+        out_ref[rows, c * PAIR : (c + 1) * PAIR] = value
+
+    attend_pairs(q_ref, kv_ref, lo_ref, hi_ref, bias, put)
 
 
 def attend_norm_body(groups, edge_ref, q_ref, kv_ref, lo_ref, hi_ref, gain_ref, *rest):
     n = len(groups)
     earlier, (out_ref, low_ref, high_ref, bias, mine) = rest[:n], rest[n:]
     step = pl.program_id(0)
-    for r, half in enumerate(attend_pair(edge_ref, q_ref, kv_ref, lo_ref, hi_ref, bias)):
-        mine[step, r * TILE : (r + 1) * TILE] = half
+    fill_bias(edge_ref, bias)
+
+    def put(c, rows, value):
+        mine[step * SIDE + c, rows] = value
+
+    attend_pairs(q_ref, kv_ref, lo_ref, hi_ref, bias, put)
 
     @pl.when(step == pl.num_programs(0) - 1)
     def _():
@@ -105,10 +121,10 @@
         last = g == len(GROUPS) - 1
         base = [
             pl.BlockSpec(memory_space=pltpu.SMEM),
-            pl.BlockSpec((rows, PAIR), lambda j, s=start: (0, s + j)),
-            pl.BlockSpec((2, rows, PAIR), lambda j, s=start: (0, 0, s + j)),
-            pl.BlockSpec((2, rows, PAIR), lambda j: (0, 0, j)),
-            pl.BlockSpec((2, rows, PAIR), lambda j: (0, 0, j)),
+            pl.BlockSpec((rows, BLOCK), lambda j, s=start // SIDE: (0, s + j)),
+            pl.BlockSpec((2, rows, BLOCK), lambda j, s=start // SIDE: (0, 0, s + j)),
+            pl.BlockSpec((2, rows, BLOCK), lambda j: (0, 0, j)),
+            pl.BlockSpec((2, rows, BLOCK), lambda j: (0, 0, j)),
         ]
         scratch = [pltpu.VMEM((2, TILE, SPAN), F32)]
         cost = (pairs * 16 * rows * SPAN * PAIR, pairs * 7 * rows * PAIR * 2)
@@ -123,9 +139,9 @@
                     jax.ShapeDtypeStruct((rows, pairs * PAIR), F32),
                     cost,
                     16,
-                    grid=(pairs,),
+                    grid=(pairs // SIDE,),
                     in_specs=base,
-                    out_specs=pl.BlockSpec((rows, PAIR), lambda j: (0, j)),
+                    out_specs=pl.BlockSpec((rows, BLOCK), lambda j: (0, j)),
                     scratch_shapes=scratch,
                 )(*args)
             )
@@ -140,7 +156,7 @@
                 ],
                 cost,
                 20,
-                grid=(pairs,),
+                grid=(pairs // SIDE,),
                 in_specs=base + [whole(1, width)] + [whole(*o.shape) for o in outs],
                 out_specs=[whole(rows, width), whole(EDGE, width), whole(EDGE, width)],
                 scratch_shapes=scratch + [pltpu.VMEM((pairs, rows, PAIR), F32)],
@@ -253,7 +269,12 @@
     )(mixed, gate[:, None], place[:, None], *parts)
 
 
-def ffn_body(own, left, right, far0, far1, w_in, w_out, keep, up, down, up2, down2, *scratch):
+def ffn_body(direct, own, left, right, *rest):
+    if direct:
+        far, w_in, w_out, keep, to_right, to_left, to_far, *scratch = rest
+        far0, far1 = far.at[0], far.at[1]
+    else:
+        far0, far1, w_in, w_out, keep, up, down, up2, down2, *scratch = rest
     rows_in, hidden, first, second, sems = scratch
     n, width = own.shape[1:]
     units = hidden.shape[1]
@@ -281,7 +302,11 @@
             cols = slice(t * step, (t + 1) * step)
             part = jnp.dot(hidden[...], second[e, t], preferred_element_type=F32).astype(BF16)
             keep[e, :, cols] = part[:n]
-            if e == 0:
+            if direct:
+                to_left[e, :, cols] = part[n : 2 * n]
+                to_right[e, :, cols] = part[2 * n : 3 * n]
+                to_far[e, :, cols] = part[3 * n :]
+            elif e == 0:
                 down[1, :, cols] = part[n : 2 * n]
                 up2[:, cols] = part[2 * n : 3 * n]
                 up[0, :, cols] = part[3 * n :]
@@ -291,17 +316,18 @@
                 down[0, :, cols] = part[3 * n :]
 
 
-def ffn(own, left, right, far0, far1, w_in, w_out):
+def ffn(own, left, right, far, w_in, w_out):
+    direct = len(far) == 1
     experts, n, width = own.shape
     units = w_in.shape[2]
     pair = jax.ShapeDtypeStruct((2, n, width), BF16)
     single = jax.ShapeDtypeStruct((n, width), BF16)
     return call(
-        ffn_body,
-        [pair, pair, pair, single, single],
+        functools.partial(ffn_body, direct),
+        [pair] * 4 if direct else [pair, pair, pair, single, single],
         (experts * 4 * n * width * units * 4, 2 * experts * width * units * 2),
         50,
-        in_specs=[pl.BlockSpec(memory_space=pltpu.VMEM)] * 5 + [pl.BlockSpec(memory_space=pl.ANY)] * 2,
+        in_specs=[pl.BlockSpec(memory_space=pltpu.VMEM)] * (3 + len(far)) + [pl.BlockSpec(memory_space=pl.ANY)] * 2,
         scratch_shapes=[
             pltpu.VMEM((4 * n, width), BF16),
             pltpu.VMEM((4 * n, units), BF16),
@@ -309,7 +335,7 @@
             pltpu.VMEM((2, width // STEP, units, STEP), BF16),
             pltpu.SemaphoreType.DMA((2, 2, max(units, width) // STEP)),
         ],
-    )(own, left, right, far0, far1, w_in, w_out)
+    )(own, left, right, *far, w_in, w_out)
 
 
 def on_device(
@@ -379,40 +405,43 @@
     def near(own):
         return lax.ppermute(own, "expert", up), lax.ppermute(own, "expert", down)
 
-    def far(left, right):
-        return lax.ppermute(left[0], "expert", up), lax.ppermute(right[1], "expert", down)
+    def far(halves):
+        return lax.ppermute(halves[0], "expert", up), lax.ppermute(halves[1], "expert", down)
+
+    def home(summed, size):
+        summed = summed.reshape(local, time_count, size, width).transpose(1, 0, 2, 3)
+        return summed.reshape(time_count, local * size, width)
 
     def leave(summed, size):
-        summed = summed.reshape(local, time_count, size, width).transpose(1, 0, 2, 3)
-        summed = summed.reshape(time_count, local * size, width)
         got = lax.all_to_all(summed, "tm", split_axis=0, concat_axis=0, tiled=True)
         return got.reshape(experts * size, width)
 
     after = lambda values, *others: lax.optimization_barrier((tuple(values), others))[0]
     own_a = arrive(chunks[0], sizes[0])
     left_a, right_a = near(own_a)
-    own_b = arrive(chunks[1], sizes[1])
+    own_b = arrive(*after((chunks[1],), own_a), sizes[1])
     left_a, right_a = after((left_a, right_a), own_b)
-    far_a = far(left_a, right_a)
+    far_a = far((left_a[0], right_a[1]))
     left_b, right_b = near(own_b)
-    keep_a, go_up_a, go_down_a, up2_a, down2_a = ffn(own_a, left_a, right_a, *far_a, w_in, w_out)
+    across = [(i, (i + 2) % group_count) for i in range(group_count)]
+    far_b = lax.ppermute(own_b, "expert", across)
+    keep_a, go_up_a, go_down_a, up2_a, down2_a = ffn(own_a, left_a, right_a, far_a, w_in, w_out)
     below_a, above_a = lax.ppermute(go_up_a, "expert", up), lax.ppermute(go_down_a, "expert", down)
-    left_b, right_b = after((left_b, right_b), keep_a)
-    far_b = far(left_b, right_b)
+    (own_b,) = after((own_b,), keep_a)
+    keep_b, to_right, to_left, to_far = ffn(own_b, left_b, right_b, (far_b,), w_in, w_out)
+    below_a, above_a = after((below_a, above_a), keep_b)
     up2_a, down2_a = add(up2_a, below_a[0]), add(down2_a, above_a[0])
     up3_a, down3_a = lax.ppermute(up2_a, "expert", up), lax.ppermute(down2_a, "expert", down)
-    (own_b,) = after((own_b,), up2_a, down2_a)
-    keep_b, go_up_b, go_down_b, up2_b, down2_b = ffn(own_b, left_b, right_b, *far_b, w_in, w_out)
-    go_up_b, go_down_b = after((go_up_b, go_down_b), up3_a, down3_a)
-    below_b, above_b = lax.ppermute(go_up_b, "expert", up), lax.ppermute(go_down_b, "expert", down)
+    to_right, to_left, to_far = after((to_right, to_left, to_far), up3_a, down3_a)
+    parts_b = (
+        lax.ppermute(to_right, "expert", up),
+        lax.ppermute(to_left, "expert", down),
+        lax.ppermute(to_far, "expert", across),
+    )
     total_a = jnp.stack([add(keep_a[0], above_a[1], up3_a), add(keep_a[1], below_a[1], down3_a)])
-    back_a = leave(total_a, sizes[0])
-    below_b, above_b = after((below_b, above_b), total_a)
-    up3_b = lax.ppermute(add(up2_b, below_b[0]), "expert", up)
-    down3_b = lax.ppermute(add(down2_b, above_b[0]), "expert", down)
-    total_b = jnp.stack([add(keep_b[0], above_b[1], up3_b), add(keep_b[1], below_b[1], down3_b)])
-    (total_b,) = after((total_b,), back_a)
-    back_b = leave(total_b, sizes[1])
+    back_a = leave(home(total_a, sizes[0]), sizes[0])
+    parts_b = after(parts_b, back_a)
+    back_b = leave(home(add(keep_b, *parts_b), sizes[1]), sizes[1])
     return combine(mixed, expert_gate, place, [back_a, back_b])
 
 

time: 235 us -> 226 us (0.962)
  starting transfers between devices: 72.1 us -> 58.5 us
  waiting for transfers between devices: 53.6 us -> 66 us
  blocking collectives: 39.4 us -> 35.7 us
  Pallas kernels: 47.2 us -> 44.1 us
    all_to_all x2, waiting for transfers between devices: 23.1 us -> 10 us  [leave(): got = lax.all_to_all(summed, 'tm', split_axis=0, concat_axis=0, tiled=True)]
    ppermute x8 -> x6, waiting for transfers between devices: 9.9 us -> 22.1 us  [the longest x1 17.3 us: on_device(): lax.ppermute(to_right, 'expert', up)]
    ppermute x1, waiting for transfers between devices: 11.1 us -> 0.01 us  [on_device(): lax.ppermute(go_down_a, 'expert', down)]
    ppermute x3 -> x2, waiting for transfers between devices: 2.58 us -> 11.4 us  [on_device(): high.append(lax.ppermute(part, order, back))]
    ppermute x3 -> x2, waiting for transfers between devices: 0.01 us -> 6.64 us  [on_device(): low.append(lax.ppermute(part, order, onward))]
    ppermute x3 -> x2, starting transfers between devices: 15.7 us -> 9.46 us  [on_device(): high.append(lax.ppermute(part, order, back))]
    ppermute x8 -> x6, starting transfers between devices: 11 us -> 5.56 us  [the longest x1 2.66 us: on_device(): lax.ppermute(to_left, 'expert', down)]
    ppermute x1, waiting for transfers between devices: 0.01 us -> 4.54 us  [on_device(): lax.ppermute(down2_a, 'expert', down)]
  transfers between devices with their start and end apart: 26 -> 22, of which waited for: 8 -> 9; matrix products, arithmetic and copies ran while one was open for 5% -> 3% of each run, Pallas kernels for 17% -> 16%
where the time goes in v3:
time: 226 us; the launch traced here: 225 us
  waiting for transfers between devices  66 us (29%)
  starting transfers between devices  58.5 us (26%)
  Pallas kernels  44.1 us (20%)
  blocking collectives  35.7 us (16%)
  local copies, waits for them, and re-layouts  16.2 us (7%)
  other arithmetic  3.89 us (2%)
    all_to_all x2, blocking collectives, arrive(): own = lax.all_to_all(sent, 'tm', split_axis=0, concat_axis=0, tiled=True)  35.7 us
    pallas_call x2, Pallas kernels, ffn(): call(functools.partial(ffn_body, direct), [pair] * 4 if direct else [pair...  24.1 us
    all_to_all x2, starting transfers between devices, leave(): got = lax.all_to_all(summed, 'tm', split_axis=0, concat_axis=0, tiled=True)  17.6 us
    ppermute x1, waiting for transfers between devices, on_device(): lax.ppermute(to_right, 'expert', up)  17.3 us
    ppermute x2, waiting for transfers between devices, on_device(): high.append(lax.ppermute(part, order, back))  11.4 us
    all_to_all x2, waiting for transfers between devices, leave(): got = lax.all_to_all(summed, 'tm', split_axis=0, concat_axis=0, tiled=True)  10 us
    ppermute x2, starting transfers between devices, on_device(): high.append(lax.ppermute(part, order, back))  9.46 us
    pallas_call x1, Pallas kernels, attention(): call(attend_body, jax.ShapeDtypeStruct((rows, pairs * PAIR), F32), cost,...  7.35 us
  transfers between devices with their start and end apart: 22, of which 9 were waited for; matrix products, arithmetic and copies ran while one was open for 3% of the time, Pallas kernels for 16%

profile of v3, /device:TPU:1, one launch (start us, length us, event | category | flops | bytes accessed | tf_op | source)
XLA Modules:
  0.0 224.7 jit_solution(12742122496155481824)
XLA Ops:
  0.0 2.4 %slice.30 = bf16[2,256,1024]{2,1,0:T(8,128)(2,1)} slice(bf16[2,256,1536]{2,1,0:T(8,128)(2,1)} %kv_ref.3), slice={[0:2], [0:256], [0:1024]} | slice | bytes 2097152 | tf_op jit(solution)/shard_map/slice | solution.py:369
  2.4 4.4 %collective-permute-start.2 = (bf16[2,256,1024]{2,1,0:T(8,128)(2,1)}, bf16[2,256,1024]{2,1,0:T(8,128)(2,1)S(1)}, u32[]{:S(2)}, u32[]{:S(2)}) collective-permute-start(bf16[2,256,1024]{2,1,0:T(8,128)(2,1)} %slice.30), channel_id=1, source_target_pairs={{0,1},{1,2},{2,3},{3,4},{4,5},{5,6},{6,7},{7,8},{8,9},{9,10},{10,1... | collective-permute-start | bytes 3145736 | tf_op jit(solution)/shard_map/ppermute | solution.py:370
  6.8 4.6 %collective-permute-start.3 = (bf16[2,256,1024]{2,1,0:T(8,128)(2,1)}, bf16[2,256,1024]{2,1,0:T(8,128)(2,1)}, u32[]{:S(2)}, u32[]{:S(2)}) collective-permute-start(bf16[2,256,1024]{2,1,0:T(8,128)(2,1)} %slice.30), channel_id=1, source_target_pairs={{1,0},{2,1},{3,2},{4,3},{5,4},{6,5},{7,6},{8,7},{9,8},{10,9},{11,1... | collective-permute-start | bytes 3145736 | tf_op jit(solution)/shard_map/ppermute | solution.py:371
  11.4 1.9 slice.31
  13.3 1.9 collective-permute-start
  15.2 4.9 %collective-permute-start.1 = (bf16[2,256,512]{2,1,0:T(8,128)(2,1)}, bf16[2,256,512]{2,1,0:T(8,128)(2,1)}, u32[]{:S(2)}, u32[]{:S(2)}) collective-permute-start(bf16[2,256,512]{2,1,0:T(8,128)(2,1)} %slice.31), channel_id=1, source_target_pairs={{1,0},{2,1},{3,2},{4,3},{5,4},{6,5},{7,6},{8,7},{9,8},{10,9},{11,1... | collective-permute-start | bytes 1572872 | tf_op jit(solution)/shard_map/ppermute | solution.py:371
  20.1 0.7 broadcast_in_dim.15.gain_ref
  20.8 0.7 broadcast_in_dim.16.gain_ref
  21.5 0.7 compare_select_fusion.1
  22.3 6.6 %collective-permute-done.2.lo_ref = bf16[2,256,1024]{2,1,0:T(8,128)(2,1)S(1)} collective-permute-done((bf16[2,256,1024]{2,1,0:T(8,128)(2,1)}, bf16[2,256,1024]{2,1,0:T(8,128)(2,1)S(1)}, u32[]{:S(2)}, u32[]{:S(2)}) %collective-permute-start.2) | collective-permute-done | bytes 1048608 | tf_op jit(solution)/shard_map/ppermute | solution.py:370
  28.9 11.4 %collective-permute-done.3.hi_ref = bf16[2,256,1024]{2,1,0:T(8,128)(2,1)} collective-permute-done((bf16[2,256,1024]{2,1,0:T(8,128)(2,1)}, bf16[2,256,1024]{2,1,0:T(8,128)(2,1)}, u32[]{:S(2)}, u32[]{:S(2)}) %collective-permute-start.3) | collective-permute-done | bytes 1048608 | tf_op jit(solution)/shard_map/ppermute | solution.py:371
  40.3 1.4 copy-done
  41.7 1.1 copy-done.3
  42.8 7.3 %shard_map.118.rest_0_ = f32[256,1024]{1,0:T(8,128)S(1)} custom-call(s32[2]{0:T(128)S(1)} %add_convert_fusion.1.edge_ref, bf16[256,1536]{1,0:T(8,128)(2,1)S(1)} %copy-done.3, bf16[2,256,1536]{2,1,0:T(8,128)(2,1)S(1)} %copy-done, bf16[2,256,1024]{2,1,0:T(8,128)(2,1)S(1)} %collective-permute-done.2.lo_ref, bf16[2,256,1024]{2,1,0:T(8,128)(2,1)} %collective-permute-done.3.hi_ref), custom_call_target="tpu_custom_call" | custom-call | flops 2684354560 | bytes 3670016 | tf_op jit(solution)/shard_map/pallas_call | solution.py:137
  50.2 4.5 %shard_map.119 = (bf16[256,1536]{1,0:T(8,128)(2,1)S(1)}, bf16[16,1536]{1,0:T(8,128)(2,1)S(1)}, bf16[16,1536]{1,0:T(8,128)(2,1)S(1)}) custom-call(s32[2]{0:T(128)S(1)} %add_convert_fusion.1.edge_ref, bf16[256,1536]{1,0:T(8,128)(2,1)S(1)} %copy-done.4, bf16[2,256,1536]{2,1,0:T(8,128)(2,1)S(1)} %copy-done.1, bf16[2,256,512]{2,1,0:T(8,128)(2,1)} %collective-permute-done.lo_ref, ...), custom_call_target="tpu_custom_call" | custom-call | flops 1342177280 | bytes 1835008 | tf_op jit(solution)/shard_map/pallas_call | solution.py:150
  54.7 1.9 collective-permute-start.4
  56.7 5.6 %collective-permute-start.5 = (bf16[16,1536]{1,0:T(8,128)(2,1)S(1)}, bf16[16,1536]{1,0:T(8,128)(2,1)S(1)}, u32[]{:S(2)}, u32[]{:S(2)}) collective-permute-start(bf16[16,1536]{1,0:T(8,128)(2,1)S(1)} %get-tuple-element.40), channel_id=1, source_target_pairs={{1,0},{2,1},{3,2},{4,3},{5,4},{6,5},{7,6},{8,7},{9,8},{10,9},{11,1... | collective-permute-start | bytes 147464 | tf_op jit(solution)/shard_map/ppermute | solution.py:377
  62.3 3.6 %shard_map.120.inner_ref = bf16[224,1536]{1,0:T(8,128)(2,1)S(1)} custom-call(bf16[256,1536]{1,0:T(8,128)(2,1)S(1)} %get-tuple-element.38.normed_ref, f32[31,1536]{1,0:T(8,128)S(1)} %copy-done.2), custom_call_target="tpu_custom_call" | custom-call | flops 1365245952 | bytes 1572864 | tf_op jit(solution)/shard_map/pallas_call | solution.py:189
  65.9 1.3 shard_map.121
  67.2 21.2 %all_to_all.20 = bf16[32,8,1536]{2,1,0:T(8,128)(2,1)S(1)} all-to-all(bf16[32,8,1536]{2,1,0:T(8,128)(2,1)S(1)} %bitcast.35), channel_id=1, replica_groups=mesh['tm'=32,'expert'=4] {'tm'}, dimensions={0} | all-to-all | bytes 1572864 | tf_op jit(solution)/shard_map/all_to_all | solution.py:401
  88.4 0.2 copy.23
  88.7 0.6 copy.24
  89.3 0.2 reshape.50.own
  89.6 2.7 %collective-permute-start.7 = (bf16[2,128,1536]{2,1,0:T(8,128)(2,1)S(1)}, bf16[2,128,1536]{2,1,0:T(8,128)(2,1)}, u32[]{:S(2)}, u32[]{:S(2)}) collective-permute-start(bf16[2,128,1536]{2,1,0:T(8,128)(2,1)S(1)} %reshape.50.own), channel_id=1, source_target_pairs={{1,0},{2,1},{3,2},{0,3},{5,4},{6,5},{7,6},{4,7},{9,8},{10,9},{11,1... | collective-permute-start | bytes 2359304 | tf_op jit(solution)/shard_map/ppermute | solution.py:406
  92.2 0.1 reshape.51
  92.3 14.5 %all_to_all.21 = bf16[32,4,1536]{2,1,0:T(4,128)(2,1)S(1)} all-to-all(bf16[32,4,1536]{2,1,0:T(4,128)(2,1)S(1)} %reshape.51), channel_id=1, replica_groups=mesh['tm'=32,'expert'=4] {'tm'}, dimensions={0} | all-to-all | bytes 786432 | tf_op jit(solution)/shard_map/all_to_all | solution.py:401
  106.9 0.4 copy.26
  107.3 0.1 reshape.53.own
  107.5 2.6 %collective-permute-done.6.left = bf16[2,128,1536]{2,1,0:T(8,128)(2,1)} collective-permute-done((bf16[2,128,1536]{2,1,0:T(8,128)(2,1)S(1)}, bf16[2,128,1536]{2,1,0:T(8,128)(2,1)}, u32[]{:S(2)}, u32[]{:S(2)}) %collective-permute-start.6) | collective-permute-done | bytes 786464 | tf_op jit(solution)/shard_map/ppermute | solution.py:406
  110.1 1.0 slice_bitcast_fusion.1
  111.1 0.2 collective-permute-start.8
  111.3 1.0 slice_bitcast_fusion
  112.3 2.6 %collective-permute-start.9 = (bf16[128,1536]{1,0:T(8,128)(2,1)S(1)}, bf16[128,1536]{1,0:T(8,128)(2,1)S(1)}, u32[]{:S(2)}, u32[]{:S(2)}) collective-permute-start(bf16[128,1536]{1,0:T(8,128)(2,1)S(1)} %slice_bitcast_fusion), channel_id=1, source_target_pairs={{1,0},{2,1},{3,2},{0,3},{5,4},{6,5},{7,6},{4,7},{9,8},{10,9},{11,1... | collective-permute-start | bytes 1179656 | tf_op jit(solution)/shard_map/ppermute | solution.py:409
  115.0 2.7 %collective-permute-start.13 = (bf16[2,64,1536]{2,1,0:T(8,128)(2,1)S(1)}, bf16[2,64,1536]{2,1,0:T(8,128)(2,1)S(1)}, u32[]{:S(2)}, u32[]{:S(2)}) collective-permute-start(bf16[2,64,1536]{2,1,0:T(8,128)(2,1)S(1)} %reshape.53.own), channel_id=1, source_target_pairs={{1,0},{2,1},{3,2},{0,3},{5,4},{6,5},{7,6},{4,7},{9,8},{10,9},{11,1... | collective-permute-start | bytes 1179656 | tf_op jit(solution)/shard_map/ppermute | solution.py:406
  117.6 4.7 %collective-permute-done.8.rest_0_ = bf16[128,1536]{1,0:T(8,128)(2,1)S(1)} collective-permute-done((bf16[128,1536]{1,0:T(8,128)(2,1)S(1)}, bf16[128,1536]{1,0:T(8,128)(2,1)S(1)}, u32[]{:S(2)}, u32[]{:S(2)}) %collective-permute-start.8) | collective-permute-done | bytes 393248 | tf_op jit(solution)/shard_map/ppermute | solution.py:409
  122.4 15.4 %shard_map.122 = (bf16[2,128,1536]{2,1,0:T(8,128)(2,1)S(1)}, bf16[2,128,1536]{2,1,0:T(8,128)(2,1)S(1)}, bf16[2,128,1536]{2,1,0:T(8,128)(2,1)S(1)}, bf16[128,1536]{1,0:T(8,128)(2,1)S(1)}, bf16[128,1536]{1,0:T(8,128)(2,1)S(1)}) custom-call(bf16[2,128,1536]{2,1,0:T(8,128)(2,1)} %copy-done.5, bf16[2,128,1536]{2,1,0:T(8,128)(2,1)} %collective-permute-done.6.left, ...), custom_call_target="tpu_custom_call" | custom-call | flops 9663676416 | bytes 18874368 | tf_op jit(solution)/shard_map/pallas_call | solution.py:325
  137.8 1.5 collective-permute-start.10
  139.2 2.3 %collective-permute-start.11 = (bf16[2,128,1536]{2,1,0:T(8,128)(2,1)S(1)}, bf16[2,128,1536]{2,1,0:T(8,128)(2,1)S(1)}, u32[]{:S(2)}, u32[]{:S(2)}) collective-permute-start(bf16[2,128,1536]{2,1,0:T(8,128)(2,1)S(1)} %get-tuple-element.49), channel_id=1, source_target_pairs={{1,0},{2,1},{3,2},{0,3},{5,4},{6,5},{7,6},{4,7},{9,8},{10,9},{11,1... | collective-permute-start | bytes 2359304 | tf_op jit(solution)/shard_map/ppermute | solution.py:429
  141.6 8.7 %shard_map.123 = (bf16[2,64,1536]{2,1,0:T(8,128)(2,1)S(1)}, bf16[2,64,1536]{2,1,0:T(8,128)(2,1)S(1)}, bf16[2,64,1536]{2,1,0:T(8,128)(2,1)S(1)}, bf16[2,64,1536]{2,1,0:T(8,128)(2,1)S(1)}) custom-call(bf16[2,64,1536]{2,1,0:T(8,128)(2,1)S(1)} %reshape.53.own, bf16[2,64,1536]{2,1,0:T(8,128)(2,1)S(1)} %collective-permute-done.12.left, ...), custom_call_target="tpu_custom_call" | custom-call | flops 4831838208 | bytes 18874368 | tf_op jit(solution)/shard_map/pallas_call | solution.py:325
  150.3 5.4 %collective-permute-done.10 = bf16[2,128,1536]{2,1,0:T(8,128)(2,1)S(1)} collective-permute-done((bf16[2,128,1536]{2,1,0:T(8,128)(2,1)S(1)}, bf16[2,128,1536]{2,1,0:T(8,128)(2,1)S(1)}, u32[]{:S(2)}, u32[]{:S(2)}) %collective-permute-start.10) | collective-permute-done | bytes 786464 | tf_op jit(solution)/shard_map/ppermute | solution.py:429
  155.7 0.1 fusion
  155.8 2.8 %collective-permute-start.16 = (bf16[128,1536]{1,0:T(8,128)(2,1)S(1)}, bf16[128,1536]{1,0:T(8,128)(2,1)S(1)}, u32[]{:S(2)}, u32[]{:S(2)}) collective-permute-start(bf16[128,1536]{1,0:T(8,128)(2,1)S(1)} %fusion), channel_id=1, source_target_pairs={{1,0},{2,1},{3,2},{0,3},{5,4},{6,5},{7,6},{4,7},{9,8},{10,9},{11,1... | collective-permute-start | bytes 1179656 | tf_op jit(solution)/shard_map/ppermute | solution.py:434
  158.6 0.1 fusion.1
  158.7 4.5 %collective-permute-done.16 = bf16[128,1536]{1,0:T(8,128)(2,1)S(1)} collective-permute-done((bf16[128,1536]{1,0:T(8,128)(2,1)S(1)}, bf16[128,1536]{1,0:T(8,128)(2,1)S(1)}, u32[]{:S(2)}, u32[]{:S(2)}) %collective-permute-start.16) | collective-permute-done | bytes 393248 | tf_op jit(solution)/shard_map/ppermute | solution.py:434
  163.3 3.3 %collective-permute-done.15 = bf16[128,1536]{1,0:T(8,128)(2,1)S(1)} collective-permute-done((bf16[128,1536]{1,0:T(8,128)(2,1)S(1)}, bf16[128,1536]{1,0:T(8,128)(2,1)S(1)}, u32[]{:S(2)}, u32[]{:S(2)}) %collective-permute-start.15) | collective-permute-done | bytes 393248 | tf_op jit(solution)/shard_map/ppermute | solution.py:434
  166.6 1.0 fusion.3
  167.6 1.1 stack.21
  168.7 0.1 stack.22
  168.8 0.6 maximum_bitcast_fusion
  169.3 0.3 copy.27
  169.6 1.1 reshape.54
  170.7 9.3 %all-to-all-start.2 = ((bf16[32,8,1536]{2,1,0:T(8,128)(2,1)}), bf16[32,8,1536]{2,1,0:T(8,128)(2,1)S(1)}, u32[]{:S(2)}, u32[]{:S(2)}) async-start(bf16[32,8,1536]{2,1,0:T(8,128)(2,1)} %reshape.54), calls=%async_computation.2 | async-start | bytes 1572864 | tf_op jit(solution)/shard_map/all_to_all | solution.py:416
  180.1 2.7 %collective-permute-start.18 = (bf16[2,64,1536]{2,1,0:T(8,128)(2,1)S(1)}, bf16[2,64,1536]{2,1,0:T(8,128)(2,1)}, u32[]{:S(2)}, u32[]{:S(2)}) collective-permute-start(bf16[2,64,1536]{2,1,0:T(8,128)(2,1)S(1)} %get-tuple-element.60), channel_id=1, source_target_pairs={{1,0},{2,1},{3,2},{0,3},{5,4},{6,5},{7,6},{4,7},{9,8},{10,9},{11,1... | collective-permute-start | bytes 1179656 | tf_op jit(solution)/shard_map/ppermute | solution.py:438
  182.8 17.3 %collective-permute-done.17 = bf16[2,64,1536]{2,1,0:T(8,128)(2,1)S(1)} collective-permute-done((bf16[2,64,1536]{2,1,0:T(8,128)(2,1)S(1)}, bf16[2,64,1536]{2,1,0:T(8,128)(2,1)S(1)}, u32[]{:S(2)}, u32[]{:S(2)}) %collective-permute-start.17) | collective-permute-done | bytes 393248 | tf_op jit(solution)/shard_map/ppermute | solution.py:437
  200.1 1.3 add_convert_fusion
  201.4 0.1 reshape.56
  201.6 0.3 copy.28
  201.8 0.9 reshape.57
  202.7 8.3 %all-to-all-start.3 = ((bf16[32,4,1536]{2,1,0:T(4,128)(2,1)}), bf16[32,4,1536]{2,1,0:T(4,128)(2,1)S(1)}, u32[]{:S(2)}, u32[]{:S(2)}) async-start(bf16[32,4,1536]{2,1,0:T(4,128)(2,1)} %reshape.57), calls=%async_computation.3 | async-start | bytes 786432 | tf_op jit(solution)/shard_map/all_to_all | solution.py:416
  211.1 0.1 copy.30.place_ref
  211.2 0.1 copy.29.gate_ref
  211.3 10.0 %all-to-all-done.3 = bf16[32,4,1536]{2,1,0:T(4,128)(2,1)S(1)} async-done(((bf16[32,4,1536]{2,1,0:T(4,128)(2,1)}), bf16[32,4,1536]{2,1,0:T(4,128)(2,1)S(1)}, u32[]{:S(2)}, u32[]{:S(2)}) %all-to-all-start.3) | async-done | bytes 393248 | tf_op jit(solution)/shard_map/all_to_all | solution.py:416
  221.4 0.1 reshape.58.rest_1_
  221.5 3.2 %shard_map.124 = bf16[256,1536]{1,0:T(8,128)(2,1)} custom-call(bf16[256,1536]{1,0:T(8,128)(2,1)S(1)} %get-tuple-element.41.mixed_ref, f32[256,1]{1,0:T(8,128)S(1)} %copy.29.gate_ref, s32[256,1]{1,0:T(8,128)S(1)} %copy.30.place_ref, bf16[256,1536]{1,0:T(8,128)(2,1)S(1)} %bitcast.34, bf16[128,1536]{1,0:T(8,128)(2,1)S(1)} %reshape.58.rest_1_), custom_call_target="tpu_custom_call" | custom-call | flops 301989888 | bytes 3145728 | tf_op jit(solution)/shard_map/pallas_call | solution.py:261
  (33 shorter events, 0.5 us)
Async XLA Ops:
  0.0 50.2 %copy-start.1 = (bf16[2,256,1536]{2,1,0:T(8,128)(2,1)S(1)}, bf16[2,256,1536]{2,1,0:T(8,128)(2,1)}, u32[]{:S(2)}) copy-start(bf16[2,256,1536]{2,1,0:T(8,128)(2,1)} %kv_ref.3) | copy-start | bytes 4718596
  0.0 62.3 %copy-start.2 = (f32[31,1536]{1,0:T(8,128)S(1)}, f32[31,1536]{1,0:T(8,128)}, u32[]{:S(2)}) copy-start(f32[31,1536]{1,0:T(8,128)} %taps_ref.3) | copy-start | bytes 571396
  2.4 26.5 %collective-permute-start.2 = (bf16[2,256,1024]{2,1,0:T(8,128)(2,1)}, bf16[2,256,1024]{2,1,0:T(8,128)(2,1)S(1)}, u32[]{:S(2)}, u32[]{:S(2)}) collective-permute-start(bf16[2,256,1024]{2,1,0:T(8,128)(2,1)} %slice.30), channel_id=1, source_target_pairs={{0,1},{1,2},{2,3},{3,4},{4,5},{5,6},{6,7},{7,8},{8,9},{9,10},{10,1... | collective-permute-start | bytes 3145736 | tf_op jit(solution)/shard_map/ppermute | solution.py:370
  6.8 33.5 %collective-permute-start.3 = (bf16[2,256,1024]{2,1,0:T(8,128)(2,1)}, bf16[2,256,1024]{2,1,0:T(8,128)(2,1)}, u32[]{:S(2)}, u32[]{:S(2)}) collective-permute-start(bf16[2,256,1024]{2,1,0:T(8,128)(2,1)} %slice.30), channel_id=1, source_target_pairs={{1,0},{2,1},{3,2},{4,3},{5,4},{6,5},{7,6},{8,7},{9,8},{10,9},{11,1... | collective-permute-start | bytes 3145736 | tf_op jit(solution)/shard_map/ppermute | solution.py:371
  13.3 36.9 %collective-permute-start = (bf16[2,256,512]{2,1,0:T(8,128)(2,1)}, bf16[2,256,512]{2,1,0:T(8,128)(2,1)}, u32[]{:S(2)}, u32[]{:S(2)}) collective-permute-start(bf16[2,256,512]{2,1,0:T(8,128)(2,1)} %slice.31), channel_id=1, source_target_pairs={{0,1},{1,2},{2,3},{3,4},{4,5},{5,6},{6,7},{7,8},{8,9},{9,10},{10,1... | collective-permute-start | bytes 1572872 | tf_op jit(solution)/shard_map/ppermute | solution.py:370
  15.2 35.0 %collective-permute-start.1 = (bf16[2,256,512]{2,1,0:T(8,128)(2,1)}, bf16[2,256,512]{2,1,0:T(8,128)(2,1)}, u32[]{:S(2)}, u32[]{:S(2)}) collective-permute-start(bf16[2,256,512]{2,1,0:T(8,128)(2,1)} %slice.31), channel_id=1, source_target_pairs={{1,0},{2,1},{3,2},{4,3},{5,4},{6,5},{7,6},{8,7},{9,8},{10,9},{11,1... | collective-permute-start | bytes 1572872 | tf_op jit(solution)/shard_map/ppermute | solution.py:371
  40.3 1.4 copy-start
  41.7 1.1 copy-start.3
  42.8 7.4 %copy-start.4 = (bf16[256,1536]{1,0:T(8,128)(2,1)S(1)}, bf16[256,1536]{1,0:T(8,128)(2,1)}, u32[]{:S(2)}) copy-start(bf16[256,1536]{1,0:T(8,128)(2,1)} %q_ref.3) | copy-start | bytes 2359300
  54.7 11.1 %collective-permute-start.4 = (bf16[16,1536]{1,0:T(8,128)(2,1)S(1)}, bf16[16,1536]{1,0:T(8,128)(2,1)S(1)}, u32[]{:S(2)}, u32[]{:S(2)}) collective-permute-start(bf16[16,1536]{1,0:T(8,128)(2,1)S(1)} %get-tuple-element.39), channel_id=1, source_target_pairs={{0,1},{1,2},{2,3},{3,4},{4,5},{5,6},{6,7},{7,8},{8,9},{9,10},{10,1... | collective-permute-start | bytes 147464 | tf_op jit(solution)/shard_map/ppermute | solution.py:376
  56.7 9.2 %collective-permute-start.5 = (bf16[16,1536]{1,0:T(8,128)(2,1)S(1)}, bf16[16,1536]{1,0:T(8,128)(2,1)S(1)}, u32[]{:S(2)}, u32[]{:S(2)}) collective-permute-start(bf16[16,1536]{1,0:T(8,128)(2,1)S(1)} %get-tuple-element.40), channel_id=1, source_target_pairs={{1,0},{2,1},{3,2},{4,3},{5,4},{6,5},{7,6},{8,7},{9,8},{10,9},{11,1... | collective-permute-start | bytes 147464 | tf_op jit(solution)/shard_map/ppermute | solution.py:377
  89.5 32.9 %copy-start.5 = (bf16[2,128,1536]{2,1,0:T(8,128)(2,1)}, bf16[2,128,1536]{2,1,0:T(8,128)(2,1)S(1)}, u32[]{:S(2)}) copy-start(bf16[2,128,1536]{2,1,0:T(8,128)(2,1)S(1)} %reshape.50.own) | copy-start | bytes 2359300
  89.5 20.6 %collective-permute-start.6 = (bf16[2,128,1536]{2,1,0:T(8,128)(2,1)S(1)}, bf16[2,128,1536]{2,1,0:T(8,128)(2,1)}, u32[]{:S(2)}, u32[]{:S(2)}) collective-permute-start(bf16[2,128,1536]{2,1,0:T(8,128)(2,1)S(1)} %reshape.50.own), channel_id=1, source_target_pairs={{0,1},{1,2},{2,3},{3,0},{4,5},{5,6},{6,7},{7,4},{8,9},{9,10},{10,1... | collective-permute-start | bytes 2359304 | tf_op jit(solution)/shard_map/ppermute | solution.py:406
  89.6 20.5 %collective-permute-start.7 = (bf16[2,128,1536]{2,1,0:T(8,128)(2,1)S(1)}, bf16[2,128,1536]{2,1,0:T(8,128)(2,1)}, u32[]{:S(2)}, u32[]{:S(2)}) collective-permute-start(bf16[2,128,1536]{2,1,0:T(8,128)(2,1)S(1)} %reshape.50.own), channel_id=1, source_target_pairs={{1,0},{2,1},{3,2},{0,3},{5,4},{6,5},{7,6},{4,7},{9,8},{10,9},{11,1... | collective-permute-start | bytes 2359304 | tf_op jit(solution)/shard_map/ppermute | solution.py:406
  111.1 11.2 %collective-permute-start.8 = (bf16[128,1536]{1,0:T(8,128)(2,1)S(1)}, bf16[128,1536]{1,0:T(8,128)(2,1)S(1)}, u32[]{:S(2)}, u32[]{:S(2)}) collective-permute-start(bf16[128,1536]{1,0:T(8,128)(2,1)S(1)} %slice_bitcast_fusion.1), channel_id=1, source_target_pairs={{0,1},{1,2},{2,3},{3,0},{4,5},{5,6},{6,7},{7,4},{8,9},{9,10},{10,1... | collective-permute-start | bytes 1179656 | tf_op jit(solution)/shard_map/ppermute | solution.py:409
  112.3 10.0 %collective-permute-start.9 = (bf16[128,1536]{1,0:T(8,128)(2,1)S(1)}, bf16[128,1536]{1,0:T(8,128)(2,1)S(1)}, u32[]{:S(2)}, u32[]{:S(2)}) collective-permute-start(bf16[128,1536]{1,0:T(8,128)(2,1)S(1)} %slice_bitcast_fusion), channel_id=1, source_target_pairs={{1,0},{2,1},{3,2},{0,3},{5,4},{6,5},{7,6},{4,7},{9,8},{10,9},{11,1... | collective-permute-start | bytes 1179656 | tf_op jit(solution)/shard_map/ppermute | solution.py:409
  115.0 26.6 %collective-permute-start.12 = (bf16[2,64,1536]{2,1,0:T(8,128)(2,1)S(1)}, bf16[2,64,1536]{2,1,0:T(8,128)(2,1)S(1)}, u32[]{:S(2)}, u32[]{:S(2)}) collective-permute-start(bf16[2,64,1536]{2,1,0:T(8,128)(2,1)S(1)} %reshape.53.own), channel_id=1, source_target_pairs={{0,1},{1,2},{2,3},{3,0},{4,5},{5,6},{6,7},{7,4},{8,9},{9,10},{10,1... | collective-permute-start | bytes 1179656 | tf_op jit(solution)/shard_map/ppermute | solution.py:406
  115.0 26.6 %collective-permute-start.13 = (bf16[2,64,1536]{2,1,0:T(8,128)(2,1)S(1)}, bf16[2,64,1536]{2,1,0:T(8,128)(2,1)S(1)}, u32[]{:S(2)}, u32[]{:S(2)}) collective-permute-start(bf16[2,64,1536]{2,1,0:T(8,128)(2,1)S(1)} %reshape.53.own), channel_id=1, source_target_pairs={{1,0},{2,1},{3,2},{0,3},{5,4},{6,5},{7,6},{4,7},{9,8},{10,9},{11,1... | collective-permute-start | bytes 1179656 | tf_op jit(solution)/shard_map/ppermute | solution.py:406
  117.6 23.9 %collective-permute-start.14 = (bf16[2,64,1536]{2,1,0:T(8,128)(2,1)S(1)}, bf16[2,64,1536]{2,1,0:T(8,128)(2,1)S(1)}, u32[]{:S(2)}, u32[]{:S(2)}) collective-permute-start(bf16[2,64,1536]{2,1,0:T(8,128)(2,1)S(1)} %reshape.53.own), channel_id=1, source_target_pairs={{0,2},{1,3},{2,0},{3,1},{4,6},{5,7},{6,4},{7,5},{8,10},{9,11},{10,... | collective-permute-start | bytes 1179656 | tf_op jit(solution)/shard_map/ppermute | solution.py:427
  137.8 17.9 %collective-permute-start.10 = (bf16[2,128,1536]{2,1,0:T(8,128)(2,1)S(1)}, bf16[2,128,1536]{2,1,0:T(8,128)(2,1)S(1)}, u32[]{:S(2)}, u32[]{:S(2)}) collective-permute-start(bf16[2,128,1536]{2,1,0:T(8,128)(2,1)S(1)} %get-tuple-element.48), channel_id=1, source_target_pairs={{0,1},{1,2},{2,3},{3,0},{4,5},{5,6},{6,7},{7,4},{8,9},{9,10},{10,1... | collective-permute-start | bytes 2359304 | tf_op jit(solution)/shard_map/ppermute | solution.py:429
  139.2 16.5 %collective-permute-start.11 = (bf16[2,128,1536]{2,1,0:T(8,128)(2,1)S(1)}, bf16[2,128,1536]{2,1,0:T(8,128)(2,1)S(1)}, u32[]{:S(2)}, u32[]{:S(2)}) collective-permute-start(bf16[2,128,1536]{2,1,0:T(8,128)(2,1)S(1)} %get-tuple-element.49), channel_id=1, source_target_pairs={{1,0},{2,1},{3,2},{0,3},{5,4},{6,5},{7,6},{4,7},{9,8},{10,9},{11,1... | collective-permute-start | bytes 2359304 | tf_op jit(solution)/shard_map/ppermute | solution.py:429
  150.3 60.9 %copy-start.6 = (f32[256]{0:T(256)S(1)}, f32[256]{0:T(256)}, u32[]{:S(2)}) copy-start(f32[256]{0:T(256)} %param.17) | copy-start | bytes 3076
  155.8 7.5 %collective-permute-start.16 = (bf16[128,1536]{1,0:T(8,128)(2,1)S(1)}, bf16[128,1536]{1,0:T(8,128)(2,1)S(1)}, u32[]{:S(2)}, u32[]{:S(2)}) collective-permute-start(bf16[128,1536]{1,0:T(8,128)(2,1)S(1)} %fusion), channel_id=1, source_target_pairs={{1,0},{2,1},{3,2},{0,3},{5,4},{6,5},{7,6},{4,7},{9,8},{10,9},{11,1... | collective-permute-start | bytes 1179656 | tf_op jit(solution)/shard_map/ppermute | solution.py:434
  158.7 7.9 %collective-permute-start.15 = (bf16[128,1536]{1,0:T(8,128)(2,1)S(1)}, bf16[128,1536]{1,0:T(8,128)(2,1)S(1)}, u32[]{:S(2)}, u32[]{:S(2)}) collective-permute-start(bf16[128,1536]{1,0:T(8,128)(2,1)S(1)} %fusion.1), channel_id=1, source_target_pairs={{0,1},{1,2},{2,3},{3,0},{4,5},{5,6},{6,7},{7,4},{8,9},{9,10},{10,1... | collective-permute-start | bytes 1179656 | tf_op jit(solution)/shard_map/ppermute | solution.py:434
  170.7 29.4 %all-to-all-start.2 = ((bf16[32,8,1536]{2,1,0:T(8,128)(2,1)}), bf16[32,8,1536]{2,1,0:T(8,128)(2,1)S(1)}, u32[]{:S(2)}, u32[]{:S(2)}) async-start(bf16[32,8,1536]{2,1,0:T(8,128)(2,1)} %reshape.54), calls=%async_computation.2 | async-start | bytes 1572864 | tf_op jit(solution)/shard_map/all_to_all | solution.py:416
  180.0 20.1 %collective-permute-start.17 = (bf16[2,64,1536]{2,1,0:T(8,128)(2,1)S(1)}, bf16[2,64,1536]{2,1,0:T(8,128)(2,1)S(1)}, u32[]{:S(2)}, u32[]{:S(2)}) collective-permute-start(bf16[2,64,1536]{2,1,0:T(8,128)(2,1)S(1)} %get-tuple-element.59), channel_id=1, source_target_pairs={{0,1},{1,2},{2,3},{3,0},{4,5},{5,6},{6,7},{7,4},{8,9},{9,10},{10,1... | collective-permute-start | bytes 1179656 | tf_op jit(solution)/shard_map/ppermute | solution.py:437
  180.1 20.0 %collective-permute-start.18 = (bf16[2,64,1536]{2,1,0:T(8,128)(2,1)S(1)}, bf16[2,64,1536]{2,1,0:T(8,128)(2,1)}, u32[]{:S(2)}, u32[]{:S(2)}) collective-permute-start(bf16[2,64,1536]{2,1,0:T(8,128)(2,1)S(1)} %get-tuple-element.60), channel_id=1, source_target_pairs={{1,0},{2,1},{3,2},{0,3},{5,4},{6,5},{7,6},{4,7},{9,8},{10,9},{11,1... | collective-permute-start | bytes 1179656 | tf_op jit(solution)/shard_map/ppermute | solution.py:438
  182.8 17.3 %collective-permute-start.19 = (bf16[2,64,1536]{2,1,0:T(8,128)(2,1)S(1)}, bf16[2,64,1536]{2,1,0:T(8,128)(2,1)}, u32[]{:S(2)}, u32[]{:S(2)}) collective-permute-start(bf16[2,64,1536]{2,1,0:T(8,128)(2,1)S(1)} %get-tuple-element.61), channel_id=1, source_target_pairs={{0,2},{1,3},{2,0},{3,1},{4,6},{5,7},{6,4},{7,5},{8,10},{9,11},{10,... | collective-permute-start | bytes 1179656 | tf_op jit(solution)/shard_map/ppermute | solution.py:439
  202.7 18.6 %all-to-all-start.3 = ((bf16[32,4,1536]{2,1,0:T(4,128)(2,1)}), bf16[32,4,1536]{2,1,0:T(4,128)(2,1)S(1)}, u32[]{:S(2)}, u32[]{:S(2)}) async-start(bf16[32,4,1536]{2,1,0:T(4,128)(2,1)} %reshape.57), calls=%async_computation.3 | async-start | bytes 786432 | tf_op jit(solution)/shard_map/all_to_all | solution.py:416

commit v4 on v3

--- a/solution.py
+++ b/solution.py
@@ -13,7 +13,7 @@
 TILE = 128
 SPAN = 2 * HALF + TILE
 EDGE = 16
-GROUPS = (8, 4)
+GROUPS = (6, 6)
 SIDE = 2
 BLOCK = SIDE * PAIR
 MIB = 1024 * 1024
@@ -138,7 +138,7 @@
                     attend_body,
                     jax.ShapeDtypeStruct((rows, pairs * PAIR), F32),
                     cost,
-                    16,
+                    58,
                     grid=(pairs // SIDE,),
                     in_specs=base,
                     out_specs=pl.BlockSpec((rows, BLOCK), lambda j: (0, j)),
@@ -155,7 +155,7 @@
                     jax.ShapeDtypeStruct((EDGE, width), BF16),
                 ],
                 cost,
-                20,
+                58,
                 grid=(pairs // SIDE,),
                 in_specs=base + [whole(1, width)] + [whole(*o.shape) for o in outs],
                 out_specs=[whole(rows, width), whole(EDGE, width), whole(EDGE, width)],
@@ -238,28 +238,31 @@
     )(normed, inner, low, high, taps, gain[None], place[None])
 
 
-def combine_body(mixed_ref, gate_ref, place_ref, *rest):
+def combine_body(counts, mixed_ref, gate_ref, place_ref, *rest):
     parts, out_ref = rest[:-1], rest[-1]
     rows = mixed_ref.shape[0]
     total = None
     first = 0
-    for part in parts:
-        count = part.shape[0]
+    for part, count in zip(parts, counts):
+        times = part.shape[0] // count
         place = first + lax.broadcasted_iota(jnp.int32, (rows, count), 1)
         pick = jnp.where(place == place_ref[...], 1.0, 0.0).astype(BF16)
-        got = jnp.dot(pick, part[...], preferred_element_type=F32)
+        got = jnp.dot(
+            jnp.concatenate([pick] * times, axis=1), part[...], preferred_element_type=F32
+        )
         total = got if total is None else total + got
         first += count
-    out_ref[...] = (mixed_ref[...].astype(F32) + gate_ref[...] * total).astype(BF16)
-
-
-def combine(mixed, gate, place, parts):
+    picked = total.astype(BF16).astype(F32)
+    out_ref[...] = (mixed_ref[...].astype(F32) + gate_ref[...] * picked).astype(BF16)
+
+
+def combine(mixed, gate, place, parts, counts):
     rows, width = mixed.shape
     block = 256
     column = lambda n: pl.BlockSpec((n, block), lambda j: (0, j))
     fixed = pl.BlockSpec((rows, 1), lambda j: (0, 0))
     return call(
-        combine_body,
+        functools.partial(combine_body, counts),
         jax.ShapeDtypeStruct((rows, width), BF16),
         (2 * sum(p.shape[0] for p in parts) * rows * width, 8 * rows * width),
         16,
@@ -271,7 +274,8 @@
 
 def ffn_body(direct, own, left, right, *rest):
     if direct:
-        far, w_in, w_out, keep, to_right, to_left, to_far, *scratch = rest
+        far, me, w_in, w_out, out, *scratch = rest
+        places = [(me[0] + k) % 4 for k in (0, 3, 1, 2)]
         far0, far1 = far.at[0], far.at[1]
     else:
         far0, far1, w_in, w_out, keep, up, down, up2, down2, *scratch = rest
@@ -301,12 +305,12 @@
             copies[e, 1, t].wait()
             cols = slice(t * step, (t + 1) * step)
             part = jnp.dot(hidden[...], second[e, t], preferred_element_type=F32).astype(BF16)
+            if direct:
+                for k, at in enumerate(places):
+                    out[at, e, :, cols] = part[k * n : (k + 1) * n]
+                continue
             keep[e, :, cols] = part[:n]
-            if direct:
-                to_left[e, :, cols] = part[n : 2 * n]
-                to_right[e, :, cols] = part[2 * n : 3 * n]
-                to_far[e, :, cols] = part[3 * n :]
-            elif e == 0:
+            if e == 0:
                 down[1, :, cols] = part[n : 2 * n]
                 up2[:, cols] = part[2 * n : 3 * n]
                 up[0, :, cols] = part[3 * n :]
@@ -316,18 +320,20 @@
                 down[0, :, cols] = part[3 * n :]
 
 
-def ffn(own, left, right, far, w_in, w_out):
-    direct = len(far) == 1
+def ffn(own, left, right, far, w_in, w_out, me=None):
+    direct = me is not None
     experts, n, width = own.shape
     units = w_in.shape[2]
     pair = jax.ShapeDtypeStruct((2, n, width), BF16)
     single = jax.ShapeDtypeStruct((n, width), BF16)
     return call(
         functools.partial(ffn_body, direct),
-        [pair] * 4 if direct else [pair, pair, pair, single, single],
+        jax.ShapeDtypeStruct((4, 2, n, width), BF16) if direct else [pair, pair, pair, single, single],
         (experts * 4 * n * width * units * 4, 2 * experts * width * units * 2),
         50,
-        in_specs=[pl.BlockSpec(memory_space=pltpu.VMEM)] * (3 + len(far)) + [pl.BlockSpec(memory_space=pl.ANY)] * 2,
+        in_specs=[pl.BlockSpec(memory_space=pltpu.VMEM)] * (3 + len(far))
+        + [pl.BlockSpec(memory_space=pltpu.SMEM)] * direct
+        + [pl.BlockSpec(memory_space=pl.ANY)] * 2,
         scratch_shapes=[
             pltpu.VMEM((4 * n, width), BF16),
             pltpu.VMEM((4 * n, units), BF16),
@@ -335,7 +341,7 @@
             pltpu.VMEM((2, width // STEP, units, STEP), BF16),
             pltpu.SemaphoreType.DMA((2, 2, max(units, width) // STEP)),
         ],
-    )(own, left, right, *far, w_in, w_out)
+    )(own, left, right, *far, *([me] if direct else []), w_in, w_out)
 
 
 def on_device(
@@ -428,21 +434,19 @@
     keep_a, go_up_a, go_down_a, up2_a, down2_a = ffn(own_a, left_a, right_a, far_a, w_in, w_out)
     below_a, above_a = lax.ppermute(go_up_a, "expert", up), lax.ppermute(go_down_a, "expert", down)
     (own_b,) = after((own_b,), keep_a)
-    keep_b, to_right, to_left, to_far = ffn(own_b, left_b, right_b, (far_b,), w_in, w_out)
-    below_a, above_a = after((below_a, above_a), keep_b)
+    me = lax.axis_index("expert").astype(jnp.int32)[None]
+    parts_b = ffn(own_b, left_b, right_b, (far_b,), w_in, w_out, me)
+    parts_b = parts_b.reshape(group_count, local, time_count, sizes[1], width).transpose(0, 2, 1, 3, 4)
+    parts_b = parts_b.reshape(devices, local * sizes[1], width)
+    back_b = lax.all_to_all(parts_b, ("expert", "tm"), split_axis=0, concat_axis=0, tiled=True)
+    back_b = back_b.reshape(group_count * experts * sizes[1], width)
+    below_a, above_a = after((below_a, above_a), parts_b)
     up2_a, down2_a = add(up2_a, below_a[0]), add(down2_a, above_a[0])
     up3_a, down3_a = lax.ppermute(up2_a, "expert", up), lax.ppermute(down2_a, "expert", down)
-    to_right, to_left, to_far = after((to_right, to_left, to_far), up3_a, down3_a)
-    parts_b = (
-        lax.ppermute(to_right, "expert", up),
-        lax.ppermute(to_left, "expert", down),
-        lax.ppermute(to_far, "expert", across),
-    )
     total_a = jnp.stack([add(keep_a[0], above_a[1], up3_a), add(keep_a[1], below_a[1], down3_a)])
-    back_a = leave(home(total_a, sizes[0]), sizes[0])
-    parts_b = after(parts_b, back_a)
-    back_b = leave(home(add(keep_b, *parts_b), sizes[1]), sizes[1])
-    return combine(mixed, expert_gate, place, [back_a, back_b])
+    (total_a,) = after((home(total_a, sizes[0]),), back_b)
+    back_a = leave(total_a, sizes[0])
+    return combine(mixed, expert_gate, place, [back_a, back_b], [experts * c for c in sizes])
 
 
 def solution(mesh):

time: 226 us -> 225 us (level)
  starting transfers between devices: 58.5 us -> 53.3 us
  Pallas kernels: 44.1 us -> 47.5 us
    ppermute x3 -> x0, waiting for transfers between devices: 17.3 us -> none  [the longest x1 17.3 us: on_device(): lax.ppermute(to_right, 'expert', up)]
    ppermute x1, waiting for transfers between devices: 4.54 us -> 21.6 us  [on_device(): lax.ppermute(down2_a, 'expert', down)]
    all_to_all x2 -> x1, starting transfers between devices: 17.6 us -> 6.38 us  [leave(): got = lax.all_to_all(summed, 'tm', split_axis=0, concat_axis=0, tiled=True)]
    all_to_all x0 -> x1, starting transfers between devices: none -> 8.56 us  [on_device(): lax.all_to_all(parts_b, ('expert', 'tm'), split_axis=0, concat_axis=0, ti...]
    reshape x2 -> x3, local copies, waits for them, and re-layouts: 0.24 us -> 5.77 us  [the longest x1 2.73 us: on_device(): back_b = back_b.reshape(group_count * experts * sizes[1], width)]
    ppermute x1, waiting for transfers between devices: 5.41 us -> 0.01 us  [on_device(): lax.ppermute(go_up_a, 'expert', up)]
    ppermute x2, waiting for transfers between devices: 11.4 us -> 16.1 us  [on_device(): high.append(lax.ppermute(part, order, back))]
    all_to_all x2 -> x1, waiting for transfers between devices: 10 us -> 13.9 us  [leave(): got = lax.all_to_all(summed, 'tm', split_axis=0, concat_axis=0, tiled=True)]
  transfers between devices with their start and end apart: 22 -> 19, of which waited for: 9 -> 8; matrix products, arithmetic and copies ran while one was open for 3% -> 7% of each run, Pallas kernels for 16% -> 16%
where the time goes in v4:
time: 225 us; the launch traced here: 224 us
  waiting for transfers between devices  64.7 us (29%)
  starting transfers between devices  53.3 us (24%)
  Pallas kernels  47.5 us (21%)
  blocking collectives  35.8 us (16%)
  local copies, waits for them, and re-layouts  17.7 us (8%)
  other arithmetic  4.92 us (2%)
    all_to_all x2, blocking collectives, arrive(): own = lax.all_to_all(sent, 'tm', split_axis=0, concat_axis=0, tiled=True)  35.8 us
    pallas_call x2, Pallas kernels, ffn(): call(functools.partial(ffn_body, direct), jax.ShapeDtypeStruct((4, 2, n,...  25.2 us
    ppermute x1, waiting for transfers between devices, on_device(): lax.ppermute(down2_a, 'expert', down)  21.6 us
    ppermute x2, waiting for transfers between devices, on_device(): high.append(lax.ppermute(part, order, back))  16.1 us
    all_to_all x1, waiting for transfers between devices, leave(): got = lax.all_to_all(summed, 'tm', split_axis=0, concat_axis=0, tiled=True)  13.9 us
    ppermute x2, starting transfers between devices, on_device(): high.append(lax.ppermute(part, order, back))  9.45 us
    all_to_all x1, starting transfers between devices, on_device(): lax.all_to_all(parts_b, ('expert', 'tm'), split_axis=0, concat_axis=0, ti...  8.56 us
    pallas_call x1, Pallas kernels, attention(): call(functools.partial(attend_norm_body, GROUPS[:-1]), [jax.ShapeDtypeStr...  7.39 us
  transfers between devices with their start and end apart: 19, of which 8 were waited for; matrix products, arithmetic and copies ran while one was open for 7% of the time, Pallas kernels for 16%

profile of v4, /device:TPU:1, one launch (start us, length us, event | category | flops | bytes accessed | tf_op | source)
XLA Modules:
  0.0 224.4 jit_solution(940155961350558610)
XLA Ops:
  0.0 1.3 slice.30
  1.3 4.4 %collective-permute-start.2 = (bf16[2,256,768]{2,1,0:T(8,128)(2,1)S(1)}, bf16[2,256,768]{2,1,0:T(8,128)(2,1)}, u32[]{:S(2)}, u32[]{:S(2)}) collective-permute-start(bf16[2,256,768]{2,1,0:T(8,128)(2,1)S(1)} %slice.30), channel_id=1, source_target_pairs={{0,1},{1,2},{2,3},{3,4},{4,5},{5,6},{6,7},{7,8},{8,9},{9,10},{10,1... | collective-permute-start | bytes 2359304 | tf_op jit(solution)/shard_map/ppermute | solution.py:376
  5.7 4.6 %collective-permute-start.3 = (bf16[2,256,768]{2,1,0:T(8,128)(2,1)S(1)}, bf16[2,256,768]{2,1,0:T(8,128)(2,1)}, u32[]{:S(2)}, u32[]{:S(2)}) collective-permute-start(bf16[2,256,768]{2,1,0:T(8,128)(2,1)S(1)} %slice.30), channel_id=1, source_target_pairs={{1,0},{2,1},{3,2},{4,3},{5,4},{6,5},{7,6},{8,7},{9,8},{10,9},{11,1... | collective-permute-start | bytes 2359304 | tf_op jit(solution)/shard_map/ppermute | solution.py:377
  10.4 0.1 slice.31
  10.4 1.9 collective-permute-start
  12.3 4.9 %collective-permute-start.1 = (bf16[2,256,768]{2,1,0:T(8,128)(2,1)S(1)}, bf16[2,256,768]{2,1,0:T(8,128)(2,1)S(1)}, u32[]{:S(2)}, u32[]{:S(2)}) collective-permute-start(bf16[2,256,768]{2,1,0:T(8,128)(2,1)S(1)} %slice.31), channel_id=1, source_target_pairs={{1,0},{2,1},{3,2},{4,3},{5,4},{6,5},{7,6},{8,7},{9,8},{10,9},{11,1... | collective-permute-start | bytes 2359304 | tf_op jit(solution)/shard_map/ppermute | solution.py:377
  17.2 0.6 broadcast_in_dim.18.gain_ref
  17.8 0.7 add_convert_fusion.edge_ref
  18.5 3.4 %collective-permute-done.2.lo_ref = bf16[2,256,768]{2,1,0:T(8,128)(2,1)} collective-permute-done((bf16[2,256,768]{2,1,0:T(8,128)(2,1)S(1)}, bf16[2,256,768]{2,1,0:T(8,128)(2,1)}, u32[]{:S(2)}, u32[]{:S(2)}) %collective-permute-start.2) | collective-permute-done | bytes 786464 | tf_op jit(solution)/shard_map/ppermute | solution.py:376
  21.9 14.2 %collective-permute-done.3.hi_ref = bf16[2,256,768]{2,1,0:T(8,128)(2,1)} collective-permute-done((bf16[2,256,768]{2,1,0:T(8,128)(2,1)S(1)}, bf16[2,256,768]{2,1,0:T(8,128)(2,1)}, u32[]{:S(2)}, u32[]{:S(2)}) %collective-permute-start.3) | collective-permute-done | bytes 786464 | tf_op jit(solution)/shard_map/ppermute | solution.py:377
  36.1 6.5 %shard_map.118.rest_0_ = f32[256,768]{1,0:T(8,128)} custom-call(s32[2]{0:T(128)} %add_convert_fusion.edge_ref, bf16[256,1536]{1,0:T(8,128)(2,1)} %q_ref.3, bf16[2,256,1536]{2,1,0:T(8,128)(2,1)} %kv_ref.3, bf16[2,256,768]{2,1,0:T(8,128)(2,1)} %collective-permute-done.2.lo_ref, bf16[2,256,768]{2,1,0:T(8,128)(2,1)} %collective-permute-done.3.hi_ref), custom_call_target="tpu_custom_call" | custom-call | flops 2013265920 | bytes 2752512 | tf_op jit(solution)/shard_map/pallas_call | solution.py:137
  42.7 1.9 collective-permute-done.1.hi_ref
  44.5 0.9 copy-done.16
  45.4 7.4 %shard_map.119 = (bf16[256,1536]{1,0:T(8,128)(2,1)}, bf16[16,1536]{1,0:T(8,128)(2,1)}, bf16[16,1536]{1,0:T(8,128)(2,1)}) custom-call(s32[2]{0:T(128)} %add_convert_fusion.edge_ref, bf16[256,1536]{1,0:T(8,128)(2,1)} %q_ref.3, bf16[2,256,1536]{2,1,0:T(8,128)(2,1)} %kv_ref.3, bf16[2,256,768]{2,1,0:T(8,128)(2,1)} %copy-done.15, bf16[2,256,768]{2,1,0:T(8,128)(2,1)} %copy-done.16, ...), custom_call_target="tpu_custom_call" | custom-call | flops 2013265920 | bytes 2752512 | tf_op jit(solution)/shard_map/pallas_call | solution.py:150
  52.8 1.9 collective-permute-start.4
  54.7 5.6 %collective-permute-start.5 = (bf16[16,1536]{1,0:T(8,128)(2,1)}, bf16[16,1536]{1,0:T(8,128)(2,1)S(1)}, u32[]{:S(2)}, u32[]{:S(2)}) collective-permute-start(bf16[16,1536]{1,0:T(8,128)(2,1)} %get-tuple-element.31), channel_id=1, source_target_pairs={{1,0},{2,1},{3,2},{4,3},{5,4},{6,5},{7,6},{8,7},{9,8},{10,9},{11,1... | collective-permute-start | bytes 147464 | tf_op jit(solution)/shard_map/ppermute | solution.py:383
  60.4 1.1 copy-done.2
  61.5 3.6 %shard_map.120.inner_ref = bf16[224,1536]{1,0:T(8,128)(2,1)S(1)} custom-call(bf16[256,1536]{1,0:T(8,128)(2,1)S(1)} %copy-done.2, f32[31,1536]{1,0:T(8,128)S(1)} %copy-done.4), custom_call_target="tpu_custom_call" | custom-call | flops 1365245952 | bytes 1572864 | tf_op jit(solution)/shard_map/pallas_call | solution.py:189
  65.1 1.4 shard_map.121
  66.5 21.4 %all_to_all.20 = bf16[32,8,1536]{2,1,0:T(8,128)(2,1)S(1)} all-to-all(bf16[32,8,1536]{2,1,0:T(8,128)(2,1)S(1)} %bitcast.38), channel_id=1, replica_groups=mesh['tm'=32,'expert'=4] {'tm'}, dimensions={0} | all-to-all | bytes 1572864 | tf_op jit(solution)/shard_map/all_to_all | solution.py:407
  87.9 0.2 copy.23
  88.1 0.6 copy.24
  88.7 0.2 reshape.50.own
  88.9 0.1 collective-permute-start.6
  89.0 2.7 %collective-permute-start.7 = (bf16[2,128,1536]{2,1,0:T(8,128)(2,1)S(1)}, bf16[2,128,1536]{2,1,0:T(8,128)(2,1)}, u32[]{:S(2)}, u32[]{:S(2)}) collective-permute-start(bf16[2,128,1536]{2,1,0:T(8,128)(2,1)S(1)} %reshape.50.own), channel_id=1, source_target_pairs={{1,0},{2,1},{3,2},{0,3},{5,4},{6,5},{7,6},{4,7},{9,8},{10,9},{11,1... | collective-permute-start | bytes 2359304 | tf_op jit(solution)/shard_map/ppermute | solution.py:412
  91.7 0.1 reshape.51
  91.8 14.5 %all_to_all.21 = bf16[32,4,1536]{2,1,0:T(4,128)(2,1)S(1)} all-to-all(bf16[32,4,1536]{2,1,0:T(4,128)(2,1)S(1)} %reshape.51), channel_id=1, replica_groups=mesh['tm'=32,'expert'=4] {'tm'}, dimensions={0} | all-to-all | bytes 786432 | tf_op jit(solution)/shard_map/all_to_all | solution.py:407
  106.3 0.1 copy.25
  106.3 0.4 copy.26
  106.8 0.1 reshape.53.own
  106.9 2.5 %collective-permute-done.6.left = bf16[2,128,1536]{2,1,0:T(8,128)(2,1)S(1)} collective-permute-done((bf16[2,128,1536]{2,1,0:T(8,128)(2,1)S(1)}, bf16[2,128,1536]{2,1,0:T(8,128)(2,1)S(1)}, u32[]{:S(2)}, u32[]{:S(2)}) %collective-permute-start.6) | collective-permute-done | bytes 786464 | tf_op jit(solution)/shard_map/ppermute | solution.py:412
  109.5 0.5 collective-permute-start.8
  110.0 1.0 slice_bitcast_fusion
  111.0 2.3 %collective-permute-start.9 = (bf16[128,1536]{1,0:T(8,128)(2,1)S(1)}, bf16[128,1536]{1,0:T(8,128)(2,1)S(1)}, u32[]{:S(2)}, u32[]{:S(2)}) collective-permute-start(bf16[128,1536]{1,0:T(8,128)(2,1)S(1)} %slice_bitcast_fusion), channel_id=1, source_target_pairs={{1,0},{2,1},{3,2},{0,3},{5,4},{6,5},{7,6},{4,7},{9,8},{10,9},{11,1... | collective-permute-start | bytes 1179656 | tf_op jit(solution)/shard_map/ppermute | solution.py:415
  113.3 2.7 %collective-permute-start.13 = (bf16[2,64,1536]{2,1,0:T(8,128)(2,1)S(1)}, bf16[2,64,1536]{2,1,0:T(8,128)(2,1)S(1)}, u32[]{:S(2)}, u32[]{:S(2)}) collective-permute-start(bf16[2,64,1536]{2,1,0:T(8,128)(2,1)S(1)} %reshape.53.own), channel_id=1, source_target_pairs={{1,0},{2,1},{3,2},{0,3},{5,4},{6,5},{7,6},{4,7},{9,8},{10,9},{11,1... | collective-permute-start | bytes 1179656 | tf_op jit(solution)/shard_map/ppermute | solution.py:412
  116.0 4.7 %collective-permute-done.8.rest_0_ = bf16[128,1536]{1,0:T(8,128)(2,1)S(1)} collective-permute-done((bf16[128,1536]{1,0:T(8,128)(2,1)S(1)}, bf16[128,1536]{1,0:T(8,128)(2,1)S(1)}, u32[]{:S(2)}, u32[]{:S(2)}) %collective-permute-start.8) | collective-permute-done | bytes 393248 | tf_op jit(solution)/shard_map/ppermute | solution.py:415
  120.7 0.0 collective-permute-done.9.rest_1_
  120.8 16.5 %shard_map.122 = (bf16[2,128,1536]{2,1,0:T(8,128)(2,1)S(1)}, bf16[2,128,1536]{2,1,0:T(8,128)(2,1)}, bf16[2,128,1536]{2,1,0:T(8,128)(2,1)}, bf16[128,1536]{1,0:T(8,128)(2,1)S(1)}, bf16[128,1536]{1,0:T(8,128)(2,1)S(1)}) custom-call(bf16[2,128,1536]{2,1,0:T(8,128)(2,1)} %copy-done.6, bf16[2,128,1536]{2,1,0:T(8,128)(2,1)} %copy-done.7, ...), custom_call_target="tpu_custom_call" | custom-call | flops 9663676416 | bytes 18874368 | tf_op jit(solution)/shard_map/pallas_call | solution.py:329
  137.3 0.9 copy-done
  138.1 1.5 collective-permute-start.10
  139.6 1.9 collective-permute-start.11
  141.6 8.7 %shard_map.123 = bf16[4,2,64,1536]{3,2,1,0:T(8,128)(2,1)S(1)} custom-call(bf16[2,64,1536]{2,1,0:T(8,128)(2,1)S(1)} %reshape.53.own, bf16[2,64,1536]{2,1,0:T(8,128)(2,1)S(1)} %collective-permute-done.12.left, bf16[2,64,1536]{2,1,0:T(8,128)(2,1)S(1)} %collective-permute-done.13.right, bf16[2,64,1536]{2,1,0:T(8,128)(2,1)S(1)} %collective-permute-done.14.rest_0_, ...), custom_call_target="tpu_custom_call" | custom-call | flops 4831838208 | bytes 18874368 | tf_op jit(solution)/shard_map/pallas_call | solution.py:329
  150.3 1.5 reshape.54
  151.8 2.5 %copy.27 = bf16[4,32,2,2,1536]{4,3,2,1,0:T(2,128)(2,1)S(1)} copy(bf16[4,32,2,2,1536]{4,3,1,2,0:T(2,128)(2,1)} %bitcast.41) | data formatting | bytes 3145728 | tf_op jit(solution)/shard_map/transpose | solution.py:439
  154.3 1.5 reshape.55
  155.8 8.6 %all-to-all-start.2 = ((bf16[128,4,1536]{2,1,0:T(4,128)(2,1)}), bf16[128,4,1536]{2,1,0:T(4,128)(2,1)}, u32[]{:S(2)}, u32[]{:S(2)}) async-start(bf16[128,4,1536]{2,1,0:T(4,128)(2,1)} %reshape.55), calls=%async_computation.2 | async-start | bytes 3145728 | tf_op jit(solution)/shard_map/all_to_all | solution.py:441
  164.4 1.2 fusion
  165.6 3.3 %collective-permute-start.16 = (bf16[128,1536]{1,0:T(8,128)(2,1)S(1)}, bf16[128,1536]{1,0:T(8,128)(2,1)S(1)}, u32[]{:S(2)}, u32[]{:S(2)}) collective-permute-start(bf16[128,1536]{1,0:T(8,128)(2,1)S(1)} %fusion), channel_id=1, source_target_pairs={{1,0},{2,1},{3,2},{0,3},{5,4},{6,5},{7,6},{4,7},{9,8},{10,9},{11,1... | collective-permute-start | bytes 1179656 | tf_op jit(solution)/shard_map/ppermute | solution.py:445
  168.9 1.1 fusion.1
  170.0 0.1 collective-permute-start.15
  170.1 21.6 %collective-permute-done.16 = bf16[128,1536]{1,0:T(8,128)(2,1)S(1)} collective-permute-done((bf16[128,1536]{1,0:T(8,128)(2,1)S(1)}, bf16[128,1536]{1,0:T(8,128)(2,1)S(1)}, u32[]{:S(2)}, u32[]{:S(2)}) %collective-permute-start.16) | collective-permute-done | bytes 393248 | tf_op jit(solution)/shard_map/ppermute | solution.py:445
  191.7 2.3 %collective-permute-done.15 = bf16[128,1536]{1,0:T(8,128)(2,1)S(1)} collective-permute-done((bf16[128,1536]{1,0:T(8,128)(2,1)S(1)}, bf16[128,1536]{1,0:T(8,128)(2,1)S(1)}, u32[]{:S(2)}, u32[]{:S(2)}) %collective-permute-start.15) | collective-permute-done | bytes 393248 | tf_op jit(solution)/shard_map/ppermute | solution.py:445
  194.1 1.4 fusion.3
  195.5 0.1 stack.21
  195.6 0.1 stack.22
  195.7 0.6 maximum_bitcast_fusion
  196.2 0.3 copy.28
  196.5 1.1 reshape.56
  197.6 2.7 %reshape.57.rest_1_ = bf16[512,1536]{1,0:T(8,128)(2,1)S(1)} reshape(bf16[128,4,1536]{2,1,0:T(4,128)(2,1)} %all-to-all-done.2) | data formatting | bytes 3145728 | tf_op jit(solution)/shard_map/reshape | solution.py:442
  200.3 6.4 %all-to-all-start.3 = ((bf16[32,8,1536]{2,1,0:T(8,128)(2,1)}), bf16[32,8,1536]{2,1,0:T(8,128)(2,1)S(1)}, u32[]{:S(2)}, u32[]{:S(2)}) async-start(bf16[32,8,1536]{2,1,0:T(8,128)(2,1)} %reshape.56), calls=%async_computation.3 | async-start | bytes 1572864 | tf_op jit(solution)/shard_map/all_to_all | solution.py:422
  206.7 0.1 copy.30.place_ref
  206.9 0.1 copy.29.gate_ref
  207.0 13.9 %all-to-all-done.3 = bf16[32,8,1536]{2,1,0:T(8,128)(2,1)S(1)} async-done(((bf16[32,8,1536]{2,1,0:T(8,128)(2,1)}), bf16[32,8,1536]{2,1,0:T(8,128)(2,1)S(1)}, u32[]{:S(2)}, u32[]{:S(2)}) %all-to-all-start.3) | async-done | bytes 786464 | tf_op jit(solution)/shard_map/all_to_all | solution.py:422
  221.0 3.4 %shard_map.124 = bf16[256,1536]{1,0:T(8,128)(2,1)} custom-call(bf16[256,1536]{1,0:T(8,128)(2,1)S(1)} %get-tuple-element.32.mixed_ref, f32[256,1]{1,0:T(8,128)S(1)} %copy.29.gate_ref, s32[256,1]{1,0:T(8,128)S(1)} %copy.30.place_ref, bf16[256,1536]{1,0:T(8,128)(2,1)S(1)} %bitcast.37, bf16[512,1536]{1,0:T(8,128)(2,1)S(1)} %reshape.57.rest_1_), custom_call_target="tpu_custom_call" | custom-call | flops 603979776 | bytes 3145728 | tf_op jit(solution)/shard_map/pallas_call | solution.py:264
  (46 shorter events, 0.1 us)
Async XLA Ops:
  0.0 10.3 %copy-start.5 = (bf16[2,256,1536]{2,1,0:T(8,128)(2,1)S(1)}, bf16[2,256,1536]{2,1,0:T(8,128)(2,1)}, u32[]{:S(2)}) copy-start(bf16[2,256,1536]{2,1,0:T(8,128)(2,1)} %kv_ref.3) | copy-start | bytes 4718596
  0.0 17.2 %copy-start.8 = (f32[1536]{0:T(1024)S(1)}, f32[1536]{0:T(1024)}, u32[]{:S(2)}) copy-start(f32[1536]{0:T(1024)} %param.15) | copy-start | bytes 18436
  0.0 17.8 %copy-start.9 = (f32[1536]{0:T(1024)S(1)}, f32[1536]{0:T(1024)}, u32[]{:S(2)}) copy-start(f32[1536]{0:T(1024)} %param.16) | copy-start | bytes 18436
  0.0 18.5 %copy-start.13 = (s32[256]{0:T(256)S(1)}, s32[256]{0:T(256)}, u32[]{:S(2)}) copy-start(s32[256]{0:T(256)} %param.18) | copy-start | bytes 3076
  0.0 18.5 %copy-start.12 = (s32[256]{0:T(256)S(1)}, s32[256]{0:T(256)}, u32[]{:S(2)}) copy-start(s32[256]{0:T(256)} %param.19) | copy-start | bytes 3076
  0.0 18.5 %copy-start.14 = (s32[256]{0:T(256)S(1)}, s32[256]{0:T(256)}, u32[]{:S(2)}) copy-start(s32[256]{0:T(256)} %param.20) | copy-start | bytes 3076
  0.0 18.5 %copy-start.11 = (s32[256]{0:T(256)S(1)}, s32[256]{0:T(256)}, u32[]{:S(2)}) copy-start(s32[256]{0:T(256)} %param.21) | copy-start | bytes 3076
  1.3 20.6 %collective-permute-start.2 = (bf16[2,256,768]{2,1,0:T(8,128)(2,1)S(1)}, bf16[2,256,768]{2,1,0:T(8,128)(2,1)}, u32[]{:S(2)}, u32[]{:S(2)}) collective-permute-start(bf16[2,256,768]{2,1,0:T(8,128)(2,1)S(1)} %slice.30), channel_id=1, source_target_pairs={{0,1},{1,2},{2,3},{3,4},{4,5},{5,6},{6,7},{7,8},{8,9},{9,10},{10,1... | collective-permute-start | bytes 2359304 | tf_op jit(solution)/shard_map/ppermute | solution.py:376
  5.7 30.4 %collective-permute-start.3 = (bf16[2,256,768]{2,1,0:T(8,128)(2,1)S(1)}, bf16[2,256,768]{2,1,0:T(8,128)(2,1)}, u32[]{:S(2)}, u32[]{:S(2)}) collective-permute-start(bf16[2,256,768]{2,1,0:T(8,128)(2,1)S(1)} %slice.30), channel_id=1, source_target_pairs={{1,0},{2,1},{3,2},{4,3},{5,4},{6,5},{7,6},{8,7},{9,8},{10,9},{11,1... | collective-permute-start | bytes 2359304 | tf_op jit(solution)/shard_map/ppermute | solution.py:377
  10.4 32.2 %collective-permute-start = (bf16[2,256,768]{2,1,0:T(8,128)(2,1)S(1)}, bf16[2,256,768]{2,1,0:T(8,128)(2,1)S(1)}, u32[]{:S(2)}, u32[]{:S(2)}) collective-permute-start(bf16[2,256,768]{2,1,0:T(8,128)(2,1)S(1)} %slice.31), channel_id=1, source_target_pairs={{0,1},{1,2},{2,3},{3,4},{4,5},{5,6},{6,7},{7,8},{8,9},{9,10},{10,1... | collective-permute-start | bytes 2359304 | tf_op jit(solution)/shard_map/ppermute | solution.py:376
  12.3 32.2 %collective-permute-start.1 = (bf16[2,256,768]{2,1,0:T(8,128)(2,1)S(1)}, bf16[2,256,768]{2,1,0:T(8,128)(2,1)S(1)}, u32[]{:S(2)}, u32[]{:S(2)}) collective-permute-start(bf16[2,256,768]{2,1,0:T(8,128)(2,1)S(1)} %slice.31), channel_id=1, source_target_pairs={{1,0},{2,1},{3,2},{4,3},{5,4},{6,5},{7,6},{8,7},{9,8},{10,9},{11,1... | collective-permute-start | bytes 2359304 | tf_op jit(solution)/shard_map/ppermute | solution.py:377
  42.6 17.7 %copy-start.4 = (f32[31,1536]{1,0:T(8,128)S(1)}, f32[31,1536]{1,0:T(8,128)}, u32[]{:S(2)}) copy-start(f32[31,1536]{1,0:T(8,128)} %taps_ref.3) | copy-start | bytes 571396
  42.6 1.9 copy-start.15
  44.5 0.9 copy-start.16
  52.8 12.2 %collective-permute-start.4 = (bf16[16,1536]{1,0:T(8,128)(2,1)}, bf16[16,1536]{1,0:T(8,128)(2,1)S(1)}, u32[]{:S(2)}, u32[]{:S(2)}) collective-permute-start(bf16[16,1536]{1,0:T(8,128)(2,1)} %get-tuple-element.30), channel_id=1, source_target_pairs={{0,1},{1,2},{2,3},{3,4},{4,5},{5,6},{6,7},{7,8},{8,9},{9,10},{10,1... | collective-permute-start | bytes 147464 | tf_op jit(solution)/shard_map/ppermute | solution.py:382
  54.7 10.3 %collective-permute-start.5 = (bf16[16,1536]{1,0:T(8,128)(2,1)}, bf16[16,1536]{1,0:T(8,128)(2,1)S(1)}, u32[]{:S(2)}, u32[]{:S(2)}) collective-permute-start(bf16[16,1536]{1,0:T(8,128)(2,1)} %get-tuple-element.31), channel_id=1, source_target_pairs={{1,0},{2,1},{3,2},{4,3},{5,4},{6,5},{7,6},{8,7},{9,8},{10,9},{11,1... | collective-permute-start | bytes 147464 | tf_op jit(solution)/shard_map/ppermute | solution.py:383
  60.4 1.1 copy-start.2
  61.5 3.6 %copy-start.3 = (bf16[256,1536]{1,0:T(8,128)(2,1)S(1)}, bf16[256,1536]{1,0:T(8,128)(2,1)}, u32[]{:S(2)}) copy-start(bf16[256,1536]{1,0:T(8,128)(2,1)} %get-tuple-element.29.normed_ref) | copy-start | bytes 2359300
  88.9 17.8 %copy-start.6 = (bf16[2,128,1536]{2,1,0:T(8,128)(2,1)}, bf16[2,128,1536]{2,1,0:T(8,128)(2,1)S(1)}, u32[]{:S(2)}) copy-start(bf16[2,128,1536]{2,1,0:T(8,128)(2,1)S(1)} %reshape.50.own) | copy-start | bytes 2359300
  88.9 20.5 %collective-permute-start.6 = (bf16[2,128,1536]{2,1,0:T(8,128)(2,1)S(1)}, bf16[2,128,1536]{2,1,0:T(8,128)(2,1)S(1)}, u32[]{:S(2)}, u32[]{:S(2)}) collective-permute-start(bf16[2,128,1536]{2,1,0:T(8,128)(2,1)S(1)} %reshape.50.own), channel_id=1, source_target_pairs={{0,1},{1,2},{2,3},{3,0},{4,5},{5,6},{6,7},{7,4},{8,9},{9,10},{10,1... | collective-permute-start | bytes 2359304 | tf_op jit(solution)/shard_map/ppermute | solution.py:412
  89.0 20.4 %collective-permute-start.7 = (bf16[2,128,1536]{2,1,0:T(8,128)(2,1)S(1)}, bf16[2,128,1536]{2,1,0:T(8,128)(2,1)}, u32[]{:S(2)}, u32[]{:S(2)}) collective-permute-start(bf16[2,128,1536]{2,1,0:T(8,128)(2,1)S(1)} %reshape.50.own), channel_id=1, source_target_pairs={{1,0},{2,1},{3,2},{0,3},{5,4},{6,5},{7,6},{4,7},{9,8},{10,9},{11,1... | collective-permute-start | bytes 2359304 | tf_op jit(solution)/shard_map/ppermute | solution.py:412
  109.5 11.3 %copy-start.7 = (bf16[2,128,1536]{2,1,0:T(8,128)(2,1)}, bf16[2,128,1536]{2,1,0:T(8,128)(2,1)S(1)}, u32[]{:S(2)}) copy-start(bf16[2,128,1536]{2,1,0:T(8,128)(2,1)S(1)} %collective-permute-done.6.left) | copy-start | bytes 2359300
  109.5 11.2 %collective-permute-start.8 = (bf16[128,1536]{1,0:T(8,128)(2,1)S(1)}, bf16[128,1536]{1,0:T(8,128)(2,1)S(1)}, u32[]{:S(2)}, u32[]{:S(2)}) collective-permute-start(bf16[128,1536]{1,0:T(8,128)(2,1)S(1)} %slice_bitcast_fusion.1), channel_id=1, source_target_pairs={{0,1},{1,2},{2,3},{3,0},{4,5},{5,6},{6,7},{7,4},{8,9},{9,10},{10,1... | collective-permute-start | bytes 1179656 | tf_op jit(solution)/shard_map/ppermute | solution.py:415
  111.0 9.8 %collective-permute-start.9 = (bf16[128,1536]{1,0:T(8,128)(2,1)S(1)}, bf16[128,1536]{1,0:T(8,128)(2,1)S(1)}, u32[]{:S(2)}, u32[]{:S(2)}) collective-permute-start(bf16[128,1536]{1,0:T(8,128)(2,1)S(1)} %slice_bitcast_fusion), channel_id=1, source_target_pairs={{1,0},{2,1},{3,2},{0,3},{5,4},{6,5},{7,6},{4,7},{9,8},{10,9},{11,1... | collective-permute-start | bytes 1179656 | tf_op jit(solution)/shard_map/ppermute | solution.py:415
  113.3 28.2 %collective-permute-start.12 = (bf16[2,64,1536]{2,1,0:T(8,128)(2,1)S(1)}, bf16[2,64,1536]{2,1,0:T(8,128)(2,1)S(1)}, u32[]{:S(2)}, u32[]{:S(2)}) collective-permute-start(bf16[2,64,1536]{2,1,0:T(8,128)(2,1)S(1)} %reshape.53.own), channel_id=1, source_target_pairs={{0,1},{1,2},{2,3},{3,0},{4,5},{5,6},{6,7},{7,4},{8,9},{9,10},{10,1... | collective-permute-start | bytes 1179656 | tf_op jit(solution)/shard_map/ppermute | solution.py:412
  113.3 28.2 %collective-permute-start.13 = (bf16[2,64,1536]{2,1,0:T(8,128)(2,1)S(1)}, bf16[2,64,1536]{2,1,0:T(8,128)(2,1)S(1)}, u32[]{:S(2)}, u32[]{:S(2)}) collective-permute-start(bf16[2,64,1536]{2,1,0:T(8,128)(2,1)S(1)} %reshape.53.own), channel_id=1, source_target_pairs={{1,0},{2,1},{3,2},{0,3},{5,4},{6,5},{7,6},{4,7},{9,8},{10,9},{11,1... | collective-permute-start | bytes 1179656 | tf_op jit(solution)/shard_map/ppermute | solution.py:412
  116.0 25.6 %collective-permute-start.14 = (bf16[2,64,1536]{2,1,0:T(8,128)(2,1)S(1)}, bf16[2,64,1536]{2,1,0:T(8,128)(2,1)S(1)}, u32[]{:S(2)}, u32[]{:S(2)}) collective-permute-start(bf16[2,64,1536]{2,1,0:T(8,128)(2,1)S(1)} %reshape.53.own), channel_id=1, source_target_pairs={{0,2},{1,3},{2,0},{3,1},{4,6},{5,7},{6,4},{7,5},{8,10},{9,11},{10,... | collective-permute-start | bytes 1179656 | tf_op jit(solution)/shard_map/ppermute | solution.py:433
  137.3 0.9 copy-start
  138.1 26.2 %collective-permute-start.10 = (bf16[2,128,1536]{2,1,0:T(8,128)(2,1)}, bf16[2,128,1536]{2,1,0:T(8,128)(2,1)}, u32[]{:S(2)}, u32[]{:S(2)}) collective-permute-start(bf16[2,128,1536]{2,1,0:T(8,128)(2,1)} %get-tuple-element.39), channel_id=1, source_target_pairs={{0,1},{1,2},{2,3},{3,0},{4,5},{5,6},{6,7},{7,4},{8,9},{9,10},{10,1... | collective-permute-start | bytes 2359304 | tf_op jit(solution)/shard_map/ppermute | solution.py:435
  139.6 24.7 %collective-permute-start.11 = (bf16[2,128,1536]{2,1,0:T(8,128)(2,1)}, bf16[2,128,1536]{2,1,0:T(8,128)(2,1)}, u32[]{:S(2)}, u32[]{:S(2)}) collective-permute-start(bf16[2,128,1536]{2,1,0:T(8,128)(2,1)} %get-tuple-element.40), channel_id=1, source_target_pairs={{1,0},{2,1},{3,2},{0,3},{5,4},{6,5},{7,6},{4,7},{9,8},{10,9},{11,1... | collective-permute-start | bytes 2359304 | tf_op jit(solution)/shard_map/ppermute | solution.py:435
  155.8 41.8 %all-to-all-start.2 = ((bf16[128,4,1536]{2,1,0:T(4,128)(2,1)}), bf16[128,4,1536]{2,1,0:T(4,128)(2,1)}, u32[]{:S(2)}, u32[]{:S(2)}) async-start(bf16[128,4,1536]{2,1,0:T(4,128)(2,1)} %reshape.55), calls=%async_computation.2 | async-start | bytes 3145728 | tf_op jit(solution)/shard_map/all_to_all | solution.py:441
  164.4 29.7 %copy-start.1 = (bf16[2,128,1536]{2,1,0:T(8,128)(2,1)S(1)}, bf16[2,128,1536]{2,1,0:T(8,128)(2,1)}, u32[]{:S(2)}) copy-start(bf16[2,128,1536]{2,1,0:T(8,128)(2,1)} %copy-done) | copy-start | bytes 2359300
  165.6 26.2 %collective-permute-start.16 = (bf16[128,1536]{1,0:T(8,128)(2,1)S(1)}, bf16[128,1536]{1,0:T(8,128)(2,1)S(1)}, u32[]{:S(2)}, u32[]{:S(2)}) collective-permute-start(bf16[128,1536]{1,0:T(8,128)(2,1)S(1)} %fusion), channel_id=1, source_target_pairs={{1,0},{2,1},{3,2},{0,3},{5,4},{6,5},{7,6},{4,7},{9,8},{10,9},{11,1... | collective-permute-start | bytes 1179656 | tf_op jit(solution)/shard_map/ppermute | solution.py:445
  170.0 24.1 %collective-permute-start.15 = (bf16[128,1536]{1,0:T(8,128)(2,1)S(1)}, bf16[128,1536]{1,0:T(8,128)(2,1)S(1)}, u32[]{:S(2)}, u32[]{:S(2)}) collective-permute-start(bf16[128,1536]{1,0:T(8,128)(2,1)S(1)} %fusion.1), channel_id=1, source_target_pairs={{0,1},{1,2},{2,3},{3,0},{4,5},{5,6},{6,7},{7,4},{8,9},{9,10},{10,1... | collective-permute-start | bytes 1179656 | tf_op jit(solution)/shard_map/ppermute | solution.py:445
  200.3 6.5 %copy-start.10 = (f32[256]{0:T(256)S(1)}, f32[256]{0:T(256)}, u32[]{:S(2)}) copy-start(f32[256]{0:T(256)} %param.17) | copy-start | bytes 3076
  200.3 20.6 %all-to-all-start.3 = ((bf16[32,8,1536]{2,1,0:T(8,128)(2,1)}), bf16[32,8,1536]{2,1,0:T(8,128)(2,1)S(1)}, u32[]{:S(2)}, u32[]{:S(2)}) async-start(bf16[32,8,1536]{2,1,0:T(8,128)(2,1)} %reshape.56), calls=%async_computation.3 | async-start | bytes 1572864 | tf_op jit(solution)/shard_map/all_to_all | solution.py:422

commit v5 on v3

--- a/solution.py
+++ b/solution.py
@@ -18,6 +18,7 @@
 BLOCK = SIDE * PAIR
 MIB = 1024 * 1024
 STEP = 512
+DEVICES = 32
 F32 = jnp.float32
 BF16 = jnp.bfloat16
 
@@ -138,7 +139,7 @@
                     attend_body,
                     jax.ShapeDtypeStruct((rows, pairs * PAIR), F32),
                     cost,
-                    16,
+                    58,
                     grid=(pairs // SIDE,),
                     in_specs=base,
                     out_specs=pl.BlockSpec((rows, BLOCK), lambda j: (0, j)),
@@ -219,19 +220,21 @@
     expert_in = (mixed * scale * gain_ref[...]).astype(BF16)
     first = 0
     for out_ref in outs:
-        count = out_ref.shape[0]
+        copies, count, _ = out_ref.shape
         place = first + lax.broadcasted_iota(jnp.int32, (count, rows), 0)
         pick = jnp.where(place == place_ref[...], 1.0, 0.0).astype(BF16)
-        out_ref[...] = jnp.dot(pick, expert_in, preferred_element_type=F32).astype(BF16)
+        sent = jnp.dot(pick, expert_in, preferred_element_type=F32).astype(BF16)
+        for z in range(copies):
+            out_ref[z] = sent
         first += count
 
 
-def dispatch(normed, inner, low, high, taps, gain, place, counts):
+def dispatch(normed, inner, low, high, taps, gain, place, counts, copies):
     rows, width = normed.shape
     return call(
         dispatch_body,
         [jax.ShapeDtypeStruct((rows, width), BF16)]
-        + [jax.ShapeDtypeStruct((count, width), BF16) for count in counts],
+        + [jax.ShapeDtypeStruct((copies, count, width), BF16) for count in counts],
         (2 * sum(counts) * rows * width, 8 * rows * width),
         24,
         scratch_shapes=[pltpu.VMEM((2, 3 * EDGE, PAIR), F32)],
@@ -269,14 +272,24 @@
     )(mixed, gate[:, None], place[:, None], *parts)
 
 
-def ffn_body(direct, own, left, right, *rest):
+def by_expert(n, axis):
+    slots = n // DEVICES
+    shift = slots.bit_length() - 1
+    row = lax.broadcasted_iota(jnp.int32, (2 * n, 2 * n), axis)
+    e = jnp.where(row >= n, 1, 0)
+    r = row - e * n
+    place = ((r >> shift) << (shift + 1)) + (e << shift) + (r & (slots - 1))
+    return jnp.where(place == lax.broadcasted_iota(jnp.int32, (2 * n, 2 * n), 1 - axis), 1.0, 0.0).astype(BF16)
+
+
+def ffn_body(direct, me, arrived, w_in, w_out, *rest):
     if direct:
-        far, w_in, w_out, keep, to_right, to_left, to_far, *scratch = rest
-        far0, far1 = far.at[0], far.at[1]
+        keep, to_right, to_left, to_far, *scratch = rest
     else:
-        far0, far1, w_in, w_out, keep, up, down, up2, down2, *scratch = rest
+        keep, up, down, up2, down2, *scratch = rest
     rows_in, hidden, first, second, sems = scratch
-    n, width = own.shape[1:]
+    n = arrived.shape[1] // 2
+    width = arrived.shape[2]
     units = hidden.shape[1]
     step = STEP
     copies = {}
@@ -288,14 +301,15 @@
                     weight.at[e, :, cols], held.at[e, t], sems.at[e, which, t]
                 )
                 copies[e, which, t].start()
+    order = by_expert(n, 0)
+    for k, off in enumerate((0, 3, 1, 2)):
+        block = jnp.dot(order, arrived[(me[0] + off) % 4], preferred_element_type=F32).astype(BF16)
+        rows_in[0, k * n : (k + 1) * n] = block[:n]
+        rows_in[1, k * n : (k + 1) * n] = block[n:]
     for e in range(2):
-        rows_in[:n] = own[e]
-        rows_in[n : 2 * n] = left[e]
-        rows_in[2 * n : 3 * n] = right[e]
-        rows_in[3 * n :] = (far0 if e == 0 else far1)[...]
         for t in range(units // step):
             copies[e, 0, t].wait()
-            part = jnp.dot(rows_in[...], first[e, t], preferred_element_type=F32)
+            part = jnp.dot(rows_in[e], first[e, t], preferred_element_type=F32)
             hidden[:, t * step : (t + 1) * step] = silu(part).astype(BF16)
         for t in range(width // step):
             copies[e, 1, t].wait()
@@ -316,26 +330,51 @@
                 down[0, :, cols] = part[3 * n :]
 
 
-def ffn(own, left, right, far, w_in, w_out):
-    direct = len(far) == 1
-    experts, n, width = own.shape
-    units = w_in.shape[2]
+def ffn(direct, me, arrived, w_in, w_out):
+    n = arrived.shape[1] // 2
+    experts, width, units = w_in.shape
     pair = jax.ShapeDtypeStruct((2, n, width), BF16)
     single = jax.ShapeDtypeStruct((n, width), BF16)
     return call(
         functools.partial(ffn_body, direct),
         [pair] * 4 if direct else [pair, pair, pair, single, single],
         (experts * 4 * n * width * units * 4, 2 * experts * width * units * 2),
-        50,
-        in_specs=[pl.BlockSpec(memory_space=pltpu.VMEM)] * (3 + len(far)) + [pl.BlockSpec(memory_space=pl.ANY)] * 2,
+        42,
+        in_specs=[
+            pl.BlockSpec(memory_space=pltpu.SMEM),
+            pl.BlockSpec(memory_space=pltpu.VMEM),
+            pl.BlockSpec(memory_space=pl.ANY),
+            pl.BlockSpec(memory_space=pl.ANY),
+        ],
         scratch_shapes=[
-            pltpu.VMEM((4 * n, width), BF16),
+            pltpu.VMEM((2, 4 * n, width), BF16),
             pltpu.VMEM((4 * n, units), BF16),
             pltpu.VMEM((2, units // STEP, width, STEP), BF16),
             pltpu.VMEM((2, width // STEP, units, STEP), BF16),
             pltpu.SemaphoreType.DMA((2, 2, max(units, width) // STEP)),
         ],
-    )(own, left, right, *far, w_in, w_out)
+    )(me, arrived, w_in, w_out)
+
+
+def home_body(terms, *refs):
+    ins, out_ref = refs[:-1], refs[-1]
+    sums = []
+    for chosen in terms:
+        values = [(ins[i][...] if lead is None else ins[i][lead]).astype(F32) for i, lead in chosen]
+        sums.append(sum(values[1:], values[0]).astype(BF16))
+    rows = jnp.concatenate(sums, axis=0)
+    order = by_expert(rows.shape[0] // 2, 1)
+    out_ref[...] = jnp.dot(order, rows, preferred_element_type=F32).astype(BF16)
+
+
+def home(terms, *arrays):
+    _, n, width = arrays[0].shape
+    return call(
+        functools.partial(home_body, terms),
+        jax.ShapeDtypeStruct((2 * n, width), BF16),
+        (8 * n * n * width, 16 * n * width),
+        24,
+    )(*arrays)
 
 
 def on_device(
@@ -389,7 +428,7 @@
         experts * early + served * (slots - early) + slot - early,
     )
     mixed, *chunks = dispatch(
-        normed, inner, before, after, conv_kernel, ffn_gain, place, [experts * c for c in sizes]
+        normed, inner, before, after, conv_kernel, ffn_gain, place, [experts * c for c in sizes], group_count
     )
 
     up = [(i, (i + 1) % group_count) for i in range(group_count)]
@@ -397,38 +436,24 @@
     add = lambda *vs: sum(v.astype(F32) for v in vs).astype(BF16)
 
     def arrive(chunk, size):
-        sent = chunk.reshape(time_count, local * size, width)
-        own = lax.all_to_all(sent, "tm", split_axis=0, concat_axis=0, tiled=True)
-        own = own.reshape(time_count, local, size, width).transpose(1, 0, 2, 3)
-        return own.reshape(local, time_count * size, width)
-
-    def near(own):
-        return lax.ppermute(own, "expert", up), lax.ppermute(own, "expert", down)
-
-    def far(halves):
-        return lax.ppermute(halves[0], "expert", up), lax.ppermute(halves[1], "expert", down)
-
-    def home(summed, size):
-        summed = summed.reshape(local, time_count, size, width).transpose(1, 0, 2, 3)
-        return summed.reshape(time_count, local * size, width)
+        sent = chunk.reshape(devices, local * size, width)
+        got = lax.all_to_all(sent, ("expert", "tm"), split_axis=0, concat_axis=0, tiled=True)
+        return got.reshape(group_count, experts * size, width)
 
     def leave(summed, size):
+        summed = summed.reshape(time_count, local * size, width)
         got = lax.all_to_all(summed, "tm", split_axis=0, concat_axis=0, tiled=True)
         return got.reshape(experts * size, width)
 
     after = lambda values, *others: lax.optimization_barrier((tuple(values), others))[0]
-    own_a = arrive(chunks[0], sizes[0])
-    left_a, right_a = near(own_a)
-    own_b = arrive(*after((chunks[1],), own_a), sizes[1])
-    left_a, right_a = after((left_a, right_a), own_b)
-    far_a = far((left_a[0], right_a[1]))
-    left_b, right_b = near(own_b)
+    me = lax.axis_index("expert").astype(jnp.int32)[None]
     across = [(i, (i + 2) % group_count) for i in range(group_count)]
-    far_b = lax.ppermute(own_b, "expert", across)
-    keep_a, go_up_a, go_down_a, up2_a, down2_a = ffn(own_a, left_a, right_a, far_a, w_in, w_out)
+    rows_a = arrive(chunks[0], sizes[0])
+    rows_b = arrive(*after((chunks[1],), rows_a), sizes[1])
+    keep_a, go_up_a, go_down_a, up2_a, down2_a = ffn(False, me, rows_a, w_in, w_out)
     below_a, above_a = lax.ppermute(go_up_a, "expert", up), lax.ppermute(go_down_a, "expert", down)
-    (own_b,) = after((own_b,), keep_a)
-    keep_b, to_right, to_left, to_far = ffn(own_b, left_b, right_b, (far_b,), w_in, w_out)
+    (rows_b,) = after((rows_b,), keep_a)
+    keep_b, to_right, to_left, to_far = ffn(True, me, rows_b, w_in, w_out)
     below_a, above_a = after((below_a, above_a), keep_b)
     up2_a, down2_a = add(up2_a, below_a[0]), add(down2_a, above_a[0])
     up3_a, down3_a = lax.ppermute(up2_a, "expert", up), lax.ppermute(down2_a, "expert", down)
@@ -438,10 +463,12 @@
         lax.ppermute(to_left, "expert", down),
         lax.ppermute(to_far, "expert", across),
     )
-    total_a = jnp.stack([add(keep_a[0], above_a[1], up3_a), add(keep_a[1], below_a[1], down3_a)])
-    back_a = leave(home(total_a, sizes[0]), sizes[0])
+    terms = (((0, 0), (1, 1), (3, None)), ((0, 1), (2, 1), (4, None)))
+    total_a = home(terms, keep_a, above_a, below_a, up3_a, down3_a)
+    back_a = leave(total_a, sizes[0])
     parts_b = after(parts_b, back_a)
-    back_b = leave(home(add(keep_b, *parts_b), sizes[1]), sizes[1])
+    total_b = home([[(i, e) for i in range(4)] for e in range(2)], keep_b, *parts_b)
+    back_b = leave(total_b, sizes[1])
     return combine(mixed, expert_gate, place, [back_a, back_b])
 
 

time: 226 us -> 230 us (1.018)
  blocking collectives: 35.7 us -> 50.1 us
  starting transfers between devices: 58.5 us -> 53.9 us
  other arithmetic: 3.89 us -> 0.8 us
  local copies, waits for them, and re-layouts: 16.2 us -> 13.2 us
    all_to_all x2 -> x1, blocking collectives: 35.7 us -> 50.1 us  [arrive(): lax.all_to_all(sent, ('expert', 'tm'), split_axis=0, concat_axis=0, tiled...]
    ppermute x7 -> x0, starting transfers between devices: 8.23 us -> none  [the longest x4 5.41 us: near(): return (lax.ppermute(own, 'expert', up), lax.ppermute(own, 'expert', down))]
    ppermute x7 -> x0, waiting for transfers between devices: 7.39 us -> none  [the longest x1 4.7 us: far(): lax.ppermute(halves[0], 'expert', up)]
    all_to_all x0 -> x1, starting transfers between devices: none -> 5.27 us  [arrive(): lax.all_to_all(sent, ('expert', 'tm'), split_axis=0, concat_axis=0, tiled...]
    reshape x6 -> x3, local copies, waits for them, and re-layouts: 2.52 us -> 7.45 us  [the longest x1 3.88 us: arrive(): sent = chunk.reshape(devices, local * size, width)]
    all_to_all x0 -> x1, waiting for transfers between devices: none -> 4.52 us  [arrive(): lax.all_to_all(sent, ('expert', 'tm'), split_axis=0, concat_axis=0, tiled...]
    ppermute x1, waiting for transfers between devices: 4.54 us -> 8.54 us  [on_device(): lax.ppermute(down2_a, 'expert', down)]
    ppermute x1, waiting for transfers between devices: 3.28 us -> 0.29 us  [on_device(): lax.ppermute(up2_a, 'expert', up)]
  transfers between devices with their start and end apart: 22 -> 16, of which waited for: 9 -> 8; matrix products, arithmetic and copies ran while one was open for 3% -> 2% of each run, Pallas kernels for 16% -> 15%
where the time goes in v5:
time: 230 us; the launch traced here: 229 us
  waiting for transfers between devices  64.9 us (28%)
  starting transfers between devices  53.9 us (23%)
  blocking collectives  50.1 us (22%)
  Pallas kernels  45.7 us (20%)
  local copies, waits for them, and re-layouts  13.2 us (6%)
    all_to_all x1, blocking collectives, arrive(): lax.all_to_all(sent, ('expert', 'tm'), split_axis=0, concat_axis=0, tiled...  50.1 us
    pallas_call x2, Pallas kernels, ffn(): call(functools.partial(ffn_body, direct), [pair] * 4 if direct else [pair...  23.6 us
    all_to_all x2, starting transfers between devices, leave(): got = lax.all_to_all(summed, 'tm', split_axis=0, concat_axis=0, tiled=True)  17.5 us
    ppermute x1, waiting for transfers between devices, on_device(): lax.ppermute(to_right, 'expert', up)  17.4 us
    ppermute x2, waiting for transfers between devices, on_device(): high.append(lax.ppermute(part, order, back))  11.4 us
    all_to_all x2, waiting for transfers between devices, leave(): got = lax.all_to_all(summed, 'tm', split_axis=0, concat_axis=0, tiled=True)  10 us
    ppermute x2, starting transfers between devices, on_device(): high.append(lax.ppermute(part, order, back))  9.45 us
    ppermute x2, waiting for transfers between devices, on_device(): low.append(lax.ppermute(part, order, onward))  8.58 us
  transfers between devices with their start and end apart: 16, of which 8 were waited for; matrix products, arithmetic and copies ran while one was open for 2% of the time, Pallas kernels for 15%

profile of v5, /device:TPU:1, one launch (start us, length us, event | category | flops | bytes accessed | tf_op | source)
XLA Modules:
  0.0 229.2 jit_solution(7500137354708012524)
XLA Ops:
  0.0 1.3 slice.12
  1.4 4.4 %collective-permute-start.2 = (bf16[2,256,1024]{2,1,0:T(8,128)(2,1)S(1)}, bf16[2,256,1024]{2,1,0:T(8,128)(2,1)}, u32[]{:S(2)}, u32[]{:S(2)}) collective-permute-start(bf16[2,256,1024]{2,1,0:T(8,128)(2,1)S(1)} %slice.12), channel_id=1, source_target_pairs={{0,1},{1,2},{2,3},{3,4},{4,5},{5,6},{6,7},{7,8},{8,9},{9,10},{10,1... | collective-permute-start | bytes 3145736 | tf_op jit(solution)/shard_map/ppermute | solution.py:409
  5.8 4.6 %collective-permute-start.3 = (bf16[2,256,1024]{2,1,0:T(8,128)(2,1)S(1)}, bf16[2,256,1024]{2,1,0:T(8,128)(2,1)}, u32[]{:S(2)}, u32[]{:S(2)}) collective-permute-start(bf16[2,256,1024]{2,1,0:T(8,128)(2,1)S(1)} %slice.12), channel_id=1, source_target_pairs={{1,0},{2,1},{3,2},{4,3},{5,4},{6,5},{7,6},{8,7},{9,8},{10,9},{11,1... | collective-permute-start | bytes 3145736 | tf_op jit(solution)/shard_map/ppermute | solution.py:410
  10.4 1.1 slice.13
  11.5 1.9 collective-permute-start
  13.4 4.9 %collective-permute-start.1 = (bf16[2,256,512]{2,1,0:T(8,128)(2,1)S(1)}, bf16[2,256,512]{2,1,0:T(8,128)(2,1)S(1)}, u32[]{:S(2)}, u32[]{:S(2)}) collective-permute-start(bf16[2,256,512]{2,1,0:T(8,128)(2,1)S(1)} %slice.13), channel_id=1, source_target_pairs={{1,0},{2,1},{3,2},{4,3},{5,4},{6,5},{7,6},{8,7},{9,8},{10,9},{11,1... | collective-permute-start | bytes 1572872 | tf_op jit(solution)/shard_map/ppermute | solution.py:410
  18.3 0.6 add_convert_fusion.edge_ref
  18.9 0.0 copy-done.20
  19.0 0.0 copy-start.1
  19.0 0.0 copy-start.11
  19.0 8.6 %collective-permute-done.2.lo_ref = bf16[2,256,1024]{2,1,0:T(8,128)(2,1)} collective-permute-done((bf16[2,256,1024]{2,1,0:T(8,128)(2,1)S(1)}, bf16[2,256,1024]{2,1,0:T(8,128)(2,1)}, u32[]{:S(2)}, u32[]{:S(2)}) %collective-permute-start.2) | collective-permute-done | bytes 1048608 | tf_op jit(solution)/shard_map/ppermute | solution.py:409
  27.6 11.4 %collective-permute-done.3.hi_ref = bf16[2,256,1024]{2,1,0:T(8,128)(2,1)} collective-permute-done((bf16[2,256,1024]{2,1,0:T(8,128)(2,1)S(1)}, bf16[2,256,1024]{2,1,0:T(8,128)(2,1)}, u32[]{:S(2)}, u32[]{:S(2)}) %collective-permute-start.3) | collective-permute-done | bytes 1048608 | tf_op jit(solution)/shard_map/ppermute | solution.py:410
  39.0 8.1 %shard_map.118.rest_0_ = f32[256,1024]{1,0:T(8,128)} custom-call(s32[2]{0:T(128)} %add_convert_fusion.edge_ref, bf16[256,1536]{1,0:T(8,128)(2,1)} %q_ref.3, bf16[2,256,1536]{2,1,0:T(8,128)(2,1)} %kv_ref.3, bf16[2,256,1024]{2,1,0:T(8,128)(2,1)} %collective-permute-done.2.lo_ref, bf16[2,256,1024]{2,1,0:T(8,128)(2,1)} %collective-permute-done.3.hi_ref), custom_call_target="tpu_custom_call" | custom-call | flops 2684354560 | bytes 3670016 | tf_op jit(solution)/shard_map/pallas_call | solution.py:138
  47.0 0.0 collective-permute-done.lo_ref
  47.1 0.0 collective-permute-done.1.hi_ref
  47.1 1.3 copy-done.19
  48.4 4.0 %shard_map.119 = (bf16[256,1536]{1,0:T(8,128)(2,1)S(1)}, bf16[16,1536]{1,0:T(8,128)(2,1)S(1)}, bf16[16,1536]{1,0:T(8,128)(2,1)S(1)}) custom-call(s32[2]{0:T(128)S(1)} %copy-done.18, bf16[256,1536]{1,0:T(8,128)(2,1)S(1)} %copy-done.11, bf16[2,256,1536]{2,1,0:T(8,128)(2,1)S(1)} %copy-done.1, bf16[2,256,512]{2,1,0:T(8,128)(2,1)S(1)} %collective-permute-done.lo_ref, ...), custom_call_target="tpu_custom_call" | custom-call | flops 1342177280 | bytes 1835008 | tf_op jit(solution)/shard_map/pallas_call | solution.py:151
  52.4 1.9 collective-permute-start.4
  54.3 5.7 %collective-permute-start.5 = (bf16[16,1536]{1,0:T(8,128)(2,1)S(1)}, bf16[16,1536]{1,0:T(8,128)(2,1)S(1)}, u32[]{:S(2)}, u32[]{:S(2)}) collective-permute-start(bf16[16,1536]{1,0:T(8,128)(2,1)S(1)} %get-tuple-element.38), channel_id=1, source_target_pairs={{1,0},{2,1},{3,2},{4,3},{5,4},{6,5},{7,6},{8,7},{9,8},{10,9},{11,1... | collective-permute-start | bytes 147464 | tf_op jit(solution)/shard_map/ppermute | solution.py:416
  60.0 3.6 %shard_map.120.inner_ref = bf16[224,1536]{1,0:T(8,128)(2,1)S(1)} custom-call(bf16[256,1536]{1,0:T(8,128)(2,1)S(1)} %get-tuple-element.36.normed_ref, f32[31,1536]{1,0:T(8,128)S(1)} %copy-done.10), custom_call_target="tpu_custom_call" | custom-call | flops 1365245952 | bytes 1572864 | tf_op jit(solution)/shard_map/pallas_call | solution.py:190
  63.6 0.0 collective-permute-done.4.low_ref
  63.6 0.0 collective-permute-done.5.high_ref
  63.6 1.3 shard_map.121
  64.9 0.0 copy-start.2
  65.0 50.1 %all_to_all.20 = bf16[128,8,1536]{2,1,0:T(8,128)(2,1)S(1)} all-to-all(bf16[128,8,1536]{2,1,0:T(8,128)(2,1)S(1)} %bitcast.17), channel_id=1, replica_groups=mesh['tm'=32,'expert'=4] {'expert','tm'}, dimensions={0} | all-to-all | bytes 6291456 | tf_op jit(solution)/shard_map/all_to_all | solution.py:440
  115.1 0.0 copy-done
  115.1 3.9 %reshape.30 = bf16[128,4,1536]{2,1,0:T(4,128)(2,1)} reshape(bf16[4,128,1536]{2,1,0:T(8,128)(2,1)} %copy-done) | data formatting | bytes 3145728 | tf_op jit(solution)/shard_map/reshape | solution.py:439
  119.0 5.3 %all-to-all-start.1 = ((bf16[128,4,1536]{2,1,0:T(4,128)(2,1)}), bf16[128,4,1536]{2,1,0:T(4,128)(2,1)}, u32[]{:S(2)}, u32[]{:S(2)}) async-start(bf16[128,4,1536]{2,1,0:T(4,128)(2,1)} %reshape.30), calls=%async_computation.1 | async-start | bytes 3145728 | tf_op jit(solution)/shard_map/all_to_all | solution.py:440
  124.2 14.8 %shard_map.122 = (bf16[2,128,1536]{2,1,0:T(8,128)(2,1)S(1)}, bf16[2,128,1536]{2,1,0:T(8,128)(2,1)}, bf16[2,128,1536]{2,1,0:T(8,128)(2,1)}, bf16[128,1536]{1,0:T(8,128)(2,1)S(1)}, bf16[128,1536]{1,0:T(8,128)(2,1)S(1)}) custom-call(s32[1]{0:T(128)} %bitcast.5.me, bf16[4,256,1536]{2,1,0:T(8,128)(2,1)S(1)} %bitcast.16, bf16[2,1536,1536]{2,1,0:T(8,128)(2,1)} %w_in.3, ...), custom_call_target="tpu_custom_call" | custom-call | flops 9663676416 | bytes 18874368 | tf_op jit(solution)/shard_map/pallas_call | solution.py:338
  139.1 0.9 copy-done.4
  139.9 0.8 copy-done.6
  140.7 1.7 collective-permute-start.6
  142.4 1.7 collective-permute-start.7
  144.1 4.5 %all-to-all-done.1 = bf16[128,4,1536]{2,1,0:T(4,128)(2,1)} async-done(((bf16[128,4,1536]{2,1,0:T(4,128)(2,1)}), bf16[128,4,1536]{2,1,0:T(4,128)(2,1)}, u32[]{:S(2)}, u32[]{:S(2)}) %all-to-all-start.1) | async-done | bytes 1572896 | tf_op jit(solution)/shard_map/all_to_all | solution.py:440
  148.6 2.7 %reshape.31.arrived = bf16[4,128,1536]{2,1,0:T(8,128)(2,1)S(1)} reshape(bf16[128,4,1536]{2,1,0:T(4,128)(2,1)} %all-to-all-done.1) | data formatting | bytes 3145728 | tf_op jit(solution)/shard_map/reshape | solution.py:441
  151.4 8.8 %shard_map.123 = (bf16[2,64,1536]{2,1,0:T(8,128)(2,1)S(1)}, bf16[2,64,1536]{2,1,0:T(8,128)(2,1)S(1)}, bf16[2,64,1536]{2,1,0:T(8,128)(2,1)S(1)}, bf16[2,64,1536]{2,1,0:T(8,128)(2,1)S(1)}) custom-call(s32[1]{0:T(128)} %bitcast.5.me, bf16[4,128,1536]{2,1,0:T(8,128)(2,1)S(1)} %reshape.31.arrived, bf16[2,1536,1536]{2,1,0:T(8,128)(2,1)} %w_in.3, ...), custom_call_target="tpu_custom_call" | custom-call | flops 4831838208 | bytes 18874368 | tf_op jit(solution)/shard_map/pallas_call | solution.py:338
  160.2 0.0 copy-start.8
  160.2 4.1 %collective-permute-done.6.refs_2_ = bf16[2,128,1536]{2,1,0:T(8,128)(2,1)S(1)} collective-permute-done((bf16[2,128,1536]{2,1,0:T(8,128)(2,1)}, bf16[2,128,1536]{2,1,0:T(8,128)(2,1)S(1)}, u32[]{:S(2)}, u32[]{:S(2)}) %collective-permute-start.6) | collective-permute-done | bytes 786464 | tf_op jit(solution)/shard_map/ppermute | solution.py:454
  164.4 0.0 collective-permute-done.7.refs_1_
  164.4 0.1 fusion
  164.5 0.2 collective-permute-start.9
  164.6 0.1 fusion.1
  164.7 1.5 collective-permute-start.8
  166.2 8.5 %collective-permute-done.9.refs_4_ = bf16[128,1536]{1,0:T(8,128)(2,1)S(1)} collective-permute-done((bf16[128,1536]{1,0:T(8,128)(2,1)S(1)}, bf16[128,1536]{1,0:T(8,128)(2,1)S(1)}, u32[]{:S(2)}, u32[]{:S(2)}) %collective-permute-start.9) | collective-permute-done | bytes 393248 | tf_op jit(solution)/shard_map/ppermute | solution.py:459
  174.7 0.3 collective-permute-done.8.refs_3_
  175.0 1.4 shard_map.124
  176.5 9.5 %all-to-all-start.2 = ((bf16[32,8,1536]{2,1,0:T(8,128)(2,1)}), bf16[32,8,1536]{2,1,0:T(8,128)(2,1)S(1)}, u32[]{:S(2)}, u32[]{:S(2)}) async-start(bf16[32,8,1536]{2,1,0:T(8,128)(2,1)} %bitcast.10), calls=%async_computation.2 | async-start | bytes 1572864 | tf_op jit(solution)/shard_map/all_to_all | solution.py:445
  186.0 0.1 collective-permute-start.10
  186.1 2.7 %collective-permute-start.11 = (bf16[2,64,1536]{2,1,0:T(8,128)(2,1)S(1)}, bf16[2,64,1536]{2,1,0:T(8,128)(2,1)S(1)}, u32[]{:S(2)}, u32[]{:S(2)}) collective-permute-start(bf16[2,64,1536]{2,1,0:T(8,128)(2,1)S(1)} %copy-done.15), channel_id=1, source_target_pairs={{1,0},{2,1},{3,2},{0,3},{5,4},{6,5},{7,6},{4,7},{9,8},{10,9},{11,1... | collective-permute-start | bytes 1179656 | tf_op jit(solution)/shard_map/ppermute | solution.py:463
  188.7 0.0 collective-permute-start.12
  188.7 17.4 %collective-permute-done.10.refs_1_ = bf16[2,64,1536]{2,1,0:T(8,128)(2,1)S(1)} collective-permute-done((bf16[2,64,1536]{2,1,0:T(8,128)(2,1)S(1)}, bf16[2,64,1536]{2,1,0:T(8,128)(2,1)S(1)}, u32[]{:S(2)}, u32[]{:S(2)}) %collective-permute-start.10) | collective-permute-done | bytes 393248 | tf_op jit(solution)/shard_map/ppermute | solution.py:462
  206.2 0.0 collective-permute-done.11.refs_2_
  206.2 0.0 collective-permute-done.12.refs_3_
  206.2 0.0 all-to-all-done.2
  206.2 0.0 copy-start.22
  206.2 0.4 shard_map.125
  206.6 0.0 copy-start.3
  206.6 0.8 reshape.34
  207.4 8.1 %all-to-all-start.3 = ((bf16[32,4,1536]{2,1,0:T(4,128)(2,1)}), bf16[32,4,1536]{2,1,0:T(4,128)(2,1)S(1)}, u32[]{:S(2)}, u32[]{:S(2)}) async-start(bf16[32,4,1536]{2,1,0:T(4,128)(2,1)} %reshape.34), calls=%async_computation.3 | async-start | bytes 786432 | tf_op jit(solution)/shard_map/all_to_all | solution.py:445
  215.5 0.1 copy.14.place_ref
  215.6 0.1 copy.13.gate_ref
  215.8 10.0 %all-to-all-done.3 = bf16[32,4,1536]{2,1,0:T(4,128)(2,1)S(1)} async-done(((bf16[32,4,1536]{2,1,0:T(4,128)(2,1)}), bf16[32,4,1536]{2,1,0:T(4,128)(2,1)S(1)}, u32[]{:S(2)}, u32[]{:S(2)}) %all-to-all-start.3) | async-done | bytes 393248 | tf_op jit(solution)/shard_map/all_to_all | solution.py:445
  225.8 0.1 reshape.35.rest_1_
  225.9 3.3 %shard_map.126 = bf16[256,1536]{1,0:T(8,128)(2,1)} custom-call(bf16[256,1536]{1,0:T(8,128)(2,1)S(1)} %copy-done.3, f32[256,1]{1,0:T(8,128)S(1)} %copy.13.gate_ref, s32[256,1]{1,0:T(8,128)S(1)} %copy.14.place_ref, bf16[256,1536]{1,0:T(8,128)(2,1)S(1)} %bitcast.18, bf16[128,1536]{1,0:T(8,128)(2,1)S(1)} %reshape.35.rest_1_), custom_call_target="tpu_custom_call" | custom-call | flops 301989888 | bytes 3145728 | tf_op jit(solution)/shard_map/pallas_call | solution.py:264
  (46 shorter events, 0.1 us)
Async XLA Ops:
  0.0 18.9 %copy-start.20 = (f32[1536]{0:T(1024)S(1)}, f32[1536]{0:T(1024)}, u32[]{:S(2)}) copy-start(f32[1536]{0:T(1024)} %param.15) | copy-start | bytes 18436
  0.0 18.9 %copy-start.21 = (f32[1536]{0:T(1024)S(1)}, f32[1536]{0:T(1024)}, u32[]{:S(2)}) copy-start(f32[1536]{0:T(1024)} %param.16) | copy-start | bytes 18436
  0.0 18.9 %copy-start.25 = (s32[256]{0:T(256)S(1)}, s32[256]{0:T(256)}, u32[]{:S(2)}) copy-start(s32[256]{0:T(256)} %param.18) | copy-start | bytes 3076
  0.0 18.9 %copy-start.24 = (s32[256]{0:T(256)S(1)}, s32[256]{0:T(256)}, u32[]{:S(2)}) copy-start(s32[256]{0:T(256)} %param.19) | copy-start | bytes 3076
  0.0 18.9 %copy-start.26 = (s32[256]{0:T(256)S(1)}, s32[256]{0:T(256)}, u32[]{:S(2)}) copy-start(s32[256]{0:T(256)} %param.20) | copy-start | bytes 3076
  0.0 18.9 %copy-start.23 = (s32[256]{0:T(256)S(1)}, s32[256]{0:T(256)}, u32[]{:S(2)}) copy-start(s32[256]{0:T(256)} %param.21) | copy-start | bytes 3076
  1.4 26.2 %collective-permute-start.2 = (bf16[2,256,1024]{2,1,0:T(8,128)(2,1)S(1)}, bf16[2,256,1024]{2,1,0:T(8,128)(2,1)}, u32[]{:S(2)}, u32[]{:S(2)}) collective-permute-start(bf16[2,256,1024]{2,1,0:T(8,128)(2,1)S(1)} %slice.12), channel_id=1, source_target_pairs={{0,1},{1,2},{2,3},{3,4},{4,5},{5,6},{6,7},{7,8},{8,9},{9,10},{10,1... | collective-permute-start | bytes 3145736 | tf_op jit(solution)/shard_map/ppermute | solution.py:409
  5.8 33.2 %collective-permute-start.3 = (bf16[2,256,1024]{2,1,0:T(8,128)(2,1)S(1)}, bf16[2,256,1024]{2,1,0:T(8,128)(2,1)}, u32[]{:S(2)}, u32[]{:S(2)}) collective-permute-start(bf16[2,256,1024]{2,1,0:T(8,128)(2,1)S(1)} %slice.12), channel_id=1, source_target_pairs={{1,0},{2,1},{3,2},{4,3},{5,4},{6,5},{7,6},{8,7},{9,8},{10,9},{11,1... | collective-permute-start | bytes 3145736 | tf_op jit(solution)/shard_map/ppermute | solution.py:410
  11.5 35.6 %collective-permute-start = (bf16[2,256,512]{2,1,0:T(8,128)(2,1)S(1)}, bf16[2,256,512]{2,1,0:T(8,128)(2,1)S(1)}, u32[]{:S(2)}, u32[]{:S(2)}) collective-permute-start(bf16[2,256,512]{2,1,0:T(8,128)(2,1)S(1)} %slice.13), channel_id=1, source_target_pairs={{0,1},{1,2},{2,3},{3,4},{4,5},{5,6},{6,7},{7,8},{8,9},{9,10},{10,1... | collective-permute-start | bytes 1572872 | tf_op jit(solution)/shard_map/ppermute | solution.py:409
  13.4 33.7 %collective-permute-start.1 = (bf16[2,256,512]{2,1,0:T(8,128)(2,1)S(1)}, bf16[2,256,512]{2,1,0:T(8,128)(2,1)S(1)}, u32[]{:S(2)}, u32[]{:S(2)}) collective-permute-start(bf16[2,256,512]{2,1,0:T(8,128)(2,1)S(1)} %slice.13), channel_id=1, source_target_pairs={{1,0},{2,1},{3,2},{4,3},{5,4},{6,5},{7,6},{8,7},{9,8},{10,9},{11,1... | collective-permute-start | bytes 1572872 | tf_op jit(solution)/shard_map/ppermute | solution.py:410
  19.0 28.1 %copy-start.1 = (bf16[2,256,1536]{2,1,0:T(8,128)(2,1)S(1)}, bf16[2,256,1536]{2,1,0:T(8,128)(2,1)}, u32[]{:S(2)}) copy-start(bf16[2,256,1536]{2,1,0:T(8,128)(2,1)} %kv_ref.3) | copy-start | bytes 4718596
  19.0 28.1 %copy-start.11 = (bf16[256,1536]{1,0:T(8,128)(2,1)S(1)}, bf16[256,1536]{1,0:T(8,128)(2,1)}, u32[]{:S(2)}) copy-start(bf16[256,1536]{1,0:T(8,128)(2,1)} %q_ref.3) | copy-start | bytes 2359300
  19.0 28.1 %copy-start.18 = (s32[2]{0:T(128)S(1)}, s32[2]{0:T(128)}, u32[]{:S(2)}) copy-start(s32[2]{0:T(128)} %add_convert_fusion.edge_ref) | copy-start | bytes 28
  47.0 12.9 %copy-start.10 = (f32[31,1536]{1,0:T(8,128)S(1)}, f32[31,1536]{1,0:T(8,128)}, u32[]{:S(2)}) copy-start(f32[31,1536]{1,0:T(8,128)} %taps_ref.3) | copy-start | bytes 571396
  47.1 1.3 copy-start.19
  52.4 11.2 %collective-permute-start.4 = (bf16[16,1536]{1,0:T(8,128)(2,1)S(1)}, bf16[16,1536]{1,0:T(8,128)(2,1)S(1)}, u32[]{:S(2)}, u32[]{:S(2)}) collective-permute-start(bf16[16,1536]{1,0:T(8,128)(2,1)S(1)} %get-tuple-element.37), channel_id=1, source_target_pairs={{0,1},{1,2},{2,3},{3,4},{4,5},{5,6},{6,7},{7,8},{8,9},{9,10},{10,1... | collective-permute-start | bytes 147464 | tf_op jit(solution)/shard_map/ppermute | solution.py:415
  54.3 9.3 %collective-permute-start.5 = (bf16[16,1536]{1,0:T(8,128)(2,1)S(1)}, bf16[16,1536]{1,0:T(8,128)(2,1)S(1)}, u32[]{:S(2)}, u32[]{:S(2)}) collective-permute-start(bf16[16,1536]{1,0:T(8,128)(2,1)S(1)} %get-tuple-element.38), channel_id=1, source_target_pairs={{1,0},{2,1},{3,2},{4,3},{5,4},{6,5},{7,6},{8,7},{9,8},{10,9},{11,1... | collective-permute-start | bytes 147464 | tf_op jit(solution)/shard_map/ppermute | solution.py:416
  64.9 50.1 %copy-start = (bf16[4,128,1536]{2,1,0:T(8,128)(2,1)}, bf16[4,128,1536]{2,1,0:T(8,128)(2,1)S(1)}, u32[]{:S(2)}) copy-start(bf16[4,128,1536]{2,1,0:T(8,128)(2,1)S(1)} %get-tuple-element.45) | copy-start | bytes 4718596
  64.9 50.1 %copy-start.2 = (bf16[256,1536]{1,0:T(8,128)(2,1)}, bf16[256,1536]{1,0:T(8,128)(2,1)S(1)}, u32[]{:S(2)}) copy-start(bf16[256,1536]{1,0:T(8,128)(2,1)S(1)} %get-tuple-element.39.mixed_ref) | copy-start | bytes 2359300
  119.0 29.7 %all-to-all-start.1 = ((bf16[128,4,1536]{2,1,0:T(4,128)(2,1)}), bf16[128,4,1536]{2,1,0:T(4,128)(2,1)}, u32[]{:S(2)}, u32[]{:S(2)}) async-start(bf16[128,4,1536]{2,1,0:T(4,128)(2,1)} %reshape.30), calls=%async_computation.1 | async-start | bytes 3145728 | tf_op jit(solution)/shard_map/all_to_all | solution.py:440
  139.1 0.9 copy-start.4
  139.9 0.8 copy-start.6
  140.7 23.7 %collective-permute-start.6 = (bf16[2,128,1536]{2,1,0:T(8,128)(2,1)}, bf16[2,128,1536]{2,1,0:T(8,128)(2,1)S(1)}, u32[]{:S(2)}, u32[]{:S(2)}) collective-permute-start(bf16[2,128,1536]{2,1,0:T(8,128)(2,1)} %get-tuple-element.42), channel_id=1, source_target_pairs={{0,1},{1,2},{2,3},{3,0},{4,5},{5,6},{6,7},{7,4},{8,9},{9,10},{10,1... | collective-permute-start | bytes 2359304 | tf_op jit(solution)/shard_map/ppermute | solution.py:454
  142.4 22.0 %collective-permute-start.7 = (bf16[2,128,1536]{2,1,0:T(8,128)(2,1)}, bf16[2,128,1536]{2,1,0:T(8,128)(2,1)S(1)}, u32[]{:S(2)}, u32[]{:S(2)}) collective-permute-start(bf16[2,128,1536]{2,1,0:T(8,128)(2,1)} %get-tuple-element.43), channel_id=1, source_target_pairs={{1,0},{2,1},{3,2},{0,3},{5,4},{6,5},{7,6},{4,7},{9,8},{10,9},{11,1... | collective-permute-start | bytes 2359304 | tf_op jit(solution)/shard_map/ppermute | solution.py:454
  151.4 13.0 %copy-start.7 = (bf16[128,1536]{1,0:T(8,128)(2,1)S(1)}, bf16[128,1536]{1,0:T(8,128)(2,1)}, u32[]{:S(2)}) copy-start(bf16[128,1536]{1,0:T(8,128)(2,1)} %copy-done.6) | copy-start | bytes 1179652
  160.2 16.2 %copy-start.8 = (bf16[2,64,1536]{2,1,0:T(8,128)(2,1)}, bf16[2,64,1536]{2,1,0:T(8,128)(2,1)S(1)}, u32[]{:S(2)}) copy-start(bf16[2,64,1536]{2,1,0:T(8,128)(2,1)S(1)} %get-tuple-element.47.refs_0_) | copy-start | bytes 1179652
  160.2 16.2 %copy-start.12 = (bf16[2,64,1536]{2,1,0:T(8,128)(2,1)}, bf16[2,64,1536]{2,1,0:T(8,128)(2,1)S(1)}, u32[]{:S(2)}) copy-start(bf16[2,64,1536]{2,1,0:T(8,128)(2,1)S(1)} %get-tuple-element.57) | copy-start | bytes 1179652
  160.2 16.2 %copy-start.14 = (bf16[2,64,1536]{2,1,0:T(8,128)(2,1)}, bf16[2,64,1536]{2,1,0:T(8,128)(2,1)S(1)}, u32[]{:S(2)}) copy-start(bf16[2,64,1536]{2,1,0:T(8,128)(2,1)S(1)} %get-tuple-element.56) | copy-start | bytes 1179652
  160.2 16.2 %copy-start.16 = (bf16[2,64,1536]{2,1,0:T(8,128)(2,1)}, bf16[2,64,1536]{2,1,0:T(8,128)(2,1)S(1)}, u32[]{:S(2)}) copy-start(bf16[2,64,1536]{2,1,0:T(8,128)(2,1)S(1)} %get-tuple-element.55) | copy-start | bytes 1179652
  160.2 14.8 %copy-start.5 = (bf16[2,128,1536]{2,1,0:T(8,128)(2,1)S(1)}, bf16[2,128,1536]{2,1,0:T(8,128)(2,1)}, u32[]{:S(2)}) copy-start(bf16[2,128,1536]{2,1,0:T(8,128)(2,1)} %copy-done.4) | copy-start | bytes 2359300
  164.5 10.2 %collective-permute-start.9 = (bf16[128,1536]{1,0:T(8,128)(2,1)S(1)}, bf16[128,1536]{1,0:T(8,128)(2,1)S(1)}, u32[]{:S(2)}, u32[]{:S(2)}) collective-permute-start(bf16[128,1536]{1,0:T(8,128)(2,1)S(1)} %fusion), channel_id=1, source_target_pairs={{1,0},{2,1},{3,2},{0,3},{5,4},{6,5},{7,6},{4,7},{9,8},{10,9},{11,1... | collective-permute-start | bytes 1179656 | tf_op jit(solution)/shard_map/ppermute | solution.py:459
  164.7 10.3 %collective-permute-start.8 = (bf16[128,1536]{1,0:T(8,128)(2,1)S(1)}, bf16[128,1536]{1,0:T(8,128)(2,1)S(1)}, u32[]{:S(2)}, u32[]{:S(2)}) collective-permute-start(bf16[128,1536]{1,0:T(8,128)(2,1)S(1)} %fusion.1), channel_id=1, source_target_pairs={{0,1},{1,2},{2,3},{3,0},{4,5},{5,6},{6,7},{7,4},{8,9},{9,10},{10,1... | collective-permute-start | bytes 1179656 | tf_op jit(solution)/shard_map/ppermute | solution.py:459
  176.4 9.5 %copy-start.17 = (bf16[2,64,1536]{2,1,0:T(8,128)(2,1)S(1)}, bf16[2,64,1536]{2,1,0:T(8,128)(2,1)}, u32[]{:S(2)}) copy-start(bf16[2,64,1536]{2,1,0:T(8,128)(2,1)} %copy-done.16) | copy-start | bytes 1179652
  176.4 9.6 %copy-start.15 = (bf16[2,64,1536]{2,1,0:T(8,128)(2,1)S(1)}, bf16[2,64,1536]{2,1,0:T(8,128)(2,1)}, u32[]{:S(2)}) copy-start(bf16[2,64,1536]{2,1,0:T(8,128)(2,1)} %copy-done.14) | copy-start | bytes 1179652
  176.5 12.3 %copy-start.13 = (bf16[2,64,1536]{2,1,0:T(8,128)(2,1)S(1)}, bf16[2,64,1536]{2,1,0:T(8,128)(2,1)}, u32[]{:S(2)}) copy-start(bf16[2,64,1536]{2,1,0:T(8,128)(2,1)} %copy-done.12) | copy-start | bytes 1179652
  176.5 29.7 %copy-start.9 = (bf16[2,64,1536]{2,1,0:T(8,128)(2,1)S(1)}, bf16[2,64,1536]{2,1,0:T(8,128)(2,1)}, u32[]{:S(2)}) copy-start(bf16[2,64,1536]{2,1,0:T(8,128)(2,1)} %copy-done.8) | copy-start | bytes 1179652
  176.5 29.7 %all-to-all-start.2 = ((bf16[32,8,1536]{2,1,0:T(8,128)(2,1)}), bf16[32,8,1536]{2,1,0:T(8,128)(2,1)S(1)}, u32[]{:S(2)}, u32[]{:S(2)}) async-start(bf16[32,8,1536]{2,1,0:T(8,128)(2,1)} %bitcast.10), calls=%async_computation.2 | async-start | bytes 1572864 | tf_op jit(solution)/shard_map/all_to_all | solution.py:445
  186.0 20.2 %collective-permute-start.10 = (bf16[2,64,1536]{2,1,0:T(8,128)(2,1)S(1)}, bf16[2,64,1536]{2,1,0:T(8,128)(2,1)S(1)}, u32[]{:S(2)}, u32[]{:S(2)}) collective-permute-start(bf16[2,64,1536]{2,1,0:T(8,128)(2,1)S(1)} %copy-done.17), channel_id=1, source_target_pairs={{0,1},{1,2},{2,3},{3,0},{4,5},{5,6},{6,7},{7,4},{8,9},{9,10},{10,1... | collective-permute-start | bytes 1179656 | tf_op jit(solution)/shard_map/ppermute | solution.py:462
  186.1 20.1 %collective-permute-start.11 = (bf16[2,64,1536]{2,1,0:T(8,128)(2,1)S(1)}, bf16[2,64,1536]{2,1,0:T(8,128)(2,1)S(1)}, u32[]{:S(2)}, u32[]{:S(2)}) collective-permute-start(bf16[2,64,1536]{2,1,0:T(8,128)(2,1)S(1)} %copy-done.15), channel_id=1, source_target_pairs={{1,0},{2,1},{3,2},{0,3},{5,4},{6,5},{7,6},{4,7},{9,8},{10,9},{11,1... | collective-permute-start | bytes 1179656 | tf_op jit(solution)/shard_map/ppermute | solution.py:463
  188.7 17.4 %collective-permute-start.12 = (bf16[2,64,1536]{2,1,0:T(8,128)(2,1)S(1)}, bf16[2,64,1536]{2,1,0:T(8,128)(2,1)S(1)}, u32[]{:S(2)}, u32[]{:S(2)}) collective-permute-start(bf16[2,64,1536]{2,1,0:T(8,128)(2,1)S(1)} %copy-done.13), channel_id=1, source_target_pairs={{0,2},{1,3},{2,0},{3,1},{4,6},{5,7},{6,4},{7,5},{8,10},{9,11},{10,... | collective-permute-start | bytes 1179656 | tf_op jit(solution)/shard_map/ppermute | solution.py:464
  206.2 9.5 %copy-start.22 = (f32[256]{0:T(256)S(1)}, f32[256]{0:T(256)}, u32[]{:S(2)}) copy-start(f32[256]{0:T(256)} %param.17) | copy-start | bytes 3076
  206.6 19.3 %copy-start.3 = (bf16[256,1536]{1,0:T(8,128)(2,1)S(1)}, bf16[256,1536]{1,0:T(8,128)(2,1)}, u32[]{:S(2)}) copy-start(bf16[256,1536]{1,0:T(8,128)(2,1)} %copy-done.2) | copy-start | bytes 2359300
  207.4 18.4 %all-to-all-start.3 = ((bf16[32,4,1536]{2,1,0:T(4,128)(2,1)}), bf16[32,4,1536]{2,1,0:T(4,128)(2,1)S(1)}, u32[]{:S(2)}, u32[]{:S(2)}) async-start(bf16[32,4,1536]{2,1,0:T(4,128)(2,1)} %reshape.34), calls=%async_computation.3 | async-start | bytes 786432 | tf_op jit(solution)/shard_map/all_to_all | solution.py:445

commit v6 on v5

--- a/solution.py
+++ b/solution.py
@@ -220,21 +220,19 @@
     expert_in = (mixed * scale * gain_ref[...]).astype(BF16)
     first = 0
     for out_ref in outs:
-        copies, count, _ = out_ref.shape
+        count = out_ref.shape[0]
         place = first + lax.broadcasted_iota(jnp.int32, (count, rows), 0)
         pick = jnp.where(place == place_ref[...], 1.0, 0.0).astype(BF16)
-        sent = jnp.dot(pick, expert_in, preferred_element_type=F32).astype(BF16)
-        for z in range(copies):
-            out_ref[z] = sent
+        out_ref[...] = jnp.dot(pick, expert_in, preferred_element_type=F32).astype(BF16)
         first += count
 
 
-def dispatch(normed, inner, low, high, taps, gain, place, counts, copies):
+def dispatch(normed, inner, low, high, taps, gain, place, counts):
     rows, width = normed.shape
     return call(
         dispatch_body,
         [jax.ShapeDtypeStruct((rows, width), BF16)]
-        + [jax.ShapeDtypeStruct((copies, count, width), BF16) for count in counts],
+        + [jax.ShapeDtypeStruct((count, width), BF16) for count in counts],
         (2 * sum(counts) * rows * width, 8 * rows * width),
         24,
         scratch_shapes=[pltpu.VMEM((2, 3 * EDGE, PAIR), F32)],
@@ -274,22 +272,23 @@
 
 def by_expert(n, axis):
     slots = n // DEVICES
-    shift = slots.bit_length() - 1
     row = lax.broadcasted_iota(jnp.int32, (2 * n, 2 * n), axis)
     e = jnp.where(row >= n, 1, 0)
     r = row - e * n
-    place = ((r >> shift) << (shift + 1)) + (e << shift) + (r & (slots - 1))
+    device = (r * (4096 // slots + 1)) >> 12
+    place = device * slots + e * slots + r
     return jnp.where(place == lax.broadcasted_iota(jnp.int32, (2 * n, 2 * n), 1 - axis), 1.0, 0.0).astype(BF16)
 
 
-def ffn_body(direct, me, arrived, w_in, w_out, *rest):
+def ffn_body(direct, own, left, right, *rest):
+    far, (w_in, w_out, *rest) = (rest[:1], rest[1:]) if direct else (rest[:2], rest[2:])
     if direct:
         keep, to_right, to_left, to_far, *scratch = rest
     else:
         keep, up, down, up2, down2, *scratch = rest
     rows_in, hidden, first, second, sems = scratch
-    n = arrived.shape[1] // 2
-    width = arrived.shape[2]
+    n = own.shape[0] // 2
+    width = own.shape[1]
     units = hidden.shape[1]
     step = STEP
     copies = {}
@@ -302,8 +301,9 @@
                 )
                 copies[e, which, t].start()
     order = by_expert(n, 0)
-    for k, off in enumerate((0, 3, 1, 2)):
-        block = jnp.dot(order, arrived[(me[0] + off) % 4], preferred_element_type=F32).astype(BF16)
+    for k, refs in enumerate(((own,), (left,), (right,), far)):
+        block = jnp.concatenate([ref[...] for ref in refs], axis=0)
+        block = jnp.dot(order, block, preferred_element_type=F32).astype(BF16)
         rows_in[0, k * n : (k + 1) * n] = block[:n]
         rows_in[1, k * n : (k + 1) * n] = block[n:]
     for e in range(2):
@@ -330,8 +330,9 @@
                 down[0, :, cols] = part[3 * n :]
 
 
-def ffn(direct, me, arrived, w_in, w_out):
-    n = arrived.shape[1] // 2
+def ffn(own, left, right, far, w_in, w_out):
+    direct = len(far) == 1
+    n = own.shape[0] // 2
     experts, width, units = w_in.shape
     pair = jax.ShapeDtypeStruct((2, n, width), BF16)
     single = jax.ShapeDtypeStruct((n, width), BF16)
@@ -341,8 +342,7 @@
         (experts * 4 * n * width * units * 4, 2 * experts * width * units * 2),
         42,
         in_specs=[
-            pl.BlockSpec(memory_space=pltpu.SMEM),
-            pl.BlockSpec(memory_space=pltpu.VMEM),
+            *[pl.BlockSpec(memory_space=pltpu.VMEM)] * (3 + len(far)),
             pl.BlockSpec(memory_space=pl.ANY),
             pl.BlockSpec(memory_space=pl.ANY),
         ],
@@ -353,7 +353,7 @@
             pltpu.VMEM((2, width // STEP, units, STEP), BF16),
             pltpu.SemaphoreType.DMA((2, 2, max(units, width) // STEP)),
         ],
-    )(me, arrived, w_in, w_out)
+    )(own, left, right, *far, w_in, w_out)
 
 
 def home_body(terms, *refs):
@@ -419,7 +419,7 @@
     local = w_in.shape[0]
     experts = local * time_count
     slots = max(2, 3 * frame_rows // (2 * experts))
-    early = 2 * slots // 3
+    early = slots // 2
     sizes = (early, slots - early)
     served = jnp.where(overflow == 1, secondary, primary)
     place = jnp.where(
@@ -428,7 +428,7 @@
         experts * early + served * (slots - early) + slot - early,
     )
     mixed, *chunks = dispatch(
-        normed, inner, before, after, conv_kernel, ffn_gain, place, [experts * c for c in sizes], group_count
+        normed, inner, before, after, conv_kernel, ffn_gain, place, [experts * c for c in sizes]
     )
 
     up = [(i, (i + 1) % group_count) for i in range(group_count)]
@@ -436,9 +436,12 @@
     add = lambda *vs: sum(v.astype(F32) for v in vs).astype(BF16)
 
     def arrive(chunk, size):
-        sent = chunk.reshape(devices, local * size, width)
-        got = lax.all_to_all(sent, ("expert", "tm"), split_axis=0, concat_axis=0, tiled=True)
-        return got.reshape(group_count, experts * size, width)
+        sent = chunk.reshape(time_count, local * size, width)
+        got = lax.all_to_all(sent, "tm", split_axis=0, concat_axis=0, tiled=True)
+        return got.reshape(experts * size, width)
+
+    def near(own):
+        return lax.ppermute(own, "expert", up), lax.ppermute(own, "expert", down)
 
     def leave(summed, size):
         summed = summed.reshape(time_count, local * size, width)
@@ -446,14 +449,19 @@
         return got.reshape(experts * size, width)
 
     after = lambda values, *others: lax.optimization_barrier((tuple(values), others))[0]
-    me = lax.axis_index("expert").astype(jnp.int32)[None]
     across = [(i, (i + 2) % group_count) for i in range(group_count)]
-    rows_a = arrive(chunks[0], sizes[0])
-    rows_b = arrive(*after((chunks[1],), rows_a), sizes[1])
-    keep_a, go_up_a, go_down_a, up2_a, down2_a = ffn(False, me, rows_a, w_in, w_out)
+    own_a = arrive(chunks[0], sizes[0])
+    left_a, right_a = near(own_a)
+    own_b = arrive(*after((chunks[1],), own_a), sizes[1])
+    left_a, right_a = after((left_a, right_a), own_b)
+    half = own_a.shape[0] // 2
+    far_a = lax.ppermute(left_a[:half], "expert", up), lax.ppermute(right_a[half:], "expert", down)
+    left_b, right_b = near(own_b)
+    far_b = lax.ppermute(own_b, "expert", across)
+    keep_a, go_up_a, go_down_a, up2_a, down2_a = ffn(own_a, left_a, right_a, far_a, w_in, w_out)
     below_a, above_a = lax.ppermute(go_up_a, "expert", up), lax.ppermute(go_down_a, "expert", down)
-    (rows_b,) = after((rows_b,), keep_a)
-    keep_b, to_right, to_left, to_far = ffn(True, me, rows_b, w_in, w_out)
+    (own_b,) = after((own_b,), keep_a)
+    keep_b, to_right, to_left, to_far = ffn(own_b, left_b, right_b, (far_b,), w_in, w_out)
     below_a, above_a = after((below_a, above_a), keep_b)
     up2_a, down2_a = add(up2_a, below_a[0]), add(down2_a, above_a[0])
     up3_a, down3_a = lax.ppermute(up2_a, "expert", up), lax.ppermute(down2_a, "expert", down)

time: 230 us -> 228 us (level)
  blocking collectives: 50.1 us -> 61.1 us
  waiting for transfers between devices: 64.9 us -> 54.3 us
  starting transfers between devices: 53.9 us -> 47.8 us
    ppermute x1, waiting for transfers between devices: 17.4 us -> 0.01 us  [on_device(): lax.ppermute(to_right, 'expert', up)]
    ppermute x0 -> x7, waiting for transfers between devices: none -> 14 us  [the longest x4 9.5 us: near(): return (lax.ppermute(own, 'expert', up), lax.ppermute(own, 'expert', down))]
    all_to_all x1 -> x3, blocking collectives: 50.1 us -> 61.1 us  [the longest x2 40.4 us: arrive(): got = lax.all_to_all(sent, 'tm', split_axis=0, concat_axis=0, tiled=True)]
    all_to_all x2 -> x1, starting transfers between devices: 17.5 us -> 7.88 us  [leave(): got = lax.all_to_all(summed, 'tm', split_axis=0, concat_axis=0, tiled=True)]
    ppermute x0 -> x7, starting transfers between devices: none -> 8.25 us  [the longest x4 5.41 us: near(): return (lax.ppermute(own, 'expert', up), lax.ppermute(own, 'expert', down))]
    all_to_all x1 -> x0, starting transfers between devices: 5.27 us -> none  [arrive(): lax.all_to_all(sent, ('expert', 'tm'), split_axis=0, concat_axis=0, tiled...]
    all_to_all x1 -> x0, waiting for transfers between devices: 4.52 us -> none  [arrive(): lax.all_to_all(sent, ('expert', 'tm'), split_axis=0, concat_axis=0, tiled...]
    ppermute x1, waiting for transfers between devices: 4.11 us -> 0.01 us  [on_device(): lax.ppermute(go_up_a, 'expert', up)]
  transfers between devices with their start and end apart: 16 -> 21, of which waited for: 8 -> 7; matrix products, arithmetic and copies ran while one was open for 2% -> 4% of each run, Pallas kernels for 15% -> 16%
where the time goes in v6:
time: 228 us; the launch traced here: 227 us
  blocking collectives  61.1 us (27%)
  waiting for transfers between devices  54.3 us (24%)
  starting transfers between devices  47.8 us (21%)
  Pallas kernels  47.6 us (21%)
  local copies, waits for them, and re-layouts  14.3 us (6%)
    all_to_all x2, blocking collectives, arrive(): got = lax.all_to_all(sent, 'tm', split_axis=0, concat_axis=0, tiled=True)  40.4 us
    pallas_call x2, Pallas kernels, ffn(): call(functools.partial(ffn_body, direct), [pair] * 4 if direct else [pair...  24.6 us
    all_to_all x1, blocking collectives, leave(): got = lax.all_to_all(summed, 'tm', split_axis=0, concat_axis=0, tiled=True)  20.8 us
    all_to_all x1, waiting for transfers between devices, leave(): got = lax.all_to_all(summed, 'tm', split_axis=0, concat_axis=0, tiled=True)  14 us
    ppermute x2, waiting for transfers between devices, on_device(): high.append(lax.ppermute(part, order, back))  11.4 us
    ppermute x4, waiting for transfers between devices, near(): return (lax.ppermute(own, 'expert', up), lax.ppermute(own, 'expert', down))  9.5 us
    ppermute x2, starting transfers between devices, on_device(): high.append(lax.ppermute(part, order, back))  9.46 us
    pallas_call x1, Pallas kernels, attention(): call(attend_body, jax.ShapeDtypeStruct((rows, pairs * PAIR), F32), cost,...  8.08 us
  transfers between devices with their start and end apart: 21, of which 7 were waited for; matrix products, arithmetic and copies ran while one was open for 4% of the time, Pallas kernels for 16%

profile of v6, /device:TPU:1, one launch (start us, length us, event | category | flops | bytes accessed | tf_op | source)
XLA Modules:
  0.0 227.0 jit_solution(16011803678573042290)
XLA Ops:
  0.0 2.4 %slice.18 = bf16[2,256,1024]{2,1,0:T(8,128)(2,1)} slice(bf16[2,256,1536]{2,1,0:T(8,128)(2,1)} %kv_ref.3), slice={[0:2], [0:256], [0:1024]} | slice | bytes 2097152 | tf_op jit(solution)/shard_map/slice | solution.py:408
  2.4 4.4 %collective-permute-start.2 = (bf16[2,256,1024]{2,1,0:T(8,128)(2,1)}, bf16[2,256,1024]{2,1,0:T(8,128)(2,1)}, u32[]{:S(2)}, u32[]{:S(2)}) collective-permute-start(bf16[2,256,1024]{2,1,0:T(8,128)(2,1)} %slice.18), channel_id=1, source_target_pairs={{0,1},{1,2},{2,3},{3,4},{4,5},{5,6},{6,7},{7,8},{8,9},{9,10},{10,1... | collective-permute-start | bytes 3145736 | tf_op jit(solution)/shard_map/ppermute | solution.py:409
  6.8 4.6 %collective-permute-start.3 = (bf16[2,256,1024]{2,1,0:T(8,128)(2,1)}, bf16[2,256,1024]{2,1,0:T(8,128)(2,1)}, u32[]{:S(2)}, u32[]{:S(2)}) collective-permute-start(bf16[2,256,1024]{2,1,0:T(8,128)(2,1)} %slice.18), channel_id=1, source_target_pairs={{1,0},{2,1},{3,2},{4,3},{5,4},{6,5},{7,6},{8,7},{9,8},{10,9},{11,1... | collective-permute-start | bytes 3145736 | tf_op jit(solution)/shard_map/ppermute | solution.py:410
  11.4 1.1 slice.19
  12.5 1.9 collective-permute-start
  14.4 4.9 %collective-permute-start.1 = (bf16[2,256,512]{2,1,0:T(8,128)(2,1)S(1)}, bf16[2,256,512]{2,1,0:T(8,128)(2,1)}, u32[]{:S(2)}, u32[]{:S(2)}) collective-permute-start(bf16[2,256,512]{2,1,0:T(8,128)(2,1)S(1)} %slice.19), channel_id=1, source_target_pairs={{1,0},{2,1},{3,2},{4,3},{5,4},{6,5},{7,6},{8,7},{9,8},{10,9},{11,1... | collective-permute-start | bytes 1572872 | tf_op jit(solution)/shard_map/ppermute | solution.py:410
  19.3 0.6 add_convert_fusion.edge_ref
  20.0 0.7 broadcast_in_dim.15.gain_ref
  20.7 0.7 broadcast_in_dim.16.gain_ref
  21.4 0.7 compare_select_fusion.1
  22.1 6.8 %collective-permute-done.2.lo_ref = bf16[2,256,1024]{2,1,0:T(8,128)(2,1)} collective-permute-done((bf16[2,256,1024]{2,1,0:T(8,128)(2,1)}, bf16[2,256,1024]{2,1,0:T(8,128)(2,1)}, u32[]{:S(2)}, u32[]{:S(2)}) %collective-permute-start.2) | collective-permute-done | bytes 1048608 | tf_op jit(solution)/shard_map/ppermute | solution.py:409
  28.9 11.4 %collective-permute-done.3.hi_ref = bf16[2,256,1024]{2,1,0:T(8,128)(2,1)} collective-permute-done((bf16[2,256,1024]{2,1,0:T(8,128)(2,1)}, bf16[2,256,1024]{2,1,0:T(8,128)(2,1)}, u32[]{:S(2)}, u32[]{:S(2)}) %collective-permute-start.3) | collective-permute-done | bytes 1048608 | tf_op jit(solution)/shard_map/ppermute | solution.py:410
  40.3 8.1 %shard_map.118.rest_0_ = f32[256,1024]{1,0:T(8,128)} custom-call(s32[2]{0:T(128)} %add_convert_fusion.edge_ref, bf16[256,1536]{1,0:T(8,128)(2,1)} %q_ref.3, bf16[2,256,1536]{2,1,0:T(8,128)(2,1)} %kv_ref.3, bf16[2,256,1024]{2,1,0:T(8,128)(2,1)} %collective-permute-done.2.lo_ref, bf16[2,256,1024]{2,1,0:T(8,128)(2,1)} %collective-permute-done.3.hi_ref), custom_call_target="tpu_custom_call" | custom-call | flops 2684354560 | bytes 3670016 | tf_op jit(solution)/shard_map/pallas_call | solution.py:138
  48.4 1.2 copy-done.6
  49.7 4.5 %shard_map.119 = (bf16[256,1536]{1,0:T(8,128)(2,1)S(1)}, bf16[16,1536]{1,0:T(8,128)(2,1)S(1)}, bf16[16,1536]{1,0:T(8,128)(2,1)S(1)}) custom-call(s32[2]{0:T(128)S(1)} %copy-done.5, bf16[256,1536]{1,0:T(8,128)(2,1)S(1)} %copy-done.4, bf16[2,256,1536]{2,1,0:T(8,128)(2,1)S(1)} %copy-done, bf16[2,256,512]{2,1,0:T(8,128)(2,1)} %collective-permute-done.lo_ref, ...), custom_call_target="tpu_custom_call" | custom-call | flops 1342177280 | bytes 1835008 | tf_op jit(solution)/shard_map/pallas_call | solution.py:151
  54.1 1.9 collective-permute-start.4
  56.1 5.6 %collective-permute-start.5 = (bf16[16,1536]{1,0:T(8,128)(2,1)S(1)}, bf16[16,1536]{1,0:T(8,128)(2,1)S(1)}, u32[]{:S(2)}, u32[]{:S(2)}) collective-permute-start(bf16[16,1536]{1,0:T(8,128)(2,1)S(1)} %get-tuple-element.40), channel_id=1, source_target_pairs={{1,0},{2,1},{3,2},{4,3},{5,4},{6,5},{7,6},{8,7},{9,8},{10,9},{11,1... | collective-permute-start | bytes 147464 | tf_op jit(solution)/shard_map/ppermute | solution.py:416
  61.7 3.6 %shard_map.120.inner_ref = bf16[224,1536]{1,0:T(8,128)(2,1)S(1)} custom-call(bf16[256,1536]{1,0:T(8,128)(2,1)S(1)} %get-tuple-element.38.normed_ref, f32[31,1536]{1,0:T(8,128)S(1)} %copy-done.1), custom_call_target="tpu_custom_call" | custom-call | flops 1365245952 | bytes 1572864 | tf_op jit(solution)/shard_map/pallas_call | solution.py:190
  65.3 1.4 shard_map.121
  66.7 0.2 reshape.28
  66.9 21.3 %all_to_all.20 = bf16[32,6,1536]{2,1,0:T(8,128)(2,1)} all-to-all(bf16[32,6,1536]{2,1,0:T(8,128)(2,1)S(1)} %reshape.28), channel_id=1, replica_groups=mesh['tm'=32,'expert'=4] {'tm'}, dimensions={0} | all-to-all | bytes 1179648 | tf_op jit(solution)/shard_map/all_to_all | solution.py:440
  88.3 1.3 reshape.29.own
  89.6 0.1 collective-permute-start.6
  89.7 2.7 %collective-permute-start.7 = (bf16[192,1536]{1,0:T(8,128)(2,1)S(1)}, bf16[192,1536]{1,0:T(8,128)(2,1)S(1)}, u32[]{:S(2)}, u32[]{:S(2)}) collective-permute-start(bf16[192,1536]{1,0:T(8,128)(2,1)S(1)} %reshape.29.own), channel_id=1, source_target_pairs={{1,0},{2,1},{3,2},{0,3},{5,4},{6,5},{7,6},{4,7},{9,8},{10,9},{11,1... | collective-permute-start | bytes 1769480 | tf_op jit(solution)/shard_map/ppermute | solution.py:444
  92.4 1.1 reshape.30
  93.4 19.0 %all_to_all.21 = bf16[32,6,1536]{2,1,0:T(8,128)(2,1)} all-to-all(bf16[32,6,1536]{2,1,0:T(8,128)(2,1)} %reshape.30), channel_id=1, replica_groups=mesh['tm'=32,'expert'=4] {'tm'}, dimensions={0} | all-to-all | bytes 1179648 | tf_op jit(solution)/shard_map/all_to_all | solution.py:440
  112.5 1.3 reshape.31.own
  113.8 0.0 collective-permute-done.6.left
  113.8 0.0 copy-start.2
  113.9 0.1 collective-permute-start.8
  114.0 2.8 %collective-permute-start.9 = (bf16[96,1536]{1,0:T(8,128)(2,1)S(1)}, bf16[96,1536]{1,0:T(8,128)(2,1)S(1)}, u32[]{:S(2)}, u32[]{:S(2)}) collective-permute-start(bf16[96,1536]{1,0:T(8,128)(2,1)S(1)} %slice.21), channel_id=1, source_target_pairs={{1,0},{2,1},{3,2},{0,3},{5,4},{6,5},{7,6},{4,7},{9,8},{10,9},{11,1... | collective-permute-start | bytes 884744 | tf_op jit(solution)/shard_map/ppermute | solution.py:458
  116.7 0.0 collective-permute-start.12
  116.7 2.7 %collective-permute-start.13 = (bf16[192,1536]{1,0:T(8,128)(2,1)S(1)}, bf16[192,1536]{1,0:T(8,128)(2,1)S(1)}, u32[]{:S(2)}, u32[]{:S(2)}) collective-permute-start(bf16[192,1536]{1,0:T(8,128)(2,1)S(1)} %reshape.31.own), channel_id=1, source_target_pairs={{1,0},{2,1},{3,2},{0,3},{5,4},{6,5},{7,6},{4,7},{9,8},{10,9},{11,1... | collective-permute-start | bytes 1769480 | tf_op jit(solution)/shard_map/ppermute | solution.py:444
  119.4 0.0 collective-permute-start.14
  119.4 4.5 %collective-permute-done.8.rest_0_ = bf16[96,1536]{1,0:T(8,128)(2,1)S(1)} collective-permute-done((bf16[96,1536]{1,0:T(8,128)(2,1)S(1)}, bf16[96,1536]{1,0:T(8,128)(2,1)S(1)}, u32[]{:S(2)}, u32[]{:S(2)}) %collective-permute-start.8) | collective-permute-done | bytes 294944 | tf_op jit(solution)/shard_map/ppermute | solution.py:458
  123.9 1.1 copy-done.3
  125.0 11.7 %shard_map.122 = (bf16[2,96,1536]{2,1,0:T(8,128)(2,1)S(1)}, bf16[2,96,1536]{2,1,0:T(8,128)(2,1)S(1)}, bf16[2,96,1536]{2,1,0:T(8,128)(2,1)S(1)}, bf16[96,1536]{1,0:T(8,128)(2,1)S(1)}, bf16[96,1536]{1,0:T(8,128)(2,1)S(1)}) custom-call(bf16[192,1536]{1,0:T(8,128)(2,1)S(1)} %reshape.29.own, bf16[192,1536]{1,0:T(8,128)(2,1)S(1)} %collective-permute-done.6.left, ...), custom_call_target="tpu_custom_call" | custom-call | flops 7247757312 | bytes 18874368 | tf_op jit(solution)/shard_map/pallas_call | solution.py:339
  136.7 0.1 collective-permute-start.10
  136.8 2.9 %collective-permute-start.11 = (bf16[2,96,1536]{2,1,0:T(8,128)(2,1)S(1)}, bf16[2,96,1536]{2,1,0:T(8,128)(2,1)S(1)}, u32[]{:S(2)}, u32[]{:S(2)}) collective-permute-start(bf16[2,96,1536]{2,1,0:T(8,128)(2,1)S(1)} %get-tuple-element.49), channel_id=1, source_target_pairs={{1,0},{2,1},{3,2},{0,3},{5,4},{6,5},{7,6},{4,7},{9,8},{10,9},{11,1... | collective-permute-start | bytes 1769480 | tf_op jit(solution)/shard_map/ppermute | solution.py:462
  139.7 9.5 %collective-permute-done.12.left = bf16[192,1536]{1,0:T(8,128)(2,1)S(1)} collective-permute-done((bf16[192,1536]{1,0:T(8,128)(2,1)S(1)}, bf16[192,1536]{1,0:T(8,128)(2,1)S(1)}, u32[]{:S(2)}, u32[]{:S(2)}) %collective-permute-start.12) | collective-permute-done | bytes 589856 | tf_op jit(solution)/shard_map/ppermute | solution.py:444
  149.2 0.0 collective-permute-done.13.right
  149.2 0.0 collective-permute-done.14.rest_0_
  149.2 12.9 %shard_map.123 = (bf16[2,96,1536]{2,1,0:T(8,128)(2,1)S(1)}, bf16[2,96,1536]{2,1,0:T(8,128)(2,1)}, bf16[2,96,1536]{2,1,0:T(8,128)(2,1)}, bf16[2,96,1536]{2,1,0:T(8,128)(2,1)}) custom-call(bf16[192,1536]{1,0:T(8,128)(2,1)S(1)} %reshape.31.own, bf16[192,1536]{1,0:T(8,128)(2,1)S(1)} %collective-permute-done.12.left, ...), custom_call_target="tpu_custom_call" | custom-call | flops 7247757312 | bytes 18874368 | tf_op jit(solution)/shard_map/pallas_call | solution.py:339
  162.1 0.0 copy-start.7
  162.1 0.1 fusion
  162.2 2.7 %collective-permute-start.16 = (bf16[96,1536]{1,0:T(8,128)(2,1)S(1)}, bf16[96,1536]{1,0:T(8,128)(2,1)S(1)}, u32[]{:S(2)}, u32[]{:S(2)}) collective-permute-start(bf16[96,1536]{1,0:T(8,128)(2,1)S(1)} %fusion), channel_id=1, source_target_pairs={{1,0},{2,1},{3,2},{0,3},{5,4},{6,5},{7,6},{4,7},{9,8},{10,9},{11,1... | collective-permute-start | bytes 884744 | tf_op jit(solution)/shard_map/ppermute | solution.py:467
  164.9 0.1 fusion.1
  164.9 0.1 collective-permute-start.15
  165.0 4.8 %collective-permute-done.16.refs_4_ = bf16[96,1536]{1,0:T(8,128)(2,1)S(1)} collective-permute-done((bf16[96,1536]{1,0:T(8,128)(2,1)S(1)}, bf16[96,1536]{1,0:T(8,128)(2,1)S(1)}, u32[]{:S(2)}, u32[]{:S(2)}) %collective-permute-start.16) | collective-permute-done | bytes 294944 | tf_op jit(solution)/shard_map/ppermute | solution.py:467
  169.8 3.3 %collective-permute-done.15.refs_3_ = bf16[96,1536]{1,0:T(8,128)(2,1)S(1)} collective-permute-done((bf16[96,1536]{1,0:T(8,128)(2,1)S(1)}, bf16[96,1536]{1,0:T(8,128)(2,1)S(1)}, u32[]{:S(2)}, u32[]{:S(2)}) %collective-permute-start.15) | collective-permute-done | bytes 294944 | tf_op jit(solution)/shard_map/ppermute | solution.py:467
  173.1 0.0 collective-permute-start.17
  173.1 2.7 %collective-permute-start.18 = (bf16[2,96,1536]{2,1,0:T(8,128)(2,1)}, bf16[2,96,1536]{2,1,0:T(8,128)(2,1)}, u32[]{:S(2)}, u32[]{:S(2)}) collective-permute-start(bf16[2,96,1536]{2,1,0:T(8,128)(2,1)} %get-tuple-element.60), channel_id=1, source_target_pairs={{1,0},{2,1},{3,2},{0,3},{5,4},{6,5},{7,6},{4,7},{9,8},{10,9},{11,1... | collective-permute-start | bytes 1769480 | tf_op jit(solution)/shard_map/ppermute | solution.py:471
  175.7 0.4 shard_map.124
  176.2 0.2 reshape.32
  176.4 20.8 %all_to_all.22 = bf16[32,6,1536]{2,1,0:T(8,128)(2,1)} all-to-all(bf16[32,6,1536]{2,1,0:T(8,128)(2,1)S(1)} %reshape.32), channel_id=1, replica_groups=mesh['tm'=32,'expert'=4] {'tm'}, dimensions={0} | all-to-all | bytes 1179648 | tf_op jit(solution)/shard_map/all_to_all | solution.py:448
  197.2 1.3 reshape.33.rest_0_
  198.6 1.8 shard_map.125
  200.3 1.1 reshape.34
  201.4 7.9 %all-to-all-start.3 = ((bf16[32,6,1536]{2,1,0:T(8,128)(2,1)}), bf16[32,6,1536]{2,1,0:T(8,128)(2,1)S(1)}, u32[]{:S(2)}, u32[]{:S(2)}) async-start(bf16[32,6,1536]{2,1,0:T(8,128)(2,1)} %reshape.34), calls=%async_computation.3 | async-start | bytes 1572864 | tf_op jit(solution)/shard_map/all_to_all | solution.py:448
  209.3 0.1 copy.14.place_ref
  209.5 0.1 copy.13.gate_ref
  209.6 14.0 %all-to-all-done.3 = bf16[32,6,1536]{2,1,0:T(8,128)(2,1)S(1)} async-done(((bf16[32,6,1536]{2,1,0:T(8,128)(2,1)}), bf16[32,6,1536]{2,1,0:T(8,128)(2,1)S(1)}, u32[]{:S(2)}, u32[]{:S(2)}) %all-to-all-start.3) | async-done | bytes 589856 | tf_op jit(solution)/shard_map/all_to_all | solution.py:448
  223.6 0.2 reshape.35.rest_1_
  223.8 3.2 %shard_map.126 = bf16[256,1536]{1,0:T(8,128)(2,1)} custom-call(bf16[256,1536]{1,0:T(8,128)(2,1)S(1)} %get-tuple-element.41.mixed_ref, f32[256,1]{1,0:T(8,128)S(1)} %copy.13.gate_ref, s32[256,1]{1,0:T(8,128)S(1)} %copy.14.place_ref, bf16[192,1536]{1,0:T(8,128)(2,1)S(1)} %reshape.33.rest_0_, bf16[192,1536]{1,0:T(8,128)(2,1)S(1)} %reshape.35.rest_1_), custom_call_target="tpu_custom_call" | custom-call | flops 301989888 | bytes 3145728 | tf_op jit(solution)/shard_map/pallas_call | solution.py:262
  (26 shorter events, 0.1 us)
Async XLA Ops:
  0.0 48.4 %copy-start = (bf16[2,256,1536]{2,1,0:T(8,128)(2,1)S(1)}, bf16[2,256,1536]{2,1,0:T(8,128)(2,1)}, u32[]{:S(2)}) copy-start(bf16[2,256,1536]{2,1,0:T(8,128)(2,1)} %kv_ref.3) | copy-start | bytes 4718596
  0.0 48.4 %copy-start.4 = (bf16[256,1536]{1,0:T(8,128)(2,1)S(1)}, bf16[256,1536]{1,0:T(8,128)(2,1)}, u32[]{:S(2)}) copy-start(bf16[256,1536]{1,0:T(8,128)(2,1)} %q_ref.3) | copy-start | bytes 2359300
  0.0 61.7 %copy-start.1 = (f32[31,1536]{1,0:T(8,128)S(1)}, f32[31,1536]{1,0:T(8,128)}, u32[]{:S(2)}) copy-start(f32[31,1536]{1,0:T(8,128)} %taps_ref.3) | copy-start | bytes 571396
  2.4 26.5 %collective-permute-start.2 = (bf16[2,256,1024]{2,1,0:T(8,128)(2,1)}, bf16[2,256,1024]{2,1,0:T(8,128)(2,1)}, u32[]{:S(2)}, u32[]{:S(2)}) collective-permute-start(bf16[2,256,1024]{2,1,0:T(8,128)(2,1)} %slice.18), channel_id=1, source_target_pairs={{0,1},{1,2},{2,3},{3,4},{4,5},{5,6},{6,7},{7,8},{8,9},{9,10},{10,1... | collective-permute-start | bytes 3145736 | tf_op jit(solution)/shard_map/ppermute | solution.py:409
  6.8 33.5 %collective-permute-start.3 = (bf16[2,256,1024]{2,1,0:T(8,128)(2,1)}, bf16[2,256,1024]{2,1,0:T(8,128)(2,1)}, u32[]{:S(2)}, u32[]{:S(2)}) collective-permute-start(bf16[2,256,1024]{2,1,0:T(8,128)(2,1)} %slice.18), channel_id=1, source_target_pairs={{1,0},{2,1},{3,2},{4,3},{5,4},{6,5},{7,6},{8,7},{9,8},{10,9},{11,1... | collective-permute-start | bytes 3145736 | tf_op jit(solution)/shard_map/ppermute | solution.py:410
  12.5 35.9 %collective-permute-start = (bf16[2,256,512]{2,1,0:T(8,128)(2,1)S(1)}, bf16[2,256,512]{2,1,0:T(8,128)(2,1)}, u32[]{:S(2)}, u32[]{:S(2)}) collective-permute-start(bf16[2,256,512]{2,1,0:T(8,128)(2,1)S(1)} %slice.19), channel_id=1, source_target_pairs={{0,1},{1,2},{2,3},{3,4},{4,5},{5,6},{6,7},{7,8},{8,9},{9,10},{10,1... | collective-permute-start | bytes 1572872 | tf_op jit(solution)/shard_map/ppermute | solution.py:409
  14.4 34.0 %collective-permute-start.1 = (bf16[2,256,512]{2,1,0:T(8,128)(2,1)S(1)}, bf16[2,256,512]{2,1,0:T(8,128)(2,1)}, u32[]{:S(2)}, u32[]{:S(2)}) collective-permute-start(bf16[2,256,512]{2,1,0:T(8,128)(2,1)S(1)} %slice.19), channel_id=1, source_target_pairs={{1,0},{2,1},{3,2},{4,3},{5,4},{6,5},{7,6},{8,7},{9,8},{10,9},{11,1... | collective-permute-start | bytes 1572872 | tf_op jit(solution)/shard_map/ppermute | solution.py:410
  20.0 28.5 %copy-start.5 = (s32[2]{0:T(128)S(1)}, s32[2]{0:T(128)}, u32[]{:S(2)}) copy-start(s32[2]{0:T(128)} %add_convert_fusion.edge_ref) | copy-start | bytes 28
  48.4 1.2 copy-start.6
  54.1 11.1 %collective-permute-start.4 = (bf16[16,1536]{1,0:T(8,128)(2,1)S(1)}, bf16[16,1536]{1,0:T(8,128)(2,1)S(1)}, u32[]{:S(2)}, u32[]{:S(2)}) collective-permute-start(bf16[16,1536]{1,0:T(8,128)(2,1)S(1)} %get-tuple-element.39), channel_id=1, source_target_pairs={{0,1},{1,2},{2,3},{3,4},{4,5},{5,6},{6,7},{7,8},{8,9},{9,10},{10,1... | collective-permute-start | bytes 147464 | tf_op jit(solution)/shard_map/ppermute | solution.py:415
  56.1 9.2 %collective-permute-start.5 = (bf16[16,1536]{1,0:T(8,128)(2,1)S(1)}, bf16[16,1536]{1,0:T(8,128)(2,1)S(1)}, u32[]{:S(2)}, u32[]{:S(2)}) collective-permute-start(bf16[16,1536]{1,0:T(8,128)(2,1)S(1)} %get-tuple-element.40), channel_id=1, source_target_pairs={{1,0},{2,1},{3,2},{4,3},{5,4},{6,5},{7,6},{8,7},{9,8},{10,9},{11,1... | collective-permute-start | bytes 147464 | tf_op jit(solution)/shard_map/ppermute | solution.py:416
  89.6 24.2 %collective-permute-start.6 = (bf16[192,1536]{1,0:T(8,128)(2,1)S(1)}, bf16[192,1536]{1,0:T(8,128)(2,1)S(1)}, u32[]{:S(2)}, u32[]{:S(2)}) collective-permute-start(bf16[192,1536]{1,0:T(8,128)(2,1)S(1)} %reshape.29.own), channel_id=1, source_target_pairs={{0,1},{1,2},{2,3},{3,0},{4,5},{5,6},{6,7},{7,4},{8,9},{9,10},{10,1... | collective-permute-start | bytes 1769480 | tf_op jit(solution)/shard_map/ppermute | solution.py:444
  89.7 24.1 %collective-permute-start.7 = (bf16[192,1536]{1,0:T(8,128)(2,1)S(1)}, bf16[192,1536]{1,0:T(8,128)(2,1)S(1)}, u32[]{:S(2)}, u32[]{:S(2)}) collective-permute-start(bf16[192,1536]{1,0:T(8,128)(2,1)S(1)} %reshape.29.own), channel_id=1, source_target_pairs={{1,0},{2,1},{3,2},{0,3},{5,4},{6,5},{7,6},{4,7},{9,8},{10,9},{11,1... | collective-permute-start | bytes 1769480 | tf_op jit(solution)/shard_map/ppermute | solution.py:444
  113.8 10.1 %copy-start.2 = (bf16[192,1536]{1,0:T(8,128)(2,1)}, bf16[192,1536]{1,0:T(8,128)(2,1)S(1)}, u32[]{:S(2)}) copy-start(bf16[192,1536]{1,0:T(8,128)(2,1)S(1)} %collective-permute-done.7.right) | copy-start | bytes 1769476
  113.9 10.0 %collective-permute-start.8 = (bf16[96,1536]{1,0:T(8,128)(2,1)S(1)}, bf16[96,1536]{1,0:T(8,128)(2,1)S(1)}, u32[]{:S(2)}, u32[]{:S(2)}) collective-permute-start(bf16[96,1536]{1,0:T(8,128)(2,1)S(1)} %slice.20), channel_id=1, source_target_pairs={{0,1},{1,2},{2,3},{3,0},{4,5},{5,6},{6,7},{7,4},{8,9},{9,10},{10,1... | collective-permute-start | bytes 884744 | tf_op jit(solution)/shard_map/ppermute | solution.py:458
  114.0 9.9 %collective-permute-start.9 = (bf16[96,1536]{1,0:T(8,128)(2,1)S(1)}, bf16[96,1536]{1,0:T(8,128)(2,1)S(1)}, u32[]{:S(2)}, u32[]{:S(2)}) collective-permute-start(bf16[96,1536]{1,0:T(8,128)(2,1)S(1)} %slice.21), channel_id=1, source_target_pairs={{1,0},{2,1},{3,2},{0,3},{5,4},{6,5},{7,6},{4,7},{9,8},{10,9},{11,1... | collective-permute-start | bytes 884744 | tf_op jit(solution)/shard_map/ppermute | solution.py:458
  116.7 32.4 %collective-permute-start.12 = (bf16[192,1536]{1,0:T(8,128)(2,1)S(1)}, bf16[192,1536]{1,0:T(8,128)(2,1)S(1)}, u32[]{:S(2)}, u32[]{:S(2)}) collective-permute-start(bf16[192,1536]{1,0:T(8,128)(2,1)S(1)} %reshape.31.own), channel_id=1, source_target_pairs={{0,1},{1,2},{2,3},{3,0},{4,5},{5,6},{6,7},{7,4},{8,9},{9,10},{10,1... | collective-permute-start | bytes 1769480 | tf_op jit(solution)/shard_map/ppermute | solution.py:444
  116.7 32.4 %collective-permute-start.13 = (bf16[192,1536]{1,0:T(8,128)(2,1)S(1)}, bf16[192,1536]{1,0:T(8,128)(2,1)S(1)}, u32[]{:S(2)}, u32[]{:S(2)}) collective-permute-start(bf16[192,1536]{1,0:T(8,128)(2,1)S(1)} %reshape.31.own), channel_id=1, source_target_pairs={{1,0},{2,1},{3,2},{0,3},{5,4},{6,5},{7,6},{4,7},{9,8},{10,9},{11,1... | collective-permute-start | bytes 1769480 | tf_op jit(solution)/shard_map/ppermute | solution.py:444
  119.4 29.7 %collective-permute-start.14 = (bf16[192,1536]{1,0:T(8,128)(2,1)S(1)}, bf16[192,1536]{1,0:T(8,128)(2,1)S(1)}, u32[]{:S(2)}, u32[]{:S(2)}) collective-permute-start(bf16[192,1536]{1,0:T(8,128)(2,1)S(1)} %reshape.31.own), channel_id=1, source_target_pairs={{0,2},{1,3},{2,0},{3,1},{4,6},{5,7},{6,4},{7,5},{8,10},{9,11},{10,... | collective-permute-start | bytes 1769480 | tf_op jit(solution)/shard_map/ppermute | solution.py:460
  123.9 1.1 copy-start.3
  136.7 25.4 %collective-permute-start.10 = (bf16[2,96,1536]{2,1,0:T(8,128)(2,1)S(1)}, bf16[2,96,1536]{2,1,0:T(8,128)(2,1)S(1)}, u32[]{:S(2)}, u32[]{:S(2)}) collective-permute-start(bf16[2,96,1536]{2,1,0:T(8,128)(2,1)S(1)} %get-tuple-element.48), channel_id=1, source_target_pairs={{0,1},{1,2},{2,3},{3,0},{4,5},{5,6},{6,7},{7,4},{8,9},{9,10},{10,1... | collective-permute-start | bytes 1769480 | tf_op jit(solution)/shard_map/ppermute | solution.py:462
  136.8 25.3 %collective-permute-start.11 = (bf16[2,96,1536]{2,1,0:T(8,128)(2,1)S(1)}, bf16[2,96,1536]{2,1,0:T(8,128)(2,1)S(1)}, u32[]{:S(2)}, u32[]{:S(2)}) collective-permute-start(bf16[2,96,1536]{2,1,0:T(8,128)(2,1)S(1)} %get-tuple-element.49), channel_id=1, source_target_pairs={{1,0},{2,1},{3,2},{0,3},{5,4},{6,5},{7,6},{4,7},{9,8},{10,9},{11,1... | collective-permute-start | bytes 1769480 | tf_op jit(solution)/shard_map/ppermute | solution.py:462
  162.1 47.4 %copy-start.7 = (f32[256]{0:T(256)S(1)}, f32[256]{0:T(256)}, u32[]{:S(2)}) copy-start(f32[256]{0:T(256)} %param.17) | copy-start | bytes 3076
  162.2 7.6 %collective-permute-start.16 = (bf16[96,1536]{1,0:T(8,128)(2,1)S(1)}, bf16[96,1536]{1,0:T(8,128)(2,1)S(1)}, u32[]{:S(2)}, u32[]{:S(2)}) collective-permute-start(bf16[96,1536]{1,0:T(8,128)(2,1)S(1)} %fusion), channel_id=1, source_target_pairs={{1,0},{2,1},{3,2},{0,3},{5,4},{6,5},{7,6},{4,7},{9,8},{10,9},{11,1... | collective-permute-start | bytes 884744 | tf_op jit(solution)/shard_map/ppermute | solution.py:467
  164.9 8.1 %collective-permute-start.15 = (bf16[96,1536]{1,0:T(8,128)(2,1)S(1)}, bf16[96,1536]{1,0:T(8,128)(2,1)S(1)}, u32[]{:S(2)}, u32[]{:S(2)}) collective-permute-start(bf16[96,1536]{1,0:T(8,128)(2,1)S(1)} %fusion.1), channel_id=1, source_target_pairs={{0,1},{1,2},{2,3},{3,0},{4,5},{5,6},{6,7},{7,4},{8,9},{9,10},{10,1... | collective-permute-start | bytes 884744 | tf_op jit(solution)/shard_map/ppermute | solution.py:467
  173.1 25.5 %collective-permute-start.17 = (bf16[2,96,1536]{2,1,0:T(8,128)(2,1)}, bf16[2,96,1536]{2,1,0:T(8,128)(2,1)S(1)}, u32[]{:S(2)}, u32[]{:S(2)}) collective-permute-start(bf16[2,96,1536]{2,1,0:T(8,128)(2,1)} %get-tuple-element.59), channel_id=1, source_target_pairs={{0,1},{1,2},{2,3},{3,0},{4,5},{5,6},{6,7},{7,4},{8,9},{9,10},{10,1... | collective-permute-start | bytes 1769480 | tf_op jit(solution)/shard_map/ppermute | solution.py:470
  173.1 25.5 %collective-permute-start.18 = (bf16[2,96,1536]{2,1,0:T(8,128)(2,1)}, bf16[2,96,1536]{2,1,0:T(8,128)(2,1)}, u32[]{:S(2)}, u32[]{:S(2)}) collective-permute-start(bf16[2,96,1536]{2,1,0:T(8,128)(2,1)} %get-tuple-element.60), channel_id=1, source_target_pairs={{1,0},{2,1},{3,2},{0,3},{5,4},{6,5},{7,6},{4,7},{9,8},{10,9},{11,1... | collective-permute-start | bytes 1769480 | tf_op jit(solution)/shard_map/ppermute | solution.py:471
  175.7 22.8 %collective-permute-start.19 = (bf16[2,96,1536]{2,1,0:T(8,128)(2,1)}, bf16[2,96,1536]{2,1,0:T(8,128)(2,1)}, u32[]{:S(2)}, u32[]{:S(2)}) collective-permute-start(bf16[2,96,1536]{2,1,0:T(8,128)(2,1)} %get-tuple-element.61), channel_id=1, source_target_pairs={{0,2},{1,3},{2,0},{3,1},{4,6},{5,7},{6,4},{7,5},{8,10},{9,11},{10,... | collective-permute-start | bytes 1769480 | tf_op jit(solution)/shard_map/ppermute | solution.py:472
  201.4 22.2 %all-to-all-start.3 = ((bf16[32,6,1536]{2,1,0:T(8,128)(2,1)}), bf16[32,6,1536]{2,1,0:T(8,128)(2,1)S(1)}, u32[]{:S(2)}, u32[]{:S(2)}) async-start(bf16[32,6,1536]{2,1,0:T(8,128)(2,1)} %reshape.34), calls=%async_computation.3 | async-start | bytes 1572864 | tf_op jit(solution)/shard_map/all_to_all | solution.py:448

commit v7 on v6

--- a/solution.py
+++ b/solution.py
@@ -419,7 +419,7 @@
     local = w_in.shape[0]
     experts = local * time_count
     slots = max(2, 3 * frame_rows // (2 * experts))
-    early = slots // 2
+    early = 2 * slots // 3
     sizes = (early, slots - early)
     served = jnp.where(overflow == 1, secondary, primary)
     place = jnp.where(

time: 228 us -> 217 us (0.952)
  blocking collectives: 61.1 us -> 36.3 us
  waiting for transfers between devices: 54.3 us -> 64.7 us
  starting transfers between devices: 47.8 us -> 56.2 us
  local copies, waits for them, and re-layouts: 14.3 us -> 10.1 us
    all_to_all x1 -> x0, blocking collectives: 20.8 us -> none  [leave(): got = lax.all_to_all(summed, 'tm', split_axis=0, concat_axis=0, tiled=True)]
    ppermute x1, waiting for transfers between devices: 0.01 us -> 17.5 us  [on_device(): lax.ppermute(to_right, 'expert', up)]
    all_to_all x1 -> x2, starting transfers between devices: 7.88 us -> 17.6 us  [leave(): got = lax.all_to_all(summed, 'tm', split_axis=0, concat_axis=0, tiled=True)]
    ppermute x4, waiting for transfers between devices: 9.5 us -> 0.79 us  [near(): return (lax.ppermute(own, 'expert', up), lax.ppermute(own, 'expert', down))]
    ppermute x1, waiting for transfers between devices: 0.01 us -> 5.52 us  [on_device(): lax.ppermute(go_up_a, 'expert', up)]
    all_to_all x2, blocking collectives: 40.4 us -> 36.3 us  [arrive(): got = lax.all_to_all(sent, 'tm', split_axis=0, concat_axis=0, tiled=True)]
    all_to_all x1 -> x2, waiting for transfers between devices: 14 us -> 10 us  [leave(): got = lax.all_to_all(summed, 'tm', split_axis=0, concat_axis=0, tiled=True)]
  transfers between devices with their start and end apart: 21 -> 22, of which waited for: 7 -> 10; matrix products, arithmetic and copies ran while one was open for 4% -> 3% of each run, Pallas kernels for 16% -> 17%
where the time goes in v7:
time: 217 us; the launch traced here: 216 us
  waiting for transfers between devices  64.7 us (30%)
  starting transfers between devices  56.2 us (26%)
  Pallas kernels  46.9 us (22%)
  blocking collectives  36.3 us (17%)
  local copies, waits for them, and re-layouts  10.1 us (5%)
    all_to_all x2, blocking collectives, arrive(): got = lax.all_to_all(sent, 'tm', split_axis=0, concat_axis=0, tiled=True)  36.3 us
    pallas_call x2, Pallas kernels, ffn(): call(functools.partial(ffn_body, direct), [pair] * 4 if direct else [pair...  24.3 us
    all_to_all x2, starting transfers between devices, leave(): got = lax.all_to_all(summed, 'tm', split_axis=0, concat_axis=0, tiled=True)  17.6 us
    ppermute x1, waiting for transfers between devices, on_device(): lax.ppermute(to_right, 'expert', up)  17.5 us
    ppermute x2, waiting for transfers between devices, on_device(): high.append(lax.ppermute(part, order, back))  11.4 us
    all_to_all x2, waiting for transfers between devices, leave(): got = lax.all_to_all(summed, 'tm', split_axis=0, concat_axis=0, tiled=True)  10 us
    ppermute x2, starting transfers between devices, on_device(): high.append(lax.ppermute(part, order, back))  9.46 us
    pallas_call x1, Pallas kernels, attention(): call(attend_body, jax.ShapeDtypeStruct((rows, pairs * PAIR), F32), cost,...  8.08 us
  transfers between devices with their start and end apart: 22, of which 10 were waited for; matrix products, arithmetic and copies ran while one was open for 3% of the time, Pallas kernels for 17%

profile of v7, /device:TPU:1, one launch (start us, length us, event | category | flops | bytes accessed | tf_op | source)
XLA Modules:
  0.0 216.1 jit_solution(17484123422445244629)
XLA Ops:
  0.0 2.4 %slice.18 = bf16[2,256,1024]{2,1,0:T(8,128)(2,1)} slice(bf16[2,256,1536]{2,1,0:T(8,128)(2,1)} %kv_ref.3), slice={[0:2], [0:256], [0:1024]} | slice | bytes 2097152 | tf_op jit(solution)/shard_map/slice | solution.py:408
  2.4 4.4 %collective-permute-start.2 = (bf16[2,256,1024]{2,1,0:T(8,128)(2,1)}, bf16[2,256,1024]{2,1,0:T(8,128)(2,1)}, u32[]{:S(2)}, u32[]{:S(2)}) collective-permute-start(bf16[2,256,1024]{2,1,0:T(8,128)(2,1)} %slice.18), channel_id=1, source_target_pairs={{0,1},{1,2},{2,3},{3,4},{4,5},{5,6},{6,7},{7,8},{8,9},{9,10},{10,1... | collective-permute-start | bytes 3145736 | tf_op jit(solution)/shard_map/ppermute | solution.py:409
  6.8 4.6 %collective-permute-start.3 = (bf16[2,256,1024]{2,1,0:T(8,128)(2,1)}, bf16[2,256,1024]{2,1,0:T(8,128)(2,1)}, u32[]{:S(2)}, u32[]{:S(2)}) collective-permute-start(bf16[2,256,1024]{2,1,0:T(8,128)(2,1)} %slice.18), channel_id=1, source_target_pairs={{1,0},{2,1},{3,2},{4,3},{5,4},{6,5},{7,6},{8,7},{9,8},{10,9},{11,1... | collective-permute-start | bytes 3145736 | tf_op jit(solution)/shard_map/ppermute | solution.py:410
  11.4 1.9 slice.19
  13.3 1.9 collective-permute-start
  15.2 4.9 %collective-permute-start.1 = (bf16[2,256,512]{2,1,0:T(8,128)(2,1)}, bf16[2,256,512]{2,1,0:T(8,128)(2,1)}, u32[]{:S(2)}, u32[]{:S(2)}) collective-permute-start(bf16[2,256,512]{2,1,0:T(8,128)(2,1)} %slice.19), channel_id=1, source_target_pairs={{1,0},{2,1},{3,2},{4,3},{5,4},{6,5},{7,6},{8,7},{9,8},{10,9},{11,1... | collective-permute-start | bytes 1572872 | tf_op jit(solution)/shard_map/ppermute | solution.py:410
  20.1 0.7 add_convert_fusion.edge_ref
  20.7 0.7 broadcast_in_dim.15.gain_ref
  21.4 0.7 broadcast_in_dim.16.gain_ref
  22.2 0.7 compare_select_fusion.1
  22.9 6.0 %collective-permute-done.2.lo_ref = bf16[2,256,1024]{2,1,0:T(8,128)(2,1)} collective-permute-done((bf16[2,256,1024]{2,1,0:T(8,128)(2,1)}, bf16[2,256,1024]{2,1,0:T(8,128)(2,1)}, u32[]{:S(2)}, u32[]{:S(2)}) %collective-permute-start.2) | collective-permute-done | bytes 1048608 | tf_op jit(solution)/shard_map/ppermute | solution.py:409
  28.9 11.4 %collective-permute-done.3.hi_ref = bf16[2,256,1024]{2,1,0:T(8,128)(2,1)} collective-permute-done((bf16[2,256,1024]{2,1,0:T(8,128)(2,1)}, bf16[2,256,1024]{2,1,0:T(8,128)(2,1)}, u32[]{:S(2)}, u32[]{:S(2)}) %collective-permute-start.3) | collective-permute-done | bytes 1048608 | tf_op jit(solution)/shard_map/ppermute | solution.py:410
  40.3 8.1 %shard_map.118.rest_0_ = f32[256,1024]{1,0:T(8,128)} custom-call(s32[2]{0:T(128)} %add_convert_fusion.edge_ref, bf16[256,1536]{1,0:T(8,128)(2,1)} %q_ref.3, bf16[2,256,1536]{2,1,0:T(8,128)(2,1)} %kv_ref.3, bf16[2,256,1024]{2,1,0:T(8,128)(2,1)} %collective-permute-done.2.lo_ref, bf16[2,256,1024]{2,1,0:T(8,128)(2,1)} %collective-permute-done.3.hi_ref), custom_call_target="tpu_custom_call" | custom-call | flops 2684354560 | bytes 3670016 | tf_op jit(solution)/shard_map/pallas_call | solution.py:138
  48.4 0.0 collective-permute-done.lo_ref
  48.4 0.0 collective-permute-done.1.hi_ref
  48.4 1.2 copy-done.4
  49.7 4.4 %shard_map.119 = (bf16[256,1536]{1,0:T(8,128)(2,1)S(1)}, bf16[16,1536]{1,0:T(8,128)(2,1)S(1)}, bf16[16,1536]{1,0:T(8,128)(2,1)S(1)}) custom-call(s32[2]{0:T(128)S(1)} %copy-done.3, bf16[256,1536]{1,0:T(8,128)(2,1)S(1)} %copy-done.2, bf16[2,256,1536]{2,1,0:T(8,128)(2,1)S(1)} %copy-done, bf16[2,256,512]{2,1,0:T(8,128)(2,1)S(1)} %collective-permute-done.lo_ref, ...), custom_call_target="tpu_custom_call" | custom-call | flops 1342177280 | bytes 1835008 | tf_op jit(solution)/shard_map/pallas_call | solution.py:151
  54.1 1.9 collective-permute-start.4
  56.0 5.6 %collective-permute-start.5 = (bf16[16,1536]{1,0:T(8,128)(2,1)S(1)}, bf16[16,1536]{1,0:T(8,128)(2,1)S(1)}, u32[]{:S(2)}, u32[]{:S(2)}) collective-permute-start(bf16[16,1536]{1,0:T(8,128)(2,1)S(1)} %get-tuple-element.40), channel_id=1, source_target_pairs={{1,0},{2,1},{3,2},{4,3},{5,4},{6,5},{7,6},{8,7},{9,8},{10,9},{11,1... | collective-permute-start | bytes 147464 | tf_op jit(solution)/shard_map/ppermute | solution.py:416
  61.6 3.6 %shard_map.120.inner_ref = bf16[224,1536]{1,0:T(8,128)(2,1)S(1)} custom-call(bf16[256,1536]{1,0:T(8,128)(2,1)S(1)} %get-tuple-element.38.normed_ref, f32[31,1536]{1,0:T(8,128)S(1)} %copy-done.1), custom_call_target="tpu_custom_call" | custom-call | flops 1365245952 | bytes 1572864 | tf_op jit(solution)/shard_map/pallas_call | solution.py:190
  65.2 0.0 collective-permute-done.5.high_ref
  65.2 1.4 shard_map.121
  66.7 21.2 %all_to_all.20 = bf16[32,8,1536]{2,1,0:T(8,128)(2,1)S(1)} all-to-all(bf16[32,8,1536]{2,1,0:T(8,128)(2,1)S(1)} %bitcast.19), channel_id=1, replica_groups=mesh['tm'=32,'expert'=4] {'tm'}, dimensions={0} | all-to-all | bytes 1572864 | tf_op jit(solution)/shard_map/all_to_all | solution.py:440
  87.9 0.0 collective-permute-start.6
  87.9 2.7 %collective-permute-start.7 = (bf16[256,1536]{1,0:T(8,128)(2,1)S(1)}, bf16[256,1536]{1,0:T(8,128)(2,1)S(1)}, u32[]{:S(2)}, u32[]{:S(2)}) collective-permute-start(bf16[256,1536]{1,0:T(8,128)(2,1)S(1)} %bitcast.17), channel_id=1, source_target_pairs={{1,0},{2,1},{3,2},{0,3},{5,4},{6,5},{7,6},{4,7},{9,8},{10,9},{11,1... | collective-permute-start | bytes 2359304 | tf_op jit(solution)/shard_map/ppermute | solution.py:444
  90.6 0.8 reshape.30
  91.4 15.1 %all_to_all.21 = bf16[32,4,1536]{2,1,0:T(4,128)(2,1)} all-to-all(bf16[32,4,1536]{2,1,0:T(4,128)(2,1)} %reshape.30), channel_id=1, replica_groups=mesh['tm'=32,'expert'=4] {'tm'}, dimensions={0} | all-to-all | bytes 786432 | tf_op jit(solution)/shard_map/all_to_all | solution.py:440
  106.5 1.1 reshape.31.own
  107.6 0.8 collective-permute-done.6.left
  108.3 0.0 collective-permute-done.7.right
  108.4 0.2 collective-permute-start.8
  108.6 2.6 %collective-permute-start.9 = (bf16[128,1536]{1,0:T(8,128)(2,1)S(1)}, bf16[128,1536]{1,0:T(8,128)(2,1)S(1)}, u32[]{:S(2)}, u32[]{:S(2)}) collective-permute-start(bf16[128,1536]{1,0:T(8,128)(2,1)S(1)} %slice.21), channel_id=1, source_target_pairs={{1,0},{2,1},{3,2},{0,3},{5,4},{6,5},{7,6},{4,7},{9,8},{10,9},{11,1... | collective-permute-start | bytes 1179656 | tf_op jit(solution)/shard_map/ppermute | solution.py:458
  111.2 0.0 collective-permute-start.12
  111.2 2.7 %collective-permute-start.13 = (bf16[128,1536]{1,0:T(8,128)(2,1)S(1)}, bf16[128,1536]{1,0:T(8,128)(2,1)S(1)}, u32[]{:S(2)}, u32[]{:S(2)}) collective-permute-start(bf16[128,1536]{1,0:T(8,128)(2,1)S(1)} %reshape.31.own), channel_id=1, source_target_pairs={{1,0},{2,1},{3,2},{0,3},{5,4},{6,5},{7,6},{4,7},{9,8},{10,9},{11,1... | collective-permute-start | bytes 1179656 | tf_op jit(solution)/shard_map/ppermute | solution.py:444
  113.9 0.0 collective-permute-start.14
  113.9 5.7 %collective-permute-done.8.rest_0_ = bf16[128,1536]{1,0:T(8,128)(2,1)S(1)} collective-permute-done((bf16[128,1536]{1,0:T(8,128)(2,1)S(1)}, bf16[128,1536]{1,0:T(8,128)(2,1)S(1)}, u32[]{:S(2)}, u32[]{:S(2)}) %collective-permute-start.8) | collective-permute-done | bytes 393248 | tf_op jit(solution)/shard_map/ppermute | solution.py:458
  119.6 14.4 %shard_map.122 = (bf16[2,128,1536]{2,1,0:T(8,128)(2,1)S(1)}, bf16[2,128,1536]{2,1,0:T(8,128)(2,1)S(1)}, bf16[2,128,1536]{2,1,0:T(8,128)(2,1)S(1)}, bf16[128,1536]{1,0:T(8,128)(2,1)S(1)}, bf16[128,1536]{1,0:T(8,128)(2,1)S(1)}) custom-call(bf16[256,1536]{1,0:T(8,128)(2,1)S(1)} %bitcast.18, bf16[256,1536]{1,0:T(8,128)(2,1)S(1)} %collective-permute-done.6.left, ...), custom_call_target="tpu_custom_call" | custom-call | flops 9663676416 | bytes 18874368 | tf_op jit(solution)/shard_map/pallas_call | solution.py:339
  134.0 0.5 collective-permute-start.10
  134.6 2.3 %collective-permute-start.11 = (bf16[2,128,1536]{2,1,0:T(8,128)(2,1)S(1)}, bf16[2,128,1536]{2,1,0:T(8,128)(2,1)S(1)}, u32[]{:S(2)}, u32[]{:S(2)}) collective-permute-start(bf16[2,128,1536]{2,1,0:T(8,128)(2,1)S(1)} %get-tuple-element.49), channel_id=1, source_target_pairs={{1,0},{2,1},{3,2},{0,3},{5,4},{6,5},{7,6},{4,7},{9,8},{10,9},{11,1... | collective-permute-start | bytes 2359304 | tf_op jit(solution)/shard_map/ppermute | solution.py:462
  136.9 0.3 collective-permute-done.14.rest_0_
  137.1 9.9 %shard_map.123 = (bf16[2,64,1536]{2,1,0:T(8,128)(2,1)S(1)}, bf16[2,64,1536]{2,1,0:T(8,128)(2,1)}, bf16[2,64,1536]{2,1,0:T(8,128)(2,1)}, bf16[2,64,1536]{2,1,0:T(8,128)(2,1)S(1)}) custom-call(bf16[128,1536]{1,0:T(8,128)(2,1)S(1)} %reshape.31.own, bf16[128,1536]{1,0:T(8,128)(2,1)S(1)} %collective-permute-done.12.left, ...), custom_call_target="tpu_custom_call" | custom-call | flops 4831838208 | bytes 18874368 | tf_op jit(solution)/shard_map/pallas_call | solution.py:339
  147.0 0.0 copy-start.5
  147.0 5.5 %collective-permute-done.10.refs_2_ = bf16[2,128,1536]{2,1,0:T(8,128)(2,1)S(1)} collective-permute-done((bf16[2,128,1536]{2,1,0:T(8,128)(2,1)S(1)}, bf16[2,128,1536]{2,1,0:T(8,128)(2,1)S(1)}, u32[]{:S(2)}, u32[]{:S(2)}) %collective-permute-start.10) | collective-permute-done | bytes 786464 | tf_op jit(solution)/shard_map/ppermute | solution.py:462
  152.6 0.0 collective-permute-done.11.refs_1_
  152.6 0.1 fusion
  152.7 1.2 collective-permute-start.16
  153.8 0.1 fusion.1
  153.9 0.4 collective-permute-start.15
  154.4 5.7 %collective-permute-done.16.refs_4_ = bf16[128,1536]{1,0:T(8,128)(2,1)S(1)} collective-permute-done((bf16[128,1536]{1,0:T(8,128)(2,1)S(1)}, bf16[128,1536]{1,0:T(8,128)(2,1)S(1)}, u32[]{:S(2)}, u32[]{:S(2)}) %collective-permute-start.16) | collective-permute-done | bytes 393248 | tf_op jit(solution)/shard_map/ppermute | solution.py:467
  160.1 1.8 collective-permute-done.15.refs_3_
  161.9 1.4 shard_map.124
  163.3 9.3 %all-to-all-start.2 = ((bf16[32,8,1536]{2,1,0:T(8,128)(2,1)}), bf16[32,8,1536]{2,1,0:T(8,128)(2,1)S(1)}, u32[]{:S(2)}, u32[]{:S(2)}) async-start(bf16[32,8,1536]{2,1,0:T(8,128)(2,1)} %bitcast.9), calls=%async_computation.2 | async-start | bytes 1572864 | tf_op jit(solution)/shard_map/all_to_all | solution.py:448
  172.6 0.1 collective-permute-start.17
  172.7 2.7 %collective-permute-start.18 = (bf16[2,64,1536]{2,1,0:T(8,128)(2,1)}, bf16[2,64,1536]{2,1,0:T(8,128)(2,1)S(1)}, u32[]{:S(2)}, u32[]{:S(2)}) collective-permute-start(bf16[2,64,1536]{2,1,0:T(8,128)(2,1)} %get-tuple-element.60), channel_id=1, source_target_pairs={{1,0},{2,1},{3,2},{0,3},{5,4},{6,5},{7,6},{4,7},{9,8},{10,9},{11,1... | collective-permute-start | bytes 1179656 | tf_op jit(solution)/shard_map/ppermute | solution.py:471
  175.4 0.0 collective-permute-start.19
  175.4 17.5 %collective-permute-done.17.refs_1_ = bf16[2,64,1536]{2,1,0:T(8,128)(2,1)S(1)} collective-permute-done((bf16[2,64,1536]{2,1,0:T(8,128)(2,1)}, bf16[2,64,1536]{2,1,0:T(8,128)(2,1)S(1)}, u32[]{:S(2)}, u32[]{:S(2)}) %collective-permute-start.17) | collective-permute-done | bytes 393248 | tf_op jit(solution)/shard_map/ppermute | solution.py:470
  192.9 0.4 shard_map.125
  193.3 0.8 reshape.34
  194.1 8.3 %all-to-all-start.3 = ((bf16[32,4,1536]{2,1,0:T(4,128)(2,1)}), bf16[32,4,1536]{2,1,0:T(4,128)(2,1)S(1)}, u32[]{:S(2)}, u32[]{:S(2)}) async-start(bf16[32,4,1536]{2,1,0:T(4,128)(2,1)} %reshape.34), calls=%async_computation.3 | async-start | bytes 786432 | tf_op jit(solution)/shard_map/all_to_all | solution.py:448
  202.4 0.1 copy.14.place_ref
  202.6 0.1 copy.13.gate_ref
  202.7 10.0 %all-to-all-done.3 = bf16[32,4,1536]{2,1,0:T(4,128)(2,1)S(1)} async-done(((bf16[32,4,1536]{2,1,0:T(4,128)(2,1)}), bf16[32,4,1536]{2,1,0:T(4,128)(2,1)S(1)}, u32[]{:S(2)}, u32[]{:S(2)}) %all-to-all-start.3) | async-done | bytes 393248 | tf_op jit(solution)/shard_map/all_to_all | solution.py:448
  212.7 0.1 reshape.35.rest_1_
  212.8 3.3 %shard_map.126 = bf16[256,1536]{1,0:T(8,128)(2,1)} custom-call(bf16[256,1536]{1,0:T(8,128)(2,1)S(1)} %get-tuple-element.41.mixed_ref, f32[256,1]{1,0:T(8,128)S(1)} %copy.13.gate_ref, s32[256,1]{1,0:T(8,128)S(1)} %copy.14.place_ref, bf16[256,1536]{1,0:T(8,128)(2,1)S(1)} %bitcast.15, bf16[128,1536]{1,0:T(8,128)(2,1)S(1)} %reshape.35.rest_1_), custom_call_target="tpu_custom_call" | custom-call | flops 301989888 | bytes 3145728 | tf_op jit(solution)/shard_map/pallas_call | solution.py:262
  (19 shorter events, 0.1 us)
Async XLA Ops:
  0.0 48.4 %copy-start = (bf16[2,256,1536]{2,1,0:T(8,128)(2,1)S(1)}, bf16[2,256,1536]{2,1,0:T(8,128)(2,1)}, u32[]{:S(2)}) copy-start(bf16[2,256,1536]{2,1,0:T(8,128)(2,1)} %kv_ref.3) | copy-start | bytes 4718596
  0.0 48.4 %copy-start.2 = (bf16[256,1536]{1,0:T(8,128)(2,1)S(1)}, bf16[256,1536]{1,0:T(8,128)(2,1)}, u32[]{:S(2)}) copy-start(bf16[256,1536]{1,0:T(8,128)(2,1)} %q_ref.3) | copy-start | bytes 2359300
  0.0 61.6 %copy-start.1 = (f32[31,1536]{1,0:T(8,128)S(1)}, f32[31,1536]{1,0:T(8,128)}, u32[]{:S(2)}) copy-start(f32[31,1536]{1,0:T(8,128)} %taps_ref.3) | copy-start | bytes 571396
  2.4 26.5 %collective-permute-start.2 = (bf16[2,256,1024]{2,1,0:T(8,128)(2,1)}, bf16[2,256,1024]{2,1,0:T(8,128)(2,1)}, u32[]{:S(2)}, u32[]{:S(2)}) collective-permute-start(bf16[2,256,1024]{2,1,0:T(8,128)(2,1)} %slice.18), channel_id=1, source_target_pairs={{0,1},{1,2},{2,3},{3,4},{4,5},{5,6},{6,7},{7,8},{8,9},{9,10},{10,1... | collective-permute-start | bytes 3145736 | tf_op jit(solution)/shard_map/ppermute | solution.py:409
  6.8 33.5 %collective-permute-start.3 = (bf16[2,256,1024]{2,1,0:T(8,128)(2,1)}, bf16[2,256,1024]{2,1,0:T(8,128)(2,1)}, u32[]{:S(2)}, u32[]{:S(2)}) collective-permute-start(bf16[2,256,1024]{2,1,0:T(8,128)(2,1)} %slice.18), channel_id=1, source_target_pairs={{1,0},{2,1},{3,2},{4,3},{5,4},{6,5},{7,6},{8,7},{9,8},{10,9},{11,1... | collective-permute-start | bytes 3145736 | tf_op jit(solution)/shard_map/ppermute | solution.py:410
  13.3 35.1 %collective-permute-start = (bf16[2,256,512]{2,1,0:T(8,128)(2,1)}, bf16[2,256,512]{2,1,0:T(8,128)(2,1)S(1)}, u32[]{:S(2)}, u32[]{:S(2)}) collective-permute-start(bf16[2,256,512]{2,1,0:T(8,128)(2,1)} %slice.19), channel_id=1, source_target_pairs={{0,1},{1,2},{2,3},{3,4},{4,5},{5,6},{6,7},{7,8},{8,9},{9,10},{10,1... | collective-permute-start | bytes 1572872 | tf_op jit(solution)/shard_map/ppermute | solution.py:409
  15.2 33.2 %collective-permute-start.1 = (bf16[2,256,512]{2,1,0:T(8,128)(2,1)}, bf16[2,256,512]{2,1,0:T(8,128)(2,1)}, u32[]{:S(2)}, u32[]{:S(2)}) collective-permute-start(bf16[2,256,512]{2,1,0:T(8,128)(2,1)} %slice.19), channel_id=1, source_target_pairs={{1,0},{2,1},{3,2},{4,3},{5,4},{6,5},{7,6},{8,7},{9,8},{10,9},{11,1... | collective-permute-start | bytes 1572872 | tf_op jit(solution)/shard_map/ppermute | solution.py:410
  20.7 27.7 %copy-start.3 = (s32[2]{0:T(128)S(1)}, s32[2]{0:T(128)}, u32[]{:S(2)}) copy-start(s32[2]{0:T(128)} %add_convert_fusion.edge_ref) | copy-start | bytes 28
  48.4 1.2 copy-start.4
  54.1 11.1 %collective-permute-start.4 = (bf16[16,1536]{1,0:T(8,128)(2,1)S(1)}, bf16[16,1536]{1,0:T(8,128)(2,1)S(1)}, u32[]{:S(2)}, u32[]{:S(2)}) collective-permute-start(bf16[16,1536]{1,0:T(8,128)(2,1)S(1)} %get-tuple-element.39), channel_id=1, source_target_pairs={{0,1},{1,2},{2,3},{3,4},{4,5},{5,6},{6,7},{7,8},{8,9},{9,10},{10,1... | collective-permute-start | bytes 147464 | tf_op jit(solution)/shard_map/ppermute | solution.py:415
  56.0 9.2 %collective-permute-start.5 = (bf16[16,1536]{1,0:T(8,128)(2,1)S(1)}, bf16[16,1536]{1,0:T(8,128)(2,1)S(1)}, u32[]{:S(2)}, u32[]{:S(2)}) collective-permute-start(bf16[16,1536]{1,0:T(8,128)(2,1)S(1)} %get-tuple-element.40), channel_id=1, source_target_pairs={{1,0},{2,1},{3,2},{4,3},{5,4},{6,5},{7,6},{8,7},{9,8},{10,9},{11,1... | collective-permute-start | bytes 147464 | tf_op jit(solution)/shard_map/ppermute | solution.py:416
  87.9 20.5 %collective-permute-start.6 = (bf16[256,1536]{1,0:T(8,128)(2,1)S(1)}, bf16[256,1536]{1,0:T(8,128)(2,1)S(1)}, u32[]{:S(2)}, u32[]{:S(2)}) collective-permute-start(bf16[256,1536]{1,0:T(8,128)(2,1)S(1)} %bitcast.16), channel_id=1, source_target_pairs={{0,1},{1,2},{2,3},{3,0},{4,5},{5,6},{6,7},{7,4},{8,9},{9,10},{10,1... | collective-permute-start | bytes 2359304 | tf_op jit(solution)/shard_map/ppermute | solution.py:444
  87.9 20.5 %collective-permute-start.7 = (bf16[256,1536]{1,0:T(8,128)(2,1)S(1)}, bf16[256,1536]{1,0:T(8,128)(2,1)S(1)}, u32[]{:S(2)}, u32[]{:S(2)}) collective-permute-start(bf16[256,1536]{1,0:T(8,128)(2,1)S(1)} %bitcast.17), channel_id=1, source_target_pairs={{1,0},{2,1},{3,2},{0,3},{5,4},{6,5},{7,6},{4,7},{9,8},{10,9},{11,1... | collective-permute-start | bytes 2359304 | tf_op jit(solution)/shard_map/ppermute | solution.py:444
  108.4 11.2 %collective-permute-start.8 = (bf16[128,1536]{1,0:T(8,128)(2,1)S(1)}, bf16[128,1536]{1,0:T(8,128)(2,1)S(1)}, u32[]{:S(2)}, u32[]{:S(2)}) collective-permute-start(bf16[128,1536]{1,0:T(8,128)(2,1)S(1)} %slice.20), channel_id=1, source_target_pairs={{0,1},{1,2},{2,3},{3,0},{4,5},{5,6},{6,7},{7,4},{8,9},{9,10},{10,1... | collective-permute-start | bytes 1179656 | tf_op jit(solution)/shard_map/ppermute | solution.py:458
  108.6 11.0 %collective-permute-start.9 = (bf16[128,1536]{1,0:T(8,128)(2,1)S(1)}, bf16[128,1536]{1,0:T(8,128)(2,1)S(1)}, u32[]{:S(2)}, u32[]{:S(2)}) collective-permute-start(bf16[128,1536]{1,0:T(8,128)(2,1)S(1)} %slice.21), channel_id=1, source_target_pairs={{1,0},{2,1},{3,2},{0,3},{5,4},{6,5},{7,6},{4,7},{9,8},{10,9},{11,1... | collective-permute-start | bytes 1179656 | tf_op jit(solution)/shard_map/ppermute | solution.py:458
  111.2 25.6 %collective-permute-start.12 = (bf16[128,1536]{1,0:T(8,128)(2,1)S(1)}, bf16[128,1536]{1,0:T(8,128)(2,1)S(1)}, u32[]{:S(2)}, u32[]{:S(2)}) collective-permute-start(bf16[128,1536]{1,0:T(8,128)(2,1)S(1)} %reshape.31.own), channel_id=1, source_target_pairs={{0,1},{1,2},{2,3},{3,0},{4,5},{5,6},{6,7},{7,4},{8,9},{9,10},{10,1... | collective-permute-start | bytes 1179656 | tf_op jit(solution)/shard_map/ppermute | solution.py:444
  111.2 25.6 %collective-permute-start.13 = (bf16[128,1536]{1,0:T(8,128)(2,1)S(1)}, bf16[128,1536]{1,0:T(8,128)(2,1)S(1)}, u32[]{:S(2)}, u32[]{:S(2)}) collective-permute-start(bf16[128,1536]{1,0:T(8,128)(2,1)S(1)} %reshape.31.own), channel_id=1, source_target_pairs={{1,0},{2,1},{3,2},{0,3},{5,4},{6,5},{7,6},{4,7},{9,8},{10,9},{11,1... | collective-permute-start | bytes 1179656 | tf_op jit(solution)/shard_map/ppermute | solution.py:444
  113.9 23.2 %collective-permute-start.14 = (bf16[128,1536]{1,0:T(8,128)(2,1)S(1)}, bf16[128,1536]{1,0:T(8,128)(2,1)S(1)}, u32[]{:S(2)}, u32[]{:S(2)}) collective-permute-start(bf16[128,1536]{1,0:T(8,128)(2,1)S(1)} %reshape.31.own), channel_id=1, source_target_pairs={{0,2},{1,3},{2,0},{3,1},{4,6},{5,7},{6,4},{7,5},{8,10},{9,11},{10,... | collective-permute-start | bytes 1179656 | tf_op jit(solution)/shard_map/ppermute | solution.py:460
  134.0 18.5 %collective-permute-start.10 = (bf16[2,128,1536]{2,1,0:T(8,128)(2,1)S(1)}, bf16[2,128,1536]{2,1,0:T(8,128)(2,1)S(1)}, u32[]{:S(2)}, u32[]{:S(2)}) collective-permute-start(bf16[2,128,1536]{2,1,0:T(8,128)(2,1)S(1)} %get-tuple-element.48), channel_id=1, source_target_pairs={{0,1},{1,2},{2,3},{3,0},{4,5},{5,6},{6,7},{7,4},{8,9},{9,10},{10,1... | collective-permute-start | bytes 2359304 | tf_op jit(solution)/shard_map/ppermute | solution.py:462
  134.6 18.0 %collective-permute-start.11 = (bf16[2,128,1536]{2,1,0:T(8,128)(2,1)S(1)}, bf16[2,128,1536]{2,1,0:T(8,128)(2,1)S(1)}, u32[]{:S(2)}, u32[]{:S(2)}) collective-permute-start(bf16[2,128,1536]{2,1,0:T(8,128)(2,1)S(1)} %get-tuple-element.49), channel_id=1, source_target_pairs={{1,0},{2,1},{3,2},{0,3},{5,4},{6,5},{7,6},{4,7},{9,8},{10,9},{11,1... | collective-permute-start | bytes 2359304 | tf_op jit(solution)/shard_map/ppermute | solution.py:462
  147.0 55.6 %copy-start.5 = (f32[256]{0:T(256)S(1)}, f32[256]{0:T(256)}, u32[]{:S(2)}) copy-start(f32[256]{0:T(256)} %param.17) | copy-start | bytes 3076
  152.7 7.4 %collective-permute-start.16 = (bf16[128,1536]{1,0:T(8,128)(2,1)S(1)}, bf16[128,1536]{1,0:T(8,128)(2,1)S(1)}, u32[]{:S(2)}, u32[]{:S(2)}) collective-permute-start(bf16[128,1536]{1,0:T(8,128)(2,1)S(1)} %fusion), channel_id=1, source_target_pairs={{1,0},{2,1},{3,2},{0,3},{5,4},{6,5},{7,6},{4,7},{9,8},{10,9},{11,1... | collective-permute-start | bytes 1179656 | tf_op jit(solution)/shard_map/ppermute | solution.py:467
  153.9 7.9 %collective-permute-start.15 = (bf16[128,1536]{1,0:T(8,128)(2,1)S(1)}, bf16[128,1536]{1,0:T(8,128)(2,1)S(1)}, u32[]{:S(2)}, u32[]{:S(2)}) collective-permute-start(bf16[128,1536]{1,0:T(8,128)(2,1)S(1)} %fusion.1), channel_id=1, source_target_pairs={{0,1},{1,2},{2,3},{3,0},{4,5},{5,6},{6,7},{7,4},{8,9},{9,10},{10,1... | collective-permute-start | bytes 1179656 | tf_op jit(solution)/shard_map/ppermute | solution.py:467
  163.3 29.6 %all-to-all-start.2 = ((bf16[32,8,1536]{2,1,0:T(8,128)(2,1)}), bf16[32,8,1536]{2,1,0:T(8,128)(2,1)S(1)}, u32[]{:S(2)}, u32[]{:S(2)}) async-start(bf16[32,8,1536]{2,1,0:T(8,128)(2,1)} %bitcast.9), calls=%async_computation.2 | async-start | bytes 1572864 | tf_op jit(solution)/shard_map/all_to_all | solution.py:448
  172.6 20.3 %collective-permute-start.17 = (bf16[2,64,1536]{2,1,0:T(8,128)(2,1)}, bf16[2,64,1536]{2,1,0:T(8,128)(2,1)S(1)}, u32[]{:S(2)}, u32[]{:S(2)}) collective-permute-start(bf16[2,64,1536]{2,1,0:T(8,128)(2,1)} %get-tuple-element.59), channel_id=1, source_target_pairs={{0,1},{1,2},{2,3},{3,0},{4,5},{5,6},{6,7},{7,4},{8,9},{9,10},{10,1... | collective-permute-start | bytes 1179656 | tf_op jit(solution)/shard_map/ppermute | solution.py:470
  172.7 20.2 %collective-permute-start.18 = (bf16[2,64,1536]{2,1,0:T(8,128)(2,1)}, bf16[2,64,1536]{2,1,0:T(8,128)(2,1)S(1)}, u32[]{:S(2)}, u32[]{:S(2)}) collective-permute-start(bf16[2,64,1536]{2,1,0:T(8,128)(2,1)} %get-tuple-element.60), channel_id=1, source_target_pairs={{1,0},{2,1},{3,2},{0,3},{5,4},{6,5},{7,6},{4,7},{9,8},{10,9},{11,1... | collective-permute-start | bytes 1179656 | tf_op jit(solution)/shard_map/ppermute | solution.py:471
  175.4 17.5 %collective-permute-start.19 = (bf16[2,64,1536]{2,1,0:T(8,128)(2,1)S(1)}, bf16[2,64,1536]{2,1,0:T(8,128)(2,1)S(1)}, u32[]{:S(2)}, u32[]{:S(2)}) collective-permute-start(bf16[2,64,1536]{2,1,0:T(8,128)(2,1)S(1)} %get-tuple-element.61), channel_id=1, source_target_pairs={{0,2},{1,3},{2,0},{3,1},{4,6},{5,7},{6,4},{7,5},{8,10},{9,11},{10,... | collective-permute-start | bytes 1179656 | tf_op jit(solution)/shard_map/ppermute | solution.py:472
  194.1 18.6 %all-to-all-start.3 = ((bf16[32,4,1536]{2,1,0:T(4,128)(2,1)}), bf16[32,4,1536]{2,1,0:T(4,128)(2,1)S(1)}, u32[]{:S(2)}, u32[]{:S(2)}) async-start(bf16[32,4,1536]{2,1,0:T(4,128)(2,1)} %reshape.34), calls=%async_computation.3 | async-start | bytes 786432 | tf_op jit(solution)/shard_map/all_to_all | solution.py:448

commit v8 on v7

--- a/solution.py
+++ b/solution.py
@@ -256,7 +256,7 @@
 
 def combine(mixed, gate, place, parts):
     rows, width = mixed.shape
-    block = 256
+    block = width // 2
     column = lambda n: pl.BlockSpec((n, block), lambda j: (0, j))
     fixed = pl.BlockSpec((rows, 1), lambda j: (0, 0))
     return call(
@@ -419,7 +419,7 @@
     local = w_in.shape[0]
     experts = local * time_count
     slots = max(2, 3 * frame_rows // (2 * experts))
-    early = 2 * slots // 3
+    early = slots // 3
     sizes = (early, slots - early)
     served = jnp.where(overflow == 1, secondary, primary)
     place = jnp.where(
@@ -452,30 +452,31 @@
     across = [(i, (i + 2) % group_count) for i in range(group_count)]
     own_a = arrive(chunks[0], sizes[0])
     left_a, right_a = near(own_a)
+    far_a = lax.ppermute(own_a, "expert", across)
     own_b = arrive(*after((chunks[1],), own_a), sizes[1])
-    left_a, right_a = after((left_a, right_a), own_b)
-    half = own_a.shape[0] // 2
-    far_a = lax.ppermute(left_a[:half], "expert", up), lax.ppermute(right_a[half:], "expert", down)
     left_b, right_b = near(own_b)
-    far_b = lax.ppermute(own_b, "expert", across)
-    keep_a, go_up_a, go_down_a, up2_a, down2_a = ffn(own_a, left_a, right_a, far_a, w_in, w_out)
-    below_a, above_a = lax.ppermute(go_up_a, "expert", up), lax.ppermute(go_down_a, "expert", down)
-    (own_b,) = after((own_b,), keep_a)
-    keep_b, to_right, to_left, to_far = ffn(own_b, left_b, right_b, (far_b,), w_in, w_out)
-    below_a, above_a = after((below_a, above_a), keep_b)
-    up2_a, down2_a = add(up2_a, below_a[0]), add(down2_a, above_a[0])
-    up3_a, down3_a = lax.ppermute(up2_a, "expert", up), lax.ppermute(down2_a, "expert", down)
-    to_right, to_left, to_far = after((to_right, to_left, to_far), up3_a, down3_a)
-    parts_b = (
+    left_a, right_a, far_a = after((left_a, right_a, far_a), own_b)
+    keep_a, to_right, to_left, to_far = ffn(own_a, left_a, right_a, (far_a,), w_in, w_out)
+    left_b, right_b = after((left_b, right_b), keep_a)
+    half = own_b.shape[0] // 2
+    far_b = lax.ppermute(left_b[:half], "expert", up), lax.ppermute(right_b[half:], "expert", down)
+    to_right, to_left, to_far = after((to_right, to_left, to_far), *far_b)
+    parts_a = (
         lax.ppermute(to_right, "expert", up),
         lax.ppermute(to_left, "expert", down),
         lax.ppermute(to_far, "expert", across),
     )
+    keep_b, go_up, go_down, up2, down2 = ffn(own_b, left_b, right_b, far_b, w_in, w_out)
+    parts_a = after(parts_a, keep_b)
+    go_up, go_down = after((go_up, go_down), *parts_a)
+    below, above = lax.ppermute(go_up, "expert", up), lax.ppermute(go_down, "expert", down)
+    total_a = home([[(i, e) for i in range(4)] for e in range(2)], keep_a, *parts_a)
+    back_a = leave(total_a, sizes[0])
+    below, above = after((below, above), back_a)
+    up2, down2 = add(up2, below[0]), add(down2, above[0])
+    up3, down3 = lax.ppermute(up2, "expert", up), lax.ppermute(down2, "expert", down)
     terms = (((0, 0), (1, 1), (3, None)), ((0, 1), (2, 1), (4, None)))
-    total_a = home(terms, keep_a, above_a, below_a, up3_a, down3_a)
-    back_a = leave(total_a, sizes[0])
-    parts_b = after(parts_b, back_a)
-    total_b = home([[(i, e) for i in range(4)] for e in range(2)], keep_b, *parts_b)
+    total_b = home(terms, keep_b, above, below, up3, down3)
     back_b = leave(total_b, sizes[1])
     return combine(mixed, expert_gate, place, [back_a, back_b])
 

time: 217 us -> 221 us (1.018)
  waiting for transfers between devices: 64.7 us -> 75.1 us
  starting transfers between devices: 56.2 us -> 47.7 us
    all_to_all x0 -> x1, blocking collectives: none -> 20.3 us  [leave(): got = lax.all_to_all(summed, 'tm', split_axis=0, concat_axis=0, tiled=True)]
    all_to_all x2 -> x1, blocking collectives: 36.3 us -> 17.3 us  [arrive(): got = lax.all_to_all(sent, 'tm', split_axis=0, concat_axis=0, tiled=True)]
    ppermute x1, waiting for transfers between devices: 17.5 us -> 0.01 us  [on_device(): lax.ppermute(to_right, 'expert', up)]
    all_to_all x2 -> x1, starting transfers between devices: 17.6 us -> 4.51 us  [leave(): got = lax.all_to_all(summed, 'tm', split_axis=0, concat_axis=0, tiled=True)]
    all_to_all x0 -> x1, waiting for transfers between devices: none -> 10.6 us  [arrive(): got = lax.all_to_all(sent, 'tm', split_axis=0, concat_axis=0, tiled=True)]
    ppermute x4, waiting for transfers between devices: 0.79 us -> 11 us  [near(): return (lax.ppermute(own, 'expert', up), lax.ppermute(own, 'expert', down))]
    all_to_all x2 -> x1, waiting for transfers between devices: 10 us -> 14 us  [leave(): got = lax.all_to_all(summed, 'tm', split_axis=0, concat_axis=0, tiled=True)]
    all_to_all x0 -> x1, starting transfers between devices: none -> 3.71 us  [arrive(): got = lax.all_to_all(sent, 'tm', split_axis=0, concat_axis=0, tiled=True)]
  transfers between devices with their start and end apart: 22 -> 22, of which waited for: 10 -> 12; matrix products, arithmetic and copies ran while one was open for 3% -> 4% of each run, Pallas kernels for 17% -> 17%
where the time goes in v8:
time: 221 us; the launch traced here: 220 us
  waiting for transfers between devices  75.1 us (34%)
  starting transfers between devices  47.7 us (22%)
  Pallas kernels  46.4 us (21%)
  blocking collectives  37.6 us (17%)
  local copies, waits for them, and re-layouts  9.39 us (4%)
  other arithmetic  3.49 us (2%)
    pallas_call x2, Pallas kernels, ffn(): call(functools.partial(ffn_body, direct), [pair] * 4 if direct else [pair...  24.6 us
    all_to_all x1, blocking collectives, leave(): got = lax.all_to_all(summed, 'tm', split_axis=0, concat_axis=0, tiled=True)  20.3 us
    all_to_all x1, blocking collectives, arrive(): got = lax.all_to_all(sent, 'tm', split_axis=0, concat_axis=0, tiled=True)  17.3 us
    all_to_all x1, waiting for transfers between devices, leave(): got = lax.all_to_all(summed, 'tm', split_axis=0, concat_axis=0, tiled=True)  14 us
    ppermute x2, waiting for transfers between devices, on_device(): high.append(lax.ppermute(part, order, back))  11.4 us
    ppermute x4, waiting for transfers between devices, near(): return (lax.ppermute(own, 'expert', up), lax.ppermute(own, 'expert', down))  11 us
    all_to_all x1, waiting for transfers between devices, arrive(): got = lax.all_to_all(sent, 'tm', split_axis=0, concat_axis=0, tiled=True)  10.6 us
    ppermute x2, starting transfers between devices, on_device(): high.append(lax.ppermute(part, order, back))  9.46 us
  transfers between devices with their start and end apart: 22, of which 12 were waited for; matrix products, arithmetic and copies ran while one was open for 4% of the time, Pallas kernels for 17%

profile of v8, /device:TPU:1, one launch (start us, length us, event | category | flops | bytes accessed | tf_op | source)
XLA Modules:
  0.0 219.9 jit_solution(9488975966468563368)
XLA Ops:
  0.0 2.4 %slice.18 = bf16[2,256,1024]{2,1,0:T(8,128)(2,1)} slice(bf16[2,256,1536]{2,1,0:T(8,128)(2,1)} %kv_ref.3), slice={[0:2], [0:256], [0:1024]} | slice | bytes 2097152 | tf_op jit(solution)/shard_map/slice | solution.py:408
  2.4 4.4 %collective-permute-start.2 = (bf16[2,256,1024]{2,1,0:T(8,128)(2,1)}, bf16[2,256,1024]{2,1,0:T(8,128)(2,1)}, u32[]{:S(2)}, u32[]{:S(2)}) collective-permute-start(bf16[2,256,1024]{2,1,0:T(8,128)(2,1)} %slice.18), channel_id=1, source_target_pairs={{0,1},{1,2},{2,3},{3,4},{4,5},{5,6},{6,7},{7,8},{8,9},{9,10},{10,1... | collective-permute-start | bytes 3145736 | tf_op jit(solution)/shard_map/ppermute | solution.py:409
  6.8 4.6 %collective-permute-start.3 = (bf16[2,256,1024]{2,1,0:T(8,128)(2,1)}, bf16[2,256,1024]{2,1,0:T(8,128)(2,1)}, u32[]{:S(2)}, u32[]{:S(2)}) collective-permute-start(bf16[2,256,1024]{2,1,0:T(8,128)(2,1)} %slice.18), channel_id=1, source_target_pairs={{1,0},{2,1},{3,2},{4,3},{5,4},{6,5},{7,6},{8,7},{9,8},{10,9},{11,1... | collective-permute-start | bytes 3145736 | tf_op jit(solution)/shard_map/ppermute | solution.py:410
  11.4 1.9 slice.19
  13.3 1.9 collective-permute-start
  15.2 4.9 %collective-permute-start.1 = (bf16[2,256,512]{2,1,0:T(8,128)(2,1)}, bf16[2,256,512]{2,1,0:T(8,128)(2,1)}, u32[]{:S(2)}, u32[]{:S(2)}) collective-permute-start(bf16[2,256,512]{2,1,0:T(8,128)(2,1)} %slice.19), channel_id=1, source_target_pairs={{1,0},{2,1},{3,2},{4,3},{5,4},{6,5},{7,6},{8,7},{9,8},{10,9},{11,1... | collective-permute-start | bytes 1572872 | tf_op jit(solution)/shard_map/ppermute | solution.py:410
  20.1 0.6 add_convert_fusion.edge_ref
  20.7 0.7 broadcast_in_dim.15.gain_ref
  21.4 0.7 broadcast_in_dim.16.gain_ref
  22.1 0.7 compare_select_fusion.1
  22.8 6.1 %collective-permute-done.2.lo_ref = bf16[2,256,1024]{2,1,0:T(8,128)(2,1)} collective-permute-done((bf16[2,256,1024]{2,1,0:T(8,128)(2,1)}, bf16[2,256,1024]{2,1,0:T(8,128)(2,1)}, u32[]{:S(2)}, u32[]{:S(2)}) %collective-permute-start.2) | collective-permute-done | bytes 1048608 | tf_op jit(solution)/shard_map/ppermute | solution.py:409
  28.9 11.4 %collective-permute-done.3.hi_ref = bf16[2,256,1024]{2,1,0:T(8,128)(2,1)} collective-permute-done((bf16[2,256,1024]{2,1,0:T(8,128)(2,1)}, bf16[2,256,1024]{2,1,0:T(8,128)(2,1)}, u32[]{:S(2)}, u32[]{:S(2)}) %collective-permute-start.3) | collective-permute-done | bytes 1048608 | tf_op jit(solution)/shard_map/ppermute | solution.py:410
  40.3 8.1 %shard_map.118.rest_0_ = f32[256,1024]{1,0:T(8,128)} custom-call(s32[2]{0:T(128)} %add_convert_fusion.edge_ref, bf16[256,1536]{1,0:T(8,128)(2,1)} %q_ref.3, bf16[2,256,1536]{2,1,0:T(8,128)(2,1)} %kv_ref.3, bf16[2,256,1024]{2,1,0:T(8,128)(2,1)} %collective-permute-done.2.lo_ref, bf16[2,256,1024]{2,1,0:T(8,128)(2,1)} %collective-permute-done.3.hi_ref), custom_call_target="tpu_custom_call" | custom-call | flops 2684354560 | bytes 3670016 | tf_op jit(solution)/shard_map/pallas_call | solution.py:138
  48.4 0.0 collective-permute-done.lo_ref
  48.4 0.0 collective-permute-done.1.hi_ref
  48.4 1.2 copy-done.6
  49.7 4.4 %shard_map.119 = (bf16[256,1536]{1,0:T(8,128)(2,1)S(1)}, bf16[16,1536]{1,0:T(8,128)(2,1)S(1)}, bf16[16,1536]{1,0:T(8,128)(2,1)S(1)}) custom-call(s32[2]{0:T(128)S(1)} %copy-done.5, bf16[256,1536]{1,0:T(8,128)(2,1)S(1)} %copy-done.4, bf16[2,256,1536]{2,1,0:T(8,128)(2,1)S(1)} %copy-done, bf16[2,256,512]{2,1,0:T(8,128)(2,1)S(1)} %collective-permute-done.lo_ref, ...), custom_call_target="tpu_custom_call" | custom-call | flops 1342177280 | bytes 1835008 | tf_op jit(solution)/shard_map/pallas_call | solution.py:151
  54.1 1.9 collective-permute-start.4
  56.0 5.6 %collective-permute-start.5 = (bf16[16,1536]{1,0:T(8,128)(2,1)S(1)}, bf16[16,1536]{1,0:T(8,128)(2,1)S(1)}, u32[]{:S(2)}, u32[]{:S(2)}) collective-permute-start(bf16[16,1536]{1,0:T(8,128)(2,1)S(1)} %get-tuple-element.44), channel_id=1, source_target_pairs={{1,0},{2,1},{3,2},{4,3},{5,4},{6,5},{7,6},{8,7},{9,8},{10,9},{11,1... | collective-permute-start | bytes 147464 | tf_op jit(solution)/shard_map/ppermute | solution.py:416
  61.6 3.6 %shard_map.120.inner_ref = bf16[224,1536]{1,0:T(8,128)(2,1)S(1)} custom-call(bf16[256,1536]{1,0:T(8,128)(2,1)S(1)} %get-tuple-element.42.normed_ref, f32[31,1536]{1,0:T(8,128)S(1)} %copy-done.3), custom_call_target="tpu_custom_call" | custom-call | flops 1365245952 | bytes 1572864 | tf_op jit(solution)/shard_map/pallas_call | solution.py:190
  65.2 0.0 collective-permute-done.4.low_ref
  65.2 2.2 %shard_map.121 = (bf16[256,1536]{1,0:T(8,128)(2,1)S(1)}, bf16[128,1536]{1,0:T(8,128)(2,1)S(1)}, bf16[256,1536]{1,0:T(8,128)(2,1)}) custom-call(bf16[256,1536]{1,0:T(8,128)(2,1)S(1)} %get-tuple-element.42.normed_ref, bf16[224,1536]{1,0:T(8,128)(2,1)S(1)} %shard_map.120.inner_ref, bf16[16,1536]{1,0:T(8,128)(2,1)S(1)} %collective-permute-done.4.low_ref, ...), custom_call_target="tpu_custom_call" | custom-call | flops 301989888 | bytes 3145728 | tf_op jit(solution)/shard_map/pallas_call | solution.py:232
  67.4 0.1 reshape.28
  67.5 17.3 %all_to_all.20 = bf16[32,4,1536]{2,1,0:T(4,128)(2,1)S(1)} all-to-all(bf16[32,4,1536]{2,1,0:T(4,128)(2,1)S(1)} %reshape.28), channel_id=1, replica_groups=mesh['tm'=32,'expert'=4] {'tm'}, dimensions={0} | all-to-all | bytes 786432 | tf_op jit(solution)/shard_map/all_to_all | solution.py:440
  84.8 0.1 reshape.29.own
  84.9 3.7 %all-to-all-start.1 = ((bf16[32,8,1536]{2,1,0:T(8,128)(2,1)}), bf16[32,8,1536]{2,1,0:T(8,128)(2,1)S(1)}, u32[]{:S(2)}, u32[]{:S(2)}) async-start(bf16[32,8,1536]{2,1,0:T(8,128)(2,1)} %bitcast.5), calls=%async_computation.1 | async-start | bytes 1572864 | tf_op jit(solution)/shard_map/all_to_all | solution.py:440
  88.6 0.1 collective-permute-start.6
  88.7 2.7 %collective-permute-start.7 = (bf16[128,1536]{1,0:T(8,128)(2,1)S(1)}, bf16[128,1536]{1,0:T(8,128)(2,1)S(1)}, u32[]{:S(2)}, u32[]{:S(2)}) collective-permute-start(bf16[128,1536]{1,0:T(8,128)(2,1)S(1)} %reshape.29.own), channel_id=1, source_target_pairs={{1,0},{2,1},{3,2},{0,3},{5,4},{6,5},{7,6},{4,7},{9,8},{10,9},{11,1... | collective-permute-start | bytes 1179656 | tf_op jit(solution)/shard_map/ppermute | solution.py:444
  91.4 0.7 collective-permute-start.8
  92.1 10.6 %all-to-all-done.1 = bf16[32,8,1536]{2,1,0:T(8,128)(2,1)S(1)} async-done(((bf16[32,8,1536]{2,1,0:T(8,128)(2,1)}), bf16[32,8,1536]{2,1,0:T(8,128)(2,1)S(1)}, u32[]{:S(2)}, u32[]{:S(2)}) %all-to-all-start.1) | async-done | bytes 786464 | tf_op jit(solution)/shard_map/all_to_all | solution.py:440
  102.7 2.0 collective-permute-start.10
  104.7 0.0 collective-permute-start.9
  104.7 0.0 collective-permute-done.6.left
  104.7 2.8 %collective-permute-done.7.right = bf16[128,1536]{1,0:T(8,128)(2,1)S(1)} collective-permute-done((bf16[128,1536]{1,0:T(8,128)(2,1)S(1)}, bf16[128,1536]{1,0:T(8,128)(2,1)S(1)}, u32[]{:S(2)}, u32[]{:S(2)}) %collective-permute-start.7) | collective-permute-done | bytes 393248 | tf_op jit(solution)/shard_map/ppermute | solution.py:444
  107.5 2.0 collective-permute-done.8.rest_0_
  109.5 9.0 %shard_map.122 = (bf16[2,64,1536]{2,1,0:T(8,128)(2,1)S(1)}, bf16[2,64,1536]{2,1,0:T(8,128)(2,1)S(1)}, bf16[2,64,1536]{2,1,0:T(8,128)(2,1)S(1)}, bf16[2,64,1536]{2,1,0:T(8,128)(2,1)S(1)}) custom-call(bf16[128,1536]{1,0:T(8,128)(2,1)S(1)} %reshape.29.own, bf16[128,1536]{1,0:T(8,128)(2,1)S(1)} %collective-permute-done.6.left, ...), custom_call_target="tpu_custom_call" | custom-call | flops 4831838208 | bytes 18874368 | tf_op jit(solution)/shard_map/pallas_call | solution.py:339
  118.6 6.3 %collective-permute-done.10.right = bf16[256,1536]{1,0:T(8,128)(2,1)S(1)} collective-permute-done((bf16[256,1536]{1,0:T(8,128)(2,1)S(1)}, bf16[256,1536]{1,0:T(8,128)(2,1)S(1)}, u32[]{:S(2)}, u32[]{:S(2)}) %collective-permute-start.10) | collective-permute-done | bytes 786464 | tf_op jit(solution)/shard_map/ppermute | solution.py:444
  124.8 2.0 collective-permute-done.9.left
  126.8 1.0 collective-permute-start.11
  127.9 1.8 collective-permute-start.12
  129.7 8.7 %collective-permute-done.11.rest_0_ = bf16[128,1536]{1,0:T(8,128)(2,1)S(1)} collective-permute-done((bf16[128,1536]{1,0:T(8,128)(2,1)S(1)}, bf16[128,1536]{1,0:T(8,128)(2,1)S(1)}, u32[]{:S(2)}, u32[]{:S(2)}) %collective-permute-start.11) | collective-permute-done | bytes 393248 | tf_op jit(solution)/shard_map/ppermute | solution.py:462
  138.4 2.7 %collective-permute-start.14 = (bf16[2,64,1536]{2,1,0:T(8,128)(2,1)S(1)}, bf16[2,64,1536]{2,1,0:T(8,128)(2,1)S(1)}, u32[]{:S(2)}, u32[]{:S(2)}) collective-permute-start(bf16[2,64,1536]{2,1,0:T(8,128)(2,1)S(1)} %get-tuple-element.59), channel_id=1, source_target_pairs={{1,0},{2,1},{3,2},{0,3},{5,4},{6,5},{7,6},{4,7},{9,8},{10,9},{11,1... | collective-permute-start | bytes 1179656 | tf_op jit(solution)/shard_map/ppermute | solution.py:466
  141.0 1.0 collective-permute-start.15
  142.0 15.5 %shard_map.123 = (bf16[2,128,1536]{2,1,0:T(8,128)(2,1)S(1)}, bf16[2,128,1536]{2,1,0:T(8,128)(2,1)}, bf16[2,128,1536]{2,1,0:T(8,128)(2,1)}, bf16[128,1536]{1,0:T(8,128)(2,1)S(1)}, bf16[128,1536]{1,0:T(8,128)(2,1)S(1)}) custom-call(bf16[256,1536]{1,0:T(8,128)(2,1)S(1)} %bitcast.18, bf16[256,1536]{1,0:T(8,128)(2,1)S(1)} %collective-permute-done.9.left, ...), custom_call_target="tpu_custom_call" | custom-call | flops 9663676416 | bytes 18874368 | tf_op jit(solution)/shard_map/pallas_call | solution.py:339
  157.6 0.0 copy-start.7
  157.6 0.3 collective-permute-done.15.refs_3_
  157.9 0.6 collective-permute-start.16
  158.5 2.1 collective-permute-start.17
  160.6 0.4 shard_map.124
  161.0 0.8 reshape.32
  161.8 20.3 %all_to_all.21 = bf16[32,4,1536]{2,1,0:T(4,128)(2,1)} all-to-all(bf16[32,4,1536]{2,1,0:T(4,128)(2,1)} %reshape.32), channel_id=1, replica_groups=mesh['tm'=32,'expert'=4] {'tm'}, dimensions={0} | all-to-all | bytes 786432 | tf_op jit(solution)/shard_map/all_to_all | solution.py:448
  182.1 1.1 reshape.33.rest_0_
  183.2 1.1 fusion
  184.3 0.6 collective-permute-start.19
  184.9 1.1 fusion.1
  186.0 1.0 collective-permute-start.18
  187.0 8.2 %collective-permute-done.19.refs_4_ = bf16[128,1536]{1,0:T(8,128)(2,1)S(1)} collective-permute-done((bf16[128,1536]{1,0:T(8,128)(2,1)S(1)}, bf16[128,1536]{1,0:T(8,128)(2,1)S(1)}, u32[]{:S(2)}, u32[]{:S(2)}) %collective-permute-start.19) | collective-permute-done | bytes 393248 | tf_op jit(solution)/shard_map/ppermute | solution.py:477
  195.2 2.7 %collective-permute-done.18.refs_3_ = bf16[128,1536]{1,0:T(8,128)(2,1)S(1)} collective-permute-done((bf16[128,1536]{1,0:T(8,128)(2,1)S(1)}, bf16[128,1536]{1,0:T(8,128)(2,1)S(1)}, u32[]{:S(2)}, u32[]{:S(2)}) %collective-permute-start.18) | collective-permute-done | bytes 393248 | tf_op jit(solution)/shard_map/ppermute | solution.py:477
  197.9 1.4 shard_map.125
  199.3 4.5 %all-to-all-start.3 = ((bf16[32,8,1536]{2,1,0:T(8,128)(2,1)}), bf16[32,8,1536]{2,1,0:T(8,128)(2,1)S(1)}, u32[]{:S(2)}, u32[]{:S(2)}) async-start(bf16[32,8,1536]{2,1,0:T(8,128)(2,1)} %bitcast.9), calls=%async_computation.3 | async-start | bytes 1572864 | tf_op jit(solution)/shard_map/all_to_all | solution.py:448
  203.8 0.1 copy.14.place_ref
  203.9 0.1 copy.13.gate_ref
  204.1 14.0 %all-to-all-done.3 = bf16[32,8,1536]{2,1,0:T(8,128)(2,1)S(1)} async-done(((bf16[32,8,1536]{2,1,0:T(8,128)(2,1)}), bf16[32,8,1536]{2,1,0:T(8,128)(2,1)S(1)}, u32[]{:S(2)}, u32[]{:S(2)}) %all-to-all-start.3) | async-done | bytes 786464 | tf_op jit(solution)/shard_map/all_to_all | solution.py:448
  218.1 1.7 shard_map.126
  (23 shorter events, 0.1 us)
Async XLA Ops:
  0.0 48.4 %copy-start = (bf16[2,256,1536]{2,1,0:T(8,128)(2,1)S(1)}, bf16[2,256,1536]{2,1,0:T(8,128)(2,1)}, u32[]{:S(2)}) copy-start(bf16[2,256,1536]{2,1,0:T(8,128)(2,1)} %kv_ref.3) | copy-start | bytes 4718596
  0.0 48.4 %copy-start.4 = (bf16[256,1536]{1,0:T(8,128)(2,1)S(1)}, bf16[256,1536]{1,0:T(8,128)(2,1)}, u32[]{:S(2)}) copy-start(bf16[256,1536]{1,0:T(8,128)(2,1)} %q_ref.3) | copy-start | bytes 2359300
  0.0 61.6 %copy-start.3 = (f32[31,1536]{1,0:T(8,128)S(1)}, f32[31,1536]{1,0:T(8,128)}, u32[]{:S(2)}) copy-start(f32[31,1536]{1,0:T(8,128)} %taps_ref.3) | copy-start | bytes 571396
  2.4 26.5 %collective-permute-start.2 = (bf16[2,256,1024]{2,1,0:T(8,128)(2,1)}, bf16[2,256,1024]{2,1,0:T(8,128)(2,1)}, u32[]{:S(2)}, u32[]{:S(2)}) collective-permute-start(bf16[2,256,1024]{2,1,0:T(8,128)(2,1)} %slice.18), channel_id=1, source_target_pairs={{0,1},{1,2},{2,3},{3,4},{4,5},{5,6},{6,7},{7,8},{8,9},{9,10},{10,1... | collective-permute-start | bytes 3145736 | tf_op jit(solution)/shard_map/ppermute | solution.py:409
  6.8 33.5 %collective-permute-start.3 = (bf16[2,256,1024]{2,1,0:T(8,128)(2,1)}, bf16[2,256,1024]{2,1,0:T(8,128)(2,1)}, u32[]{:S(2)}, u32[]{:S(2)}) collective-permute-start(bf16[2,256,1024]{2,1,0:T(8,128)(2,1)} %slice.18), channel_id=1, source_target_pairs={{1,0},{2,1},{3,2},{4,3},{5,4},{6,5},{7,6},{8,7},{9,8},{10,9},{11,1... | collective-permute-start | bytes 3145736 | tf_op jit(solution)/shard_map/ppermute | solution.py:410
  13.3 35.1 %collective-permute-start = (bf16[2,256,512]{2,1,0:T(8,128)(2,1)}, bf16[2,256,512]{2,1,0:T(8,128)(2,1)S(1)}, u32[]{:S(2)}, u32[]{:S(2)}) collective-permute-start(bf16[2,256,512]{2,1,0:T(8,128)(2,1)} %slice.19), channel_id=1, source_target_pairs={{0,1},{1,2},{2,3},{3,4},{4,5},{5,6},{6,7},{7,8},{8,9},{9,10},{10,1... | collective-permute-start | bytes 1572872 | tf_op jit(solution)/shard_map/ppermute | solution.py:409
  15.2 33.2 %collective-permute-start.1 = (bf16[2,256,512]{2,1,0:T(8,128)(2,1)}, bf16[2,256,512]{2,1,0:T(8,128)(2,1)}, u32[]{:S(2)}, u32[]{:S(2)}) collective-permute-start(bf16[2,256,512]{2,1,0:T(8,128)(2,1)} %slice.19), channel_id=1, source_target_pairs={{1,0},{2,1},{3,2},{4,3},{5,4},{6,5},{7,6},{8,7},{9,8},{10,9},{11,1... | collective-permute-start | bytes 1572872 | tf_op jit(solution)/shard_map/ppermute | solution.py:410
  20.7 27.8 %copy-start.5 = (s32[2]{0:T(128)S(1)}, s32[2]{0:T(128)}, u32[]{:S(2)}) copy-start(s32[2]{0:T(128)} %add_convert_fusion.edge_ref) | copy-start | bytes 28
  48.4 1.2 copy-start.6
  54.1 11.1 %collective-permute-start.4 = (bf16[16,1536]{1,0:T(8,128)(2,1)S(1)}, bf16[16,1536]{1,0:T(8,128)(2,1)S(1)}, u32[]{:S(2)}, u32[]{:S(2)}) collective-permute-start(bf16[16,1536]{1,0:T(8,128)(2,1)S(1)} %get-tuple-element.43), channel_id=1, source_target_pairs={{0,1},{1,2},{2,3},{3,4},{4,5},{5,6},{6,7},{7,8},{8,9},{9,10},{10,1... | collective-permute-start | bytes 147464 | tf_op jit(solution)/shard_map/ppermute | solution.py:415
  56.0 9.2 %collective-permute-start.5 = (bf16[16,1536]{1,0:T(8,128)(2,1)S(1)}, bf16[16,1536]{1,0:T(8,128)(2,1)S(1)}, u32[]{:S(2)}, u32[]{:S(2)}) collective-permute-start(bf16[16,1536]{1,0:T(8,128)(2,1)S(1)} %get-tuple-element.44), channel_id=1, source_target_pairs={{1,0},{2,1},{3,2},{4,3},{5,4},{6,5},{7,6},{8,7},{9,8},{10,9},{11,1... | collective-permute-start | bytes 147464 | tf_op jit(solution)/shard_map/ppermute | solution.py:416
  84.9 17.8 %all-to-all-start.1 = ((bf16[32,8,1536]{2,1,0:T(8,128)(2,1)}), bf16[32,8,1536]{2,1,0:T(8,128)(2,1)S(1)}, u32[]{:S(2)}, u32[]{:S(2)}) async-start(bf16[32,8,1536]{2,1,0:T(8,128)(2,1)} %bitcast.5), calls=%async_computation.1 | async-start | bytes 1572864 | tf_op jit(solution)/shard_map/all_to_all | solution.py:440
  88.6 16.1 %collective-permute-start.6 = (bf16[128,1536]{1,0:T(8,128)(2,1)S(1)}, bf16[128,1536]{1,0:T(8,128)(2,1)S(1)}, u32[]{:S(2)}, u32[]{:S(2)}) collective-permute-start(bf16[128,1536]{1,0:T(8,128)(2,1)S(1)} %reshape.29.own), channel_id=1, source_target_pairs={{0,1},{1,2},{2,3},{3,0},{4,5},{5,6},{6,7},{7,4},{8,9},{9,10},{10,1... | collective-permute-start | bytes 1179656 | tf_op jit(solution)/shard_map/ppermute | solution.py:444
  88.7 18.8 %collective-permute-start.7 = (bf16[128,1536]{1,0:T(8,128)(2,1)S(1)}, bf16[128,1536]{1,0:T(8,128)(2,1)S(1)}, u32[]{:S(2)}, u32[]{:S(2)}) collective-permute-start(bf16[128,1536]{1,0:T(8,128)(2,1)S(1)} %reshape.29.own), channel_id=1, source_target_pairs={{1,0},{2,1},{3,2},{0,3},{5,4},{6,5},{7,6},{4,7},{9,8},{10,9},{11,1... | collective-permute-start | bytes 1179656 | tf_op jit(solution)/shard_map/ppermute | solution.py:444
  91.4 18.1 %collective-permute-start.8 = (bf16[128,1536]{1,0:T(8,128)(2,1)S(1)}, bf16[128,1536]{1,0:T(8,128)(2,1)S(1)}, u32[]{:S(2)}, u32[]{:S(2)}) collective-permute-start(bf16[128,1536]{1,0:T(8,128)(2,1)S(1)} %reshape.29.own), channel_id=1, source_target_pairs={{0,2},{1,3},{2,0},{3,1},{4,6},{5,7},{6,4},{7,5},{8,10},{9,11},{10,... | collective-permute-start | bytes 1179656 | tf_op jit(solution)/shard_map/ppermute | solution.py:455
  102.7 22.1 %collective-permute-start.10 = (bf16[256,1536]{1,0:T(8,128)(2,1)S(1)}, bf16[256,1536]{1,0:T(8,128)(2,1)S(1)}, u32[]{:S(2)}, u32[]{:S(2)}) collective-permute-start(bf16[256,1536]{1,0:T(8,128)(2,1)S(1)} %bitcast.16), channel_id=1, source_target_pairs={{1,0},{2,1},{3,2},{0,3},{5,4},{6,5},{7,6},{4,7},{9,8},{10,9},{11,1... | collective-permute-start | bytes 2359304 | tf_op jit(solution)/shard_map/ppermute | solution.py:444
  104.7 22.1 %collective-permute-start.9 = (bf16[256,1536]{1,0:T(8,128)(2,1)S(1)}, bf16[256,1536]{1,0:T(8,128)(2,1)S(1)}, u32[]{:S(2)}, u32[]{:S(2)}) collective-permute-start(bf16[256,1536]{1,0:T(8,128)(2,1)S(1)} %bitcast.17), channel_id=1, source_target_pairs={{0,1},{1,2},{2,3},{3,0},{4,5},{5,6},{6,7},{7,4},{8,9},{9,10},{10,1... | collective-permute-start | bytes 2359304 | tf_op jit(solution)/shard_map/ppermute | solution.py:444
  126.8 11.5 %collective-permute-start.11 = (bf16[128,1536]{1,0:T(8,128)(2,1)S(1)}, bf16[128,1536]{1,0:T(8,128)(2,1)S(1)}, u32[]{:S(2)}, u32[]{:S(2)}) collective-permute-start(bf16[128,1536]{1,0:T(8,128)(2,1)S(1)} %slice.20), channel_id=1, source_target_pairs={{0,1},{1,2},{2,3},{3,0},{4,5},{5,6},{6,7},{7,4},{8,9},{9,10},{10,1... | collective-permute-start | bytes 1179656 | tf_op jit(solution)/shard_map/ppermute | solution.py:462
  127.9 10.5 %collective-permute-start.12 = (bf16[128,1536]{1,0:T(8,128)(2,1)S(1)}, bf16[128,1536]{1,0:T(8,128)(2,1)S(1)}, u32[]{:S(2)}, u32[]{:S(2)}) collective-permute-start(bf16[128,1536]{1,0:T(8,128)(2,1)S(1)} %slice.21), channel_id=1, source_target_pairs={{1,0},{2,1},{3,2},{0,3},{5,4},{6,5},{7,6},{4,7},{9,8},{10,9},{11,1... | collective-permute-start | bytes 1179656 | tf_op jit(solution)/shard_map/ppermute | solution.py:462
  138.4 19.2 %collective-permute-start.13 = (bf16[2,64,1536]{2,1,0:T(8,128)(2,1)S(1)}, bf16[2,64,1536]{2,1,0:T(8,128)(2,1)S(1)}, u32[]{:S(2)}, u32[]{:S(2)}) collective-permute-start(bf16[2,64,1536]{2,1,0:T(8,128)(2,1)S(1)} %get-tuple-element.58), channel_id=1, source_target_pairs={{0,1},{1,2},{2,3},{3,0},{4,5},{5,6},{6,7},{7,4},{8,9},{9,10},{10,1... | collective-permute-start | bytes 1179656 | tf_op jit(solution)/shard_map/ppermute | solution.py:465
  138.4 19.2 %collective-permute-start.14 = (bf16[2,64,1536]{2,1,0:T(8,128)(2,1)S(1)}, bf16[2,64,1536]{2,1,0:T(8,128)(2,1)S(1)}, u32[]{:S(2)}, u32[]{:S(2)}) collective-permute-start(bf16[2,64,1536]{2,1,0:T(8,128)(2,1)S(1)} %get-tuple-element.59), channel_id=1, source_target_pairs={{1,0},{2,1},{3,2},{0,3},{5,4},{6,5},{7,6},{4,7},{9,8},{10,9},{11,1... | collective-permute-start | bytes 1179656 | tf_op jit(solution)/shard_map/ppermute | solution.py:466
  141.0 16.9 %collective-permute-start.15 = (bf16[2,64,1536]{2,1,0:T(8,128)(2,1)S(1)}, bf16[2,64,1536]{2,1,0:T(8,128)(2,1)S(1)}, u32[]{:S(2)}, u32[]{:S(2)}) collective-permute-start(bf16[2,64,1536]{2,1,0:T(8,128)(2,1)S(1)} %get-tuple-element.60), channel_id=1, source_target_pairs={{0,2},{1,3},{2,0},{3,1},{4,6},{5,7},{6,4},{7,5},{8,10},{9,11},{10,... | collective-permute-start | bytes 1179656 | tf_op jit(solution)/shard_map/ppermute | solution.py:467
  157.5 1.0 copy-start.1
  157.6 3.1 %copy-start.2 = (bf16[128,1536]{1,0:T(8,128)(2,1)}, bf16[128,1536]{1,0:T(8,128)(2,1)S(1)}, u32[]{:S(2)}) copy-start(bf16[128,1536]{1,0:T(8,128)(2,1)S(1)} %get-tuple-element.72) | copy-start | bytes 1179652
  157.6 46.4 %copy-start.7 = (f32[256]{0:T(256)S(1)}, f32[256]{0:T(256)}, u32[]{:S(2)}) copy-start(f32[256]{0:T(256)} %param.17) | copy-start | bytes 3076
  157.9 25.3 %collective-permute-start.16 = (bf16[2,128,1536]{2,1,0:T(8,128)(2,1)}, bf16[2,128,1536]{2,1,0:T(8,128)(2,1)S(1)}, u32[]{:S(2)}, u32[]{:S(2)}) collective-permute-start(bf16[2,128,1536]{2,1,0:T(8,128)(2,1)} %get-tuple-element.67), channel_id=1, source_target_pairs={{0,1},{1,2},{2,3},{3,0},{4,5},{5,6},{6,7},{7,4},{8,9},{9,10},{10,1... | collective-permute-start | bytes 2359304 | tf_op jit(solution)/shard_map/ppermute | solution.py:472
  158.5 24.7 %collective-permute-start.17 = (bf16[2,128,1536]{2,1,0:T(8,128)(2,1)}, bf16[2,128,1536]{2,1,0:T(8,128)(2,1)S(1)}, u32[]{:S(2)}, u32[]{:S(2)}) collective-permute-start(bf16[2,128,1536]{2,1,0:T(8,128)(2,1)} %get-tuple-element.68), channel_id=1, source_target_pairs={{1,0},{2,1},{3,2},{0,3},{5,4},{6,5},{7,6},{4,7},{9,8},{10,9},{11,1... | collective-permute-start | bytes 2359304 | tf_op jit(solution)/shard_map/ppermute | solution.py:472
  184.3 10.9 %collective-permute-start.19 = (bf16[128,1536]{1,0:T(8,128)(2,1)S(1)}, bf16[128,1536]{1,0:T(8,128)(2,1)S(1)}, u32[]{:S(2)}, u32[]{:S(2)}) collective-permute-start(bf16[128,1536]{1,0:T(8,128)(2,1)S(1)} %fusion), channel_id=1, source_target_pairs={{1,0},{2,1},{3,2},{0,3},{5,4},{6,5},{7,6},{4,7},{9,8},{10,9},{11,1... | collective-permute-start | bytes 1179656 | tf_op jit(solution)/shard_map/ppermute | solution.py:477
  186.0 11.8 %collective-permute-start.18 = (bf16[128,1536]{1,0:T(8,128)(2,1)S(1)}, bf16[128,1536]{1,0:T(8,128)(2,1)S(1)}, u32[]{:S(2)}, u32[]{:S(2)}) collective-permute-start(bf16[128,1536]{1,0:T(8,128)(2,1)S(1)} %fusion.1), channel_id=1, source_target_pairs={{0,1},{1,2},{2,3},{3,0},{4,5},{5,6},{6,7},{7,4},{8,9},{9,10},{10,1... | collective-permute-start | bytes 1179656 | tf_op jit(solution)/shard_map/ppermute | solution.py:477
  199.3 18.9 %all-to-all-start.3 = ((bf16[32,8,1536]{2,1,0:T(8,128)(2,1)}), bf16[32,8,1536]{2,1,0:T(8,128)(2,1)S(1)}, u32[]{:S(2)}, u32[]{:S(2)}) async-start(bf16[32,8,1536]{2,1,0:T(8,128)(2,1)} %bitcast.9), calls=%async_computation.3 | async-start | bytes 1572864 | tf_op jit(solution)/shard_map/all_to_all | solution.py:448

commit v9 on v7

--- a/solution.py
+++ b/solution.py
@@ -256,7 +256,7 @@
 
 def combine(mixed, gate, place, parts):
     rows, width = mixed.shape
-    block = 256
+    block = width // 2
     column = lambda n: pl.BlockSpec((n, block), lambda j: (0, j))
     fixed = pl.BlockSpec((rows, 1), lambda j: (0, 0))
     return call(

time: 217 us -> 215 us (level)
  no operation moved by 1% of the time
where the time goes in v9:
time: 215 us
  waiting for transfers between devices  64.7 us (30%)
  starting transfers between devices  56.2 us (26%)
  Pallas kernels  45.4 us (21%)
  blocking collectives  36.3 us (17%)
  local copies, waits for them, and re-layouts  10.1 us (5%)
    all_to_all x2, blocking collectives, arrive(): got = lax.all_to_all(sent, 'tm', split_axis=0, concat_axis=0, tiled=True)  36.3 us
    pallas_call x2, Pallas kernels, ffn(): call(functools.partial(ffn_body, direct), [pair] * 4 if direct else [pair...  24.3 us
    all_to_all x2, starting transfers between devices, leave(): got = lax.all_to_all(summed, 'tm', split_axis=0, concat_axis=0, tiled=True)  17.6 us
    ppermute x1, waiting for transfers between devices, on_device(): lax.ppermute(to_right, 'expert', up)  17.5 us
    ppermute x2, waiting for transfers between devices, on_device(): high.append(lax.ppermute(part, order, back))  11.4 us
    all_to_all x2, waiting for transfers between devices, leave(): got = lax.all_to_all(summed, 'tm', split_axis=0, concat_axis=0, tiled=True)  10 us
    ppermute x2, starting transfers between devices, on_device(): high.append(lax.ppermute(part, order, back))  9.46 us
    pallas_call x1, Pallas kernels, attention(): call(attend_body, jax.ShapeDtypeStruct((rows, pairs * PAIR), F32), cost,...  8.08 us
  transfers between devices with their start and end apart: 22, of which 10 were waited for; matrix products, arithmetic and copies ran while one was open for 3% of the time, Pallas kernels for 17%

profile of v9, /device:TPU:1, one launch (start us, length us, event | category | flops | bytes accessed | tf_op | source)
XLA Modules:
  0.0 214.6 jit_solution(9065976200872718657)
XLA Ops:
  0.0 2.4 %slice.18 = bf16[2,256,1024]{2,1,0:T(8,128)(2,1)} slice(bf16[2,256,1536]{2,1,0:T(8,128)(2,1)} %kv_ref.3), slice={[0:2], [0:256], [0:1024]} | slice | bytes 2097152 | tf_op jit(solution)/shard_map/slice | solution.py:408
  2.4 4.4 %collective-permute-start.2 = (bf16[2,256,1024]{2,1,0:T(8,128)(2,1)}, bf16[2,256,1024]{2,1,0:T(8,128)(2,1)}, u32[]{:S(2)}, u32[]{:S(2)}) collective-permute-start(bf16[2,256,1024]{2,1,0:T(8,128)(2,1)} %slice.18), channel_id=1, source_target_pairs={{0,1},{1,2},{2,3},{3,4},{4,5},{5,6},{6,7},{7,8},{8,9},{9,10},{10,1... | collective-permute-start | bytes 3145736 | tf_op jit(solution)/shard_map/ppermute | solution.py:409
  6.8 4.6 %collective-permute-start.3 = (bf16[2,256,1024]{2,1,0:T(8,128)(2,1)}, bf16[2,256,1024]{2,1,0:T(8,128)(2,1)}, u32[]{:S(2)}, u32[]{:S(2)}) collective-permute-start(bf16[2,256,1024]{2,1,0:T(8,128)(2,1)} %slice.18), channel_id=1, source_target_pairs={{1,0},{2,1},{3,2},{4,3},{5,4},{6,5},{7,6},{8,7},{9,8},{10,9},{11,1... | collective-permute-start | bytes 3145736 | tf_op jit(solution)/shard_map/ppermute | solution.py:410
  11.4 1.9 slice.19
  13.3 1.9 collective-permute-start
  15.2 4.9 %collective-permute-start.1 = (bf16[2,256,512]{2,1,0:T(8,128)(2,1)}, bf16[2,256,512]{2,1,0:T(8,128)(2,1)}, u32[]{:S(2)}, u32[]{:S(2)}) collective-permute-start(bf16[2,256,512]{2,1,0:T(8,128)(2,1)} %slice.19), channel_id=1, source_target_pairs={{1,0},{2,1},{3,2},{4,3},{5,4},{6,5},{7,6},{8,7},{9,8},{10,9},{11,1... | collective-permute-start | bytes 1572872 | tf_op jit(solution)/shard_map/ppermute | solution.py:410
  20.1 0.7 add_convert_fusion.edge_ref
  20.7 0.7 broadcast_in_dim.15.gain_ref
  21.4 0.7 broadcast_in_dim.16.gain_ref
  22.2 0.7 compare_select_fusion.1
  22.9 6.0 %collective-permute-done.2.lo_ref = bf16[2,256,1024]{2,1,0:T(8,128)(2,1)} collective-permute-done((bf16[2,256,1024]{2,1,0:T(8,128)(2,1)}, bf16[2,256,1024]{2,1,0:T(8,128)(2,1)}, u32[]{:S(2)}, u32[]{:S(2)}) %collective-permute-start.2) | collective-permute-done | bytes 1048608 | tf_op jit(solution)/shard_map/ppermute | solution.py:409
  28.9 11.4 %collective-permute-done.3.hi_ref = bf16[2,256,1024]{2,1,0:T(8,128)(2,1)} collective-permute-done((bf16[2,256,1024]{2,1,0:T(8,128)(2,1)}, bf16[2,256,1024]{2,1,0:T(8,128)(2,1)}, u32[]{:S(2)}, u32[]{:S(2)}) %collective-permute-start.3) | collective-permute-done | bytes 1048608 | tf_op jit(solution)/shard_map/ppermute | solution.py:410
  40.3 8.1 %shard_map.118.rest_0_ = f32[256,1024]{1,0:T(8,128)} custom-call(s32[2]{0:T(128)} %add_convert_fusion.edge_ref, bf16[256,1536]{1,0:T(8,128)(2,1)} %q_ref.3, bf16[2,256,1536]{2,1,0:T(8,128)(2,1)} %kv_ref.3, bf16[2,256,1024]{2,1,0:T(8,128)(2,1)} %collective-permute-done.2.lo_ref, bf16[2,256,1024]{2,1,0:T(8,128)(2,1)} %collective-permute-done.3.hi_ref), custom_call_target="tpu_custom_call" | custom-call | flops 2684354560 | bytes 3670016 | tf_op jit(solution)/shard_map/pallas_call | solution.py:138
  48.4 0.0 collective-permute-done.lo_ref
  48.4 0.0 collective-permute-done.1.hi_ref
  48.4 1.2 copy-done.4
  49.7 4.4 %shard_map.119 = (bf16[256,1536]{1,0:T(8,128)(2,1)S(1)}, bf16[16,1536]{1,0:T(8,128)(2,1)S(1)}, bf16[16,1536]{1,0:T(8,128)(2,1)S(1)}) custom-call(s32[2]{0:T(128)S(1)} %copy-done.3, bf16[256,1536]{1,0:T(8,128)(2,1)S(1)} %copy-done.2, bf16[2,256,1536]{2,1,0:T(8,128)(2,1)S(1)} %copy-done, bf16[2,256,512]{2,1,0:T(8,128)(2,1)S(1)} %collective-permute-done.lo_ref, ...), custom_call_target="tpu_custom_call" | custom-call | flops 1342177280 | bytes 1835008 | tf_op jit(solution)/shard_map/pallas_call | solution.py:151
  54.1 1.9 collective-permute-start.4
  56.0 5.6 %collective-permute-start.5 = (bf16[16,1536]{1,0:T(8,128)(2,1)S(1)}, bf16[16,1536]{1,0:T(8,128)(2,1)S(1)}, u32[]{:S(2)}, u32[]{:S(2)}) collective-permute-start(bf16[16,1536]{1,0:T(8,128)(2,1)S(1)} %get-tuple-element.40), channel_id=1, source_target_pairs={{1,0},{2,1},{3,2},{4,3},{5,4},{6,5},{7,6},{8,7},{9,8},{10,9},{11,1... | collective-permute-start | bytes 147464 | tf_op jit(solution)/shard_map/ppermute | solution.py:416
  61.6 3.6 %shard_map.120.inner_ref = bf16[224,1536]{1,0:T(8,128)(2,1)S(1)} custom-call(bf16[256,1536]{1,0:T(8,128)(2,1)S(1)} %get-tuple-element.38.normed_ref, f32[31,1536]{1,0:T(8,128)S(1)} %copy-done.1), custom_call_target="tpu_custom_call" | custom-call | flops 1365245952 | bytes 1572864 | tf_op jit(solution)/shard_map/pallas_call | solution.py:190
  65.2 0.0 collective-permute-done.4.low_ref
  65.2 0.0 collective-permute-done.5.high_ref
  65.2 1.4 shard_map.121
  66.7 21.2 %all_to_all.20 = bf16[32,8,1536]{2,1,0:T(8,128)(2,1)S(1)} all-to-all(bf16[32,8,1536]{2,1,0:T(8,128)(2,1)S(1)} %bitcast.19), channel_id=1, replica_groups=mesh['tm'=32,'expert'=4] {'tm'}, dimensions={0} | all-to-all | bytes 1572864 | tf_op jit(solution)/shard_map/all_to_all | solution.py:440
  87.9 0.0 collective-permute-start.6
  87.9 2.7 %collective-permute-start.7 = (bf16[256,1536]{1,0:T(8,128)(2,1)S(1)}, bf16[256,1536]{1,0:T(8,128)(2,1)S(1)}, u32[]{:S(2)}, u32[]{:S(2)}) collective-permute-start(bf16[256,1536]{1,0:T(8,128)(2,1)S(1)} %bitcast.17), channel_id=1, source_target_pairs={{1,0},{2,1},{3,2},{0,3},{5,4},{6,5},{7,6},{4,7},{9,8},{10,9},{11,1... | collective-permute-start | bytes 2359304 | tf_op jit(solution)/shard_map/ppermute | solution.py:444
  90.6 0.8 reshape.30
  91.4 15.1 %all_to_all.21 = bf16[32,4,1536]{2,1,0:T(4,128)(2,1)} all-to-all(bf16[32,4,1536]{2,1,0:T(4,128)(2,1)} %reshape.30), channel_id=1, replica_groups=mesh['tm'=32,'expert'=4] {'tm'}, dimensions={0} | all-to-all | bytes 786432 | tf_op jit(solution)/shard_map/all_to_all | solution.py:440
  106.5 1.1 reshape.31.own
  107.6 0.8 collective-permute-done.6.left
  108.3 0.0 collective-permute-done.7.right
  108.4 0.2 collective-permute-start.8
  108.6 2.6 %collective-permute-start.9 = (bf16[128,1536]{1,0:T(8,128)(2,1)S(1)}, bf16[128,1536]{1,0:T(8,128)(2,1)S(1)}, u32[]{:S(2)}, u32[]{:S(2)}) collective-permute-start(bf16[128,1536]{1,0:T(8,128)(2,1)S(1)} %slice.21), channel_id=1, source_target_pairs={{1,0},{2,1},{3,2},{0,3},{5,4},{6,5},{7,6},{4,7},{9,8},{10,9},{11,1... | collective-permute-start | bytes 1179656 | tf_op jit(solution)/shard_map/ppermute | solution.py:458
  111.2 2.7 %collective-permute-start.13 = (bf16[128,1536]{1,0:T(8,128)(2,1)S(1)}, bf16[128,1536]{1,0:T(8,128)(2,1)S(1)}, u32[]{:S(2)}, u32[]{:S(2)}) collective-permute-start(bf16[128,1536]{1,0:T(8,128)(2,1)S(1)} %reshape.31.own), channel_id=1, source_target_pairs={{1,0},{2,1},{3,2},{0,3},{5,4},{6,5},{7,6},{4,7},{9,8},{10,9},{11,1... | collective-permute-start | bytes 1179656 | tf_op jit(solution)/shard_map/ppermute | solution.py:444
  113.9 0.0 collective-permute-start.14
  113.9 5.7 %collective-permute-done.8.rest_0_ = bf16[128,1536]{1,0:T(8,128)(2,1)S(1)} collective-permute-done((bf16[128,1536]{1,0:T(8,128)(2,1)S(1)}, bf16[128,1536]{1,0:T(8,128)(2,1)S(1)}, u32[]{:S(2)}, u32[]{:S(2)}) %collective-permute-start.8) | collective-permute-done | bytes 393248 | tf_op jit(solution)/shard_map/ppermute | solution.py:458
  119.6 14.4 %shard_map.122 = (bf16[2,128,1536]{2,1,0:T(8,128)(2,1)S(1)}, bf16[2,128,1536]{2,1,0:T(8,128)(2,1)S(1)}, bf16[2,128,1536]{2,1,0:T(8,128)(2,1)S(1)}, bf16[128,1536]{1,0:T(8,128)(2,1)S(1)}, bf16[128,1536]{1,0:T(8,128)(2,1)S(1)}) custom-call(bf16[256,1536]{1,0:T(8,128)(2,1)S(1)} %bitcast.18, bf16[256,1536]{1,0:T(8,128)(2,1)S(1)} %collective-permute-done.6.left, ...), custom_call_target="tpu_custom_call" | custom-call | flops 9663676416 | bytes 18874368 | tf_op jit(solution)/shard_map/pallas_call | solution.py:339
  134.0 0.5 collective-permute-start.10
  134.6 2.3 %collective-permute-start.11 = (bf16[2,128,1536]{2,1,0:T(8,128)(2,1)S(1)}, bf16[2,128,1536]{2,1,0:T(8,128)(2,1)S(1)}, u32[]{:S(2)}, u32[]{:S(2)}) collective-permute-start(bf16[2,128,1536]{2,1,0:T(8,128)(2,1)S(1)} %get-tuple-element.49), channel_id=1, source_target_pairs={{1,0},{2,1},{3,2},{0,3},{5,4},{6,5},{7,6},{4,7},{9,8},{10,9},{11,1... | collective-permute-start | bytes 2359304 | tf_op jit(solution)/shard_map/ppermute | solution.py:462
  136.9 0.3 collective-permute-done.14.rest_0_
  137.1 9.9 %shard_map.123 = (bf16[2,64,1536]{2,1,0:T(8,128)(2,1)S(1)}, bf16[2,64,1536]{2,1,0:T(8,128)(2,1)}, bf16[2,64,1536]{2,1,0:T(8,128)(2,1)}, bf16[2,64,1536]{2,1,0:T(8,128)(2,1)S(1)}) custom-call(bf16[128,1536]{1,0:T(8,128)(2,1)S(1)} %reshape.31.own, bf16[128,1536]{1,0:T(8,128)(2,1)S(1)} %collective-permute-done.12.left, ...), custom_call_target="tpu_custom_call" | custom-call | flops 4831838208 | bytes 18874368 | tf_op jit(solution)/shard_map/pallas_call | solution.py:339
  147.0 0.0 copy-start.5
  147.0 5.5 %collective-permute-done.10.refs_2_ = bf16[2,128,1536]{2,1,0:T(8,128)(2,1)S(1)} collective-permute-done((bf16[2,128,1536]{2,1,0:T(8,128)(2,1)S(1)}, bf16[2,128,1536]{2,1,0:T(8,128)(2,1)S(1)}, u32[]{:S(2)}, u32[]{:S(2)}) %collective-permute-start.10) | collective-permute-done | bytes 786464 | tf_op jit(solution)/shard_map/ppermute | solution.py:462
  152.6 0.0 collective-permute-done.11.refs_1_
  152.6 0.1 fusion
  152.7 1.2 collective-permute-start.16
  153.8 0.1 fusion.1
  153.9 0.4 collective-permute-start.15
  154.4 5.7 %collective-permute-done.16.refs_4_ = bf16[128,1536]{1,0:T(8,128)(2,1)S(1)} collective-permute-done((bf16[128,1536]{1,0:T(8,128)(2,1)S(1)}, bf16[128,1536]{1,0:T(8,128)(2,1)S(1)}, u32[]{:S(2)}, u32[]{:S(2)}) %collective-permute-start.16) | collective-permute-done | bytes 393248 | tf_op jit(solution)/shard_map/ppermute | solution.py:467
  160.1 1.8 collective-permute-done.15.refs_3_
  161.9 1.4 shard_map.124
  163.3 9.3 %all-to-all-start.2 = ((bf16[32,8,1536]{2,1,0:T(8,128)(2,1)}), bf16[32,8,1536]{2,1,0:T(8,128)(2,1)S(1)}, u32[]{:S(2)}, u32[]{:S(2)}) async-start(bf16[32,8,1536]{2,1,0:T(8,128)(2,1)} %bitcast.9), calls=%async_computation.2 | async-start | bytes 1572864 | tf_op jit(solution)/shard_map/all_to_all | solution.py:448
  172.6 0.1 collective-permute-start.17
  172.7 2.7 %collective-permute-start.18 = (bf16[2,64,1536]{2,1,0:T(8,128)(2,1)}, bf16[2,64,1536]{2,1,0:T(8,128)(2,1)S(1)}, u32[]{:S(2)}, u32[]{:S(2)}) collective-permute-start(bf16[2,64,1536]{2,1,0:T(8,128)(2,1)} %get-tuple-element.60), channel_id=1, source_target_pairs={{1,0},{2,1},{3,2},{0,3},{5,4},{6,5},{7,6},{4,7},{9,8},{10,9},{11,1... | collective-permute-start | bytes 1179656 | tf_op jit(solution)/shard_map/ppermute | solution.py:471
  175.4 0.0 collective-permute-start.19
  175.4 17.5 %collective-permute-done.17.refs_1_ = bf16[2,64,1536]{2,1,0:T(8,128)(2,1)S(1)} collective-permute-done((bf16[2,64,1536]{2,1,0:T(8,128)(2,1)}, bf16[2,64,1536]{2,1,0:T(8,128)(2,1)S(1)}, u32[]{:S(2)}, u32[]{:S(2)}) %collective-permute-start.17) | collective-permute-done | bytes 393248 | tf_op jit(solution)/shard_map/ppermute | solution.py:470
  192.9 0.4 shard_map.125
  193.3 0.8 reshape.34
  194.1 8.3 %all-to-all-start.3 = ((bf16[32,4,1536]{2,1,0:T(4,128)(2,1)}), bf16[32,4,1536]{2,1,0:T(4,128)(2,1)S(1)}, u32[]{:S(2)}, u32[]{:S(2)}) async-start(bf16[32,4,1536]{2,1,0:T(4,128)(2,1)} %reshape.34), calls=%async_computation.3 | async-start | bytes 786432 | tf_op jit(solution)/shard_map/all_to_all | solution.py:448
  202.4 0.1 copy.14.place_ref
  202.6 0.1 copy.13.gate_ref
  202.7 10.0 %all-to-all-done.3 = bf16[32,4,1536]{2,1,0:T(4,128)(2,1)S(1)} async-done(((bf16[32,4,1536]{2,1,0:T(4,128)(2,1)}), bf16[32,4,1536]{2,1,0:T(4,128)(2,1)S(1)}, u32[]{:S(2)}, u32[]{:S(2)}) %all-to-all-start.3) | async-done | bytes 393248 | tf_op jit(solution)/shard_map/all_to_all | solution.py:448
  212.7 0.1 reshape.35.rest_1_
  212.8 1.8 shard_map.126
  (19 shorter events, 0.1 us)
Async XLA Ops:
  0.0 48.4 %copy-start = (bf16[2,256,1536]{2,1,0:T(8,128)(2,1)S(1)}, bf16[2,256,1536]{2,1,0:T(8,128)(2,1)}, u32[]{:S(2)}) copy-start(bf16[2,256,1536]{2,1,0:T(8,128)(2,1)} %kv_ref.3) | copy-start | bytes 4718596
  0.0 48.4 %copy-start.2 = (bf16[256,1536]{1,0:T(8,128)(2,1)S(1)}, bf16[256,1536]{1,0:T(8,128)(2,1)}, u32[]{:S(2)}) copy-start(bf16[256,1536]{1,0:T(8,128)(2,1)} %q_ref.3) | copy-start | bytes 2359300
  0.0 61.6 %copy-start.1 = (f32[31,1536]{1,0:T(8,128)S(1)}, f32[31,1536]{1,0:T(8,128)}, u32[]{:S(2)}) copy-start(f32[31,1536]{1,0:T(8,128)} %taps_ref.3) | copy-start | bytes 571396
  2.4 26.5 %collective-permute-start.2 = (bf16[2,256,1024]{2,1,0:T(8,128)(2,1)}, bf16[2,256,1024]{2,1,0:T(8,128)(2,1)}, u32[]{:S(2)}, u32[]{:S(2)}) collective-permute-start(bf16[2,256,1024]{2,1,0:T(8,128)(2,1)} %slice.18), channel_id=1, source_target_pairs={{0,1},{1,2},{2,3},{3,4},{4,5},{5,6},{6,7},{7,8},{8,9},{9,10},{10,1... | collective-permute-start | bytes 3145736 | tf_op jit(solution)/shard_map/ppermute | solution.py:409
  6.8 33.5 %collective-permute-start.3 = (bf16[2,256,1024]{2,1,0:T(8,128)(2,1)}, bf16[2,256,1024]{2,1,0:T(8,128)(2,1)}, u32[]{:S(2)}, u32[]{:S(2)}) collective-permute-start(bf16[2,256,1024]{2,1,0:T(8,128)(2,1)} %slice.18), channel_id=1, source_target_pairs={{1,0},{2,1},{3,2},{4,3},{5,4},{6,5},{7,6},{8,7},{9,8},{10,9},{11,1... | collective-permute-start | bytes 3145736 | tf_op jit(solution)/shard_map/ppermute | solution.py:410
  13.3 35.1 %collective-permute-start = (bf16[2,256,512]{2,1,0:T(8,128)(2,1)}, bf16[2,256,512]{2,1,0:T(8,128)(2,1)S(1)}, u32[]{:S(2)}, u32[]{:S(2)}) collective-permute-start(bf16[2,256,512]{2,1,0:T(8,128)(2,1)} %slice.19), channel_id=1, source_target_pairs={{0,1},{1,2},{2,3},{3,4},{4,5},{5,6},{6,7},{7,8},{8,9},{9,10},{10,1... | collective-permute-start | bytes 1572872 | tf_op jit(solution)/shard_map/ppermute | solution.py:409
  15.2 33.2 %collective-permute-start.1 = (bf16[2,256,512]{2,1,0:T(8,128)(2,1)}, bf16[2,256,512]{2,1,0:T(8,128)(2,1)}, u32[]{:S(2)}, u32[]{:S(2)}) collective-permute-start(bf16[2,256,512]{2,1,0:T(8,128)(2,1)} %slice.19), channel_id=1, source_target_pairs={{1,0},{2,1},{3,2},{4,3},{5,4},{6,5},{7,6},{8,7},{9,8},{10,9},{11,1... | collective-permute-start | bytes 1572872 | tf_op jit(solution)/shard_map/ppermute | solution.py:410
  20.7 27.7 %copy-start.3 = (s32[2]{0:T(128)S(1)}, s32[2]{0:T(128)}, u32[]{:S(2)}) copy-start(s32[2]{0:T(128)} %add_convert_fusion.edge_ref) | copy-start | bytes 28
  48.4 1.2 copy-start.4
  54.1 11.1 %collective-permute-start.4 = (bf16[16,1536]{1,0:T(8,128)(2,1)S(1)}, bf16[16,1536]{1,0:T(8,128)(2,1)S(1)}, u32[]{:S(2)}, u32[]{:S(2)}) collective-permute-start(bf16[16,1536]{1,0:T(8,128)(2,1)S(1)} %get-tuple-element.39), channel_id=1, source_target_pairs={{0,1},{1,2},{2,3},{3,4},{4,5},{5,6},{6,7},{7,8},{8,9},{9,10},{10,1... | collective-permute-start | bytes 147464 | tf_op jit(solution)/shard_map/ppermute | solution.py:415
  56.0 9.2 %collective-permute-start.5 = (bf16[16,1536]{1,0:T(8,128)(2,1)S(1)}, bf16[16,1536]{1,0:T(8,128)(2,1)S(1)}, u32[]{:S(2)}, u32[]{:S(2)}) collective-permute-start(bf16[16,1536]{1,0:T(8,128)(2,1)S(1)} %get-tuple-element.40), channel_id=1, source_target_pairs={{1,0},{2,1},{3,2},{4,3},{5,4},{6,5},{7,6},{8,7},{9,8},{10,9},{11,1... | collective-permute-start | bytes 147464 | tf_op jit(solution)/shard_map/ppermute | solution.py:416
  87.9 20.5 %collective-permute-start.6 = (bf16[256,1536]{1,0:T(8,128)(2,1)S(1)}, bf16[256,1536]{1,0:T(8,128)(2,1)S(1)}, u32[]{:S(2)}, u32[]{:S(2)}) collective-permute-start(bf16[256,1536]{1,0:T(8,128)(2,1)S(1)} %bitcast.16), channel_id=1, source_target_pairs={{0,1},{1,2},{2,3},{3,0},{4,5},{5,6},{6,7},{7,4},{8,9},{9,10},{10,1... | collective-permute-start | bytes 2359304 | tf_op jit(solution)/shard_map/ppermute | solution.py:444
  87.9 20.5 %collective-permute-start.7 = (bf16[256,1536]{1,0:T(8,128)(2,1)S(1)}, bf16[256,1536]{1,0:T(8,128)(2,1)S(1)}, u32[]{:S(2)}, u32[]{:S(2)}) collective-permute-start(bf16[256,1536]{1,0:T(8,128)(2,1)S(1)} %bitcast.17), channel_id=1, source_target_pairs={{1,0},{2,1},{3,2},{0,3},{5,4},{6,5},{7,6},{4,7},{9,8},{10,9},{11,1... | collective-permute-start | bytes 2359304 | tf_op jit(solution)/shard_map/ppermute | solution.py:444
  108.4 11.2 %collective-permute-start.8 = (bf16[128,1536]{1,0:T(8,128)(2,1)S(1)}, bf16[128,1536]{1,0:T(8,128)(2,1)S(1)}, u32[]{:S(2)}, u32[]{:S(2)}) collective-permute-start(bf16[128,1536]{1,0:T(8,128)(2,1)S(1)} %slice.20), channel_id=1, source_target_pairs={{0,1},{1,2},{2,3},{3,0},{4,5},{5,6},{6,7},{7,4},{8,9},{9,10},{10,1... | collective-permute-start | bytes 1179656 | tf_op jit(solution)/shard_map/ppermute | solution.py:458
  108.6 11.0 %collective-permute-start.9 = (bf16[128,1536]{1,0:T(8,128)(2,1)S(1)}, bf16[128,1536]{1,0:T(8,128)(2,1)S(1)}, u32[]{:S(2)}, u32[]{:S(2)}) collective-permute-start(bf16[128,1536]{1,0:T(8,128)(2,1)S(1)} %slice.21), channel_id=1, source_target_pairs={{1,0},{2,1},{3,2},{0,3},{5,4},{6,5},{7,6},{4,7},{9,8},{10,9},{11,1... | collective-permute-start | bytes 1179656 | tf_op jit(solution)/shard_map/ppermute | solution.py:458
  111.2 25.6 %collective-permute-start.12 = (bf16[128,1536]{1,0:T(8,128)(2,1)S(1)}, bf16[128,1536]{1,0:T(8,128)(2,1)S(1)}, u32[]{:S(2)}, u32[]{:S(2)}) collective-permute-start(bf16[128,1536]{1,0:T(8,128)(2,1)S(1)} %reshape.31.own), channel_id=1, source_target_pairs={{0,1},{1,2},{2,3},{3,0},{4,5},{5,6},{6,7},{7,4},{8,9},{9,10},{10,1... | collective-permute-start | bytes 1179656 | tf_op jit(solution)/shard_map/ppermute | solution.py:444
  111.2 25.6 %collective-permute-start.13 = (bf16[128,1536]{1,0:T(8,128)(2,1)S(1)}, bf16[128,1536]{1,0:T(8,128)(2,1)S(1)}, u32[]{:S(2)}, u32[]{:S(2)}) collective-permute-start(bf16[128,1536]{1,0:T(8,128)(2,1)S(1)} %reshape.31.own), channel_id=1, source_target_pairs={{1,0},{2,1},{3,2},{0,3},{5,4},{6,5},{7,6},{4,7},{9,8},{10,9},{11,1... | collective-permute-start | bytes 1179656 | tf_op jit(solution)/shard_map/ppermute | solution.py:444
  113.9 23.2 %collective-permute-start.14 = (bf16[128,1536]{1,0:T(8,128)(2,1)S(1)}, bf16[128,1536]{1,0:T(8,128)(2,1)S(1)}, u32[]{:S(2)}, u32[]{:S(2)}) collective-permute-start(bf16[128,1536]{1,0:T(8,128)(2,1)S(1)} %reshape.31.own), channel_id=1, source_target_pairs={{0,2},{1,3},{2,0},{3,1},{4,6},{5,7},{6,4},{7,5},{8,10},{9,11},{10,... | collective-permute-start | bytes 1179656 | tf_op jit(solution)/shard_map/ppermute | solution.py:460
  134.0 18.5 %collective-permute-start.10 = (bf16[2,128,1536]{2,1,0:T(8,128)(2,1)S(1)}, bf16[2,128,1536]{2,1,0:T(8,128)(2,1)S(1)}, u32[]{:S(2)}, u32[]{:S(2)}) collective-permute-start(bf16[2,128,1536]{2,1,0:T(8,128)(2,1)S(1)} %get-tuple-element.48), channel_id=1, source_target_pairs={{0,1},{1,2},{2,3},{3,0},{4,5},{5,6},{6,7},{7,4},{8,9},{9,10},{10,1... | collective-permute-start | bytes 2359304 | tf_op jit(solution)/shard_map/ppermute | solution.py:462
  134.6 18.0 %collective-permute-start.11 = (bf16[2,128,1536]{2,1,0:T(8,128)(2,1)S(1)}, bf16[2,128,1536]{2,1,0:T(8,128)(2,1)S(1)}, u32[]{:S(2)}, u32[]{:S(2)}) collective-permute-start(bf16[2,128,1536]{2,1,0:T(8,128)(2,1)S(1)} %get-tuple-element.49), channel_id=1, source_target_pairs={{1,0},{2,1},{3,2},{0,3},{5,4},{6,5},{7,6},{4,7},{9,8},{10,9},{11,1... | collective-permute-start | bytes 2359304 | tf_op jit(solution)/shard_map/ppermute | solution.py:462
  147.0 55.6 %copy-start.5 = (f32[256]{0:T(256)S(1)}, f32[256]{0:T(256)}, u32[]{:S(2)}) copy-start(f32[256]{0:T(256)} %param.17) | copy-start | bytes 3076
  152.7 7.4 %collective-permute-start.16 = (bf16[128,1536]{1,0:T(8,128)(2,1)S(1)}, bf16[128,1536]{1,0:T(8,128)(2,1)S(1)}, u32[]{:S(2)}, u32[]{:S(2)}) collective-permute-start(bf16[128,1536]{1,0:T(8,128)(2,1)S(1)} %fusion), channel_id=1, source_target_pairs={{1,0},{2,1},{3,2},{0,3},{5,4},{6,5},{7,6},{4,7},{9,8},{10,9},{11,1... | collective-permute-start | bytes 1179656 | tf_op jit(solution)/shard_map/ppermute | solution.py:467
  153.9 7.9 %collective-permute-start.15 = (bf16[128,1536]{1,0:T(8,128)(2,1)S(1)}, bf16[128,1536]{1,0:T(8,128)(2,1)S(1)}, u32[]{:S(2)}, u32[]{:S(2)}) collective-permute-start(bf16[128,1536]{1,0:T(8,128)(2,1)S(1)} %fusion.1), channel_id=1, source_target_pairs={{0,1},{1,2},{2,3},{3,0},{4,5},{5,6},{6,7},{7,4},{8,9},{9,10},{10,1... | collective-permute-start | bytes 1179656 | tf_op jit(solution)/shard_map/ppermute | solution.py:467
  163.3 29.6 %all-to-all-start.2 = ((bf16[32,8,1536]{2,1,0:T(8,128)(2,1)}), bf16[32,8,1536]{2,1,0:T(8,128)(2,1)S(1)}, u32[]{:S(2)}, u32[]{:S(2)}) async-start(bf16[32,8,1536]{2,1,0:T(8,128)(2,1)} %bitcast.9), calls=%async_computation.2 | async-start | bytes 1572864 | tf_op jit(solution)/shard_map/all_to_all | solution.py:448
  172.6 20.3 %collective-permute-start.17 = (bf16[2,64,1536]{2,1,0:T(8,128)(2,1)}, bf16[2,64,1536]{2,1,0:T(8,128)(2,1)S(1)}, u32[]{:S(2)}, u32[]{:S(2)}) collective-permute-start(bf16[2,64,1536]{2,1,0:T(8,128)(2,1)} %get-tuple-element.59), channel_id=1, source_target_pairs={{0,1},{1,2},{2,3},{3,0},{4,5},{5,6},{6,7},{7,4},{8,9},{9,10},{10,1... | collective-permute-start | bytes 1179656 | tf_op jit(solution)/shard_map/ppermute | solution.py:470
  172.7 20.2 %collective-permute-start.18 = (bf16[2,64,1536]{2,1,0:T(8,128)(2,1)}, bf16[2,64,1536]{2,1,0:T(8,128)(2,1)S(1)}, u32[]{:S(2)}, u32[]{:S(2)}) collective-permute-start(bf16[2,64,1536]{2,1,0:T(8,128)(2,1)} %get-tuple-element.60), channel_id=1, source_target_pairs={{1,0},{2,1},{3,2},{0,3},{5,4},{6,5},{7,6},{4,7},{9,8},{10,9},{11,1... | collective-permute-start | bytes 1179656 | tf_op jit(solution)/shard_map/ppermute | solution.py:471
  175.4 17.5 %collective-permute-start.19 = (bf16[2,64,1536]{2,1,0:T(8,128)(2,1)S(1)}, bf16[2,64,1536]{2,1,0:T(8,128)(2,1)S(1)}, u32[]{:S(2)}, u32[]{:S(2)}) collective-permute-start(bf16[2,64,1536]{2,1,0:T(8,128)(2,1)S(1)} %get-tuple-element.61), channel_id=1, source_target_pairs={{0,2},{1,3},{2,0},{3,1},{4,6},{5,7},{6,4},{7,5},{8,10},{9,11},{10,... | collective-permute-start | bytes 1179656 | tf_op jit(solution)/shard_map/ppermute | solution.py:472
  194.1 18.6 %all-to-all-start.3 = ((bf16[32,4,1536]{2,1,0:T(4,128)(2,1)}), bf16[32,4,1536]{2,1,0:T(4,128)(2,1)S(1)}, u32[]{:S(2)}, u32[]{:S(2)}) async-start(bf16[32,4,1536]{2,1,0:T(4,128)(2,1)} %reshape.34), calls=%async_computation.3 | async-start | bytes 786432 | tf_op jit(solution)/shard_map/all_to_all | solution.py:448
